TPU v7x, 32 devices: a whole 2x2x4 slice. The times are simulated.
32 devices in a mesh: section: 2 (over core), dp: 4 (over y, x), ctx: 4 (over z).
Axes of the slice: x: 2, y: 2, z: 4, core: 2. Of those that a mesh axis runs over, the one named last changes fastest.
Arguments:
- ends: bfloat16 [2, 8, 1024, 768], P('section', 'dp', 'ctx'), may hold values from -6 to 6
- char_ends: bfloat16 [2, 8, 2048, 768], P('section', 'dp', 'ctx'), may hold values from -6 to 6
- char_ids: int32 [8, 2048], P('dp', 'ctx'), may hold values from 0 to 999
- groups: int32 [8, 2048], P('dp', 'ctx'), may hold values from -1 to 1023, as said below
- lengths: int32 [8], P('dp'), may hold values from 512 to 1024, as said below
- w_qkv: bfloat16 [2, 768, 2304], P('section'), may hold values from -0.21875 to 0.21875
- biases: float32 [2, 5, 768], P('section'), may hold values from -2 to 2
- w_out: bfloat16 [2, 768, 768], P('section'), may hold values from -1.75 to 1.75
- w_up: bfloat16 [2, 768, 3072], P('section'), may hold values from -0.21875 to 0.21875
- b_up: float32 [2, 3072], P('section'), may hold values from -2 to 2
- w_down: bfloat16 [2, 3072, 768], P('section'), may hold values from -0.109375 to 0.109375
- ln_gain: float32 [2, 4, 768], P('section'), may hold values from 0.5 to 1.5
- ln_shift: float32 [2, 4, 768], P('section'), may hold values from -1.2 to 1.2
- char_table: bfloat16 [2, 1000, 768], P('section'), may hold values from -3 to 3
- w_gru: bfloat16 [2, 768, 1536], P('section'), may hold values from -0.21875 to 0.21875
- b_gru: float32 [2, 1536], P('section')
- w_conv: bfloat16 [2, 3, 1536, 768], P('section'), may hold values from -0.09375 to 0.09375
Outputs:
- ends_out: bfloat16 [2, 8, 1024, 768], P('section', 'dp', 'ctx')
- char_ends_out: bfloat16 [2, 8, 2048, 768], P('section', 'dp', 'ctx')
- grad_w_qkv: float32 [2, 768, 2304], P('section', ('dp', 'ctx'))
- grad_biases: float32 [2, 5, 768], P('section', None, ('dp', 'ctx'))
- grad_w_out: float32 [2, 768, 768], P('section', ('dp', 'ctx'))
- grad_w_up: float32 [2, 768, 3072], P('section', ('dp', 'ctx'))
- grad_b_up: float32 [2, 3072], P('section', ('dp', 'ctx'))
- grad_w_down: float32 [2, 3072, 768], P('section', ('dp', 'ctx'))
- grad_ln_gain: float32 [2, 4, 768], P('section', None, ('dp', 'ctx'))
- grad_ln_shift: float32 [2, 4, 768], P('section', None, ('dp', 'ctx'))
- grad_char_table: float32 [2, 1000, 768], P('section', None, ('dp', 'ctx'))
- grad_w_gru: float32 [2, 768, 1536], P('section', ('dp', 'ctx'))
- grad_b_gru: float32 [2, 1536], P('section', ('dp', 'ctx'))
- grad_w_conv: float32 [2, 3, 1536, 768], P('section', None, ('dp', 'ctx'))
Inputs may be any that keep to these rules, and one draw needn't show every extreme that they name: `groups`: slots 512 * k to 512 * (k + 1) - 1 of a sequence hold, in order, the chars of its tokens 256 * k to 256 * (k + 1) - 1, each token 1 to 2 slots and some token of each such block 2, followed by empty slots (-1). `lengths`: in each aligned block of 2 sequences one has length 1024.
All inputs are finite; a program needn't handle non-finite values.
Results may differ from a plain program's by a relative error of at most 0.015.
Values may be sent and summed in bfloat16 or wider, within the bound.
A program may use at most 384 MiB of HBM per device.

v0:
```python
import functools

import jax
import jax.numpy as jnp
from jax import lax
from jax.experimental import pallas as pl
from jax.experimental.pallas import tpu as pltpu
from jax.sharding import PartitionSpec as P

HEADS = 12
CHUNKS = 8
NORM_EPS = 1e-06
MASKED = -1000000000.0
SEC, DP, CTX = "section", "dp", "ctx"
F32, BF16 = jnp.float32, jnp.bfloat16
MIB = 2**20


def contract(left, right, dims):
    return lax.dot_general(left, right, (dims, ((), ())), preferred_element_type=F32)


def mm(left, right):
    return contract(left, right, ((1,), (0,)))


def mt(left, right):
    return contract(left, right, ((1,), (1,)))


def tm(left, right):
    return contract(left, right, ((0,), (0,)))


def flip(value, axis, bit):
    return lax.ppermute(value, axis, [(i, i ^ (1 << bit)) for i in range(lax.axis_size(axis))])


def swap(value):
    return flip(value, SEC, 0)


def turned(value, by):
    count = lax.axis_size(CTX)
    return lax.ppermute(value, CTX, [(i, (i + by) % count) for i in range(count)])


def handed(value, by):
    count = lax.axis_size(CTX)
    return lax.ppermute(value, CTX, [(i, i + by) for i in range(count) if 0 <= i + by < count])


def pick(value, index, axis=0):
    return lax.dynamic_index_in_dim(value, index, axis, keepdims=False)


def interleave(value):
    rows = value.shape[0]
    return jnp.swapaxes(
        value.reshape((CHUNKS, rows // CHUNKS) + value.shape[1:]), 0, 1
    ).reshape(value.shape)


def restore(value):
    rows = value.shape[0]
    return jnp.swapaxes(
        value.reshape((rows // CHUNKS, CHUNKS) + value.shape[1:]), 0, 1
    ).reshape(value.shape)


def norm_parts(values):
    centred = values - jnp.mean(values, axis=-1, keepdims=True)
    scale = lax.rsqrt(jnp.mean(centred * centred, axis=-1, keepdims=True) + NORM_EPS)
    return centred * scale, scale


def layer_norm(values, gain, shift):
    return norm_parts(values)[0] * gain + shift


def norm_back(values, gain, grad):
    unit, scale = norm_parts(values)
    inner = grad * gain
    mean = jnp.mean(inner, axis=-1, keepdims=True)
    along = jnp.mean(inner * unit, axis=-1, keepdims=True)
    return scale * (inner - mean - unit * along), jnp.sum(grad * unit, axis=0), jnp.sum(grad, axis=0)


def gelu(values):
    return jax.nn.gelu(values, approximate=False)


def gelu_slope(values):
    cdf = 0.5 * (1.0 + lax.erf(values * (0.5**0.5)))
    return cdf + values * jnp.exp(-0.5 * values * values) * 0.3989422804014327


def column_sums(values):
    return jnp.sum(values.astype(F32), axis=0)


def params(mib):
    return pltpu.CompilerParams(vmem_limit_bytes=mib * MIB)


def attend_kernel(size, q_ref, k_ref, v_ref, seen_ref, out_ref, lse_ref):
    seen = seen_ref[...] > 0.0
    for head in range(q_ref.shape[1] // size):
        at = slice(head * size, (head + 1) * size)
        scores = mt(k_ref[:, at], q_ref[:, at]) * (size**-0.5)
        scores = jnp.where(seen, scores, MASKED)
        top = jnp.max(scores, axis=0, keepdims=True)
        weights = jnp.exp(scores - top)
        total = jnp.sum(weights, axis=0, keepdims=True)
        probs = (weights * (1.0 / total)).astype(BF16)
        out_ref[:, at] = tm(probs, v_ref[:, at]).astype(BF16)
        lse_ref[0, head : head + 1, :] = top + jnp.log(total)


def attend(query, keys, values, seen):
    rows, width = query.shape
    count = keys.shape[0]
    size = width // HEADS
    block = 2 * size
    steps = width // block
    return pl.pallas_call(
        functools.partial(attend_kernel, size),
        grid=(steps,),
        in_specs=[
            pl.BlockSpec((rows, block), lambda i: (0, i)),
            pl.BlockSpec((count, block), lambda i: (0, i)),
            pl.BlockSpec((count, block), lambda i: (0, i)),
            pl.BlockSpec((count, 1), lambda i: (0, 0)),
        ],
        out_specs=[
            pl.BlockSpec((rows, block), lambda i: (0, i)),
            pl.BlockSpec((1, 8, rows), lambda i: (i, 0, 0)),
        ],
        out_shape=[
            jax.ShapeDtypeStruct((rows, width), BF16),
            jax.ShapeDtypeStruct((steps, 8, rows), F32),
        ],
        compiler_params=params(40),
        cost_estimate=pl.CostEstimate(
            flops=4 * rows * count * width * 2, bytes_accessed=6 * count * width, transcendentals=0
        ),
    )(query, keys, values, seen)


def attend_back_kernel(
    size, q_ref, k_ref, v_ref, seen_ref, lse_ref, do_ref, dq_ref, dk_ref, dv_ref
):
    seen = seen_ref[...] > 0.0
    scale = size**-0.5
    for head in range(q_ref.shape[1] // size):
        at = slice(head * size, (head + 1) * size)
        query, keys, grad = q_ref[:, at], k_ref[:, at], do_ref[:, at]
        scores = jnp.where(seen, mt(keys, query) * scale, MASKED)
        probs = jnp.exp(scores - lse_ref[0, head : head + 1, :])
        g_probs = mt(v_ref[:, at], grad)
        row = jnp.sum(g_probs * probs, axis=0, keepdims=True)
        g_scores = (probs * (g_probs - row)).astype(BF16)
        dv_ref[:, at] = mm(probs.astype(BF16), grad).astype(BF16)
        dk_ref[:, at] = (mm(g_scores, query) * scale).astype(BF16)
        dq_ref[:, at] = (tm(g_scores, keys) * scale).astype(BF16)


def attend_back(query, keys, values, seen, lse, grad):
    rows, width = query.shape
    count = keys.shape[0]
    size = width // HEADS
    block = 2 * size
    steps = width // block
    by_rows = pl.BlockSpec((rows, block), lambda i: (0, i))
    by_keys = pl.BlockSpec((count, block), lambda i: (0, i))
    return pl.pallas_call(
        functools.partial(attend_back_kernel, size),
        grid=(steps,),
        in_specs=[
            by_rows,
            by_keys,
            by_keys,
            pl.BlockSpec((count, 1), lambda i: (0, 0)),
            pl.BlockSpec((1, 8, rows), lambda i: (i, 0, 0)),
            by_rows,
        ],
        out_specs=[by_rows, by_keys, by_keys],
        out_shape=[
            jax.ShapeDtypeStruct((rows, width), BF16),
            jax.ShapeDtypeStruct((count, width), BF16),
            jax.ShapeDtypeStruct((count, width), BF16),
        ],
        compiler_params=params(40),
        cost_estimate=pl.CostEstimate(
            flops=10 * rows * count * width * 2, bytes_accessed=12 * count * width, transcendentals=0
        ),
    )(query, keys, values, seen, lse, grad)


def gate_at(proj_ref, live_ref, at, rate, width):
    live = live_ref[at, :] > 0.0
    opened = jax.nn.sigmoid(proj_ref[at, rate : rate + width])
    return jnp.where(live, 1.0 - opened, 1.0), live, opened


def scan_kernel(proj_ref, live_ref, state_ref, decay_ref, carry_ref, total_ref):
    rows = proj_ref.shape[0]
    width = proj_ref.shape[1] // 4
    steps = rows // CHUNKS
    unroll = 8

    def step(i, carry):
        state_f, decay_f, state_b, decay_b = carry
        for u in range(unroll):
            at = pl.ds(pl.multiple_of((i * unroll + u) * CHUNKS, CHUNKS), CHUNKS)
            keep, live, opened = gate_at(proj_ref, live_ref, at, 0, width)
            inflow = jnp.where(live, opened * proj_ref[at, width : 2 * width], 0.0)
            state_f = keep * state_f + inflow
            decay_f = keep * decay_f
            state_ref[at, 0:width] = state_f
            decay_ref[at, 0:width] = decay_f
            at = pl.ds(pl.multiple_of((steps - 1 - i * unroll - u) * CHUNKS, CHUNKS), CHUNKS)
            keep, live, opened = gate_at(proj_ref, live_ref, at, 2 * width, width)
            inflow = jnp.where(live, opened * proj_ref[at, 3 * width : 4 * width], 0.0)
            state_b = keep * state_b + inflow
            decay_b = keep * decay_b
            state_ref[at, width : 2 * width] = state_b
            decay_ref[at, width : 2 * width] = decay_b
        return state_f, decay_f, state_b, decay_b

    zero = jnp.zeros((CHUNKS, width), F32)
    one = jnp.ones((CHUNKS, width), F32)
    state_f, decay_f, state_b, decay_b = lax.fori_loop(
        0, steps // unroll, step, (zero, one, zero, one)
    )
    join_chunks(carry_ref, total_ref, 0, state_f, decay_f, range(CHUNKS))
    join_chunks(carry_ref, total_ref, 2, state_b, decay_b, range(CHUNKS - 1, -1, -1))


def join_chunks(carry_ref, total_ref, slot, state, decay, order):
    width = state.shape[1]
    before = jnp.zeros((1, width), F32)
    faded = jnp.ones((1, width), F32)
    for chunk in order:
        carry_ref[slot, chunk : chunk + 1, :] = before
        carry_ref[slot + 1, chunk : chunk + 1, :] = faded
        own = decay[chunk : chunk + 1, :]
        before = own * before + state[chunk : chunk + 1, :]
        faded = own * faded
    total_ref[slot : slot + 1, :] = before
    total_ref[slot + 1 : slot + 2, :] = faded
    if slot:
        total_ref[4:8, :] = jnp.zeros((4, width), F32)


def scan_back_kernel(grad_ref, proj_ref, live_ref, state_ref, decay_ref, carry_ref, total_ref):
    rows = proj_ref.shape[0]
    width = proj_ref.shape[1] // 4
    steps = rows // CHUNKS
    unroll = 8

    def step(i, carry):
        state_f, decay_f, state_b, decay_b = carry
        for u in range(unroll):
            at = pl.ds(pl.multiple_of((steps - 1 - i * unroll - u) * CHUNKS, CHUNKS), CHUNKS)
            keep = gate_at(proj_ref, live_ref, at, 0, width)[0]
            whole = grad_ref[at, 0:width] + state_f
            state_ref[at, 0:width] = whole
            decay_ref[at, 0:width] = decay_f
            state_f = keep * whole
            decay_f = keep * decay_f
            at = pl.ds(pl.multiple_of((i * unroll + u) * CHUNKS, CHUNKS), CHUNKS)
            keep = gate_at(proj_ref, live_ref, at, 2 * width, width)[0]
            whole = grad_ref[at, width : 2 * width] + state_b
            state_ref[at, width : 2 * width] = whole
            decay_ref[at, width : 2 * width] = decay_b
            state_b = keep * whole
            decay_b = keep * decay_b
        return state_f, decay_f, state_b, decay_b

    zero = jnp.zeros((CHUNKS, width), F32)
    one = jnp.ones((CHUNKS, width), F32)
    state_f, decay_f, state_b, decay_b = lax.fori_loop(
        0, steps // unroll, step, (zero, one, zero, one)
    )
    join_chunks(carry_ref, total_ref, 0, state_f, decay_f, range(CHUNKS - 1, -1, -1))
    join_chunks(carry_ref, total_ref, 2, state_b, decay_b, range(CHUNKS))


def scan_call(kernel, width, *arrays):
    rows = arrays[0].shape[0]
    return pl.pallas_call(
        kernel,
        out_shape=[
            jax.ShapeDtypeStruct((rows, 2 * width), F32),
            jax.ShapeDtypeStruct((rows, 2 * width), F32),
            jax.ShapeDtypeStruct((4, CHUNKS, width), F32),
            jax.ShapeDtypeStruct((8, width), F32),
        ],
        compiler_params=params(40),
        cost_estimate=pl.CostEstimate(
            flops=rows * width * 200, bytes_accessed=rows * width * 32, transcendentals=0
        ),
    )(*arrays)


def joined_scan(kernel, width, place, arrays, reverse):
    state, decay, carry, total = scan_call(kernel, width, *arrays)
    count = lax.axis_size(CTX)
    others = {j: turned(total, j) for j in range(1, count)}
    zero = jnp.zeros((1, width), F32)
    entering = []
    for slot in (0, 2):
        so_far = zero
        rising = (slot == 0) != reverse
        for hop in range(count - 1, 0, -1):
            there = others[hop] if rising else others[count - hop]
            valid = (place >= hop) if rising else (place + hop < count)
            so_far = jnp.where(
                valid, there[slot + 1 : slot + 2] * so_far + there[slot : slot + 1], so_far
            )
        entering.append(carry[slot] + carry[slot + 1] * so_far)
    entering = jnp.concatenate(entering, axis=1)
    shape = (state.shape[0] // CHUNKS, CHUNKS, 2 * width)
    whole = state.reshape(shape) + decay.reshape(shape) * entering[None]
    return whole.reshape(state.shape), entering


def layer_forward(w, x, chars_in, ids, live, onehot, counts, seen, place):
    rows, width = x.shape
    n_ctx = lax.axis_size(CTX)
    x_all = jnp.concatenate([x] + [turned(x, j) for j in range(1, n_ctx)], axis=0)
    named = (ids[:, None] == jnp.arange(w["table"].shape[0])[None, :]).astype(BF16)
    chars = chars_in.astype(F32) + mm(named, w["table"])
    chars_low = chars.astype(BF16)
    proj = mm(chars_low, w["gru"]) + w["b_gru"]
    half = proj.shape[1] // 4
    states, entering = joined_scan(scan_kernel, half, place, (proj, live), False)
    pooled = mm(onehot, states.astype(BF16)) / counts
    biases, gains, shifts = w["biases"], w["gains"], w["shifts"]
    query = (mm(x, w["qkv"][:, :width]) + biases[0]).astype(BF16)
    keys = mm(x_all, w["qkv"][:, width : 2 * width]).astype(BF16)
    values = (mm(x_all, w["qkv"][:, 2 * width :]) + biases[1]).astype(BF16)
    attended, lse = attend(query, keys, values, seen)
    first = x.astype(F32) + mm(attended, w["out"]) + biases[2]
    normed = layer_norm(first, gains[0], shifts[0])
    normed_low = normed.astype(BF16)
    hidden = mm(normed_low, w["up"]) + w["b_up"]
    active = gelu(hidden).astype(BF16)
    second = normed + mm(active, w["down"]) + biases[3]
    features = layer_norm(second, gains[1], shifts[1])
    joined = jnp.concatenate([features, pooled], axis=1).astype(BF16)
    three = three_taps(joined, 1)
    conv = w["conv"]
    mixed = mm(three, conv.reshape(-1, width)) + biases[4]
    lifted = gelu(mixed)
    tok_sum = features + lifted
    chr_sum = chars + states + tm(onehot, lifted.astype(BF16))
    tok_out = layer_norm(tok_sum, gains[2], shifts[2]).astype(BF16)
    chr_out = layer_norm(chr_sum, gains[3], shifts[3]).astype(BF16)
    saved = dict(
        x=x, x_all=x_all, query=query, keys=keys, values=values, lse=lse, attended=attended,
        first=first, normed_low=normed_low, hidden=hidden, active=active, second=second,
        chars_low=chars_low, proj=proj, states=states, entering=entering, three=three,
        mixed=mixed, tok_sum=tok_sum, chr_sum=chr_sum,
    )
    return tok_out, chr_out, saved


def three_taps(values, step):
    before = handed(values[-1:], 1)
    after = handed(values[:1], -1)
    lower = jnp.concatenate([before, values[:-1]], axis=0)
    upper = jnp.concatenate([values[1:], after], axis=0)
    return jnp.concatenate([lower, values, upper][::step], axis=1)


class Halves:
    def __init__(self, section):
        self.section = section

    def inputs(self, values):
        return jnp.concatenate([values, swap(values)], axis=0)

    def grads(self, values):
        half = values.shape[1] // 2
        sent = lax.dynamic_slice_in_dim(values, (1 - self.section) * half, half, 1)
        kept = lax.dynamic_slice_in_dim(values, self.section * half, half, 1)
        return jnp.concatenate([kept, swap(sent)], axis=0)


def bits_of(axis):
    return [(axis, bit) for bit in range(lax.axis_size(axis).bit_length() - 1)]


def reduce_scattered(pairs, lead, order):
    layout = bits_of(DP)[::-1] + bits_of(CTX)[::-1]
    rows = pairs[0][0].shape[1]

    def split(value, key, axis):
        place = layout.index(key)
        shape = value.shape
        outer = lead * 2**place
        view = value.reshape(shape[:axis] + (outer, 2, shape[axis] // (2 * outer)) + shape[axis + 1 :])
        mine = (lax.axis_index(key[0]) >> key[1]) & 1
        less = shape[:axis] + (shape[axis] // 2,) + shape[axis + 1 :]
        return [pick(view, side, axis + 1).reshape(less) for side in (mine, 1 - mine)]

    total = None
    for count, key in enumerate(order):
        if count == 0:
            kept, sent = [], []
            for left, right in pairs:
                mine, other = split(left, key, 1)
                kept.append(tm(mine, right))
                sent.append(tm(other, right))
            kept, sent = (v[0] if len(v) == 1 else jnp.concatenate(v, axis=1) for v in (kept, sent))
        else:
            kept, sent = split(total, key, 0)
        layout_next = [k for k in layout if k != key]
        total = kept.astype(F32) + flip(sent.astype(BF16), *key).astype(F32)
        if count < len(order) - 1:
            total = total.astype(BF16)
        layout = layout_next
    return total


def layer_backward(w, saved, g_tok, g_chr, ids, ids_other, live, onehot, counts, seen, place, halves):
    g_tok, g_chr = g_tok.astype(F32), g_chr.astype(F32)
    rows, width = g_tok.shape
    gains = w["gains"]
    n_ctx = lax.axis_size(CTX)
    x_first = bits_of(DP) + bits_of(CTX)
    y_first = bits_of(DP)[::-1] + bits_of(CTX)
    made = {}
    d_tok, gain3, shift3 = norm_back(saved["tok_sum"], gains[2], g_tok)
    d_chr, gain4, shift4 = norm_back(saved["chr_sum"], gains[3], g_chr)
    d_lifted = d_tok + mm(onehot, d_chr.astype(BF16))
    d_mixed = (d_lifted * gelu_slope(saved["mixed"])).astype(BF16)
    made["conv"] = reduce_scattered(
        [(halves.inputs(saved["three"]), halves.grads(d_mixed))], w["conv"].shape[0], x_first
    )
    around = three_taps(d_mixed, -1)
    conv = w["conv"]
    d_joined = mt(around[:, :width], conv[0])
    for tap in range(1, conv.shape[0]):
        d_joined = d_joined + mt(around[:, tap * width : (tap + 1) * width], conv[tap])
    d_feat = d_tok + d_joined[:, :width]
    d_second, gain2, shift2 = norm_back(saved["second"], gains[1], d_feat)
    d_ffn = d_second.astype(BF16)
    made["down"] = reduce_scattered([(halves.inputs(saved["active"]), halves.grads(d_ffn))], 1, y_first)
    d_hidden = (mt(d_ffn, w["down"]) * gelu_slope(saved["hidden"])).astype(BF16)
    made["up"] = reduce_scattered(
        [(halves.inputs(saved["normed_low"]), halves.grads(d_hidden))], 1, x_first
    )
    d_normed = d_second + mt(d_hidden, w["up"])
    d_first, gain1, shift1 = norm_back(saved["first"], gains[0], d_normed)
    d_branch = d_first.astype(BF16)
    made["out"] = reduce_scattered(
        [(halves.inputs(saved["attended"]), halves.grads(d_branch))], 1, y_first
    )
    d_attended = mt(d_branch, w["out"]).astype(BF16)
    dq, dk, dv = attend_back(
        saved["query"], saved["keys"], saved["values"], seen, saved["lse"], d_attended
    )
    wide = halves.inputs(saved["x_all"])
    made["qkv"] = reduce_scattered(
        [
            (halves.inputs(saved["x"]), halves.grads(dq)),
            (wide, halves.grads(dk)),
            (wide, halves.grads(dv)),
        ],
        1,
        y_first,
    )
    qkv = w["qkv"]
    parts = mt(dk, qkv[:, width : 2 * width]) + mt(dv, qkv[:, 2 * width :])
    d_x = d_first + mt(dq, qkv[:, :width]) + parts[:rows]
    for j in range(1, n_ctx):
        d_x = d_x + turned(parts[j * rows : (j + 1) * rows].astype(BF16), n_ctx - j).astype(F32)
    d_pool = (d_joined[:, width:] / counts).astype(BF16)
    d_states = d_chr + tm(onehot, d_pool)
    proj, states, entering = saved["proj"], saved["states"], saved["entering"]
    half = proj.shape[1] // 4
    whole, _ = joined_scan(scan_back_kernel, half, place, (d_states, proj, live), True)
    pieces = []
    for side in (0, 1):
        at = slice(side * half, (side + 1) * half)
        if side == 0:
            before = jnp.concatenate([entering[:, at], states[:-CHUNKS, at]], axis=0)
        else:
            before = jnp.concatenate([states[CHUNKS:, at], entering[:, at]], axis=0)
        opened = jax.nn.sigmoid(proj[:, 2 * side * half : (2 * side + 1) * half])
        target = proj[:, (2 * side + 1) * half : (2 * side + 2) * half]
        flow = jnp.where(live > 0.0, whole[:, at] * opened, 0.0)
        pieces += [flow * (1.0 - opened) * (target - before), flow]
    d_proj = jnp.concatenate(pieces, axis=1).astype(BF16)
    made["gru"] = reduce_scattered(
        [(halves.inputs(saved["chars_low"]), halves.grads(d_proj))], 1, y_first
    )
    d_c = (d_chr + mt(d_proj, w["gru"])).astype(BF16)
    vocab = -(-w["table"].shape[0] // 256) * 256
    names = jnp.concatenate([ids, ids_other])[:, None] - halves.section * (vocab // 2)
    named = (names == jnp.arange(vocab // 2)[None, :]).astype(BF16)
    made["table"] = reduce_scattered([(halves.inputs(d_c), named)], 1, x_first)
    small = (
        jnp.stack(
            [column_sums(dq), column_sums(dv), column_sums(d_branch), column_sums(d_ffn), column_sums(d_mixed)]
        ),
        column_sums(d_hidden)[None],
        jnp.stack([gain1, gain2, gain3, gain4]),
        jnp.stack([shift1, shift2, shift3, shift4]),
        column_sums(d_proj)[None],
    )
    return d_x.astype(BF16), d_c, made, small


def on_device(
    ends, char_ends, char_ids, groups, lengths, w_qkv, biases, w_out, w_up, b_up, w_down,
    ln_gain, ln_shift, char_table, w_gru, b_gru, w_conv,
):
    section, place = lax.axis_index(SEC), lax.axis_index(CTX)
    n_dp, n_ctx = lax.axis_size(DP), lax.axis_size(CTX)
    is_first = section == 0
    names = ("gru", "table", "qkv", "out", "up", "down", "conv", "biases", "b_up", "gains", "shifts", "b_gru")
    local = (w_gru, char_table, w_qkv, w_out, w_up, w_down, w_conv, biases, b_up, ln_gain, ln_shift, b_gru)
    chars_here = jax.vmap(interleave)(char_ends[0])

    def dealt(pair):
        kept = pick(pair, section)
        got = swap(pick(pair, 1 - section))
        return jnp.where(is_first, kept, got), jnp.where(is_first, got, kept)

    x, cot_tok = dealt(ends[0])
    c, cot_chr = dealt(chars_here)
    layers = ({}, {})
    for name, value in zip(names, local):
        own = value[0]
        other = swap(own)
        layers[0][name] = jnp.where(is_first, own, other)
        layers[1][name] = jnp.where(is_first, other, own)
    rows = x.shape[0]
    ids = interleave(pick(char_ids, section))
    ids_other = interleave(pick(char_ids, 1 - section))
    group = interleave(pick(groups, section))
    live = (group >= 0).astype(F32)[:, None]
    onehot = jnp.arange(rows)[:, None] == (group - place * rows)[None, :]
    counts = jnp.sum(onehot.astype(F32), axis=1, keepdims=True)
    onehot = onehot.astype(BF16)
    shard = jnp.mod(place - jnp.arange(n_ctx), n_ctx)
    spots = (shard[:, None] * rows + jnp.arange(rows)[None, :]).reshape(-1, 1)
    seen = (spots < pick(lengths, section)).astype(F32)

    kept = []
    for layer in (0, 1):
        x, c, saved = layer_forward(layers[layer], x, c, ids, live, onehot, counts, seen, place)
        kept.append(saved)
    g_x, g_c = cot_tok, cot_chr
    halves = Halves(section)
    made, small = [None, None], [None, None]
    for layer in (1, 0):
        g_x, g_c, made[layer], small[layer] = layer_backward(
            layers[layer], kept[layer], g_x, g_c, ids, ids_other, live, onehot, counts, seen, place, halves
        )

    def gathered(grad, value):
        got = swap(jnp.where(is_first, value, grad))
        return jnp.where(is_first, jnp.stack([grad, got]), jnp.stack([got, value]))[None]

    ends_out = gathered(g_x, x)
    char_ends_out = gathered(restore(g_c), restore(c))

    whole = {}
    for name in made[0]:
        mine = jnp.where(is_first, made[0][name], made[1][name])
        got = swap(jnp.where(is_first, made[1][name], made[0][name]))
        whole[name] = (jnp.where(is_first, mine, got), jnp.where(is_first, got, mine))

    def sided(name):
        return jnp.concatenate(whole[name], axis=1)

    d_qkv = jnp.concatenate(
        [
            half[:, part * half.shape[1] // 3 : (part + 1) * half.shape[1] // 3]
            for part in range(3)
            for half in whole["qkv"]
        ],
        axis=1,
    )
    d_conv = sided("conv")
    d_conv = d_conv.reshape(w_conv.shape[1], -1, d_conv.shape[1])
    d_table = sided("table")[:, : char_table.shape[1]].T

    devices = n_dp * n_ctx

    def by_device(parts):
        return jnp.concatenate(
            [jnp.swapaxes(p.reshape(p.shape[0], devices, -1), 0, 1).reshape(devices, -1) for p in parts],
            axis=1,
        )

    packed = [by_device(parts) for parts in small]
    total = jnp.where(is_first, packed[0], packed[1]) + swap(jnp.where(is_first, packed[1], packed[0]))
    for key in bits_of(DP)[::-1] + bits_of(CTX)[::-1]:
        view = total.reshape(2, -1, total.shape[1])
        mine = (lax.axis_index(key[0]) >> key[1]) & 1
        total = pick(view, mine) + flip(pick(view, 1 - mine), *key)
    sums, at = [], 0
    for parts in small[0]:
        size = parts.size // devices
        sums.append(total[0, at : at + size].reshape(parts.shape[0], -1))
        at += size
    return (
        ends_out,
        char_ends_out,
        d_qkv[None],
        sums[0][None],
        sided("out")[None],
        sided("up")[None],
        sums[1],
        sided("down")[None],
        sums[2][None],
        sums[3][None],
        d_table[None],
        sided("gru")[None],
        sums[4],
        d_conv[None],
    )


def solution(mesh):
    both = (DP, CTX)
    held, rows, columns = P(SEC, DP, CTX), P(SEC, both), P(SEC, None, both)
    layer = P(SEC)
    in_specs = (held, held, P(DP, CTX), P(DP, CTX), P(DP)) + (layer,) * 12
    out_specs = (
        held, held, rows, columns, rows, rows, rows, rows, columns, columns, columns, rows, rows, columns,
    )
    return jax.shard_map(
        on_device, mesh=mesh, in_specs=in_specs, out_specs=out_specs, check_vma=False
    )
```

profile of v0, /device:TPU:1, one launch (start us, length us, event | category | flops | bytes accessed | tf_op | source)
XLA Modules:
  0.0 1155.5 jit_solution(17316716363639307710)
XLA Ops:
  21.9 4.8 collective-permute-start.5
  29.0 6.1 collective-permute-done.5
  41.1 4.0 fusion.397
  45.1 17.6 %collective-permute-done.4 = bf16[256,768]{1,0:T(8,128)(2,1)S(1)} collective-permute-done((bf16[256,768]{1,0:T(8,128)(2,1)S(1)}, bf16[256,768]{1,0:T(8,128)(2,1)S(1)}, u32[]{:S(2)}, u32[]{:S(2)}) %collective-permute-start.4) | collective-permute-done | bytes 393248 | tf_op jit(solution)/shard_map/ppermute | solution.py:45
  73.6 4.9 constant_dynamic-slice_fusion.31
  90.6 7.4 reshape.1223
  98.0 10.0 constant_dynamic-slice_fusion.103
  113.5 4.2 broadcast_select_fusion.6
  122.0 13.7 %shard_map.272 = (bf16[256,768]{1,0:T(8,128)(2,1)S(1)}, f32[6,8,256]{2,1,0:T(8,128)S(1)}) custom-call(bf16[256,768]{1,0:T(8,128)(2,1)S(1)} %fusion.103.q_ref, bf16[1024,768]{1,0:T(8,128)(2,1)S(1)} %convolution_convert_fusion.7.k_ref, bf16[1024,768]{1,0:T(8,128)(2,1)S(1)} %add_convert_fusion.1.v_ref, f32[1024,1]{1,0:T(8,128)S(1)} %bitcast.736), custom_call_target="tpu_custom_call" | custom-call | flops 1610612736 | bytes 4718592 | tf_op jit(solution)/shard_map/pallas_call | solution.py:126
  147.7 11.8 %fusion.6 = (bf16[256,3072]{1,0:T(8,128)(2,1)S(1)}, f32[256,3072]{1,0:T(8,128)}) fusion(f32[3072]{0:T(1024)S(1)} %get-tuple-element.332, bf16[256,768]{1,0:T(8,128)(2,1)S(1)} %fusion.214, bf16[768,3072]{1,0:T(8,128)(2,1)} %collective-permute-done.9, pred[]{:T(512)S(6)} %eq.24, bf16[1,768,3072]{2,1,0:T(8,128)(2,1)} %param.25), kind=kOutput, calls=%fused_computation.30 | convolution fusion | flops 1262223360 | bytes 14561281 | tf_op jit(solution)/shard_map/dot_general | solution.py:20
  175.0 7.1 reshape.1290
  182.0 9.0 constant_dynamic-slice_fusion.52
  191.1 8.3 broadcast_select_fusion
  199.5 8.2 fusion.384
  229.3 14.5 %pad_maximum_fusion = bf16[512,4608]{1,0:T(8,128)(2,1)} fusion(bf16[256,4608]{1,0:T(8,128)(2,1)} %collective-permute-done.135, bf16[1,1536]{1,0:T(2,128)(2,1)S(1)} %collective-permute-done.20, bf16[255,1536]{1,0:T(8,128)(2,1)S(1)} %copy-done.69, bf16[256,768]{1,0:T(8,128)(2,1)S(1)} %copy-done.74, bf16[256,768]{1,0:T(8,128)(2,1)S(1)} %copy-done.53, ...), kind=kLoop, calls=%fused_computation.6 | loop fusion | flops 33030144 | bytes 9437184 | tf_op jit(solution)/shard_map/concatenate | solution.py:383
  243.8 7.2 reshape.1345
  251.0 12.4 %constant_dynamic-slice_fusion.16 = (bf16[512,6,1,384]{3,2,1,0:T(2,128)(2,1)}, bf16[512,6,1,384]{3,2,1,0:T(2,128)(2,1)}) fusion(bf16[512,6,2,384]{3,2,1,0:T(2,128)(2,1)} %reshape.1345, s32[]{:T(128)S(6)} %select_n.820, s32[]{:T(128)S(6)} %select_n.819), kind=kLoop, calls=%fused_computation.679 | loop fusion | bytes 9437192 | tf_op jit(solution)/shard_map/jit(dynamic_index_in_dim)/dynamic_slice | solution.py:54
  263.4 11.7 %copy.200 = bf16[512,6,1,384]{0,3,1,2:T(8,128)(2,1)} copy(bf16[512,6,1,384]{3,2,1,0:T(2,128)(2,1)} %get-tuple-element.183) | data formatting | bytes 4718592
  275.0 11.6 %copy.201 = bf16[512,6,1,384]{0,3,1,2:T(8,128)(2,1)} copy(bf16[512,6,1,384]{3,2,1,0:T(2,128)(2,1)} %get-tuple-element.182) | data formatting | bytes 4718592
  302.0 14.4 %shard_map.274 = (bf16[256,768]{1,0:T(8,128)(2,1)}, f32[6,8,256]{2,1,0:T(8,128)S(1)}) custom-call(bf16[256,768]{1,0:T(8,128)(2,1)S(1)} %copy-done.17, bf16[1024,768]{1,0:T(8,128)(2,1)S(1)} %convolution_convert_fusion.6.k_ref, bf16[1024,768]{1,0:T(8,128)(2,1)S(1)} %add_convert_fusion.v_ref, f32[1024,1]{1,0:T(8,128)S(1)} %bitcast.737), custom_call_target="tpu_custom_call" | custom-call | flops 1610612736 | bytes 4718592 | tf_op jit(solution)/shard_map/pallas_call | solution.py:126
  316.4 4.4 collective-permute-start.78
  323.5 9.6 fusion.9
  348.2 4.2 constant_dynamic-slice_fusion.92
  362.6 7.8 fusion.381
  413.4 14.5 %shard_map.276 = (bf16[256,768]{1,0:T(8,128)(2,1)S(1)}, bf16[1024,768]{1,0:T(8,128)(2,1)S(1)}, bf16[1024,768]{1,0:T(8,128)(2,1)S(1)}) custom-call(bf16[256,768]{1,0:T(8,128)(2,1)S(1)} %copy-done.18, bf16[1024,768]{1,0:T(8,128)(2,1)S(1)} %copy-done.24, bf16[1024,768]{1,0:T(8,128)(2,1)S(1)} %copy-done.26, f32[1024,1]{1,0:T(8,128)S(1)} %bitcast.738, ...), custom_call_target="tpu_custom_call" | custom-call | flops 4026531840 | bytes 9437184 | tf_op jit(solution)/shard_map/pallas_call | solution.py:176
  454.6 9.7 collective-permute-start.91
  494.1 4.9 constant_dynamic-slice_fusion.25
  514.9 4.9 collective-permute-start.39
  537.7 5.1 convert_reduce_fusion.4
  542.8 6.2 multiply_reduce_fusion.6
  553.3 14.9 %shard_map.278 = (bf16[256,768]{1,0:T(8,128)(2,1)S(1)}, bf16[1024,768]{1,0:T(8,128)(2,1)S(1)}, bf16[1024,768]{1,0:T(8,128)(2,1)S(1)}) custom-call(bf16[256,768]{1,0:T(8,128)(2,1)S(1)} %copy-done.16, bf16[1024,768]{1,0:T(8,128)(2,1)S(1)} %copy-done.20, bf16[1024,768]{1,0:T(8,128)(2,1)S(1)} %copy-done.22, f32[1024,1]{1,0:T(8,128)S(1)} %bitcast.739, ...), custom_call_target="tpu_custom_call" | custom-call | flops 4026531840 | bytes 9437184 | tf_op jit(solution)/shard_map/pallas_call | solution.py:176
  613.7 5.1 add_convert_fusion.3
  634.6 4.5 convolution_convert_fusion.1
  656.3 7.0 collective-permute-done.41
  679.0 7.1 collective-permute-start.82
  698.0 4.5 collective-permute-start.59
  720.4 5.8 collective-permute-done.117
  743.7 9.6 collective-permute-done.118
  769.0 7.1 reshape.1299
  776.1 8.5 constant_dynamic-slice_fusion.91
  788.5 9.1 constant_dynamic-slice_fusion.46
  812.9 20.9 %collective-permute-done.112 = bf16[384,512]{1,0:T(8,128)(2,1)S(1)} collective-permute-done((bf16[384,512]{1,0:T(8,128)(2,1)S(1)}, bf16[384,512]{1,0:T(8,128)(2,1)S(1)}, u32[]{:S(2)}, u32[]{:S(2)}) %collective-permute-start.112) | collective-permute-done | bytes 393248 | tf_op jit(solution)/shard_map/ppermute | solution.py:36
  835.3 6.5 collective-permute-done.131
  848.9 6.0 collective-permute-done.124
  863.5 4.5 collective-permute-done.114
  873.6 7.6 collective-permute-start.121
  885.3 26.4 %collective-permute-done.125 = bf16[192,768]{1,0:T(8,128)(2,1)S(1)} collective-permute-done((bf16[192,768]{1,0:T(8,128)(2,1)S(1)}, bf16[192,768]{1,0:T(8,128)(2,1)S(1)}, u32[]{:S(2)}, u32[]{:S(2)}) %collective-permute-start.125) | collective-permute-done | bytes 294944 | tf_op jit(solution)/shard_map/ppermute | solution.py:36
  927.8 14.0 %pad_maximum_fusion.1 = bf16[512,4608]{1,0:T(8,128)(2,1)} fusion(bf16[256,4608]{1,0:T(8,128)(2,1)} %collective-permute-done.141, bf16[1,1536]{1,0:T(2,128)(2,1)S(1)} %copy-done.265, bf16[255,1536]{1,0:T(8,128)(2,1)S(1)} %copy-done.65, bf16[256,768]{1,0:T(8,128)(2,1)S(1)} %copy-done.72, bf16[256,768]{1,0:T(8,128)(2,1)S(1)} %copy-done.51, ...), kind=kLoop, calls=%fused_computation.7 | loop fusion | flops 33030144 | bytes 9437184 | tf_op jit(solution)/shard_map/concatenate | solution.py:383
  941.9 7.2 reshape.1354
  949.1 12.4 %constant_dynamic-slice_fusion.6 = (bf16[512,6,1,384]{3,2,1,0:T(2,128)(2,1)}, bf16[512,6,1,384]{3,2,1,0:T(2,128)(2,1)}) fusion(bf16[512,6,2,384]{3,2,1,0:T(2,128)(2,1)} %reshape.1354, s32[]{:T(128)S(6)} %select_n.820, s32[]{:T(128)S(6)} %select_n.819), kind=kLoop, calls=%fused_computation.669 | loop fusion | bytes 9437192 | tf_op jit(solution)/shard_map/jit(dynamic_index_in_dim)/dynamic_slice | solution.py:54
  961.5 11.6 %copy.202 = bf16[512,6,1,384]{0,3,1,2:T(8,128)(2,1)} copy(bf16[512,6,1,384]{3,2,1,0:T(2,128)(2,1)} %get-tuple-element.181) | data formatting | bytes 4718592
  973.1 10.3 copy.203
  996.4 10.7 collective-permute-start.134
  1017.9 6.5 collective-permute-done.102
  1024.8 5.0 collective-permute-done.55
  1037.3 21.6 %collective-permute-done.63 = bf16[192,1152]{1,0:T(8,128)(2,1)S(1)} collective-permute-done((bf16[192,1152]{1,0:T(8,128)(2,1)S(1)}, bf16[192,1152]{1,0:T(8,128)(2,1)S(1)}, u32[]{:S(2)}, u32[]{:S(2)}) %collective-permute-start.63) | collective-permute-done | bytes 442400 | tf_op jit(solution)/shard_map/ppermute | solution.py:36
  1060.6 7.6 collective-permute-done.64
  1069.4 5.9 collective-permute-done.65
  1078.8 7.5 collective-permute-done.89
  1090.9 6.9 collective-permute-done.90
  1102.3 8.4 collective-permute-done.108
  1113.6 9.6 collective-permute-done.144
  1125.5 13.4 %collective-permute-done.145 = bf16[576,384]{1,0:T(8,128)(2,1)S(1)} collective-permute-done((bf16[576,384]{1,0:T(8,128)(2,1)S(1)}, bf16[576,384]{1,0:T(8,128)(2,1)S(1)}, u32[]{:S(2)}, u32[]{:S(2)}) %collective-permute-start.145) | collective-permute-done | bytes 442400 | tf_op jit(solution)/shard_map/ppermute | solution.py:36
  1139.9 11.6 %collective-permute-done.146 = bf16[288,384]{1,0:T(8,128)(2,1)S(1)} collective-permute-done((bf16[288,384]{1,0:T(8,128)(2,1)S(1)}, bf16[288,384]{1,0:T(8,128)(2,1)S(1)}, u32[]{:S(2)}, u32[]{:S(2)}) %collective-permute-start.146) | collective-permute-done | bytes 221216 | tf_op jit(solution)/shard_map/ppermute | solution.py:36
  (1437 shorter events, 563.7 us)
Async XLA Ops:
  1.9 25.3 %collective-permute-start.2 = (f32[5,768]{1,0:T(8,128)S(1)}, f32[5,768]{1,0:T(8,128)}, u32[]{:S(2)}, u32[]{:S(2)}) collective-permute-start(f32[5,768]{1,0:T(8,128)S(1)} %bitcast.870), channel_id=1, source_target_pairs={{0,16},{16,0},{1,17},{17,1},{2,18},{18,2},{3,19},{19,3},{4,20},{20... | collective-permute-start | bytes 46088 | tf_op jit(solution)/shard_map/ppermute | solution.py:36
  16.1 23.5 %collective-permute-start.13 = (bf16[1000,768]{1,0:T(8,128)(2,1)}, bf16[1000,768]{1,0:T(8,128)(2,1)S(1)}, u32[]{:S(2)}, u32[]{:S(2)}) collective-permute-start(bf16[1000,768]{1,0:T(8,128)(2,1)} %bitcast.894), channel_id=1, source_target_pairs={{0,16},{16,0},{1,17},{17,1},{2,18},{18,2},{3,19},{19,3},{4,20},{20... | collective-permute-start | bytes 4608008 | tf_op jit(solution)/shard_map/ppermute | solution.py:36
  18.9 59.6 %collective-permute-start.14 = (bf16[768,1536]{1,0:T(8,128)(2,1)}, bf16[768,1536]{1,0:T(8,128)(2,1)}, u32[]{:S(2)}, u32[]{:S(2)}) collective-permute-start(bf16[768,1536]{1,0:T(8,128)(2,1)} %bitcast.893), channel_id=1, source_target_pairs={{0,16},{16,0},{1,17},{17,1},{2,18},{18,2},{3,19},{19,3},{4,20},{20... | collective-permute-start | bytes 7077896 | tf_op jit(solution)/shard_map/ppermute | solution.py:36
  27.3 84.6 %collective-permute-start.1 = (bf16[768,2304]{1,0:T(8,128)(2,1)}, bf16[768,2304]{1,0:T(8,128)(2,1)}, u32[]{:S(2)}, u32[]{:S(2)}) collective-permute-start(bf16[768,2304]{1,0:T(8,128)(2,1)} %bitcast.749), channel_id=1, source_target_pairs={{0,16},{16,0},{1,17},{17,1},{2,18},{18,2},{3,19},{19,3},{4,20},{20... | collective-permute-start | bytes 10616840 | tf_op jit(solution)/shard_map/ppermute | solution.py:36
  35.1 27.5 %collective-permute-start.4 = (bf16[256,768]{1,0:T(8,128)(2,1)S(1)}, bf16[256,768]{1,0:T(8,128)(2,1)S(1)}, u32[]{:S(2)}, u32[]{:S(2)}) collective-permute-start(bf16[256,768]{1,0:T(8,128)(2,1)S(1)} %get-tuple-element.155), channel_id=1, source_target_pairs={{0,2},{1,3},{2,0},{3,1},{4,6},{5,7},{6,4},{7,5},{8,10},{9,11},{10,... | collective-permute-start | bytes 1179656 | tf_op jit(solution)/shard_map/ppermute | solution.py:45
  36.3 28.1 %collective-permute-start.3 = (bf16[256,768]{1,0:T(8,128)(2,1)S(1)}, bf16[256,768]{1,0:T(8,128)(2,1)S(1)}, u32[]{:S(2)}, u32[]{:S(2)}) collective-permute-start(bf16[256,768]{1,0:T(8,128)(2,1)S(1)} %get-tuple-element.155), channel_id=1, source_target_pairs={{0,1},{1,2},{2,3},{3,0},{4,5},{5,6},{6,7},{7,4},{8,9},{9,10},{10,1... | collective-permute-start | bytes 1179656 | tf_op jit(solution)/shard_map/ppermute | solution.py:45
  39.6 26.2 %collective-permute-start.48 = (bf16[256,768]{1,0:T(8,128)(2,1)S(1)}, bf16[256,768]{1,0:T(8,128)(2,1)S(1)}, u32[]{:S(2)}, u32[]{:S(2)}) collective-permute-start(bf16[256,768]{1,0:T(8,128)(2,1)S(1)} %get-tuple-element.155), channel_id=1, source_target_pairs={{0,16},{16,0},{1,17},{17,1},{2,18},{18,2},{3,19},{19,3},{4,20},{20... | collective-permute-start | bytes 1179656 | tf_op jit(solution)/shard_map/ppermute | solution.py:36
  65.8 70.1 %collective-permute-start.6 = (bf16[768,768]{1,0:T(8,128)(2,1)}, bf16[768,768]{1,0:T(8,128)(2,1)}, u32[]{:S(2)}, u32[]{:S(2)}) collective-permute-start(bf16[768,768]{1,0:T(8,128)(2,1)} %bitcast.4), channel_id=1, source_target_pairs={{0,16},{16,0},{1,17},{17,1},{2,18},{18,2},{3,19},{19,3},{4,20},{20... | collective-permute-start | bytes 3538952 | tf_op jit(solution)/shard_map/ppermute | solution.py:36
  84.6 23.4 %collective-permute-start.16 = (f32[8,384]{1,0:T(8,128)S(1)}, f32[8,384]{1,0:T(8,128)}, u32[]{:S(2)}, u32[]{:S(2)}) collective-permute-start(f32[8,384]{1,0:T(8,128)S(1)} %get-tuple-element.44), channel_id=1, source_target_pairs={{0,1},{1,2},{2,3},{3,0},{4,5},{5,6},{6,7},{7,4},{8,9},{9,10},{10,1... | collective-permute-start | bytes 36872 | tf_op jit(solution)/shard_map/ppermute | solution.py:45
  84.6 23.7 %collective-permute-start.17 = (f32[8,384]{1,0:T(8,128)S(1)}, f32[8,384]{1,0:T(8,128)}, u32[]{:S(2)}, u32[]{:S(2)}) collective-permute-start(f32[8,384]{1,0:T(8,128)S(1)} %get-tuple-element.44), channel_id=1, source_target_pairs={{0,2},{1,3},{2,0},{3,1},{4,6},{5,7},{6,4},{7,5},{8,10},{9,11},{10,... | collective-permute-start | bytes 36872 | tf_op jit(solution)/shard_map/ppermute | solution.py:45
  107.9 39.7 %collective-permute-start.9 = (bf16[768,3072]{1,0:T(8,128)(2,1)}, bf16[768,3072]{1,0:T(8,128)(2,1)}, u32[]{:S(2)}, u32[]{:S(2)}) collective-permute-start(bf16[768,3072]{1,0:T(8,128)(2,1)} %bitcast.888), channel_id=1, source_target_pairs={{0,16},{16,0},{1,17},{17,1},{2,18},{18,2},{3,19},{19,3},{4,20},{20... | collective-permute-start | bytes 14155784 | tf_op jit(solution)/shard_map/ppermute | solution.py:36
  108.3 51.2 %collective-permute-start.11 = (bf16[3072,768]{1,0:T(8,128)(2,1)}, bf16[3072,768]{1,0:T(8,128)(2,1)}, u32[]{:S(2)}, u32[]{:S(2)}) collective-permute-start(bf16[3072,768]{1,0:T(8,128)(2,1)} %bitcast.879), channel_id=1, source_target_pairs={{0,16},{16,0},{1,17},{17,1},{2,18},{18,2},{3,19},{19,3},{4,20},{20... | collective-permute-start | bytes 14155784 | tf_op jit(solution)/shard_map/ppermute | solution.py:36
  108.5 82.6 %collective-permute-start.21 = (bf16[3,1536,768]{2,1,0:T(8,128)(2,1)}, bf16[3,1536,768]{2,1,0:T(8,128)(2,1)}, u32[]{:S(2)}, u32[]{:S(2)}) collective-permute-start(bf16[3,1536,768]{2,1,0:T(8,128)(2,1)} %bitcast.743), channel_id=1, source_target_pairs={{0,16},{16,0},{1,17},{17,1},{2,18},{18,2},{3,19},{19,3},{4,20},{20... | collective-permute-start | bytes 21233672 | tf_op jit(solution)/shard_map/ppermute | solution.py:36
  173.1 53.8 %collective-permute-start.135 = (bf16[256,4608]{1,0:T(8,128)(2,1)}, bf16[256,4608]{1,0:T(8,128)(2,1)}, u32[]{:S(2)}, u32[]{:S(2)}) collective-permute-start(bf16[256,4608]{1,0:T(8,128)(2,1)} %maximum_maximum_fusion), channel_id=1, source_target_pairs={{0,16},{16,0},{1,17},{17,1},{2,18},{18,2},{3,19},{19,3},{4,20},{20... | collective-permute-start | bytes 7077896 | tf_op jit(solution)/shard_map/ppermute | solution.py:36
  209.0 86.1 %collective-permute-start.24 = (bf16[256,768]{1,0:T(8,128)(2,1)}, bf16[256,768]{1,0:T(8,128)(2,1)}, u32[]{:S(2)}, u32[]{:S(2)}) collective-permute-start(bf16[256,768]{1,0:T(8,128)(2,1)} %get-tuple-element.153), channel_id=1, source_target_pairs={{0,3},{1,0},{2,1},{3,2},{4,7},{5,4},{6,5},{7,6},{8,11},{9,8},{10,9... | collective-permute-start | bytes 1179656 | tf_op jit(solution)/shard_map/ppermute | solution.py:45
  211.9 83.2 %collective-permute-start.23 = (bf16[256,768]{1,0:T(8,128)(2,1)}, bf16[256,768]{1,0:T(8,128)(2,1)}, u32[]{:S(2)}, u32[]{:S(2)}) collective-permute-start(bf16[256,768]{1,0:T(8,128)(2,1)} %get-tuple-element.153), channel_id=1, source_target_pairs={{0,2},{1,3},{2,0},{3,1},{4,6},{5,7},{6,4},{7,5},{8,10},{9,11},{10,... | collective-permute-start | bytes 1179656 | tf_op jit(solution)/shard_map/ppermute | solution.py:45
  222.0 64.7 %collective-permute-start.25 = (f32[8,384]{1,0:T(8,128)S(1)}, f32[8,384]{1,0:T(8,128)S(1)}, u32[]{:S(2)}, u32[]{:S(2)}) collective-permute-start(f32[8,384]{1,0:T(8,128)S(1)} %get-tuple-element.49), channel_id=1, source_target_pairs={{0,1},{1,2},{2,3},{3,0},{4,5},{5,6},{6,7},{7,4},{8,9},{9,10},{10,1... | collective-permute-start | bytes 36872 | tf_op jit(solution)/shard_map/ppermute | solution.py:45
  222.2 64.5 %collective-permute-start.26 = (f32[8,384]{1,0:T(8,128)S(1)}, f32[8,384]{1,0:T(8,128)S(1)}, u32[]{:S(2)}, u32[]{:S(2)}) collective-permute-start(f32[8,384]{1,0:T(8,128)S(1)} %get-tuple-element.49), channel_id=1, source_target_pairs={{0,2},{1,3},{2,0},{3,1},{4,6},{5,7},{6,4},{7,5},{8,10},{9,11},{10,... | collective-permute-start | bytes 36872 | tf_op jit(solution)/shard_map/ppermute | solution.py:45
  226.9 63.4 %collective-permute-start.27 = (f32[8,384]{1,0:T(8,128)S(1)}, f32[8,384]{1,0:T(8,128)S(1)}, u32[]{:S(2)}, u32[]{:S(2)}) collective-permute-start(f32[8,384]{1,0:T(8,128)S(1)} %get-tuple-element.49), channel_id=1, source_target_pairs={{0,3},{1,0},{2,1},{3,2},{4,7},{5,4},{6,5},{7,6},{8,11},{9,8},{10,9... | collective-permute-start | bytes 36872 | tf_op jit(solution)/shard_map/ppermute | solution.py:45
  286.7 56.7 %collective-permute-start.57 = (bf16[256,768]{1,0:T(8,128)(2,1)}, bf16[256,768]{1,0:T(8,128)(2,1)S(1)}, u32[]{:S(2)}, u32[]{:S(2)}) collective-permute-start(bf16[256,768]{1,0:T(8,128)(2,1)} %get-tuple-element.153), channel_id=1, source_target_pairs={{0,16},{16,0},{1,17},{17,1},{2,18},{18,2},{3,19},{19,3},{4,20},{20... | collective-permute-start | bytes 1179656 | tf_op jit(solution)/shard_map/ppermute | solution.py:36
  290.3 195.7 %collective-permute-start.128 = (bf16[512,768]{1,0:T(8,128)(2,1)}, bf16[512,768]{1,0:T(8,128)(2,1)}, u32[]{:S(2)}, u32[]{:S(2)}) collective-permute-start(bf16[512,768]{1,0:T(8,128)(2,1)} %copy-done.166), channel_id=1, source_target_pairs={{0,16},{16,0},{1,17},{17,1},{2,18},{18,2},{3,19},{19,3},{4,20},{20... | collective-permute-start | bytes 2359304 | tf_op jit(solution)/shard_map/ppermute | solution.py:36
  316.4 182.6 %collective-permute-start.78 = (bf16[256,768]{1,0:T(8,128)(2,1)}, bf16[256,768]{1,0:T(8,128)(2,1)}, u32[]{:S(2)}, u32[]{:S(2)}) collective-permute-start(bf16[256,768]{1,0:T(8,128)(2,1)} %get-tuple-element.45), channel_id=1, source_target_pairs={{0,16},{16,0},{1,17},{17,1},{2,18},{18,2},{3,19},{19,3},{4,20},{20... | collective-permute-start | bytes 1179656 | tf_op jit(solution)/shard_map/ppermute | solution.py:36
  397.6 56.9 %collective-permute-start.35 = (f32[8,384]{1,0:T(8,128)S(1)}, f32[8,384]{1,0:T(8,128)}, u32[]{:S(2)}, u32[]{:S(2)}) collective-permute-start(f32[8,384]{1,0:T(8,128)S(1)} %get-tuple-element.57), channel_id=1, source_target_pairs={{0,3},{1,0},{2,1},{3,2},{4,7},{5,4},{6,5},{7,6},{8,11},{9,8},{10,9... | collective-permute-start | bytes 36872 | tf_op jit(solution)/shard_map/ppermute | solution.py:45
  397.7 66.6 %collective-permute-start.36 = (f32[8,384]{1,0:T(8,128)S(1)}, f32[8,384]{1,0:T(8,128)}, u32[]{:S(2)}, u32[]{:S(2)}) collective-permute-start(f32[8,384]{1,0:T(8,128)S(1)} %get-tuple-element.57), channel_id=1, source_target_pairs={{0,2},{1,3},{2,0},{3,1},{4,6},{5,7},{6,4},{7,5},{8,10},{9,11},{10,... | collective-permute-start | bytes 36872 | tf_op jit(solution)/shard_map/ppermute | solution.py:45
  400.9 63.8 %collective-permute-start.37 = (f32[8,384]{1,0:T(8,128)S(1)}, f32[8,384]{1,0:T(8,128)}, u32[]{:S(2)}, u32[]{:S(2)}) collective-permute-start(f32[8,384]{1,0:T(8,128)S(1)} %get-tuple-element.57), channel_id=1, source_target_pairs={{0,1},{1,2},{2,3},{3,0},{4,5},{5,6},{6,7},{7,4},{8,9},{9,10},{10,1... | collective-permute-start | bytes 36872 | tf_op jit(solution)/shard_map/ppermute | solution.py:45
  454.6 32.6 %collective-permute-start.91 = (bf16[256,768]{1,0:T(8,128)(2,1)}, bf16[256,768]{1,0:T(8,128)(2,1)}, u32[]{:S(2)}, u32[]{:S(2)}) collective-permute-start(bf16[256,768]{1,0:T(8,128)(2,1)} %copy-done.123), channel_id=1, source_target_pairs={{0,16},{16,0},{1,17},{17,1},{2,18},{18,2},{3,19},{19,3},{4,20},{20... | collective-permute-start | bytes 1179656 | tf_op jit(solution)/shard_map/ppermute | solution.py:36
  464.3 41.2 %collective-permute-start.34 = (bf16[256,768]{1,0:T(8,128)(2,1)}, bf16[256,768]{1,0:T(8,128)(2,1)}, u32[]{:S(2)}, u32[]{:S(2)}) collective-permute-start(bf16[256,768]{1,0:T(8,128)(2,1)} %get-tuple-element.228), channel_id=1, source_target_pairs={{0,1},{1,2},{2,3},{3,0},{4,5},{5,6},{6,7},{7,4},{8,9},{9,10},{10,1... | collective-permute-start | bytes 1179656 | tf_op jit(solution)/shard_map/ppermute | solution.py:45
  478.0 27.4 %collective-permute-start.33 = (bf16[256,768]{1,0:T(8,128)(2,1)}, bf16[256,768]{1,0:T(8,128)(2,1)}, u32[]{:S(2)}, u32[]{:S(2)}) collective-permute-start(bf16[256,768]{1,0:T(8,128)(2,1)} %get-tuple-element.229), channel_id=1, source_target_pairs={{0,2},{1,3},{2,0},{3,1},{4,6},{5,7},{6,4},{7,5},{8,10},{9,11},{10,... | collective-permute-start | bytes 1179656 | tf_op jit(solution)/shard_map/ppermute | solution.py:45
  499.0 153.3 %collective-permute-start.92 = (bf16[256,1536]{1,0:T(8,128)(2,1)}, bf16[256,1536]{1,0:T(8,128)(2,1)}, u32[]{:S(2)}, u32[]{:S(2)}) collective-permute-start(bf16[256,1536]{1,0:T(8,128)(2,1)} %get-tuple-element.209), channel_id=1, source_target_pairs={{0,16},{16,0},{1,17},{17,1},{2,18},{18,2},{3,19},{19,3},{4,20},{20... | collective-permute-start | bytes 2359304 | tf_op jit(solution)/shard_map/ppermute | solution.py:36
  503.0 166.1 %collective-permute-start.116 = (bf16[512,768]{1,0:T(8,128)(2,1)}, bf16[512,768]{1,0:T(8,128)(2,1)}, u32[]{:S(2)}, u32[]{:S(2)}) collective-permute-start(bf16[512,768]{1,0:T(8,128)(2,1)} %get-tuple-element.366), channel_id=1, source_target_pairs={{0,16},{16,0},{1,17},{17,1},{2,18},{18,2},{3,19},{19,3},{4,20},{20... | collective-permute-start | bytes 2359304 | tf_op jit(solution)/shard_map/ppermute | solution.py:36
  533.9 66.2 %collective-permute-start.44 = (f32[8,384]{1,0:T(8,128)S(1)}, f32[8,384]{1,0:T(8,128)}, u32[]{:S(2)}, u32[]{:S(2)}) collective-permute-start(f32[8,384]{1,0:T(8,128)S(1)} %get-tuple-element.65), channel_id=1, source_target_pairs={{0,3},{1,0},{2,1},{3,2},{4,7},{5,4},{6,5},{7,6},{8,11},{9,8},{10,9... | collective-permute-start | bytes 36872 | tf_op jit(solution)/shard_map/ppermute | solution.py:45
  536.4 65.0 %collective-permute-start.45 = (f32[8,384]{1,0:T(8,128)S(1)}, f32[8,384]{1,0:T(8,128)}, u32[]{:S(2)}, u32[]{:S(2)}) collective-permute-start(f32[8,384]{1,0:T(8,128)S(1)} %get-tuple-element.65), channel_id=1, source_target_pairs={{0,2},{1,3},{2,0},{3,1},{4,6},{5,7},{6,4},{7,5},{8,10},{9,11},{10,... | collective-permute-start | bytes 36872 | tf_op jit(solution)/shard_map/ppermute | solution.py:45
  537.2 64.2 %collective-permute-start.46 = (f32[8,384]{1,0:T(8,128)S(1)}, f32[8,384]{1,0:T(8,128)}, u32[]{:S(2)}, u32[]{:S(2)}) collective-permute-start(f32[8,384]{1,0:T(8,128)S(1)} %get-tuple-element.65), channel_id=1, source_target_pairs={{0,1},{1,2},{2,3},{3,0},{4,5},{5,6},{6,7},{7,4},{8,9},{9,10},{10,1... | collective-permute-start | bytes 36872 | tf_op jit(solution)/shard_map/ppermute | solution.py:45
  600.2 47.1 %collective-permute-start.80 = (bf16[384,384]{1,0:T(8,128)(2,1)}, bf16[384,384]{1,0:T(8,128)(2,1)}, u32[]{:S(2)}, u32[]{:S(2)}) collective-permute-start(bf16[384,384]{1,0:T(8,128)(2,1)} %convolution_convert_fusion.12), channel_id=1, source_target_pairs={{0,8},{4,12},{8,0},{12,4},{1,9},{5,13},{9,1},{13,5},{2,10},{6,14},... | collective-permute-start | bytes 884744 | tf_op jit(solution)/shard_map/ppermute | solution.py:36
  601.4 30.6 %collective-permute-start.136 = (bf16[256,384]{1,0:T(8,128)(2,1)}, bf16[256,384]{1,0:T(8,128)(2,1)}, u32[]{:S(2)}, u32[]{:S(2)}) collective-permute-start(bf16[256,384]{1,0:T(8,128)(2,1)} %get-tuple-element.284), channel_id=1, source_target_pairs={{0,16},{16,0},{1,17},{17,1},{2,18},{18,2},{3,19},{19,3},{4,20},{20... | collective-permute-start | bytes 589832 | tf_op jit(solution)/shard_map/ppermute | solution.py:36
  628.7 27.5 %collective-permute-start.42 = (bf16[256,768]{1,0:T(8,128)(2,1)S(1)}, bf16[256,768]{1,0:T(8,128)(2,1)S(1)}, u32[]{:S(2)}, u32[]{:S(2)}) collective-permute-start(bf16[256,768]{1,0:T(8,128)(2,1)S(1)} %copy-done.188), channel_id=1, source_target_pairs={{0,1},{1,2},{2,3},{3,0},{4,5},{5,6},{6,7},{7,4},{8,9},{9,10},{10,1... | collective-permute-start | bytes 1179656 | tf_op jit(solution)/shard_map/ppermute | solution.py:45
  656.3 108.5 %collective-permute-start.104 = (bf16[256,3072]{1,0:T(8,128)(2,1)}, bf16[256,3072]{1,0:T(8,128)(2,1)}, u32[]{:S(2)}, u32[]{:S(2)}) collective-permute-start(bf16[256,3072]{1,0:T(8,128)(2,1)} %get-tuple-element.351), channel_id=1, source_target_pairs={{0,16},{16,0},{1,17},{17,1},{2,18},{18,2},{3,19},{19,3},{4,20},{20... | collective-permute-start | bytes 4718600 | tf_op jit(solution)/shard_map/ppermute | solution.py:36
  663.2 41.5 %collective-permute-start.52 = (bf16[1024,384]{1,0:T(8,128)(2,1)}, bf16[1024,384]{1,0:T(8,128)(2,1)}, u32[]{:S(2)}, u32[]{:S(2)}) collective-permute-start(bf16[1024,384]{1,0:T(8,128)(2,1)} %get-tuple-element.219), channel_id=1, source_target_pairs={{0,16},{16,0},{1,17},{17,1},{2,18},{18,2},{3,19},{19,3},{4,20},{20... | collective-permute-start | bytes 2359304 | tf_op jit(solution)/shard_map/ppermute | solution.py:36
  665.0 42.1 %collective-permute-start.51 = (bf16[1024,384]{1,0:T(8,128)(2,1)}, bf16[1024,384]{1,0:T(8,128)(2,1)}, u32[]{:S(2)}, u32[]{:S(2)}) collective-permute-start(bf16[1024,384]{1,0:T(8,128)(2,1)} %get-tuple-element.217), channel_id=1, source_target_pairs={{0,16},{16,0},{1,17},{17,1},{2,18},{18,2},{3,19},{19,3},{4,20},{20... | collective-permute-start | bytes 2359304 | tf_op jit(solution)/shard_map/ppermute | solution.py:36
  698.0 62.7 %collective-permute-start.59 = (bf16[1024,768]{1,0:T(8,128)(2,1)}, bf16[1024,768]{1,0:T(8,128)(2,1)}, u32[]{:S(2)}, u32[]{:S(2)}) collective-permute-start(bf16[1024,768]{1,0:T(8,128)(2,1)} %pad_maximum_fusion.5), channel_id=1, source_target_pairs={{0,16},{16,0},{1,17},{17,1},{2,18},{18,2},{3,19},{19,3},{4,20},{20... | collective-permute-start | bytes 4718600 | tf_op jit(solution)/shard_map/ppermute | solution.py:36
  704.8 222.8 %collective-permute-start.141 = (bf16[256,4608]{1,0:T(8,128)(2,1)}, bf16[256,4608]{1,0:T(8,128)(2,1)}, u32[]{:S(2)}, u32[]{:S(2)}) collective-permute-start(bf16[256,4608]{1,0:T(8,128)(2,1)} %maximum_maximum_fusion.1), channel_id=1, source_target_pairs={{0,16},{16,0},{1,17},{17,1},{2,18},{18,2},{3,19},{19,3},{4,20},{20... | collective-permute-start | bytes 7077896 | tf_op jit(solution)/shard_map/ppermute | solution.py:36
  753.3 230.2 %collective-permute-start.142 = (bf16[256,384]{1,0:T(8,128)(2,1)}, bf16[256,384]{1,0:T(8,128)(2,1)}, u32[]{:S(2)}, u32[]{:S(2)}) collective-permute-start(bf16[256,384]{1,0:T(8,128)(2,1)} %get-tuple-element.282), channel_id=1, source_target_pairs={{0,16},{16,0},{1,17},{17,1},{2,18},{18,2},{3,19},{19,3},{4,20},{20... | collective-permute-start | bytes 589832 | tf_op jit(solution)/shard_map/ppermute | solution.py:36
  759.3 25.4 %collective-permute-start.61 = (bf16[1024,384]{1,0:T(8,128)(2,1)}, bf16[1024,384]{1,0:T(8,128)(2,1)}, u32[]{:S(2)}, u32[]{:S(2)}) collective-permute-start(bf16[1024,384]{1,0:T(8,128)(2,1)} %get-tuple-element.215), channel_id=1, source_target_pairs={{0,16},{16,0},{1,17},{17,1},{2,18},{18,2},{3,19},{19,3},{4,20},{20... | collective-permute-start | bytes 2359304 | tf_op jit(solution)/shard_map/ppermute | solution.py:36
  760.7 36.9 %collective-permute-start.60 = (bf16[1024,384]{1,0:T(8,128)(2,1)}, bf16[1024,384]{1,0:T(8,128)(2,1)}, u32[]{:S(2)}, u32[]{:S(2)}) collective-permute-start(bf16[1024,384]{1,0:T(8,128)(2,1)} %get-tuple-element.213), channel_id=1, source_target_pairs={{0,16},{16,0},{1,17},{17,1},{2,18},{18,2},{3,19},{19,3},{4,20},{20... | collective-permute-start | bytes 2359304 | tf_op jit(solution)/shard_map/ppermute | solution.py:36
  764.8 40.0 %collective-permute-start.105 = (bf16[256,384]{1,0:T(8,128)(2,1)}, bf16[256,384]{1,0:T(8,128)(2,1)}, u32[]{:S(2)}, u32[]{:S(2)}) collective-permute-start(bf16[256,384]{1,0:T(8,128)(2,1)} %get-tuple-element.288), channel_id=1, source_target_pairs={{0,16},{16,0},{1,17},{17,1},{2,18},{18,2},{3,19},{19,3},{4,20},{20... | collective-permute-start | bytes 589832 | tf_op jit(solution)/shard_map/ppermute | solution.py:36
  784.7 58.5 %collective-permute-start.100 = (bf16[1536,384]{1,0:T(8,128)(2,1)}, bf16[1536,384]{1,0:T(8,128)(2,1)}, u32[]{:S(2)}, u32[]{:S(2)}) collective-permute-start(bf16[1536,384]{1,0:T(8,128)(2,1)} %convolution_convert_fusion.3), channel_id=1, source_target_pairs={{0,8},{4,12},{8,0},{12,4},{1,9},{5,13},{9,1},{13,5},{2,10},{6,14},... | collective-permute-start | bytes 3538952 | tf_op jit(solution)/shard_map/ppermute | solution.py:36
  797.6 75.9 %collective-permute-start.93 = (bf16[384,1536]{1,0:T(8,128)(2,1)}, bf16[384,1536]{1,0:T(8,128)(2,1)S(1)}, u32[]{:S(2)}, u32[]{:S(2)}) collective-permute-start(bf16[384,1536]{1,0:T(8,128)(2,1)} %convolution_convert_fusion.4), channel_id=1, source_target_pairs={{0,4},{4,0},{8,12},{12,8},{1,5},{5,1},{9,13},{13,9},{2,6},{6,2},{1... | collective-permute-start | bytes 3538952 | tf_op jit(solution)/shard_map/ppermute | solution.py:36
  804.7 29.1 %collective-permute-start.112 = (bf16[384,512]{1,0:T(8,128)(2,1)S(1)}, bf16[384,512]{1,0:T(8,128)(2,1)S(1)}, u32[]{:S(2)}, u32[]{:S(2)}) collective-permute-start(bf16[384,512]{1,0:T(8,128)(2,1)S(1)} %copy-done.344), channel_id=1, source_target_pairs={{0,4},{4,0},{8,12},{12,8},{1,5},{5,1},{9,13},{13,9},{2,6},{6,2},{1... | collective-permute-start | bytes 1179656 | tf_op jit(solution)/shard_map/ppermute | solution.py:36
  843.2 27.9 %collective-permute-start.120 = (bf16[48,512]{1,0:T(8,128)(2,1)S(1)}, bf16[48,512]{1,0:T(8,128)(2,1)S(1)}, u32[]{:S(2)}, u32[]{:S(2)}) collective-permute-start(bf16[48,512]{1,0:T(8,128)(2,1)S(1)} %copy-done.243), channel_id=1, source_target_pairs={{0,2},{1,3},{2,0},{3,1},{4,6},{5,7},{6,4},{7,5},{8,10},{9,11},{10,... | collective-permute-start | bytes 147464 | tf_op jit(solution)/shard_map/ppermute | solution.py:36
  871.0 116.7 %collective-permute-start.137 = (bf16[2304,384]{1,0:T(8,128)(2,1)}, bf16[2304,384]{1,0:T(8,128)(2,1)}, u32[]{:S(2)}, u32[]{:S(2)}) collective-permute-start(bf16[2304,384]{1,0:T(8,128)(2,1)} %convolution_convert_fusion.1), channel_id=1, source_target_pairs={{0,4},{4,0},{8,12},{12,8},{1,5},{5,1},{9,13},{13,9},{2,6},{6,2},{1... | collective-permute-start | bytes 5308424 | tf_op jit(solution)/shard_map/ppermute | solution.py:36
  872.3 40.2 %collective-permute-start.53 = (bf16[384,1152]{0,1:T(8,128)(2,1)S(1)}, bf16[384,1152]{0,1:T(8,128)(2,1)S(1)}, u32[]{:S(2)}, u32[]{:S(2)}) collective-permute-start(bf16[384,1152]{0,1:T(8,128)(2,1)S(1)} %copy-done.146), channel_id=1, source_target_pairs={{0,8},{4,12},{8,0},{12,4},{1,9},{5,13},{9,1},{13,5},{2,10},{6,14},... | collective-permute-start | bytes 2654216 | tf_op jit(solution)/shard_map/ppermute | solution.py:36
  884.0 27.7 %collective-permute-start.125 = (bf16[192,768]{1,0:T(8,128)(2,1)S(1)}, bf16[192,768]{1,0:T(8,128)(2,1)S(1)}, u32[]{:S(2)}, u32[]{:S(2)}) collective-permute-start(bf16[192,768]{1,0:T(8,128)(2,1)S(1)} %dynamic-slice_bitcast_fusion.9), channel_id=1, source_target_pairs={{0,4},{4,0},{8,12},{12,8},{1,5},{5,1},{9,13},{13,9},{2,6},{6,2},{1... | collective-permute-start | bytes 884744 | tf_op jit(solution)/shard_map/ppermute | solution.py:36
  922.0 71.1 %collective-permute-start.87 = (bf16[384,1536]{1,0:T(8,128)(2,1)}, bf16[384,1536]{1,0:T(8,128)(2,1)}, u32[]{:S(2)}, u32[]{:S(2)}) collective-permute-start(bf16[384,1536]{1,0:T(8,128)(2,1)} %convolution_convert_fusion.5), channel_id=1, source_target_pairs={{0,4},{4,0},{8,12},{12,8},{1,5},{5,1},{9,13},{13,9},{2,6},{6,2},{1... | collective-permute-start | bytes 3538952 | tf_op jit(solution)/shard_map/ppermute | solution.py:36
  924.7 86.4 %collective-permute-start.62 = (bf16[384,1152]{0,1:T(8,128)(2,1)}, bf16[384,1152]{0,1:T(8,128)(2,1)}, u32[]{:S(2)}, u32[]{:S(2)}) collective-permute-start(bf16[384,1152]{0,1:T(8,128)(2,1)} %pad_maximum_fusion.37), channel_id=1, source_target_pairs={{0,8},{4,12},{8,0},{12,4},{1,9},{5,13},{9,1},{13,5},{2,10},{6,14},... | collective-permute-start | bytes 2654216 | tf_op jit(solution)/shard_map/ppermute | solution.py:36
  927.6 103.1 %collective-permute-start.106 = (bf16[1536,384]{1,0:T(8,128)(2,1)}, bf16[1536,384]{1,0:T(8,128)(2,1)}, u32[]{:S(2)}, u32[]{:S(2)}) collective-permute-start(bf16[1536,384]{1,0:T(8,128)(2,1)} %convolution_convert_fusion.2), channel_id=1, source_target_pairs={{0,8},{4,12},{8,0},{12,4},{1,9},{5,13},{9,1},{13,5},{2,10},{6,14},... | collective-permute-start | bytes 3538952 | tf_op jit(solution)/shard_map/ppermute | solution.py:36
  987.7 28.6 %collective-permute-start.94 = (bf16[192,1536]{1,0:T(8,128)(2,1)}, bf16[192,1536]{1,0:T(8,128)(2,1)}, u32[]{:S(2)}, u32[]{:S(2)}) collective-permute-start(bf16[192,1536]{1,0:T(8,128)(2,1)} %dynamic-slice_bitcast_fusion.3), channel_id=1, source_target_pairs={{0,8},{4,12},{8,0},{12,4},{1,9},{5,13},{9,1},{13,5},{2,10},{6,14},... | collective-permute-start | bytes 1769480 | tf_op jit(solution)/shard_map/ppermute | solution.py:36
  1009.0 89.6 %collective-permute-start.143 = (bf16[2304,384]{1,0:T(8,128)(2,1)}, bf16[2304,384]{1,0:T(8,128)(2,1)}, u32[]{:S(2)}, u32[]{:S(2)}) collective-permute-start(bf16[2304,384]{1,0:T(8,128)(2,1)} %convolution_convert_fusion), channel_id=1, source_target_pairs={{0,4},{4,0},{8,12},{12,8},{1,5},{5,1},{9,13},{13,9},{2,6},{6,2},{1... | collective-permute-start | bytes 5308424 | tf_op jit(solution)/shard_map/ppermute | solution.py:36
  1011.2 64.1 %collective-permute-start.138 = (bf16[1152,384]{1,0:T(8,128)(2,1)}, bf16[1152,384]{1,0:T(8,128)(2,1)}, u32[]{:S(2)}, u32[]{:S(2)}) collective-permute-start(bf16[1152,384]{1,0:T(8,128)(2,1)} %bitcast.228), channel_id=1, source_target_pairs={{0,8},{4,12},{8,0},{12,4},{1,9},{5,13},{9,1},{13,5},{2,10},{6,14},... | collective-permute-start | bytes 2654216 | tf_op jit(solution)/shard_map/ppermute | solution.py:36
  1014.8 44.9 %collective-permute-start.88 = (bf16[192,1536]{1,0:T(8,128)(2,1)}, bf16[192,1536]{1,0:T(8,128)(2,1)S(1)}, u32[]{:S(2)}, u32[]{:S(2)}) collective-permute-start(bf16[192,1536]{1,0:T(8,128)(2,1)} %dynamic-slice_bitcast_fusion.4), channel_id=1, source_target_pairs={{0,8},{4,12},{8,0},{12,4},{1,9},{5,13},{9,1},{13,5},{2,10},{6,14},... | collective-permute-start | bytes 1769480 | tf_op jit(solution)/shard_map/ppermute | solution.py:36
  1029.9 29.1 %collective-permute-start.63 = (bf16[192,1152]{1,0:T(8,128)(2,1)S(1)}, bf16[192,1152]{1,0:T(8,128)(2,1)S(1)}, u32[]{:S(2)}, u32[]{:S(2)}) collective-permute-start(bf16[192,1152]{1,0:T(8,128)(2,1)S(1)} %dynamic-slice_bitcast_fusion.5), channel_id=1, source_target_pairs={{0,4},{4,0},{8,12},{12,8},{1,5},{5,1},{9,13},{13,9},{2,6},{6,2},{1... | collective-permute-start | bytes 1327112 | tf_op jit(solution)/shard_map/ppermute | solution.py:36
  1036.7 102.5 %collective-permute-start.103 = (bf16[192,384]{1,0:T(8,128)(2,1)S(1)}, bf16[192,384]{1,0:T(8,128)(2,1)S(1)}, u32[]{:S(2)}, u32[]{:S(2)}) collective-permute-start(bf16[192,384]{1,0:T(8,128)(2,1)S(1)} %dynamic-slice_bitcast_fusion.13), channel_id=1, source_target_pairs={{0,2},{1,3},{2,0},{3,1},{4,6},{5,7},{6,4},{7,5},{8,10},{9,11},{10,... | collective-permute-start | bytes 442376 | tf_op jit(solution)/shard_map/ppermute | solution.py:36
  1097.9 27.5 %collective-permute-start.97 = (f32[48,1536]{1,0:T(8,128)S(1)}, f32[48,1536]{1,0:T(8,128)S(1)}, u32[]{:S(2)}, u32[]{:S(2)}) collective-permute-start(f32[48,1536]{1,0:T(8,128)S(1)} %fusion.263), channel_id=1, source_target_pairs={{0,16},{16,0},{1,17},{17,1},{2,18},{18,2},{3,19},{19,3},{4,20},{20... | collective-permute-start | bytes 884744 | tf_op jit(solution)/shard_map/ppermute | solution.py:36
  1110.9 28.4 %collective-permute-start.109 = (bf16[192,384]{1,0:T(8,128)(2,1)S(1)}, bf16[192,384]{1,0:T(8,128)(2,1)S(1)}, u32[]{:S(2)}, u32[]{:S(2)}) collective-permute-start(bf16[192,384]{1,0:T(8,128)(2,1)S(1)} %dynamic-slice_bitcast_fusion.12), channel_id=1, source_target_pairs={{0,2},{1,3},{2,0},{3,1},{4,6},{5,7},{6,4},{7,5},{8,10},{9,11},{10,... | collective-permute-start | bytes 442376 | tf_op jit(solution)/shard_map/ppermute | solution.py:36
  1111.2 28.7 %collective-permute-start.140 = (bf16[288,384]{1,0:T(8,128)(2,1)S(1)}, bf16[288,384]{1,0:T(8,128)(2,1)S(1)}, u32[]{:S(2)}, u32[]{:S(2)}) collective-permute-start(bf16[288,384]{1,0:T(8,128)(2,1)S(1)} %bitcast.858), channel_id=1, source_target_pairs={{0,2},{1,3},{2,0},{3,1},{4,6},{5,7},{6,4},{7,5},{8,10},{9,11},{10,... | collective-permute-start | bytes 663560 | tf_op jit(solution)/shard_map/ppermute | solution.py:36
  (448 other events, 4136.8 us)
where the time goes:
time: 1160 us
  local copies, waits for them, and re-layouts  301 us (26%)
  waiting for transfers between devices  241 us (21%)
  matrix products  230 us (20%)
  starting transfers between devices  181 us (16%)
  other arithmetic  136 us (12%)
  Pallas kernels  61.1 us (5%)
    dot_general x82, matrix products, contract(): lax.dot_general(left, right, (dims, ((), ())), preferred_element_type=F32)  230 us
    ppermute x116, waiting for transfers between devices, flip(): lax.ppermute(value, axis, [(i, i ^ 1 << bit) for i in range(lax.axis_size...  209 us
    ppermute x116, starting transfers between devices, flip(): lax.ppermute(value, axis, [(i, i ^ 1 << bit) for i in range(lax.axis_size...  125 us
    dynamic_slice x36, local copies, waits for them, and re-layouts, pick(): return lax.dynamic_index_in_dim(value, index, axis, keepdims=False)  94.7 us
    unnamed x746, local copies, waits for them, and re-layouts  67.1 us
    concatenate x14, other arithmetic, inputs(): return jnp.concatenate([values, swap(values)], axis=0)  46 us
    reshape x12, local copies, waits for them, and re-layouts, split(): value.reshape(shape[:axis] + (outer, 2, shape[axis] // (2 * outer)) + sha...  42.7 us
    ppermute x24, starting transfers between devices, turned(): lax.ppermute(value, CTX, [(i, (i + by) % count) for i in range(count)])  35.9 us
  transfers between devices with their start and end apart: 148, of which 37 were waited for; matrix products, arithmetic and copies ran while one was open for 56% of the time, Pallas kernels for 5%

commit v1 on v0

--- a/solution.py
+++ b/solution.py
@@ -351,8 +351,7 @@
     features = layer_norm(second, gains[1], shifts[1])
     joined = jnp.concatenate([features, pooled], axis=1).astype(BF16)
     three = three_taps(joined, 1)
-    conv = w["conv"]
-    mixed = mm(three, conv.reshape(-1, width)) + biases[4]
+    mixed = mm(three, w["conv"]) + biases[4]
     lifted = gelu(mixed)
     tok_sum = features + lifted
     chr_sum = chars + states + tm(onehot, lifted.astype(BF16))
@@ -361,7 +360,7 @@
     saved = dict(
         x=x, x_all=x_all, query=query, keys=keys, values=values, lse=lse, attended=attended,
         first=first, normed_low=normed_low, hidden=hidden, active=active, second=second,
-        chars_low=chars_low, proj=proj, states=states, entering=entering, three=three,
+        chars_low=chars_low, proj=proj, states=states, entering=entering, joined=joined,
         mixed=mixed, tok_sum=tok_sum, chr_sum=chr_sum,
     )
     return tok_out, chr_out, saved
@@ -375,104 +374,253 @@
     return jnp.concatenate([lower, values, upper][::step], axis=1)
 
 
-class Halves:
-    def __init__(self, section):
-        self.section = section
-
-    def inputs(self, values):
-        return jnp.concatenate([values, swap(values)], axis=0)
-
-    def grads(self, values):
-        half = values.shape[1] // 2
-        sent = lax.dynamic_slice_in_dim(values, (1 - self.section) * half, half, 1)
-        kept = lax.dynamic_slice_in_dim(values, self.section * half, half, 1)
-        return jnp.concatenate([kept, swap(sent)], axis=0)
-
-
 def bits_of(axis):
     return [(axis, bit) for bit in range(lax.axis_size(axis).bit_length() - 1)]
 
 
-def reduce_scattered(pairs, lead, order):
-    layout = bits_of(DP)[::-1] + bits_of(CTX)[::-1]
-    rows = pairs[0][0].shape[1]
-
-    def split(value, key, axis):
-        place = layout.index(key)
-        shape = value.shape
-        outer = lead * 2**place
-        view = value.reshape(shape[:axis] + (outer, 2, shape[axis] // (2 * outer)) + shape[axis + 1 :])
-        mine = (lax.axis_index(key[0]) >> key[1]) & 1
-        less = shape[:axis] + (shape[axis] // 2,) + shape[axis + 1 :]
-        return [pick(view, side, axis + 1).reshape(less) for side in (mine, 1 - mine)]
-
-    total = None
-    for count, key in enumerate(order):
-        if count == 0:
-            kept, sent = [], []
-            for left, right in pairs:
-                mine, other = split(left, key, 1)
-                kept.append(tm(mine, right))
-                sent.append(tm(other, right))
-            kept, sent = (v[0] if len(v) == 1 else jnp.concatenate(v, axis=1) for v in (kept, sent))
+def exchange_order(x_first):
+    dp = bits_of(DP)
+    return (dp if x_first else dp[::-1]) + bits_of(CTX)
+
+
+def shard_at(place, order, n_ctx):
+    index = {DP: lax.axis_index(DP), CTX: lax.axis_index(CTX)}
+    shard = index[DP] * n_ctx + index[CTX]
+    for nth, (axis, bit) in enumerate(order):
+        if (place >> (len(order) - 1 - nth)) & 1:
+            mine = (index[axis] // (1 << bit)) % 2
+            shard = shard + (1 - 2 * mine) * ((1 << bit) * (n_ctx if axis == DP else 1))
+    return shard
+
+
+class Packing:
+    def __init__(self, section, unit, x_first):
+        self.section, self.unit, self.x_first = section, unit, x_first
+        self.arrays, self.moves, self.jobs, self.rows = [], [], [], 0
+
+    def operand(self, value, pieces=None):
+        width = value.shape[1]
+        self.arrays.append(value)
+        self.moves.append([(0, 0, width)] if pieces is None else [(b, h, h) for b, h in pieces])
+        return len(self.arrays) - 1
+
+    def local(self, *values):
+        self.arrays.extend(values)
+        self.moves.extend([None] * len(values))
+        return len(self.arrays) - len(values)
+
+    def product(self, left, right, begin, half, there, size):
+        self.jobs.append(
+            dict(left=left, right=right, begin=begin, half=half, there=there, rows=size, row=self.rows)
+        )
+        self.rows += size
+
+    def plain(self, value, size):
+        self.jobs.append(dict(left=None, plain=self.local(value), rows=size, row=self.rows))
+        self.rows += size
+
+    def run(self, collective_id):
+        order = exchange_order(self.x_first)
+        n_ctx = lax.axis_size(CTX)
+        count = lax.axis_size(DP) * n_ctx
+        unit, section = self.unit, self.section
+        if any(job["rows"] % 16 for job in self.jobs):
+            return self.run_plainly(order, n_ctx, count)
+        vmem = pl.BlockSpec(memory_space=pltpu.VMEM)
+        half = jax.ShapeDtypeStruct((count // 2, self.rows, unit), BF16)
+        most = max(job["rows"] for job in self.jobs) * count
+        coming = [
+            pltpu.VMEM((a.shape[0], sum(piece[2] for piece in move)), a.dtype)
+            for a, move in zip(self.arrays, self.moves)
+            if move
+        ]
+        copies = sum(len(move) for move in self.moves if move)
+        semaphores = [pltpu.SemaphoreType.DMA((copies,))] * 2
+        return pl.pallas_call(
+            functools.partial(pack_kernel, self.jobs, self.moves, count, order, n_ctx),
+            in_specs=[vmem] * len(self.arrays),
+            out_specs=[vmem, vmem],
+            out_shape=[half, half],
+            scratch_shapes=[pltpu.VMEM((2, most, unit), BF16), coming, semaphores],
+            compiler_params=pltpu.CompilerParams(
+                vmem_limit_bytes=56 * MIB, collective_id=collective_id, has_side_effects=True
+            ),
+            cost_estimate=pl.CostEstimate(
+                flops=count * self.rows * unit * 1024,
+                bytes_accessed=count * self.rows * unit * 4,
+                transcendentals=0,
+            ),
+        )(*self.arrays)
+
+    def run_plainly(self, order, n_ctx, count):
+        blocks = []
+        for job in self.jobs:
+            if job["left"] is None:
+                value = self.arrays[job["plain"]]
+            else:
+                left, right = job["left"], job["right"]
+                pairs = []
+                for core in (0, 1):
+                    owner = jnp.where(core == 0, self.section, 1 - self.section)
+                    one = self.other(left, owner) if core else self.arrays[left]
+                    if self.moves[right] is None:
+                        two = lax.slice_in_dim(
+                            self.arrays[right + core], job["begin"], job["begin"] + self.unit, axis=1
+                        )
+                    else:
+                        two = self.other(right, owner) if core else self.arrays[right]
+                        column = job["begin"] + self.section * job["half"]
+                        two = lax.dynamic_slice_in_dim(two, column, self.unit, 1)
+                    pairs.append(tm(one, two))
+                value = (pairs[0] + pairs[1]).astype(BF16)
+            blocks.append(value.reshape(count, job["rows"], self.unit))
+        shards = jnp.stack([shard_at(place, order, n_ctx) for place in range(count)])
+        whole = jnp.take(jnp.concatenate(blocks, axis=1), shards, axis=0)
+        return whole[count // 2 :], whole[: count // 2]
+
+    def other(self, index, owner):
+        return swap(self.arrays[index])
+
+
+def pack_kernel(jobs, moves, count, order, n_ctx, *refs):
+    arrays, (sent_ref, kept_ref, scratch, coming, semaphores) = refs[: len(moves)], refs[len(moves) :]
+    send_sems, recv_sems = semaphores
+    section = lax.axis_index(SEC)
+    unit = kept_ref.shape[2]
+    barrier = pltpu.get_barrier_semaphore()
+    pl.semaphore_signal(
+        barrier, inc=1, device_id={SEC: 1 - section}, device_id_type=pl.DeviceIdType.MESH
+    )
+    pl.semaphore_wait(barrier, 1)
+    places, copies, pending, nth, slot = {}, [], {}, 0, 0
+    for index, move in enumerate(moves):
+        if not move:
+            continue
+        target, at = coming[slot], 0
+        places[index] = target
+        pending[index] = []
+        slot += 1
+        for begin, half, width in move:
+            if half:
+                source = arrays[index].at[:, pl.ds(pl.multiple_of(begin + (1 - section) * half, 128), width)]
+            else:
+                source = arrays[index]
+            copy = pltpu.make_async_remote_copy(
+                src_ref=source,
+                dst_ref=target.at[:, at : at + width] if half else target,
+                send_sem=send_sems.at[nth],
+                recv_sem=recv_sems.at[nth],
+                device_id={SEC: 1 - section},
+                device_id_type=pl.DeviceIdType.MESH,
+            )
+            copy.start()
+            copies.append(copy)
+            pending[index].append(copy)
+            at += width
+            nth += 1
+    for turn, job in enumerate(jobs):
+        at, size = job["row"], job["rows"]
+        held = scratch.at[turn % 2]
+        if job["left"] is None:
+            held[0 : count * size, :] = arrays[job["plain"]][...]
         else:
-            kept, sent = split(total, key, 0)
-        layout_next = [k for k in layout if k != key]
-        total = kept.astype(F32) + flip(sent.astype(BF16), *key).astype(F32)
-        if count < len(order) - 1:
-            total = total.astype(BF16)
-        layout = layout_next
-    return total
-
-
-def layer_backward(w, saved, g_tok, g_chr, ids, ids_other, live, onehot, counts, seen, place, halves):
+            left, right = job["left"], job["right"]
+            for index in (left, right):
+                for copy in pending.pop(index, ()):
+                    copy.wait_recv()
+            if moves[right]:
+                column = pl.multiple_of(job["begin"] + section * job["half"], 128)
+                mine = arrays[right].at[:, pl.ds(column, unit)]
+                theirs = places[right].at[:, job["there"] : job["there"] + unit]
+            else:
+                mine, theirs = (
+                    arrays[right + core].at[:, job["begin"] : job["begin"] + unit] for core in (0, 1)
+                )
+            for begin in range(0, count * size, 768):
+                span = slice(begin, begin + 768)
+                value = tm(arrays[left][:, span], mine[...]) + tm(places[left][:, span], theirs[...])
+                held[span, :] = value.astype(BF16)
+        for place in range(count):
+            begin = pl.multiple_of(shard_at(place, order, n_ctx) * size, 16)
+            target = kept_ref if place < count // 2 else sent_ref
+            target[place % (count // 2), at : at + size, :] = held[pl.ds(begin, size), :]
+    for copy in copies:
+        copy.wait_send()
+
+
+class Halving:
+    def __init__(self, packed, x_first):
+        self.sent, self.kept = packed
+        self.order = exchange_order(x_first)
+        self.total = None
+
+    def step(self, after):
+        key, self.order = self.order[0], self.order[1:]
+        got = flip(self.sent, *key)
+        got, kept, after = lax.optimization_barrier((got, self.kept, after))
+        if not self.order:
+            self.total = kept[0].astype(F32) + got[0].astype(F32)
+            self.total, after = lax.optimization_barrier((self.total, after))
+            return after
+        cut = kept.shape[0] // 2
+        sent = (kept[cut:].astype(F32) + got[cut:].astype(F32)).astype(BF16)
+        kept = (kept[:cut].astype(F32) + got[:cut].astype(F32)).astype(BF16)
+        self.sent, self.kept, after = lax.optimization_barrier((sent, kept, after))
+        return after
+
+
+def finish(steps):
+    after = jnp.zeros((), F32)
+    for chain in steps:
+        if chain.order:
+            after = chain.step(after)
+
+
+def layer_backward(w, saved, g_tok, g_chr, ids, ids_other, live, onehot, counts, seen, place, section, earlier):
     g_tok, g_chr = g_tok.astype(F32), g_chr.astype(F32)
     rows, width = g_tok.shape
     gains = w["gains"]
     n_ctx = lax.axis_size(CTX)
-    x_first = bits_of(DP) + bits_of(CTX)
-    y_first = bits_of(DP)[::-1] + bits_of(CTX)
-    made = {}
+    count = lax.axis_size(DP) * n_ctx
+    unit = width // 2
+    block = width // count
     d_tok, gain3, shift3 = norm_back(saved["tok_sum"], gains[2], g_tok)
     d_chr, gain4, shift4 = norm_back(saved["chr_sum"], gains[3], g_chr)
     d_lifted = d_tok + mm(onehot, d_chr.astype(BF16))
     d_mixed = (d_lifted * gelu_slope(saved["mixed"])).astype(BF16)
-    made["conv"] = reduce_scattered(
-        [(halves.inputs(saved["three"]), halves.grads(d_mixed))], w["conv"].shape[0], x_first
-    )
     around = three_taps(d_mixed, -1)
-    conv = w["conv"]
+    conv = w["conv"].reshape(-1, 2 * width, width)
     d_joined = mt(around[:, :width], conv[0])
     for tap in range(1, conv.shape[0]):
         d_joined = d_joined + mt(around[:, tap * width : (tap + 1) * width], conv[tap])
     d_feat = d_tok + d_joined[:, :width]
     d_second, gain2, shift2 = norm_back(saved["second"], gains[1], d_feat)
     d_ffn = d_second.astype(BF16)
-    made["down"] = reduce_scattered([(halves.inputs(saved["active"]), halves.grads(d_ffn))], 1, y_first)
     d_hidden = (mt(d_ffn, w["down"]) * gelu_slope(saved["hidden"])).astype(BF16)
-    made["up"] = reduce_scattered(
-        [(halves.inputs(saved["normed_low"]), halves.grads(d_hidden))], 1, x_first
-    )
+    if earlier:
+        d_hidden = earlier[0].step(d_hidden)
     d_normed = d_second + mt(d_hidden, w["up"])
     d_first, gain1, shift1 = norm_back(saved["first"], gains[0], d_normed)
     d_branch = d_first.astype(BF16)
-    made["out"] = reduce_scattered(
-        [(halves.inputs(saved["attended"]), halves.grads(d_branch))], 1, y_first
-    )
+    group = Packing(section, unit, True)
+    taps = conv.shape[0]
+    left, right = group.operand(saved["joined"]), group.operand(around, [(t * width, unit) for t in range(taps)])
+    for tap in range(taps):
+        group.product(left, right, tap * width, unit, tap * unit, 2 * block)
+    ups = d_hidden.shape[1] // 2
+    left, right = group.operand(saved["normed_low"]), group.operand(d_hidden, [(0, ups)])
+    for begin in range(0, ups, unit):
+        group.product(left, right, begin, ups, begin, block)
+    left, right = group.operand(saved["attended"]), group.operand(d_branch, [(0, unit)])
+    group.product(left, right, 0, unit, 0, block)
+    first_pack = group.run(0)
+    *first_pack, d_branch = lax.optimization_barrier((*first_pack, d_branch))
     d_attended = mt(d_branch, w["out"]).astype(BF16)
     dq, dk, dv = attend_back(
         saved["query"], saved["keys"], saved["values"], seen, saved["lse"], d_attended
     )
-    wide = halves.inputs(saved["x_all"])
-    made["qkv"] = reduce_scattered(
-        [
-            (halves.inputs(saved["x"]), halves.grads(dq)),
-            (wide, halves.grads(dk)),
-            (wide, halves.grads(dv)),
-        ],
-        1,
-        y_first,
-    )
+    if earlier:
+        dq = earlier[1].step(dq)
     qkv = w["qkv"]
     parts = mt(dk, qkv[:, width : 2 * width]) + mt(dv, qkv[:, 2 * width :])
     d_x = d_first + mt(dq, qkv[:, :width]) + parts[:rows]
@@ -485,24 +633,19 @@
     whole, _ = joined_scan(scan_back_kernel, half, place, (d_states, proj, live), True)
     pieces = []
     for side in (0, 1):
-        at = slice(side * half, (side + 1) * half)
+        cols = slice(side * half, (side + 1) * half)
         if side == 0:
-            before = jnp.concatenate([entering[:, at], states[:-CHUNKS, at]], axis=0)
+            before = jnp.concatenate([entering[:, cols], states[:-CHUNKS, cols]], axis=0)
         else:
-            before = jnp.concatenate([states[CHUNKS:, at], entering[:, at]], axis=0)
+            before = jnp.concatenate([states[CHUNKS:, cols], entering[:, cols]], axis=0)
         opened = jax.nn.sigmoid(proj[:, 2 * side * half : (2 * side + 1) * half])
         target = proj[:, (2 * side + 1) * half : (2 * side + 2) * half]
-        flow = jnp.where(live > 0.0, whole[:, at] * opened, 0.0)
+        flow = jnp.where(live > 0.0, whole[:, cols] * opened, 0.0)
         pieces += [flow * (1.0 - opened) * (target - before), flow]
     d_proj = jnp.concatenate(pieces, axis=1).astype(BF16)
-    made["gru"] = reduce_scattered(
-        [(halves.inputs(saved["chars_low"]), halves.grads(d_proj))], 1, y_first
-    )
     d_c = (d_chr + mt(d_proj, w["gru"])).astype(BF16)
-    vocab = -(-w["table"].shape[0] // 256) * 256
-    names = jnp.concatenate([ids, ids_other])[:, None] - halves.section * (vocab // 2)
-    named = (names == jnp.arange(vocab // 2)[None, :]).astype(BF16)
-    made["table"] = reduce_scattered([(halves.inputs(d_c), named)], 1, x_first)
+    if earlier:
+        d_c = earlier[0].step(d_c)
     small = (
         jnp.stack(
             [column_sums(dq), column_sums(dv), column_sums(d_branch), column_sums(d_ffn), column_sums(d_mixed)]
@@ -512,7 +655,38 @@
         jnp.stack([shift1, shift2, shift3, shift4]),
         column_sums(d_proj)[None],
     )
-    return d_x.astype(BF16), d_c, made, small
+    packed = jnp.concatenate(
+        [jnp.swapaxes(p.reshape(p.shape[0], count, -1), 0, 1).reshape(count, -1) for p in small], axis=1
+    )
+    packed = jnp.pad(packed, ((0, 0), (0, 16 * unit - packed.shape[1])))
+    group = Packing(section, unit, False)
+    left, right = group.operand(saved["active"]), group.operand(d_ffn, [(0, unit)])
+    group.product(left, right, 0, unit, 0, 4 * block)
+    left, right = group.operand(saved["x"]), group.operand(dq, [(0, unit)])
+    group.product(left, right, 0, unit, 0, block)
+    left = group.operand(saved["x_all"])
+    for grad in (dk, dv):
+        group.product(left, group.operand(grad, [(0, unit)]), 0, unit, 0, block)
+    left, right = group.operand(saved["chars_low"]), group.operand(d_proj, [(0, width)])
+    for begin in range(0, width, unit):
+        group.product(left, right, begin, width, begin, block)
+    left = group.operand(d_c)
+    split = table_split(w["table"].shape[0])
+    named = []
+    for names in (ids, ids_other):
+        names = names[:, None] - section * split
+        named.append((names == jnp.arange(2 * unit)[None, :]).astype(BF16))
+    right = group.local(*named)
+    for begin in (0, unit):
+        group.product(left, right, begin, 0, 0, block)
+    group.plain(packed.astype(BF16).reshape(-1, unit), 16)
+    second_pack = group.run(1)
+    sizes = [(p.shape[0], p.size // count // p.shape[0]) for p in small]
+    return d_x.astype(BF16), d_c, first_pack, second_pack, sizes
+
+
+def table_split(vocab):
+    return -(-vocab // 256) * 128
 
 
 def on_device(
@@ -522,8 +696,8 @@
     section, place = lax.axis_index(SEC), lax.axis_index(CTX)
     n_dp, n_ctx = lax.axis_size(DP), lax.axis_size(CTX)
     is_first = section == 0
-    names = ("gru", "table", "qkv", "out", "up", "down", "conv", "biases", "b_up", "gains", "shifts", "b_gru")
-    local = (w_gru, char_table, w_qkv, w_out, w_up, w_down, w_conv, biases, b_up, ln_gain, ln_shift, b_gru)
+    names = ("gru", "table", "qkv", "out", "up", "down", "conv")
+    local = (w_gru, char_table, w_qkv, w_out, w_up, w_down, w_conv)
     chars_here = jax.vmap(interleave)(char_ends[0])
 
     def dealt(pair):
@@ -534,12 +708,21 @@
     x, cot_tok = dealt(ends[0])
     c, cot_chr = dealt(chars_here)
     layers = ({}, {})
+
+    def spread(own):
+        other = swap(own)
+        return jnp.where(is_first, own, other), jnp.where(is_first, other, own)
+
     for name, value in zip(names, local):
-        own = value[0]
-        other = swap(own)
-        layers[0][name] = jnp.where(is_first, own, other)
-        layers[1][name] = jnp.where(is_first, other, own)
-    rows = x.shape[0]
+        for layer, own in zip(layers, spread(value[0].reshape(-1, value.shape[-1]))):
+            layer[name] = own
+    vectors = (biases, b_up, ln_gain, ln_shift, b_gru)
+    for layer, own in zip(layers, spread(jnp.concatenate([v[0].reshape(-1) for v in vectors]))):
+        at = 0
+        for name, value in zip(("biases", "b_up", "gains", "shifts", "b_gru"), vectors):
+            layer[name] = own[at : at + value[0].size].reshape(value.shape[1:])
+            at += value[0].size
+    rows, width = x.shape
     ids = interleave(pick(char_ids, section))
     ids_other = interleave(pick(char_ids, 1 - section))
     group = interleave(pick(groups, section))
@@ -556,12 +739,18 @@
         x, c, saved = layer_forward(layers[layer], x, c, ids, live, onehot, counts, seen, place)
         kept.append(saved)
     g_x, g_c = cot_tok, cot_chr
-    halves = Halves(section)
-    made, small = [None, None], [None, None]
+    chains = [None, None]
     for layer in (1, 0):
-        g_x, g_c, made[layer], small[layer] = layer_backward(
-            layers[layer], kept[layer], g_x, g_c, ids, ids_other, live, onehot, counts, seen, place, halves
+        g_x, g_c, first_pack, second_pack, sizes = layer_backward(
+            layers[layer], kept[layer], g_x, g_c, ids, ids_other, live, onehot, counts, seen, place, section,
+            chains[1],
         )
+        chains[layer] = (Halving(first_pack, True), Halving(second_pack, False))
+        if layer:
+            g_x, g_c, chains[1][1].sent = lax.optimization_barrier((g_x, g_c, chains[1][1].sent))
+    (x0, y0), (x1, y1) = chains
+    finish([y1, x1, x0, y1, y0, x1, x0, y1, y0, x0, y0, x0, y0] + [x1, y1, x0, y0] * n_dp * n_ctx)
+    packs = [[chain.total for chain in pair] for pair in chains]
 
     def gathered(grad, value):
         got = swap(jnp.where(is_first, value, grad))
@@ -570,59 +759,55 @@
     ends_out = gathered(g_x, x)
     char_ends_out = gathered(restore(g_c), restore(c))
 
-    whole = {}
-    for name in made[0]:
-        mine = jnp.where(is_first, made[0][name], made[1][name])
-        got = swap(jnp.where(is_first, made[1][name], made[0][name]))
-        whole[name] = (jnp.where(is_first, mine, got), jnp.where(is_first, got, mine))
-
-    def sided(name):
-        return jnp.concatenate(whole[name], axis=1)
-
-    d_qkv = jnp.concatenate(
+    both = []
+    for one, two in zip(*packs):
+        mine = jnp.where(is_first, one, two)
+        got = swap(jnp.where(is_first, two, one))
+        both.append((jnp.where(is_first, mine, got), jnp.where(is_first, got, mine)))
+    block = width // (n_dp * n_ctx)
+
+    def columns(which, at, size, parts, crossed=False):
+        cut = [[half[at + i * size : at + (i + 1) * size] for i in range(parts)] for half in both[which]]
+        if crossed:
+            return jnp.concatenate([half[i] for i in range(parts) for half in cut], axis=1)
+        return jnp.concatenate(cut[0] + cut[1], axis=1)
+
+    d_conv = jnp.stack([columns(0, tap * 2 * block, 2 * block, 1) for tap in range(w_conv.shape[1])])
+    at = w_conv.shape[1] * 2 * block
+    ups = w_up.shape[2] // width
+    d_up = columns(0, at, block, ups)
+    d_out = columns(0, at + ups * block, block, 1)
+    d_down = columns(1, 0, ups * block, 1)
+    at = ups * block
+    d_qkv = columns(1, at, block, 3, True)
+    d_gru = columns(1, at + 3 * block, block, 2)
+    at += 5 * block
+    split = table_split(char_table.shape[1])
+    d_table = jnp.concatenate(
         [
-            half[:, part * half.shape[1] // 3 : (part + 1) * half.shape[1] // 3]
-            for part in range(3)
-            for half in whole["qkv"]
+            jnp.concatenate([half[at : at + block], half[at + block : at + 2 * block]], axis=1)[:, :take]
+            for half, take in zip(both[1], (split, char_table.shape[1] - split))
         ],
         axis=1,
-    )
-    d_conv = sided("conv")
-    d_conv = d_conv.reshape(w_conv.shape[1], -1, d_conv.shape[1])
-    d_table = sided("table")[:, : char_table.shape[1]].T
-
-    devices = n_dp * n_ctx
-
-    def by_device(parts):
-        return jnp.concatenate(
-            [jnp.swapaxes(p.reshape(p.shape[0], devices, -1), 0, 1).reshape(devices, -1) for p in parts],
-            axis=1,
-        )
-
-    packed = [by_device(parts) for parts in small]
-    total = jnp.where(is_first, packed[0], packed[1]) + swap(jnp.where(is_first, packed[1], packed[0]))
-    for key in bits_of(DP)[::-1] + bits_of(CTX)[::-1]:
-        view = total.reshape(2, -1, total.shape[1])
-        mine = (lax.axis_index(key[0]) >> key[1]) & 1
-        total = pick(view, mine) + flip(pick(view, 1 - mine), *key)
+    ).T
+    vectors = (both[1][0][at + 2 * block :] + both[1][1][at + 2 * block :]).reshape(-1)
     sums, at = [], 0
-    for parts in small[0]:
-        size = parts.size // devices
-        sums.append(total[0, at : at + size].reshape(parts.shape[0], -1))
-        at += size
+    for parts, size in sizes:
+        sums.append(vectors[at : at + parts * size].reshape(parts, size))
+        at += parts * size
     return (
         ends_out,
         char_ends_out,
         d_qkv[None],
         sums[0][None],
-        sided("out")[None],
-        sided("up")[None],
+        d_out[None],
+        d_up[None],
         sums[1],
-        sided("down")[None],
+        d_down[None],
         sums[2][None],
         sums[3][None],
         d_table[None],
-        sided("gru")[None],
+        d_gru[None],
         sums[4],
         d_conv[None],
     )

time: 1160 us -> 761 us (0.66)
  local copies, waits for them, and re-layouts: 301 us -> 60.6 us
  starting transfers between devices: 181 us -> 76.7 us
  matrix products: 230 us -> 141 us
  Pallas kernels: 61.1 us -> 148 us
  other arithmetic: 136 us -> 82.7 us
    ppermute x116 -> x30, starting transfers between devices: 125 us -> 21.6 us  [flip(): lax.ppermute(value, axis, [(i, i ^ 1 << bit) for i in range(lax.axis_size...]
    dynamic_slice x36 -> x1, local copies, waits for them, and re-layouts: 94.7 us -> 1.24 us  [pick(): return lax.dynamic_index_in_dim(value, index, axis, keepdims=False)]
    dot_general x82 -> x46, matrix products: 230 us -> 141 us  [contract(): lax.dot_general(left, right, (dims, ((), ())), preferred_element_type=F32)]
    pallas_call x0 -> x4, Pallas kernels: none -> 87.7 us  [run(): pl.pallas_call(functools.partial(pack_kernel, self.jobs, self.moves, coun...]
    ppermute x116 -> x30, waiting for transfers between devices: 209 us -> 154 us  [flip(): lax.ppermute(value, axis, [(i, i ^ 1 << bit) for i in range(lax.axis_size...]
    reshape x44 -> x10, local copies, waits for them, and re-layouts: 57.1 us -> 4.46 us  [the longest x6 2.34 us: layer_backward(): jnp.swapaxes(p.reshape(p.shape[0], count, -1), 0, 1).reshape(count, -1)]
    ppermute x24, waiting for transfers between devices: 31.4 us -> 81.3 us  [turned(): lax.ppermute(value, CTX, [(i, (i + by) % count) for i in range(count)])]
    unnamed x746 -> x525, local copies, waits for them, and re-layouts: 67.1 us -> 17.2 us
  transfers between devices with their start and end apart: 148 -> 62, of which waited for: 37 -> 14; matrix products, arithmetic and copies ran while one was open for 56% -> 29% of each run, Pallas kernels for 5% -> 18%
where the time goes in v1:
time: 761 us; the launch traced here: 750 us
  waiting for transfers between devices  236 us (31%)
  Pallas kernels  148 us (19%)
  matrix products  141 us (19%)
  other arithmetic  82.7 us (11%)
  starting transfers between devices  76.7 us (10%)
  local copies, waits for them, and re-layouts  60.6 us (8%)
    ppermute x30, waiting for transfers between devices, flip(): lax.ppermute(value, axis, [(i, i ^ 1 << bit) for i in range(lax.axis_size...  154 us
    dot_general x46, matrix products, contract(): lax.dot_general(left, right, (dims, ((), ())), preferred_element_type=F32)  141 us
    pallas_call x4, Pallas kernels, run(): pl.pallas_call(functools.partial(pack_kernel, self.jobs, self.moves, coun...  87.7 us
    ppermute x24, waiting for transfers between devices, turned(): lax.ppermute(value, CTX, [(i, (i + by) % count) for i in range(count)])  81.3 us
    ppermute x24, starting transfers between devices, turned(): lax.ppermute(value, CTX, [(i, (i + by) % count) for i in range(count)])  36.8 us
    pallas_call x2, Pallas kernels, attend_back(): pl.pallas_call(functools.partial(attend_back_kernel, size), grid=(steps,)...  29.1 us
    pallas_call x2, Pallas kernels, attend(): pl.pallas_call(functools.partial(attend_kernel, size), grid=(steps,), in_...  28 us
    ppermute x30, starting transfers between devices, flip(): lax.ppermute(value, axis, [(i, i ^ 1 << bit) for i in range(lax.axis_size...  21.6 us
  transfers between devices with their start and end apart: 62, of which 14 were waited for; matrix products, arithmetic and copies ran while one was open for 29% of the time, Pallas kernels for 18%

profile of v1, /device:TPU:1, one launch (start us, length us, event | category | flops | bytes accessed | tf_op | source)
XLA Modules:
  0.0 750.4 jit_solution(2798664475310476603)
XLA Ops:
  10.3 2.3 copy.107
  25.4 4.8 collective-permute-start.5
  31.3 3.8 fusion.347
  36.0 3.1 convolution_add_fusion.3.proj_ref
  41.7 22.8 %collective-permute-done.4 = bf16[256,768]{1,0:T(8,128)(2,1)S(1)} collective-permute-done((bf16[256,768]{1,0:T(8,128)(2,1)}, bf16[256,768]{1,0:T(8,128)(2,1)S(1)}, u32[]{:S(2)}, u32[]{:S(2)}) %collective-permute-start.4) | collective-permute-done | bytes 393248 | tf_op jit(solution)/shard_map/ppermute | solution.py:45
  64.7 2.5 pad_maximum_fusion.refs_4_
  73.9 2.5 broadcast_select_fusion.6
  78.9 2.7 convolution_convert_fusion.1.k_ref
  81.6 2.8 add_convert_fusion.9.v_ref
  84.4 13.9 %shard_map.272 = (bf16[256,768]{1,0:T(8,128)(2,1)S(1)}, f32[6,8,256]{2,1,0:T(8,128)S(1)}) custom-call(bf16[256,768]{1,0:T(8,128)(2,1)S(1)} %fusion.124.q_ref, bf16[1024,768]{1,0:T(8,128)(2,1)S(1)} %convolution_convert_fusion.1.k_ref, bf16[1024,768]{1,0:T(8,128)(2,1)S(1)} %add_convert_fusion.9.v_ref, f32[1024,1]{1,0:T(8,128)S(1)} %bitcast.291), custom_call_target="tpu_custom_call" | custom-call | flops 1610612736 | bytes 4718592 | tf_op jit(solution)/shard_map/pallas_call | solution.py:126
  101.1 11.9 %fusion.4 = (bf16[256,3072]{1,0:T(8,128)(2,1)S(1)}, f32[256,3072]{1,0:T(8,128)}) fusion(f32[3072]{0:T(1024)S(1)} %copy-done.177, bf16[256,768]{1,0:T(8,128)(2,1)S(1)} %fusion.224.refs_2_, bf16[768,3072]{1,0:T(8,128)(2,1)} %collective-permute-done.7, pred[]{:T(512)S(6)} %eq.30, bf16[1,768,3072]{2,1,0:T(8,128)(2,1)} %param.25), kind=kOutput, calls=%fused_computation.30 | convolution fusion | flops 1262223360 | bytes 14561281 | tf_op jit(solution)/shard_map/dot_general | solution.py:20
  113.1 4.4 fusion.346
  119.4 4.0 collective-permute-start.15
  124.5 4.3 broadcast_select_fusion
  128.9 5.2 fusion.327
  147.4 6.3 collective-permute-done.21
  153.7 7.1 collective-permute-start.18
  160.8 8.9 %collective-permute-done.22 = f32[8,384]{1,0:T(8,128)S(1)} collective-permute-done((f32[8,384]{1,0:T(8,128)S(1)}, f32[8,384]{1,0:T(8,128)S(1)}, u32[]{:S(2)}, u32[]{:S(2)}) %collective-permute-start.22) | collective-permute-done | bytes 12320 | tf_op jit(solution)/shard_map/ppermute | solution.py:45
  175.7 14.1 %shard_map.274 = (bf16[256,768]{1,0:T(8,128)(2,1)S(1)}, f32[6,8,256]{2,1,0:T(8,128)S(1)}) custom-call(bf16[256,768]{1,0:T(8,128)(2,1)S(1)} %fusion.125.q_ref, bf16[1024,768]{1,0:T(8,128)(2,1)S(1)} %convolution_convert_fusion.k_ref, bf16[1024,768]{1,0:T(8,128)(2,1)S(1)} %add_convert_fusion.8.v_ref, f32[1024,1]{1,0:T(8,128)S(1)} %bitcast.292), custom_call_target="tpu_custom_call" | custom-call | flops 1610612736 | bytes 4718592 | tf_op jit(solution)/shard_map/pallas_call | solution.py:126
  191.1 11.6 %fusion.7 = (bf16[256,3072]{1,0:T(8,128)(2,1)S(1)}, f32[256,3072]{1,0:T(8,128)}) fusion(f32[3072]{0:T(1024)S(1)} %copy-done.176, bf16[256,768]{1,0:T(8,128)(2,1)S(1)} %fusion.227.refs_2_, bf16[768,3072]{1,0:T(8,128)(2,1)} %collective-permute-done.7, pred[]{:T(512)S(6)} %eq.30, bf16[1,768,3072]{2,1,0:T(8,128)(2,1)} %param.25), kind=kOutput, calls=%fused_computation.33 | convolution fusion | flops 1262223360 | bytes 14561281 | tf_op jit(solution)/shard_map/dot_general | solution.py:20
  207.3 4.2 collective-permute-start.24
  212.8 3.9 fusion.324
  225.4 2.8 collective-permute-start.27
  232.5 2.7 fusion.37
  235.3 2.6 fusion.31
  242.2 2.3 collective-permute-start.31
  247.6 4.9 fusion.355
  252.5 2.4 multiply_reduce_fusion.7
  257.4 23.5 %shard_map.276 = (bf16[8,528,384]{2,1,0:T(8,128)(2,1)}, bf16[8,528,384]{2,1,0:T(8,128)(2,1)}) custom-call(bf16[256,1536]{1,0:T(8,128)(2,1)} %pad_maximum_fusion.5.refs_0_, bf16[256,2304]{1,0:T(8,128)(2,1)} %maximum_maximum_fusion.refs_1_, bf16[256,768]{1,0:T(8,128)(2,1)} %copy-done.117, bf16[256,3072]{1,0:T(8,128)(2,1)} %copy-done.235, ...), custom_call_target="tpu_custom_call" | custom-call | flops 3321888768 | bytes 12976128 | tf_op jit(solution)/shard_map/pallas_call | solution.py:439
  282.7 14.5 %shard_map.277 = (bf16[256,768]{1,0:T(8,128)(2,1)S(1)}, bf16[1024,768]{1,0:T(8,128)(2,1)S(1)}, bf16[1024,768]{1,0:T(8,128)(2,1)S(1)}) custom-call(bf16[256,768]{1,0:T(8,128)(2,1)S(1)} %copy-done.23, bf16[1024,768]{1,0:T(8,128)(2,1)S(1)} %copy-done.29, bf16[1024,768]{1,0:T(8,128)(2,1)S(1)} %copy-done.31, f32[1024,1]{1,0:T(8,128)S(1)} %bitcast.293, ...), custom_call_target="tpu_custom_call" | custom-call | flops 4026531840 | bytes 9437184 | tf_op jit(solution)/shard_map/pallas_call | solution.py:176
  300.3 4.3 fusion.131
  307.9 5.8 fusion.353
  314.7 2.6 collective-permute-start.30
  345.1 2.5 add_convert_fusion.20.refs_9_
  348.6 25.9 %shard_map.279 = (bf16[8,544,384]{2,1,0:T(8,128)(2,1)}, bf16[8,544,384]{2,1,0:T(8,128)(2,1)}) custom-call(bf16[256,3072]{1,0:T(8,128)(2,1)} %copy-done.232, bf16[256,768]{1,0:T(8,128)(2,1)} %copy-done.103, bf16[256,768]{1,0:T(8,128)(2,1)} %copy-done.90, bf16[256,768]{1,0:T(8,128)(2,1)} %copy-done.4, bf16[1024,768]{1,0:T(8,128)(2,1)} %pad_maximum_fusion.1.refs_4_, ...), custom_call_target="tpu_custom_call" | custom-call | flops 3422552064 | bytes 13369344 | tf_op jit(solution)/shard_map/pallas_call | solution.py:439
  374.5 2.6 fusion.126
  380.9 3.8 fusion.34
  393.1 2.6 fusion.32
  395.8 2.5 fusion.30
  402.9 3.6 collective-permute-start.43
  408.1 5.8 fusion.1.refs_3_
  420.8 5.4 add_convert_fusion.19.refs_9_
  426.3 4.6 add_convert_fusion.6
  430.9 5.6 multiply_reduce_fusion.3
  437.7 14.0 %shard_map.280 = (bf16[8,528,384]{2,1,0:T(8,128)(2,1)}, bf16[8,528,384]{2,1,0:T(8,128)(2,1)}) custom-call(bf16[256,1536]{1,0:T(8,128)(2,1)} %pad_maximum_fusion.4.refs_0_, bf16[256,2304]{1,0:T(8,128)(2,1)} %maximum_maximum_fusion.1.refs_1_, bf16[256,768]{1,0:T(8,128)(2,1)} %copy-done.116, bf16[256,3072]{1,0:T(8,128)(2,1)} %fusion.1.refs_3_, ...), custom_call_target="tpu_custom_call" | custom-call | flops 3321888768 | bytes 12976128 | tf_op jit(solution)/shard_map/pallas_call | solution.py:439
  454.4 14.6 %shard_map.281 = (bf16[256,768]{1,0:T(8,128)(2,1)S(1)}, bf16[1024,768]{1,0:T(8,128)(2,1)S(1)}, bf16[1024,768]{1,0:T(8,128)(2,1)S(1)}) custom-call(bf16[256,768]{1,0:T(8,128)(2,1)S(1)} %copy-done.21, bf16[1024,768]{1,0:T(8,128)(2,1)S(1)} %copy-done.25, bf16[1024,768]{1,0:T(8,128)(2,1)S(1)} %copy-done.27, f32[1024,1]{1,0:T(8,128)S(1)} %bitcast.294, ...), custom_call_target="tpu_custom_call" | custom-call | flops 4026531840 | bytes 9437184 | tf_op jit(solution)/shard_map/pallas_call | solution.py:176
  470.3 2.3 reduce.14
  473.6 4.5 fusion.138
  478.1 3.9 add_convert_fusion.2
  483.3 13.3 %collective-permute-done.42 = bf16[4,528,384]{2,1,0:T(8,128)(2,1)} collective-permute-done((bf16[4,528,384]{2,1,0:T(8,128)(2,1)}, bf16[4,528,384]{2,1,0:T(8,128)(2,1)}, u32[]{:S(2)}, u32[]{:S(2)}) %collective-permute-start.42) | collective-permute-done | bytes 1622048 | tf_op jit(solution)/shard_map/ppermute | solution.py:36
  496.6 3.2 add_convert_fusion.16
  499.8 24.3 %shard_map.283 = (bf16[8,544,384]{2,1,0:T(8,128)(2,1)}, bf16[8,544,384]{2,1,0:T(8,128)(2,1)}) custom-call(bf16[256,3072]{1,0:T(8,128)(2,1)} %copy-done.231, bf16[256,768]{1,0:T(8,128)(2,1)} %copy-done.102, bf16[256,768]{1,0:T(8,128)(2,1)} %get-tuple-element.364.refs_2_, bf16[256,768]{1,0:T(8,128)(2,1)} %copy-done.6, ...), custom_call_target="tpu_custom_call" | custom-call | flops 3422552064 | bytes 13369344 | tf_op jit(solution)/shard_map/pallas_call | solution.py:439
  525.4 3.6 fusion.356
  529.0 2.9 add_convert_fusion.4
  536.5 8.0 %collective-permute-done.40 = bf16[256,768]{1,0:T(8,128)(2,1)S(1)} collective-permute-done((bf16[256,768]{1,0:T(8,128)(2,1)S(1)}, bf16[256,768]{1,0:T(8,128)(2,1)S(1)}, u32[]{:S(2)}, u32[]{:S(2)}) %collective-permute-start.40) | collective-permute-done | bytes 393248 | tf_op jit(solution)/shard_map/ppermute | solution.py:45
  544.7 18.0 %collective-permute-done.39 = bf16[256,768]{1,0:T(8,128)(2,1)S(1)} collective-permute-done((bf16[256,768]{1,0:T(8,128)(2,1)S(1)}, bf16[256,768]{1,0:T(8,128)(2,1)S(1)}, u32[]{:S(2)}, u32[]{:S(2)}) %collective-permute-start.39) | collective-permute-done | bytes 393248 | tf_op jit(solution)/shard_map/ppermute | solution.py:45
  562.7 17.3 %collective-permute-done.38 = bf16[256,768]{1,0:T(8,128)(2,1)S(1)} collective-permute-done((bf16[256,768]{1,0:T(8,128)(2,1)S(1)}, bf16[256,768]{1,0:T(8,128)(2,1)S(1)}, u32[]{:S(2)}, u32[]{:S(2)}) %collective-permute-start.38) | collective-permute-done | bytes 393248 | tf_op jit(solution)/shard_map/ppermute | solution.py:45
  582.7 49.8 %collective-permute-done.57 = bf16[4,528,384]{2,1,0:T(8,128)(2,1)S(1)} collective-permute-done((bf16[4,528,384]{2,1,0:T(8,128)(2,1)S(1)}, bf16[4,528,384]{2,1,0:T(8,128)(2,1)S(1)}, u32[]{:S(2)}, u32[]{:S(2)}) %collective-permute-start.57) | collective-permute-done | bytes 1622048 | tf_op jit(solution)/shard_map/ppermute | solution.py:36
  639.1 13.0 %collective-permute-done.58 = bf16[2,528,384]{2,1,0:T(8,128)(2,1)S(1)} collective-permute-done((bf16[2,528,384]{2,1,0:T(8,128)(2,1)S(1)}, bf16[2,528,384]{2,1,0:T(8,128)(2,1)S(1)}, u32[]{:S(2)}, u32[]{:S(2)}) %collective-permute-start.58) | collective-permute-done | bytes 811040 | tf_op jit(solution)/shard_map/ppermute | solution.py:36
  654.0 24.7 %collective-permute-done.49 = bf16[2,544,384]{2,1,0:T(8,128)(2,1)S(1)} collective-permute-done((bf16[2,544,384]{2,1,0:T(8,128)(2,1)S(1)}, bf16[2,544,384]{2,1,0:T(8,128)(2,1)S(1)}, u32[]{:S(2)}, u32[]{:S(2)}) %collective-permute-start.49) | collective-permute-done | bytes 835616 | tf_op jit(solution)/shard_map/ppermute | solution.py:36
  679.9 2.6 collective-permute-start.61
  685.3 14.7 %collective-permute-done.55 = bf16[1,544,384]{2,1,0:T(8,128)(2,1)S(1)} collective-permute-done((bf16[1,544,384]{2,1,0:T(8,128)(2,1)S(1)}, bf16[1,544,384]{2,1,0:T(8,128)(2,1)S(1)}, u32[]{:S(2)}, u32[]{:S(2)}) %collective-permute-start.55) | collective-permute-done | bytes 417824 | tf_op jit(solution)/shard_map/ppermute | solution.py:36
  700.9 19.0 %collective-permute-done.53 = bf16[2,544,384]{2,1,0:T(8,128)(2,1)S(1)} collective-permute-done((bf16[2,544,384]{2,1,0:T(8,128)(2,1)S(1)}, bf16[2,544,384]{2,1,0:T(8,128)(2,1)S(1)}, u32[]{:S(2)}, u32[]{:S(2)}) %collective-permute-start.53) | collective-permute-done | bytes 835616 | tf_op jit(solution)/shard_map/ppermute | solution.py:36
  721.8 19.6 %collective-permute-done.54 = bf16[1,544,384]{2,1,0:T(8,128)(2,1)S(1)} collective-permute-done((bf16[1,544,384]{2,1,0:T(8,128)(2,1)S(1)}, bf16[1,544,384]{2,1,0:T(8,128)(2,1)S(1)}, u32[]{:S(2)}, u32[]{:S(2)}) %collective-permute-start.54) | collective-permute-done | bytes 417824 | tf_op jit(solution)/shard_map/ppermute | solution.py:36
  (898 shorter events, 191.8 us)
Async XLA Ops:
  4.4 14.5 %collective-permute-start.2 = (f32[14592]{0:T(1024)S(1)}, f32[14592]{0:T(1024)S(1)}, u32[]{:S(2)}, u32[]{:S(2)}) collective-permute-start(f32[14592]{0:T(1024)S(1)} %constant_dynamic-update-slice_fusion.11), channel_id=1, source_target_pairs={{0,16},{16,0},{1,17},{17,1},{2,18},{18,2},{3,19},{19,3},{4,20},{20... | collective-permute-start | bytes 175112 | tf_op jit(solution)/shard_map/ppermute | solution.py:36
  6.2 16.2 %collective-permute-start = (bf16[256,768]{1,0:T(8,128)(2,1)}, bf16[256,768]{1,0:T(8,128)(2,1)}, u32[]{:S(2)}, u32[]{:S(2)}) collective-permute-start(bf16[256,768]{1,0:T(8,128)(2,1)} %dynamic-slice_bitcast_fusion.1), channel_id=1, source_target_pairs={{0,16},{16,0},{1,17},{17,1},{2,18},{18,2},{3,19},{19,3},{4,20},{20... | collective-permute-start | bytes 1179656 | tf_op jit(solution)/shard_map/ppermute | solution.py:36
  6.7 67.2 %collective-permute-start.1 = (bf16[768,2304]{1,0:T(8,128)(2,1)}, bf16[768,2304]{1,0:T(8,128)(2,1)}, u32[]{:S(2)}, u32[]{:S(2)}) collective-permute-start(bf16[768,2304]{1,0:T(8,128)(2,1)} %bitcast.301), channel_id=1, source_target_pairs={{0,16},{16,0},{1,17},{17,1},{2,18},{18,2},{3,19},{19,3},{4,20},{20... | collective-permute-start | bytes 10616840 | tf_op jit(solution)/shard_map/ppermute | solution.py:36
  6.8 24.5 %collective-permute-start.10 = (bf16[1000,768]{1,0:T(8,128)(2,1)}, bf16[1000,768]{1,0:T(8,128)(2,1)}, u32[]{:S(2)}, u32[]{:S(2)}) collective-permute-start(bf16[1000,768]{1,0:T(8,128)(2,1)} %bitcast.335), channel_id=1, source_target_pairs={{0,16},{16,0},{1,17},{17,1},{2,18},{18,2},{3,19},{19,3},{4,20},{20... | collective-permute-start | bytes 4608008 | tf_op jit(solution)/shard_map/ppermute | solution.py:36
  7.2 27.9 %collective-permute-start.11 = (bf16[768,1536]{1,0:T(8,128)(2,1)}, bf16[768,1536]{1,0:T(8,128)(2,1)}, u32[]{:S(2)}, u32[]{:S(2)}) collective-permute-start(bf16[768,1536]{1,0:T(8,128)(2,1)} %bitcast.334), channel_id=1, source_target_pairs={{0,16},{16,0},{1,17},{17,1},{2,18},{18,2},{3,19},{19,3},{4,20},{20... | collective-permute-start | bytes 7077896 | tf_op jit(solution)/shard_map/ppermute | solution.py:36
  18.8 6.5 collective-permute-start.9
  21.7 216.2 %copy-start.128 = (f32[768]{0:T(1024)}, f32[768]{0:T(1024)S(1)}, u32[]{:S(2)}) copy-start(f32[768]{0:T(1024)S(1)} %get-tuple-element.407) | copy-start | bytes 9220
  21.7 217.5 %copy-start.130 = (f32[768]{0:T(1024)}, f32[768]{0:T(1024)S(1)}, u32[]{:S(2)}) copy-start(f32[768]{0:T(1024)S(1)} %get-tuple-element.406) | copy-start | bytes 9220
  22.4 75.9 %collective-permute-start.6 = (bf16[768,768]{1,0:T(8,128)(2,1)}, bf16[768,768]{1,0:T(8,128)(2,1)}, u32[]{:S(2)}, u32[]{:S(2)}) collective-permute-start(bf16[768,768]{1,0:T(8,128)(2,1)} %bitcast.336), channel_id=1, source_target_pairs={{0,16},{16,0},{1,17},{17,1},{2,18},{18,2},{3,19},{19,3},{4,20},{20... | collective-permute-start | bytes 3538952 | tf_op jit(solution)/shard_map/ppermute | solution.py:36
  25.4 14.7 %collective-permute-start.5 = (bf16[256,768]{1,0:T(8,128)(2,1)}, bf16[256,768]{1,0:T(8,128)(2,1)S(1)}, u32[]{:S(2)}, u32[]{:S(2)}) collective-permute-start(bf16[256,768]{1,0:T(8,128)(2,1)} %get-tuple-element.364.refs_2_), channel_id=1, source_target_pairs={{0,3},{1,0},{2,1},{3,2},{4,7},{5,4},{6,5},{7,6},{8,11},{9,8},{10,9... | collective-permute-start | bytes 1179656 | tf_op jit(solution)/shard_map/ppermute | solution.py:45
  31.3 33.3 %collective-permute-start.4 = (bf16[256,768]{1,0:T(8,128)(2,1)}, bf16[256,768]{1,0:T(8,128)(2,1)S(1)}, u32[]{:S(2)}, u32[]{:S(2)}) collective-permute-start(bf16[256,768]{1,0:T(8,128)(2,1)} %get-tuple-element.364.refs_2_), channel_id=1, source_target_pairs={{0,2},{1,3},{2,0},{3,1},{4,6},{5,7},{6,4},{7,5},{8,10},{9,11},{10,... | collective-permute-start | bytes 1179656 | tf_op jit(solution)/shard_map/ppermute | solution.py:45
  35.1 29.4 %collective-permute-start.3 = (bf16[256,768]{1,0:T(8,128)(2,1)}, bf16[256,768]{1,0:T(8,128)(2,1)S(1)}, u32[]{:S(2)}, u32[]{:S(2)}) collective-permute-start(bf16[256,768]{1,0:T(8,128)(2,1)} %get-tuple-element.364.refs_2_), channel_id=1, source_target_pairs={{0,1},{1,2},{2,3},{3,0},{4,5},{5,6},{6,7},{7,4},{8,9},{9,10},{10,1... | collective-permute-start | bytes 1179656 | tf_op jit(solution)/shard_map/ppermute | solution.py:45
  40.1 27.8 %collective-permute-start.12 = (f32[8,384]{1,0:T(8,128)S(1)}, f32[8,384]{1,0:T(8,128)S(1)}, u32[]{:S(2)}, u32[]{:S(2)}) collective-permute-start(f32[8,384]{1,0:T(8,128)S(1)} %get-tuple-element.135), channel_id=1, source_target_pairs={{0,1},{1,2},{2,3},{3,0},{4,5},{5,6},{6,7},{7,4},{8,9},{9,10},{10,1... | collective-permute-start | bytes 36872 | tf_op jit(solution)/shard_map/ppermute | solution.py:45
  64.6 4.1 collective-permute-start.13
  64.6 5.4 collective-permute-start.14
  67.8 33.3 %collective-permute-start.7 = (bf16[768,3072]{1,0:T(8,128)(2,1)}, bf16[768,3072]{1,0:T(8,128)(2,1)}, u32[]{:S(2)}, u32[]{:S(2)}) collective-permute-start(bf16[768,3072]{1,0:T(8,128)(2,1)} %bitcast.331), channel_id=1, source_target_pairs={{0,16},{16,0},{1,17},{17,1},{2,18},{18,2},{3,19},{19,3},{4,20},{20... | collective-permute-start | bytes 14155784 | tf_op jit(solution)/shard_map/ppermute | solution.py:36
  68.6 44.4 %collective-permute-start.8 = (bf16[3072,768]{1,0:T(8,128)(2,1)}, bf16[3072,768]{1,0:T(8,128)(2,1)}, u32[]{:S(2)}, u32[]{:S(2)}) collective-permute-start(bf16[3072,768]{1,0:T(8,128)(2,1)} %bitcast.322), channel_id=1, source_target_pairs={{0,16},{16,0},{1,17},{17,1},{2,18},{18,2},{3,19},{19,3},{4,20},{20... | collective-permute-start | bytes 14155784 | tf_op jit(solution)/shard_map/ppermute | solution.py:36
  70.0 54.5 %collective-permute-start.17 = (bf16[4608,768]{1,0:T(8,128)(2,1)}, bf16[4608,768]{1,0:T(8,128)(2,1)}, u32[]{:S(2)}, u32[]{:S(2)}) collective-permute-start(bf16[4608,768]{1,0:T(8,128)(2,1)} %bitcast.295), channel_id=1, source_target_pairs={{0,16},{16,0},{1,17},{17,1},{2,18},{18,2},{3,19},{19,3},{4,20},{20... | collective-permute-start | bytes 21233672 | tf_op jit(solution)/shard_map/ppermute | solution.py:36
  118.1 10.8 %collective-permute-start.16 = (bf16[1,1536]{1,0:T(2,128)(2,1)S(1)}, bf16[1,1536]{1,0:T(2,128)(2,1)S(1)}, u32[]{:S(2)}, u32[]{:S(2)}) collective-permute-start(bf16[1,1536]{1,0:T(2,128)(2,1)S(1)} %get-tuple-element.391), channel_id=1, source_target_pairs={{1,0},{2,1},{3,2},{5,4},{6,5},{7,6},{9,8},{10,9},{11,10},{13,12},{... | collective-permute-start | bytes 9224 | tf_op jit(solution)/shard_map/ppermute | solution.py:50
  119.4 9.5 %collective-permute-start.15 = (bf16[1,1536]{1,0:T(2,128)(2,1)S(1)}, bf16[1,1536]{1,0:T(2,128)(2,1)S(1)}, u32[]{:S(2)}, u32[]{:S(2)}) collective-permute-start(bf16[1,1536]{1,0:T(2,128)(2,1)S(1)} %get-tuple-element.390), channel_id=1, source_target_pairs={{0,1},{1,2},{2,3},{4,5},{5,6},{6,7},{8,9},{9,10},{10,11},{12,13},{... | collective-permute-start | bytes 9224 | tf_op jit(solution)/shard_map/ppermute | solution.py:50
  135.0 37.7 %collective-permute-start.20 = (bf16[256,768]{1,0:T(8,128)(2,1)S(1)}, bf16[256,768]{1,0:T(8,128)(2,1)S(1)}, u32[]{:S(2)}, u32[]{:S(2)}) collective-permute-start(bf16[256,768]{1,0:T(8,128)(2,1)S(1)} %add_convert_fusion.31.refs_2_), channel_id=1, source_target_pairs={{0,3},{1,0},{2,1},{3,2},{4,7},{5,4},{6,5},{7,6},{8,11},{9,8},{10,9... | collective-permute-start | bytes 1179656 | tf_op jit(solution)/shard_map/ppermute | solution.py:45
  136.1 36.7 %collective-permute-start.19 = (bf16[256,768]{1,0:T(8,128)(2,1)S(1)}, bf16[256,768]{1,0:T(8,128)(2,1)S(1)}, u32[]{:S(2)}, u32[]{:S(2)}) collective-permute-start(bf16[256,768]{1,0:T(8,128)(2,1)S(1)} %add_convert_fusion.31.refs_2_), channel_id=1, source_target_pairs={{0,2},{1,3},{2,0},{3,1},{4,6},{5,7},{6,4},{7,5},{8,10},{9,11},{10,... | collective-permute-start | bytes 1179656 | tf_op jit(solution)/shard_map/ppermute | solution.py:45
  143.0 10.7 %collective-permute-start.21 = (f32[8,384]{1,0:T(8,128)S(1)}, f32[8,384]{1,0:T(8,128)S(1)}, u32[]{:S(2)}, u32[]{:S(2)}) collective-permute-start(f32[8,384]{1,0:T(8,128)S(1)} %get-tuple-element.140), channel_id=1, source_target_pairs={{0,1},{1,2},{2,3},{3,0},{4,5},{5,6},{6,7},{7,4},{8,9},{9,10},{10,1... | collective-permute-start | bytes 36872 | tf_op jit(solution)/shard_map/ppermute | solution.py:45
  144.5 25.2 %collective-permute-start.22 = (f32[8,384]{1,0:T(8,128)S(1)}, f32[8,384]{1,0:T(8,128)S(1)}, u32[]{:S(2)}, u32[]{:S(2)}) collective-permute-start(f32[8,384]{1,0:T(8,128)S(1)} %get-tuple-element.140), channel_id=1, source_target_pairs={{0,2},{1,3},{2,0},{3,1},{4,6},{5,7},{6,4},{7,5},{8,10},{9,11},{10,... | collective-permute-start | bytes 36872 | tf_op jit(solution)/shard_map/ppermute | solution.py:45
  145.0 24.8 %collective-permute-start.23 = (f32[8,384]{1,0:T(8,128)S(1)}, f32[8,384]{1,0:T(8,128)S(1)}, u32[]{:S(2)}, u32[]{:S(2)}) collective-permute-start(f32[8,384]{1,0:T(8,128)S(1)} %get-tuple-element.140), channel_id=1, source_target_pairs={{0,3},{1,0},{2,1},{3,2},{4,7},{5,4},{6,5},{7,6},{8,11},{9,8},{10,9... | collective-permute-start | bytes 36872 | tf_op jit(solution)/shard_map/ppermute | solution.py:45
  153.7 19.0 %collective-permute-start.18 = (bf16[256,768]{1,0:T(8,128)(2,1)S(1)}, bf16[256,768]{1,0:T(8,128)(2,1)S(1)}, u32[]{:S(2)}, u32[]{:S(2)}) collective-permute-start(bf16[256,768]{1,0:T(8,128)(2,1)S(1)} %add_convert_fusion.31.refs_2_), channel_id=1, source_target_pairs={{0,1},{1,2},{2,3},{3,0},{4,5},{5,6},{6,7},{7,4},{8,9},{9,10},{10,1... | collective-permute-start | bytes 1179656 | tf_op jit(solution)/shard_map/ppermute | solution.py:45
  206.0 6.8 collective-permute-start.25
  207.3 5.5 collective-permute-start.24
  225.4 7.1 collective-permute-start.27
  229.2 6.1 collective-permute-start.26
  242.2 93.5 %collective-permute-start.31 = (f32[8,384]{1,0:T(8,128)S(1)}, f32[8,384]{1,0:T(8,128)}, u32[]{:S(2)}, u32[]{:S(2)}) collective-permute-start(f32[8,384]{1,0:T(8,128)S(1)} %get-tuple-element.151), channel_id=1, source_target_pairs={{0,3},{1,0},{2,1},{3,2},{4,7},{5,4},{6,5},{7,6},{8,11},{9,8},{10,9... | collective-permute-start | bytes 36872 | tf_op jit(solution)/shard_map/ppermute | solution.py:45
  244.5 92.8 %collective-permute-start.32 = (f32[8,384]{1,0:T(8,128)S(1)}, f32[8,384]{1,0:T(8,128)}, u32[]{:S(2)}, u32[]{:S(2)}) collective-permute-start(f32[8,384]{1,0:T(8,128)S(1)} %get-tuple-element.151), channel_id=1, source_target_pairs={{0,2},{1,3},{2,0},{3,1},{4,6},{5,7},{6,4},{7,5},{8,10},{9,11},{10,... | collective-permute-start | bytes 36872 | tf_op jit(solution)/shard_map/ppermute | solution.py:45
  245.5 93.0 %collective-permute-start.33 = (f32[8,384]{1,0:T(8,128)S(1)}, f32[8,384]{1,0:T(8,128)}, u32[]{:S(2)}, u32[]{:S(2)}) collective-permute-start(f32[8,384]{1,0:T(8,128)S(1)} %get-tuple-element.151), channel_id=1, source_target_pairs={{0,1},{1,2},{2,3},{3,0},{4,5},{5,6},{6,7},{7,4},{8,9},{9,10},{10,1... | collective-permute-start | bytes 36872 | tf_op jit(solution)/shard_map/ppermute | solution.py:45
  314.7 59.7 %collective-permute-start.30 = (bf16[256,768]{1,0:T(8,128)(2,1)}, bf16[256,768]{1,0:T(8,128)(2,1)}, u32[]{:S(2)}, u32[]{:S(2)}) collective-permute-start(bf16[256,768]{1,0:T(8,128)(2,1)} %get-tuple-element.362), channel_id=1, source_target_pairs={{0,1},{1,2},{2,3},{3,0},{4,5},{5,6},{6,7},{7,4},{8,9},{9,10},{10,1... | collective-permute-start | bytes 1179656 | tf_op jit(solution)/shard_map/ppermute | solution.py:45
  317.3 57.1 %collective-permute-start.29 = (bf16[256,768]{1,0:T(8,128)(2,1)}, bf16[256,768]{1,0:T(8,128)(2,1)}, u32[]{:S(2)}, u32[]{:S(2)}) collective-permute-start(bf16[256,768]{1,0:T(8,128)(2,1)} %get-tuple-element.363), channel_id=1, source_target_pairs={{0,2},{1,3},{2,0},{3,1},{4,6},{5,7},{6,4},{7,5},{8,10},{9,11},{10,... | collective-permute-start | bytes 1179656 | tf_op jit(solution)/shard_map/ppermute | solution.py:45
  335.7 38.7 %collective-permute-start.28 = (bf16[256,768]{1,0:T(8,128)(2,1)}, bf16[256,768]{1,0:T(8,128)(2,1)}, u32[]{:S(2)}, u32[]{:S(2)}) collective-permute-start(bf16[256,768]{1,0:T(8,128)(2,1)} %get-tuple-element.361), channel_id=1, source_target_pairs={{0,3},{1,0},{2,1},{3,2},{4,7},{5,4},{6,5},{7,6},{8,11},{9,8},{10,9... | collective-permute-start | bytes 1179656 | tf_op jit(solution)/shard_map/ppermute | solution.py:45
  337.3 88.9 %collective-permute-start.36 = (bf16[8,528,384]{2,1,0:T(8,128)(2,1)}, bf16[8,528,384]{2,1,0:T(8,128)(2,1)}, u32[]{:S(2)}, u32[]{:S(2)}) collective-permute-start(bf16[8,528,384]{2,1,0:T(8,128)(2,1)} %get-tuple-element.155), channel_id=1, source_target_pairs={{0,4},{4,0},{8,12},{12,8},{1,5},{5,1},{9,13},{13,9},{2,6},{6,2},{1... | collective-permute-start | bytes 9732104 | tf_op jit(solution)/shard_map/ppermute | solution.py:36
  384.6 8.5 %collective-permute-start.35 = (bf16[1,768]{1,0:T(2,128)(2,1)S(1)}, bf16[1,768]{1,0:T(2,128)(2,1)S(1)}, u32[]{:S(2)}, u32[]{:S(2)}) collective-permute-start(bf16[1,768]{1,0:T(2,128)(2,1)S(1)} %get-tuple-element.397), channel_id=1, source_target_pairs={{0,1},{1,2},{2,3},{4,5},{5,6},{6,7},{8,9},{9,10},{10,11},{12,13},{... | collective-permute-start | bytes 4616 | tf_op jit(solution)/shard_map/ppermute | solution.py:50
  387.1 8.6 %collective-permute-start.34 = (bf16[1,768]{1,0:T(2,128)(2,1)S(1)}, bf16[1,768]{1,0:T(2,128)(2,1)S(1)}, u32[]{:S(2)}, u32[]{:S(2)}) collective-permute-start(bf16[1,768]{1,0:T(2,128)(2,1)S(1)} %get-tuple-element.396), channel_id=1, source_target_pairs={{1,0},{2,1},{3,2},{5,4},{6,5},{7,6},{9,8},{10,9},{11,10},{13,12},{... | collective-permute-start | bytes 4616 | tf_op jit(solution)/shard_map/ppermute | solution.py:50
  388.4 89.7 %collective-permute-start.37 = (bf16[8,544,384]{2,1,0:T(8,128)(2,1)}, bf16[8,544,384]{2,1,0:T(8,128)(2,1)}, u32[]{:S(2)}, u32[]{:S(2)}) collective-permute-start(bf16[8,544,384]{2,1,0:T(8,128)(2,1)} %get-tuple-element.161), channel_id=1, source_target_pairs={{0,8},{4,12},{8,0},{12,4},{1,9},{5,13},{9,1},{13,5},{2,10},{6,14},... | collective-permute-start | bytes 10027016 | tf_op jit(solution)/shard_map/ppermute | solution.py:36
  402.9 12.5 %collective-permute-start.43 = (f32[8,384]{1,0:T(8,128)S(1)}, f32[8,384]{1,0:T(8,128)S(1)}, u32[]{:S(2)}, u32[]{:S(2)}) collective-permute-start(f32[8,384]{1,0:T(8,128)S(1)} %get-tuple-element.179), channel_id=1, source_target_pairs={{0,3},{1,0},{2,1},{3,2},{4,7},{5,4},{6,5},{7,6},{8,11},{9,8},{10,9... | collective-permute-start | bytes 36872 | tf_op jit(solution)/shard_map/ppermute | solution.py:45
  406.5 8.9 %collective-permute-start.44 = (f32[8,384]{1,0:T(8,128)S(1)}, f32[8,384]{1,0:T(8,128)S(1)}, u32[]{:S(2)}, u32[]{:S(2)}) collective-permute-start(f32[8,384]{1,0:T(8,128)S(1)} %get-tuple-element.179), channel_id=1, source_target_pairs={{0,2},{1,3},{2,0},{3,1},{4,6},{5,7},{6,4},{7,5},{8,10},{9,11},{10,... | collective-permute-start | bytes 36872 | tf_op jit(solution)/shard_map/ppermute | solution.py:45
  406.5 8.9 %collective-permute-start.45 = (f32[8,384]{1,0:T(8,128)S(1)}, f32[8,384]{1,0:T(8,128)S(1)}, u32[]{:S(2)}, u32[]{:S(2)}) collective-permute-start(f32[8,384]{1,0:T(8,128)S(1)} %get-tuple-element.179), channel_id=1, source_target_pairs={{0,1},{1,2},{2,3},{3,0},{4,5},{5,6},{6,7},{7,4},{8,9},{9,10},{10,1... | collective-permute-start | bytes 36872 | tf_op jit(solution)/shard_map/ppermute | solution.py:45
  451.8 44.8 %collective-permute-start.42 = (bf16[4,528,384]{2,1,0:T(8,128)(2,1)}, bf16[4,528,384]{2,1,0:T(8,128)(2,1)}, u32[]{:S(2)}, u32[]{:S(2)}) collective-permute-start(bf16[4,528,384]{2,1,0:T(8,128)(2,1)} %get-tuple-element.174), channel_id=1, source_target_pairs={{0,8},{4,12},{8,0},{12,4},{1,9},{5,13},{9,1},{13,5},{2,10},{6,14},... | collective-permute-start | bytes 4866056 | tf_op jit(solution)/shard_map/ppermute | solution.py:36
  452.1 76.9 %collective-permute-start.50 = (bf16[8,528,384]{2,1,0:T(8,128)(2,1)}, bf16[8,528,384]{2,1,0:T(8,128)(2,1)}, u32[]{:S(2)}, u32[]{:S(2)}) collective-permute-start(bf16[8,528,384]{2,1,0:T(8,128)(2,1)} %get-tuple-element.193), channel_id=1, source_target_pairs={{0,4},{4,0},{8,12},{12,8},{1,5},{5,1},{9,13},{13,9},{2,6},{6,2},{1... | collective-permute-start | bytes 9732104 | tf_op jit(solution)/shard_map/ppermute | solution.py:36
  524.1 113.8 %collective-permute-start.47 = (bf16[8,544,384]{2,1,0:T(8,128)(2,1)}, bf16[8,544,384]{2,1,0:T(8,128)(2,1)S(1)}, u32[]{:S(2)}, u32[]{:S(2)}) collective-permute-start(bf16[8,544,384]{2,1,0:T(8,128)(2,1)} %get-tuple-element.184), channel_id=1, source_target_pairs={{0,8},{4,12},{8,0},{12,4},{1,9},{5,13},{9,1},{13,5},{2,10},{6,14},... | collective-permute-start | bytes 10027016 | tf_op jit(solution)/shard_map/ppermute | solution.py:36
  532.0 100.5 %collective-permute-start.57 = (bf16[4,528,384]{2,1,0:T(8,128)(2,1)S(1)}, bf16[4,528,384]{2,1,0:T(8,128)(2,1)S(1)}, u32[]{:S(2)}, u32[]{:S(2)}) collective-permute-start(bf16[4,528,384]{2,1,0:T(8,128)(2,1)S(1)} %get-tuple-element.229), channel_id=1, source_target_pairs={{0,8},{4,12},{8,0},{12,4},{1,9},{5,13},{9,1},{13,5},{2,10},{6,14},... | collective-permute-start | bytes 4866056 | tf_op jit(solution)/shard_map/ppermute | solution.py:36
  532.5 12.0 %collective-permute-start.40 = (bf16[256,768]{1,0:T(8,128)(2,1)S(1)}, bf16[256,768]{1,0:T(8,128)(2,1)S(1)}, u32[]{:S(2)}, u32[]{:S(2)}) collective-permute-start(bf16[256,768]{1,0:T(8,128)(2,1)S(1)} %get-tuple-element.357), channel_id=1, source_target_pairs={{0,1},{1,2},{2,3},{3,0},{4,5},{5,6},{6,7},{7,4},{8,9},{9,10},{10,1... | collective-permute-start | bytes 1179656 | tf_op jit(solution)/shard_map/ppermute | solution.py:45
  534.6 28.0 %collective-permute-start.39 = (bf16[256,768]{1,0:T(8,128)(2,1)S(1)}, bf16[256,768]{1,0:T(8,128)(2,1)S(1)}, u32[]{:S(2)}, u32[]{:S(2)}) collective-permute-start(bf16[256,768]{1,0:T(8,128)(2,1)S(1)} %get-tuple-element.358), channel_id=1, source_target_pairs={{0,2},{1,3},{2,0},{3,1},{4,6},{5,7},{6,4},{7,5},{8,10},{9,11},{10,... | collective-permute-start | bytes 1179656 | tf_op jit(solution)/shard_map/ppermute | solution.py:45
  536.4 45.5 %collective-permute-start.51 = (bf16[2,528,384]{2,1,0:T(8,128)(2,1)S(1)}, bf16[2,528,384]{2,1,0:T(8,128)(2,1)S(1)}, u32[]{:S(2)}, u32[]{:S(2)}) collective-permute-start(bf16[2,528,384]{2,1,0:T(8,128)(2,1)S(1)} %copy-done.100), channel_id=1, source_target_pairs={{0,1},{1,0},{2,3},{3,2},{4,5},{5,4},{6,7},{7,6},{8,9},{9,8},{10,11... | collective-permute-start | bytes 2433032 | tf_op jit(solution)/shard_map/ppermute | solution.py:36
  544.5 91.2 %collective-permute-start.48 = (bf16[4,544,384]{2,1,0:T(8,128)(2,1)S(1)}, bf16[4,544,384]{2,1,0:T(8,128)(2,1)S(1)}, u32[]{:S(2)}, u32[]{:S(2)}) collective-permute-start(bf16[4,544,384]{2,1,0:T(8,128)(2,1)S(1)} %copy-done.87), channel_id=1, source_target_pairs={{0,4},{4,0},{8,12},{12,8},{1,5},{5,1},{9,13},{13,9},{2,6},{6,2},{1... | collective-permute-start | bytes 5013512 | tf_op jit(solution)/shard_map/ppermute | solution.py:36
  562.7 17.3 %collective-permute-start.38 = (bf16[256,768]{1,0:T(8,128)(2,1)S(1)}, bf16[256,768]{1,0:T(8,128)(2,1)S(1)}, u32[]{:S(2)}, u32[]{:S(2)}) collective-permute-start(bf16[256,768]{1,0:T(8,128)(2,1)S(1)} %get-tuple-element.356), channel_id=1, source_target_pairs={{0,3},{1,0},{2,1},{3,2},{4,7},{5,4},{6,5},{7,6},{8,11},{9,8},{10,9... | collective-permute-start | bytes 1179656 | tf_op jit(solution)/shard_map/ppermute | solution.py:45
  581.4 101.1 %collective-permute-start.41 = (bf16[256,768]{1,0:T(8,128)(2,1)S(1)}, bf16[256,768]{1,0:T(8,128)(2,1)S(1)}, u32[]{:S(2)}, u32[]{:S(2)}) collective-permute-start(bf16[256,768]{1,0:T(8,128)(2,1)S(1)} %get-tuple-element.473), channel_id=1, source_target_pairs={{0,16},{16,0},{1,17},{17,1},{2,18},{18,2},{3,19},{19,3},{4,20},{20... | collective-permute-start | bytes 1179656 | tf_op jit(solution)/shard_map/ppermute | solution.py:36
  582.2 55.6 %collective-permute-start.60 = (bf16[1,528,384]{2,1,0:T(8,128)(2,1)S(1)}, bf16[1,528,384]{2,1,0:T(8,128)(2,1)S(1)}, u32[]{:S(2)}, u32[]{:S(2)}) collective-permute-start(bf16[1,528,384]{2,1,0:T(8,128)(2,1)S(1)} %get-tuple-element.241), channel_id=1, source_target_pairs={{0,2},{1,3},{2,0},{3,1},{4,6},{5,7},{6,4},{7,5},{8,10},{9,11},{10,... | collective-permute-start | bytes 1216520 | tf_op jit(solution)/shard_map/ppermute | solution.py:36
  632.9 19.2 %collective-permute-start.58 = (bf16[2,528,384]{2,1,0:T(8,128)(2,1)S(1)}, bf16[2,528,384]{2,1,0:T(8,128)(2,1)S(1)}, u32[]{:S(2)}, u32[]{:S(2)}) collective-permute-start(bf16[2,528,384]{2,1,0:T(8,128)(2,1)S(1)} %get-tuple-element.233), channel_id=1, source_target_pairs={{0,1},{1,0},{2,3},{3,2},{4,5},{5,4},{6,7},{7,6},{8,9},{9,8},{10,11... | collective-permute-start | bytes 2433032 | tf_op jit(solution)/shard_map/ppermute | solution.py:36
  635.7 48.1 %collective-permute-start.46 = (bf16[512,768]{1,0:T(8,128)(2,1)S(1)}, bf16[512,768]{1,0:T(8,128)(2,1)S(1)}, u32[]{:S(2)}, u32[]{:S(2)}) collective-permute-start(bf16[512,768]{1,0:T(8,128)(2,1)S(1)} %bitcast.307), channel_id=1, source_target_pairs={{0,16},{16,0},{1,17},{17,1},{2,18},{18,2},{3,19},{19,3},{4,20},{20... | collective-permute-start | bytes 2359304 | tf_op jit(solution)/shard_map/ppermute | solution.py:36
  637.8 40.9 %collective-permute-start.49 = (bf16[2,544,384]{2,1,0:T(8,128)(2,1)S(1)}, bf16[2,544,384]{2,1,0:T(8,128)(2,1)S(1)}, u32[]{:S(2)}, u32[]{:S(2)}) collective-permute-start(bf16[2,544,384]{2,1,0:T(8,128)(2,1)S(1)} %get-tuple-element.191), channel_id=1, source_target_pairs={{0,1},{1,0},{2,3},{3,2},{4,5},{5,4},{6,7},{7,6},{8,9},{9,8},{10,11... | collective-permute-start | bytes 2506760 | tf_op jit(solution)/shard_map/ppermute | solution.py:36
  638.7 61.4 %collective-permute-start.52 = (bf16[4,544,384]{2,1,0:T(8,128)(2,1)S(1)}, bf16[4,544,384]{2,1,0:T(8,128)(2,1)S(1)}, u32[]{:S(2)}, u32[]{:S(2)}) collective-permute-start(bf16[4,544,384]{2,1,0:T(8,128)(2,1)S(1)} %get-tuple-element.213), channel_id=1, source_target_pairs={{0,4},{4,0},{8,12},{12,8},{1,5},{5,1},{9,13},{13,9},{2,6},{6,2},{1... | collective-permute-start | bytes 5013512 | tf_op jit(solution)/shard_map/ppermute | solution.py:36
  652.3 27.4 %collective-permute-start.59 = (bf16[1,528,384]{2,1,0:T(8,128)(2,1)S(1)}, bf16[1,528,384]{2,1,0:T(8,128)(2,1)S(1)}, u32[]{:S(2)}, u32[]{:S(2)}) collective-permute-start(bf16[1,528,384]{2,1,0:T(8,128)(2,1)S(1)} %get-tuple-element.237), channel_id=1, source_target_pairs={{0,2},{1,3},{2,0},{3,1},{4,6},{5,7},{6,4},{7,5},{8,10},{9,11},{10,... | collective-permute-start | bytes 1216520 | tf_op jit(solution)/shard_map/ppermute | solution.py:36
  678.9 21.1 %collective-permute-start.55 = (bf16[1,544,384]{2,1,0:T(8,128)(2,1)S(1)}, bf16[1,544,384]{2,1,0:T(8,128)(2,1)S(1)}, u32[]{:S(2)}, u32[]{:S(2)}) collective-permute-start(bf16[1,544,384]{2,1,0:T(8,128)(2,1)S(1)} %get-tuple-element.225), channel_id=1, source_target_pairs={{0,2},{1,3},{2,0},{3,1},{4,6},{5,7},{6,4},{7,5},{8,10},{9,11},{10,... | collective-permute-start | bytes 1253384 | tf_op jit(solution)/shard_map/ppermute | solution.py:36
  679.9 20.7 %collective-permute-start.61 = (f32[528,384]{1,0:T(8,128)S(1)}, f32[528,384]{1,0:T(8,128)S(1)}, u32[]{:S(2)}, u32[]{:S(2)}) collective-permute-start(f32[528,384]{1,0:T(8,128)S(1)} %broadcast_select_fusion.47), channel_id=1, source_target_pairs={{0,16},{16,0},{1,17},{17,1},{2,18},{18,2},{3,19},{19,3},{4,20},{20... | collective-permute-start | bytes 2433032 | tf_op jit(solution)/shard_map/ppermute | solution.py:36
  700.5 19.3 %collective-permute-start.53 = (bf16[2,544,384]{2,1,0:T(8,128)(2,1)S(1)}, bf16[2,544,384]{2,1,0:T(8,128)(2,1)S(1)}, u32[]{:S(2)}, u32[]{:S(2)}) collective-permute-start(bf16[2,544,384]{2,1,0:T(8,128)(2,1)S(1)} %get-tuple-element.217), channel_id=1, source_target_pairs={{0,1},{1,0},{2,3},{3,2},{4,5},{5,4},{6,7},{7,6},{8,9},{9,8},{10,11... | collective-permute-start | bytes 2506760 | tf_op jit(solution)/shard_map/ppermute | solution.py:36
  720.0 21.4 %collective-permute-start.54 = (bf16[1,544,384]{2,1,0:T(8,128)(2,1)S(1)}, bf16[1,544,384]{2,1,0:T(8,128)(2,1)S(1)}, u32[]{:S(2)}, u32[]{:S(2)}) collective-permute-start(bf16[1,544,384]{2,1,0:T(8,128)(2,1)S(1)} %get-tuple-element.221), channel_id=1, source_target_pairs={{0,2},{1,3},{2,0},{3,1},{4,6},{5,7},{6,4},{7,5},{8,10},{9,11},{10,... | collective-permute-start | bytes 1253384 | tf_op jit(solution)/shard_map/ppermute | solution.py:36
  741.6 2.6 collective-permute-start.56
  (248 other events, 2544.0 us)

commit v2 on v1

v2 whole, which is shorter than its diff:
```python
import functools

import jax
import jax.numpy as jnp
from jax import lax
from jax.experimental import pallas as pl
from jax.experimental.pallas import tpu as pltpu
from jax.sharding import PartitionSpec as P

HEADS = 12
CHUNKS = 8
NORM_EPS = 1e-06
MASKED = -1000000000.0
SEC, DP, CTX = "section", "dp", "ctx"
F32, BF16 = jnp.float32, jnp.bfloat16
MIB = 2**20


def contract(left, right, dims):
    return lax.dot_general(left, right, (dims, ((), ())), preferred_element_type=F32)


def mm(left, right):
    return contract(left, right, ((1,), (0,)))


def mt(left, right):
    return contract(left, right, ((1,), (1,)))


def tm(left, right):
    return contract(left, right, ((0,), (0,)))


def flip(value, axis, bit):
    return lax.ppermute(value, axis, [(i, i ^ (1 << bit)) for i in range(lax.axis_size(axis))])


def swap(value):
    return flip(value, SEC, 0)


def turned(value, by):
    count = lax.axis_size(CTX)
    return lax.ppermute(value, CTX, [(i, (i + by) % count) for i in range(count)])


def pick(value, index, axis=0):
    return lax.dynamic_index_in_dim(value, index, axis, keepdims=False)


def interleave(value):
    rows = value.shape[0]
    return jnp.swapaxes(
        value.reshape((CHUNKS, rows // CHUNKS) + value.shape[1:]), 0, 1
    ).reshape(value.shape)


def restore(value):
    rows = value.shape[0]
    return jnp.swapaxes(
        value.reshape((rows // CHUNKS, CHUNKS) + value.shape[1:]), 0, 1
    ).reshape(value.shape)


def params(mib):
    return pltpu.CompilerParams(vmem_limit_bytes=mib * MIB)


def attend_back_kernel(
    size, q_ref, k_ref, v_ref, seen_ref, lse_ref, do_ref, dq_ref, dk_ref, dv_ref
):
    seen = seen_ref[...] > 0.0
    scale = size**-0.5
    for head in range(q_ref.shape[1] // size):
        at = slice(head * size, (head + 1) * size)
        query, keys, grad = q_ref[:, at], k_ref[:, at], do_ref[:, at]
        scores = jnp.where(seen, mt(keys, query), MASKED)
        probs = jnp.exp(scores - lse_ref[0, head : head + 1, :])
        g_probs = mt(v_ref[:, at], grad)
        row = jnp.sum(g_probs * probs, axis=0, keepdims=True)
        g_scores = (probs * (g_probs - row)).astype(BF16)
        dv_ref[:, at] = mm(probs.astype(BF16), grad).astype(BF16)
        dk_ref[:, at] = mm(g_scores, query).astype(BF16)
        dq_ref[:, at] = (tm(g_scores, keys) * scale).astype(BF16)


def attend_back(query, keys, values, seen, lse, grad):
    rows, width = query.shape
    count = keys.shape[0]
    size = width // HEADS
    block = 2 * size
    steps = width // block
    by_rows = pl.BlockSpec((rows, block), lambda i: (0, i))
    by_keys = pl.BlockSpec((count, block), lambda i: (0, i))
    return pl.pallas_call(
        functools.partial(attend_back_kernel, size),
        grid=(steps,),
        in_specs=[
            by_rows,
            by_keys,
            by_keys,
            pl.BlockSpec((count, 1), lambda i: (0, 0)),
            pl.BlockSpec((1, 8, rows), lambda i: (i, 0, 0)),
            by_rows,
        ],
        out_specs=[by_rows, by_keys, by_keys],
        out_shape=[
            jax.ShapeDtypeStruct((rows, width), BF16),
            jax.ShapeDtypeStruct((count, width), BF16),
            jax.ShapeDtypeStruct((count, width), BF16),
        ],
        compiler_params=params(40),
        cost_estimate=pl.CostEstimate(flops=1, bytes_accessed=1, transcendentals=0),
    )(query, keys, values, seen, lse, grad)


MESH = pl.DeviceIdType.MESH


def fetch(layer, own, other, target, semaphore):
    section = lax.axis_index(SEC)
    copies = [pltpu.make_async_copy(source, target, semaphore) for source in (own, other)]

    @pl.when(section == layer)
    def _():
        copies[0].start()

    @pl.when(section != layer)
    def _():
        copies[1].start()

    return copies[0]


def greet(hops):
    barrier = pltpu.get_barrier_semaphore()
    count = lax.axis_size(CTX)
    for hop in hops:
        to = lax.rem(lax.axis_index(CTX) + hop, count)
        pl.semaphore_signal(barrier, inc=1, device_id={CTX: to}, device_id_type=MESH)
    pl.semaphore_wait(barrier, len(hops))


def send(source, target, hop, send_sem, recv_sem):
    to = lax.rem(lax.axis_index(CTX) + hop, lax.axis_size(CTX))
    copy = pltpu.make_async_remote_copy(
        src_ref=source, dst_ref=target, send_sem=send_sem, recv_sem=recv_sem,
        device_id={CTX: to}, device_id_type=MESH,
    )
    copy.start()
    return copy


class Relay:
    def __init__(self, source, slots, sems):
        self.source, self.slots, self.sems = source, slots, sems
        self.rows, self.count, self.place = source.shape[0], lax.axis_size(CTX), lax.axis_index(CTX)

    def slot(self, j):
        return self.slots.at[j * self.rows : (j + 1) * self.rows, :]

    def copies(self, step):
        n, me = self.count, self.place
        right = (me < n - 1) & (me >= step - 1)
        left = (me > 0) & (me <= n - step)
        for nth, (there, going, to, slot, held) in enumerate(
            ((1, right, step, step, step - 1), (n - 1, left, n - step, n - step, n - step + 1))
        ):
            source = self.source if step == 1 else self.slot(held)
            copy = pltpu.make_async_remote_copy(
                src_ref=source, dst_ref=self.slot(slot),
                send_sem=self.sems[0].at[2 * step - 2 + nth], recv_sem=self.sems[1].at[slot - 1],
                device_id={CTX: lax.rem(me + there, n)}, device_id_type=MESH,
            )
            yield going, held, copy

    def wait(self, slot):
        pltpu.make_async_remote_copy(
            src_ref=self.source, dst_ref=self.slot(slot),
            send_sem=self.sems[0].at[0], recv_sem=self.sems[1].at[slot - 1],
            device_id={CTX: lax.rem(self.place + 1, self.count)}, device_id_type=MESH,
        ).wait_recv()

    def start(self, step):
        for nth, (going, held, copy) in enumerate(self.copies(step)):
            if step > 1:
                came = (self.place >= step - 1) if nth == 0 else (self.place <= self.count - step)
                pl.when(came)(functools.partial(self.wait, held))
            pl.when(going)(copy.start)

    def finish(self):
        n, me = self.count, self.place
        pl.when(me == n - 1)(functools.partial(self.wait, n - 1))
        pl.when(me == 0)(functools.partial(self.wait, 1))
        for step in range(1, n):
            for going, _, copy in self.copies(step):
                pl.when(going)(copy.wait_send)


def unit_of(values):
    centred = values - jnp.mean(values, axis=1, keepdims=True)
    scale = lax.rsqrt(jnp.mean(centred * centred, axis=1, keepdims=True) + NORM_EPS)
    return centred * scale, scale


def unit_back(unit, scale, inner):
    mean = jnp.mean(inner, axis=1, keepdims=True)
    along = jnp.mean(inner * unit, axis=1, keepdims=True)
    return scale * (inner - mean - unit * along)


def gelu_pair(values):
    size = jnp.abs(values)
    bell = jnp.exp(-0.5 * values * values)
    t = 1.0 / (1.0 + (0.3275911 * 0.7071067811865476) * size)
    poly = t * (
        0.254829592 + t * (-0.284496736 + t * (1.421413741 + t * (-1.453152027 + t * 1.061405429)))
    )
    tail = 0.5 * poly * bell
    cdf = jnp.where(values >= 0.0, 1.0 - tail, tail)
    return values * cdf, cdf + values * (bell * 0.3989422804014327)


def gates(proj_ref, live_ref, at, rate, width):
    live = live_ref[at, :] > 0.0
    opened = jax.nn.sigmoid(proj_ref[at, rate : rate + width])
    return jnp.where(live, 1.0 - opened, 1.0), live, opened


def step_rows(step):
    return pl.ds(pl.multiple_of(step * CHUNKS, CHUNKS), CHUNKS)


def join_chunks(carry_ref, total_ref, slot, state, decay, order):
    width = state.shape[1]
    before = jnp.zeros((1, width), F32)
    faded = jnp.ones((1, width), F32)
    for chunk in order:
        carry_ref[slot, chunk : chunk + 1, :] = before
        carry_ref[slot + 1, chunk : chunk + 1, :] = faded
        own = decay[chunk : chunk + 1, :]
        before = own * before + state[chunk : chunk + 1, :]
        faded = own * faded
    total_ref[slot : slot + 1, :] = before
    total_ref[slot + 1 : slot + 2, :] = faded
    if slot:
        total_ref[4:8, :] = jnp.zeros((4, width), F32)


def entering_chunks(carry_ref, total_ref, inbox_ref, sems, reverse):
    count, place = lax.axis_size(CTX), lax.axis_index(CTX)
    width = total_ref.shape[1]
    copies = [
        send(total_ref, inbox_ref.at[j - 1], j, sems[0].at[j - 1], sems[1].at[j - 1])
        for j in range(1, count)
    ]
    for copy in copies:
        copy.wait()
    entering = []
    for slot in (0, 2):
        so_far = jnp.zeros((1, width), F32)
        rising = (slot == 0) != reverse
        for hop in range(count - 1, 0, -1):
            there = inbox_ref.at[(hop if rising else count - hop) - 1]
            valid = (place >= hop) if rising else (place + hop < count)
            longer = there[slot + 1 : slot + 2, :] * so_far + there[slot : slot + 1, :]
            so_far = jnp.where(valid, longer, so_far)
        entering.append(carry_ref[slot] + carry_ref[slot + 1] * so_far)
    return entering


def by_step(values):
    return values.reshape(values.shape[0] // CHUNKS, CHUNKS, values.shape[1])


def chars_kernel(
    layer, x_ref, c_ref, ids_ref, live_ref, group_ref, bias_ref, table_a, table_b, gru_a, gru_b,
    all_ref, chars_ref, low_ref, proj_ref, state_ref, entering_ref, pooled_ref,
    table_v, gru_v, decay_ref, carry_ref, total_ref, inbox_ref, fetch_sems, x_sems, total_sems,
):
    count = lax.axis_size(CTX)
    rows = x_ref.shape[0]
    width = proj_ref.shape[1] // 4
    steps = proj_ref.shape[0] // CHUNKS
    table = fetch(layer, table_a, table_b, table_v, fetch_sems.at[0])
    gru = fetch(layer, gru_a, gru_b, gru_v, fetch_sems.at[1])
    greet(range(1, count))
    relay = Relay(x_ref, all_ref, x_sems)
    relay.start(1)
    all_ref[0:rows, :] = x_ref[...]
    table.wait()
    names = lax.broadcasted_iota(jnp.int32, (c_ref.shape[0], table_v.shape[0]), 1)
    named = jnp.where(names == ids_ref[...], 1.0, 0.0).astype(BF16)
    chars = c_ref[...].astype(F32) + mm(named, table_v[...])
    chars_ref[...] = chars
    low_ref[...] = chars.astype(BF16)
    gru.wait()
    proj_ref[...] = mm(low_ref[...], gru_v[...]) + bias_ref[...]
    relay.start(2)
    unroll = 8

    def step(i, carry):
        state_f, decay_f, state_b, decay_b = carry
        for u in range(unroll):
            at = step_rows(i * unroll + u)
            keep, live, opened = gates(proj_ref, live_ref, at, 0, width)
            inflow = jnp.where(live, opened * proj_ref[at, width : 2 * width], 0.0)
            state_f = keep * state_f + inflow
            decay_f = keep * decay_f
            state_ref[at, 0:width] = state_f
            decay_ref[at, 0:width] = decay_f
            at = step_rows(steps - 1 - i * unroll - u)
            keep, live, opened = gates(proj_ref, live_ref, at, 2 * width, width)
            inflow = jnp.where(live, opened * proj_ref[at, 3 * width : 4 * width], 0.0)
            state_b = keep * state_b + inflow
            decay_b = keep * decay_b
            state_ref[at, width : 2 * width] = state_b
            decay_ref[at, width : 2 * width] = decay_b
        return state_f, decay_f, state_b, decay_b

    zero = jnp.zeros((CHUNKS, width), F32)
    one = jnp.ones((CHUNKS, width), F32)
    state_f, decay_f, state_b, decay_b = lax.fori_loop(
        0, steps // unroll, step, (zero, one, zero, one)
    )
    join_chunks(carry_ref, total_ref, 0, state_f, decay_f, range(CHUNKS))
    join_chunks(carry_ref, total_ref, 2, state_b, decay_b, range(CHUNKS - 1, -1, -1))
    entering = entering_chunks(carry_ref, total_ref, inbox_ref, total_sems, False)
    for side, carried in enumerate(entering):
        at = slice(side * width, (side + 1) * width)
        entering_ref[:, at] = carried
        whole = by_step(state_ref[:, at]) + by_step(decay_ref[:, at]) * carried[None]
        state_ref[:, at] = whole.reshape(steps * CHUNKS, width)
    tokens = lax.broadcasted_iota(jnp.int32, (rows, group_ref.shape[1]), 0)
    onehot = jnp.where(tokens == group_ref[...], 1.0, 0.0)
    counts = jnp.sum(onehot, axis=1, keepdims=True)
    pooled_ref[...] = (mm(onehot.astype(BF16), state_ref[...].astype(BF16)) / counts).astype(BF16)
    for step in range(3, count):
        relay.start(step)
    relay.finish()


VMEM_SPEC = pl.BlockSpec(memory_space=pltpu.VMEM)
ANY_SPEC = pl.BlockSpec(memory_space=pl.ANY)
DMA = pltpu.SemaphoreType.DMA


def call(kernel, plain, weights, outs, scratch, collective_id=None):
    options = {} if collective_id is None else dict(collective_id=collective_id, has_side_effects=True)
    return pl.pallas_call(
        kernel,
        in_specs=[VMEM_SPEC] * len(plain) + [ANY_SPEC] * len(weights),
        out_specs=[VMEM_SPEC] * len(outs),
        out_shape=[jax.ShapeDtypeStruct(*o) for o in outs],
        scratch_shapes=scratch,
        compiler_params=pltpu.CompilerParams(vmem_limit_bytes=58 * MIB, **options),
        cost_estimate=pl.CostEstimate(flops=1, bytes_accessed=1, transcendentals=0),
    )(*plain, *weights)


def room(weight):
    return pltpu.VMEM(weight.shape, weight.dtype)


def deal_kernel(
    lengths_ref, e_ref, ce_ref, rows_ref, columns_ref, vec_ref, inner_ref, gru_ref, table_ref,
    x_ref, cot_ref, c_ref, ccot_ref, vec0_ref, vec1_ref, inner0_ref, inner1_ref,
    ids_ref, other_ref, live_ref, row_ref, column_ref, seen_ref, gru_out, table_out,
    e_in, ce_in, vec_in, inner_in, sems,
):
    section, place = lax.axis_index(SEC), lax.axis_index(CTX)
    rows = x_ref.shape[0]
    barrier = pltpu.get_barrier_semaphore()
    pl.semaphore_signal(barrier, inc=1, device_id={SEC: 1 - section}, device_id_type=MESH)
    pl.semaphore_wait(barrier, 1)
    copies = []
    for nth, (source, target) in enumerate(
        (
            (e_ref.at[1 - section], e_in), (ce_ref.at[1 - section], ce_in), (vec_ref, vec_in),
            (inner_ref, inner_in), (table_ref, table_out), (gru_ref, gru_out),
        )
    ):
        copy = pltpu.make_async_remote_copy(
            src_ref=source, dst_ref=target, send_sem=sems[0].at[nth], recv_sem=sems[1].at[nth],
            device_id={SEC: 1 - section}, device_id_type=MESH,
        )
        copy.start()
        copies.append(copy)
    first = section == 0
    ids_ref[...] = jnp.where(first, columns_ref[:, 0:1], columns_ref[:, 1:2])
    other_ref[...] = jnp.where(first, columns_ref[:, 1:2], columns_ref[:, 0:1])
    group = jnp.where(first, columns_ref[:, 2:3], columns_ref[:, 3:4])
    live_ref[...] = jnp.where(group >= 0, 1.0, 0.0)
    column_ref[...] = group - place * rows
    row_ref[...] = jnp.where(first, rows_ref[2:3, :], rows_ref[3:4, :]) - place * rows
    length = jnp.where(first, lengths_ref[0], lengths_ref[1])
    count = lax.axis_size(CTX)
    for j in range(count):
        spots = lax.broadcasted_iota(jnp.int32, (rows, 1), 0) + lax.rem(place - j + count, count) * rows
        seen_ref[j * rows : (j + 1) * rows, :] = jnp.where(spots < length, 1.0, 0.0)
    for copy in copies:
        copy.wait()
    x_ref[...] = jnp.where(first, e_ref[0], e_in[...])
    cot_ref[...] = jnp.where(first, e_in[...], e_ref[1])
    c_ref[...] = jnp.where(first, ce_ref[0], ce_in[...])
    ccot_ref[...] = jnp.where(first, ce_in[...], ce_ref[1])
    vec0_ref[...] = jnp.where(first, vec_ref[...], vec_in[...])
    vec1_ref[...] = jnp.where(first, vec_in[...], vec_ref[...])
    inner0_ref[...] = jnp.where(first, inner_ref[...], inner_in[...])
    inner1_ref[...] = jnp.where(first, inner_in[...], inner_ref[...])


def deal(lengths, e, ce, indices, vec, inner, gru, table):
    _, rows, width = e.shape
    slots, keys = ce.shape[1], rows * lax.axis_size(CTX)
    tok, char = ((rows, width), BF16), ((slots, width), BF16)
    thin = ((slots, 1), jnp.int32)
    outs = [
        tok, tok, char, char, (vec.shape, F32), (vec.shape, F32), (inner.shape, F32), (inner.shape, F32),
        thin, thin, ((slots, 1), F32), ((1, slots), jnp.int32), thin, ((keys, 1), F32),
        (gru.shape, BF16), (table.shape, BF16),
    ]
    plain = [e, ce, indices, indices.T, vec, inner]
    return pl.pallas_call(
        deal_kernel,
        in_specs=[pl.BlockSpec(memory_space=pltpu.SMEM)] + [VMEM_SPEC] * len(plain) + [ANY_SPEC] * 2,
        out_specs=[VMEM_SPEC] * 14 + [ANY_SPEC] * 2,
        out_shape=[jax.ShapeDtypeStruct(*o) for o in outs],
        scratch_shapes=[
            pltpu.VMEM(*tok), pltpu.VMEM(*char), pltpu.VMEM(vec.shape, F32), pltpu.VMEM(inner.shape, F32),
            [DMA((6,))] * 2,
        ],
        compiler_params=pltpu.CompilerParams(
            vmem_limit_bytes=58 * MIB, collective_id=10, has_side_effects=True
        ),
        cost_estimate=pl.CostEstimate(flops=1, bytes_accessed=1, transcendentals=0),
    )(lengths, *plain, gru, table)


def chars_forward(layer, w, x, c, ids, live, group):
    rows, width = x.shape
    slots = c.shape[0]
    count = lax.axis_size(CTX)
    half = width // 2
    outs = [
        ((count * rows, width), BF16), ((slots, width), F32), ((slots, width), BF16),
        ((slots, 4 * half), F32), ((slots, width), F32), ((CHUNKS, width), F32), ((rows, width), BF16),
    ]
    pair = [DMA((count - 1,))] * 2
    scratch = [
        room(w["table"][0]), room(w["gru"][0]), pltpu.VMEM((slots, width), F32),
        pltpu.VMEM((4, CHUNKS, half), F32), pltpu.VMEM((8, half), F32),
        pltpu.VMEM((count - 1, 8, half), F32), DMA((2,)), [DMA((2 * count - 2,)), DMA((count - 1,))], pair,
    ]
    return call(
        functools.partial(chars_kernel, layer), [x, c, ids, live, group, w["b_gru"]],
        [*w["table"], *w["gru"]], outs, scratch, 2 + layer,
    )


def heads_of(block, size, head):
    lanes = lax.broadcasted_iota(jnp.int32, block.shape, 1)
    return jnp.where(lanes // size == head, block, jnp.zeros_like(block))


def tokens_kernel(
    layer, size, x_ref, seen_ref, vec_ref, bias_ref,
    qkv_a, qkv_b, out_a, out_b, up_a, up_b, down_a, down_b,
    q_ref, k_ref, v_ref, lse_ref, att_ref, unit1_ref, scale1_ref, low_ref, active_ref, slope_ref,
    unit2_ref, scale2_ref, features_ref,
    qkv_v, out_v, up_v, down_v, scores_ref, sems,
):
    rows, width = q_ref.shape
    keys = x_ref.shape[0]
    waits = [
        fetch(layer, a, b, v, sems.at[i])
        for i, (a, b, v) in enumerate(
            [(qkv_a, qkv_b, qkv_v), (out_a, out_b, out_v), (up_a, up_b, up_v), (down_a, down_b, down_v)]
        )
    ]
    waits[0].wait()
    query = (mm(x_ref[0:rows, :], qkv_v[:, 0:width]) + vec_ref[0:1, :]).astype(BF16)
    q_ref[...] = query * jnp.asarray(size**-0.5, BF16)
    for begin in range(0, keys, 256):
        at = slice(begin, begin + 256)
        k_ref[at, :] = mm(x_ref[at, :], qkv_v[:, width : 2 * width]).astype(BF16)
        v_ref[at, :] = (mm(x_ref[at, :], qkv_v[:, 2 * width : 3 * width]) + vec_ref[1:2, :]).astype(BF16)
    block = 128
    heads = block // size

    def pair(i, carry):
        at = pl.ds(pl.multiple_of(i * block, block), block)
        query = q_ref[:, at]
        lanes = lax.broadcasted_iota(jnp.int32, (rows, block), 1)
        result = None
        for head in range(heads):
            mine = heads_of(query, size, head)
            top = jnp.full((1, rows), MASKED, F32)
            for begin in range(0, keys, 256):
                span = slice(begin, begin + 256)
                scores = mt(k_ref[span, at], mine)
                scores = jnp.where(seen_ref[span, :] > 0.0, scores, MASKED)
                scores_ref[span, :] = scores
                top = jnp.maximum(top, jnp.max(scores, axis=0, keepdims=True))
            total = jnp.zeros((1, rows), F32)
            for begin in range(0, keys, 256):
                span = slice(begin, begin + 256)
                weights = jnp.exp(scores_ref[span, :] - top)
                scores_ref[span, :] = weights
                total = total + jnp.sum(weights, axis=0, keepdims=True)
            lse_ref[i, head : head + 1, :] = top + jnp.log(total)
            share = 1.0 / total
            mixed = jnp.zeros((rows, block), F32)
            for begin in range(0, keys, 256):
                span = slice(begin, begin + 256)
                probs = (scores_ref[span, :] * share).astype(BF16)
                mixed = mixed + tm(probs, v_ref[span, at])
            result = mixed if head == 0 else jnp.where(lanes // size == head, mixed, result)
        att_ref[:, at] = result.astype(BF16)
        return carry

    lax.fori_loop(0, width // block, pair, 0)
    waits[1].wait()
    first = x_ref[0:rows, :].astype(F32) + mm(att_ref[...], out_v[...]) + vec_ref[2:3, :]
    unit, scale = unit_of(first)
    unit1_ref[...] = unit
    scale1_ref[...] = scale
    normed = unit * vec_ref[5:6, :] + vec_ref[9:10, :]
    low_ref[...] = normed.astype(BF16)
    waits[2].wait()
    waits[3].wait()
    second = normed + vec_ref[3:4, :]
    for begin in range(0, active_ref.shape[1], width):
        at = slice(begin, begin + width)
        hidden = mm(low_ref[...], up_v[:, at]) + bias_ref[:, at]
        active, slope = gelu_pair(hidden)
        active_ref[:, at] = active.astype(BF16)
        slope_ref[:, at] = slope.astype(BF16)
        second = second + mm(active_ref[:, at], down_v[at, :])
    unit, scale = unit_of(second)
    unit2_ref[...] = unit
    scale2_ref[...] = scale
    features_ref[...] = unit * vec_ref[6:7, :] + vec_ref[10:11, :]


def tokens_forward(layer, w, x_all, seen, rows):
    keys, width = x_all.shape
    inner = w["up"][0].shape[1]
    size = width // HEADS
    outs = [
        ((rows, width), BF16), ((keys, width), BF16), ((keys, width), BF16), ((width // 128, 8, rows), F32),
        ((rows, width), BF16), ((rows, width), F32), ((rows, 1), F32), ((rows, width), BF16),
        ((rows, inner), BF16), ((rows, inner), BF16), ((rows, width), F32), ((rows, 1), F32),
        ((rows, width), F32),
    ]
    names = ("qkv", "out", "up", "down")
    scratch = [room(w[name][0]) for name in names] + [pltpu.VMEM((keys, rows), F32), DMA((4,))]
    return call(
        functools.partial(tokens_kernel, layer, size), [x_all, seen, w["vec"], w["b_up"]],
        [a for name in names for a in w[name]], outs, scratch,
    )


def edges(values_ref, before_ref, after_ref, sems):
    rows, count = values_ref.shape[0], lax.axis_size(CTX)
    return [
        send(values_ref.at[rows - 16 : rows, :], before_ref, 1, sems[0].at[0], sems[1].at[0]),
        send(values_ref.at[0:16, :], after_ref, count - 1, sems[0].at[1], sems[1].at[1]),
    ]


def moved(values, edge, by):
    rows = values.shape[0]
    at = lax.broadcasted_iota(jnp.int32, values.shape, 0)
    rolled = pltpu.roll(values, by % rows, 0)
    return jnp.where(at == (0 if by > 0 else rows - 1), edge, rolled)


def edge_masks():
    place = lax.axis_index(CTX)
    before = jnp.where(place > 0, 1.0, 0.0)
    after = jnp.where(place < lax.axis_size(CTX) - 1, 1.0, 0.0)
    return before, after


def uniting_kernel(
    layer, features_ref, pooled_ref, chars_ref, state_ref, column_ref, vec_ref, conv_a, conv_b,
    tok_ref, chr_ref, joined_ref, slope_ref, unit3_ref, scale3_ref, unit4_ref, scale4_ref,
    conv_v, before_ref, after_ref, fetch_sem, sems,
):
    rows, width = features_ref.shape
    conv = fetch(layer, conv_a, conv_b, conv_v, fetch_sem.at[0])
    joined_ref[:, 0:width] = features_ref[...].astype(BF16)
    joined_ref[:, width : 2 * width] = pooled_ref[...]
    greet((1, lax.axis_size(CTX) - 1))
    copies = edges(joined_ref, before_ref, after_ref, sems)
    conv.wait()
    deep = 2 * width
    taps = [conv_v.at[tap * deep : (tap + 1) * deep, :] for tap in range(3)]
    joined = joined_ref[...]
    mixed = mm(joined, taps[1][...]) + vec_ref[4:5, :]
    lower = mm(joined, taps[0][...])
    upper = mm(joined, taps[2][...])
    for copy in copies:
        copy.wait()
    has_before, has_after = edge_masks()
    edge = mm(before_ref[...], taps[0][...])[15:16, :] * has_before
    mixed = mixed + moved(lower, edge, 1)
    edge = mm(after_ref[...], taps[2][...])[0:1, :] * has_after
    mixed = mixed + moved(upper, edge, -1)
    lifted, slope = gelu_pair(mixed)
    slope_ref[...] = slope
    unit, scale = unit_of(features_ref[...] + lifted)
    unit3_ref[...] = unit
    scale3_ref[...] = scale
    tok_ref[...] = (unit * vec_ref[7:8, :] + vec_ref[11:12, :]).astype(BF16)
    slots = column_ref.shape[0]
    tokens = lax.broadcasted_iota(jnp.int32, (slots, rows), 1)
    onehot = jnp.where(tokens == column_ref[...], 1.0, 0.0).astype(BF16)
    unit, scale = unit_of(chars_ref[...] + state_ref[...] + mm(onehot, lifted.astype(BF16)))
    unit4_ref[...] = unit
    scale4_ref[...] = scale
    chr_ref[...] = (unit * vec_ref[8:9, :] + vec_ref[12:13, :]).astype(BF16)


def uniting_forward(layer, w, features, pooled, chars, states, column):
    rows, width = features.shape
    slots = chars.shape[0]
    outs = [
        ((rows, width), BF16), ((slots, width), BF16), ((rows, 2 * width), BF16), ((rows, width), F32),
        ((rows, width), F32), ((rows, 1), F32), ((slots, width), F32), ((slots, 1), F32),
    ]
    edge = pltpu.VMEM((16, 2 * width), BF16)
    scratch = [room(w["conv"][0]), edge, edge, DMA((1,)), [DMA((2,))] * 2]
    return call(
        functools.partial(uniting_kernel, layer), [features, pooled, chars, states, column, w["vec"]],
        [*w["conv"]], outs, scratch, 4 + layer,
    )


def uniting_back_kernel(
    layer, gt_ref, gc_ref, unit3_ref, scale3_ref, unit4_ref, scale4_ref, slope_ref, column_ref, group_ref,
    vec_ref, conv_a, conv_b,
    feat_ref, chr_ref, states_ref, around_ref, sums_ref,
    conv_v, mixed_ref, before_ref, after_ref, fetch_sem, sems,
):
    rows, width = gt_ref.shape
    slots = gc_ref.shape[0]
    conv = fetch(layer, conv_a, conv_b, conv_v, fetch_sem.at[0])
    grad = gt_ref[...].astype(F32)
    unit = unit3_ref[...]
    sums_ref[1:2, :] = jnp.sum(grad * unit, axis=0, keepdims=True)
    sums_ref[2:3, :] = jnp.sum(grad, axis=0, keepdims=True)
    d_tok = unit_back(unit, scale3_ref[...], grad * vec_ref[7:8, :])
    grad = gc_ref[...].astype(F32)
    unit = unit4_ref[...]
    sums_ref[3:4, :] = jnp.sum(grad * unit, axis=0, keepdims=True)
    sums_ref[4:5, :] = jnp.sum(grad, axis=0, keepdims=True)
    d_chr = unit_back(unit, scale4_ref[...], grad * vec_ref[8:9, :])
    chr_ref[...] = d_chr
    tokens = lax.broadcasted_iota(jnp.int32, (rows, slots), 0)
    onehot = jnp.where(tokens == group_ref[...], 1.0, 0.0)
    counts = jnp.sum(onehot, axis=1, keepdims=True)
    d_lifted = d_tok + mm(onehot.astype(BF16), d_chr.astype(BF16))
    low = (d_lifted * slope_ref[...]).astype(BF16)
    mixed_ref[...] = low
    greet((1, lax.axis_size(CTX) - 1))
    copies = edges(mixed_ref, before_ref, after_ref, sems)
    d_mixed = low.astype(F32)
    sums_ref[0:1, :] = jnp.sum(d_mixed, axis=0, keepdims=True)
    sums_ref[5:8, :] = jnp.zeros((3, width), F32)
    conv.wait()
    deep = 2 * width
    taps = [conv_v.at[tap * deep : (tap + 1) * deep, :] for tap in range(3)]
    joined = mt(low, taps[1][...])
    earlier = mt(low, taps[0][...])
    later = mt(low, taps[2][...])
    for copy in copies:
        copy.wait()
    has_before, has_after = edge_masks()
    before = before_ref[...].astype(F32)[15:16, :] * has_before
    after = after_ref[...].astype(F32)[0:1, :] * has_after
    around_ref[:, 0:width] = moved(d_mixed, after, -1).astype(BF16)
    around_ref[:, width : 2 * width] = low
    around_ref[:, 2 * width : 3 * width] = moved(d_mixed, before, 1).astype(BF16)
    edge = mt(after_ref[...], taps[0][...])[0:1, :] * has_after
    joined = joined + moved(earlier, edge, -1)
    edge = mt(before_ref[...], taps[2][...])[15:16, :] * has_before
    joined = joined + moved(later, edge, 1)
    feat_ref[...] = d_tok + joined[:, 0:width]
    pool = (joined[:, width : 2 * width] / counts).astype(BF16)
    tokens = lax.broadcasted_iota(jnp.int32, (slots, rows), 1)
    across = jnp.where(tokens == column_ref[...], 1.0, 0.0).astype(BF16)
    states_ref[...] = chr_ref[...] + mm(across, pool)


def uniting_back(layer, w, g_tok, g_chr, saved, column, group):
    rows, width = g_tok.shape
    slots = g_chr.shape[0]
    outs = [
        ((rows, width), F32), ((slots, width), F32), ((slots, width), F32), ((rows, 3 * width), BF16),
        ((8, width), F32),
    ]
    edge = pltpu.VMEM((16, width), BF16)
    scratch = [
        room(w["conv"][0]), pltpu.VMEM((rows, width), BF16), edge, edge, DMA((1,)), [DMA((2,))] * 2,
    ]
    plain = [g_tok, g_chr, *(saved[k] for k in ("unit3", "scale3", "unit4", "scale4", "mixed_slope"))]
    return call(
        functools.partial(uniting_back_kernel, layer), plain + [column, group, w["vec"]],
        [*w["conv"]], outs, scratch, 6 + layer,
    )


def feed_back_kernel(
    layer, feat_ref, unit2_ref, scale2_ref, slope_ref, unit1_ref, scale1_ref, vec_ref,
    out_a, out_b, up_a, up_b, down_a, down_b,
    ffn_ref, hidden_ref, first_ref, branch_ref, att_ref, sums_ref, inner_ref,
    out_v, up_v, down_v, sems,
):
    rows, width = feat_ref.shape
    waits = [
        fetch(layer, a, b, v, sems.at[i])
        for i, (a, b, v) in enumerate([(out_a, out_b, out_v), (up_a, up_b, up_v), (down_a, down_b, down_v)])
    ]
    grad = feat_ref[...]
    unit = unit2_ref[...]
    sums_ref[0:1, :] = jnp.sum(grad * unit, axis=0, keepdims=True)
    sums_ref[1:2, :] = jnp.sum(grad, axis=0, keepdims=True)
    d_second = unit_back(unit, scale2_ref[...], grad * vec_ref[6:7, :])
    low = d_second.astype(BF16)
    ffn_ref[...] = low
    sums_ref[2:3, :] = jnp.sum(low.astype(F32), axis=0, keepdims=True)
    waits[2].wait()
    waits[1].wait()
    d_normed = d_second
    for begin in range(0, hidden_ref.shape[1], width):
        at = slice(begin, begin + width)
        hidden = (mt(low, down_v[at, :]) * slope_ref[:, at].astype(F32)).astype(BF16)
        hidden_ref[:, at] = hidden
        inner_ref[:, at] = jnp.sum(hidden.astype(F32), axis=0, keepdims=True)
        d_normed = d_normed + mt(hidden, up_v[:, at])
    unit = unit1_ref[...]
    sums_ref[3:4, :] = jnp.sum(d_normed * unit, axis=0, keepdims=True)
    sums_ref[4:5, :] = jnp.sum(d_normed, axis=0, keepdims=True)
    d_first = unit_back(unit, scale1_ref[...], d_normed * vec_ref[5:6, :])
    first_ref[...] = d_first
    low = d_first.astype(BF16)
    branch_ref[...] = low
    sums_ref[5:6, :] = jnp.sum(low.astype(F32), axis=0, keepdims=True)
    sums_ref[6:8, :] = jnp.zeros((2, width), F32)
    waits[0].wait()
    att_ref[...] = mt(low, out_v[...]).astype(BF16)


def feed_back(layer, w, d_feat, saved):
    rows, width = d_feat.shape
    inner = w["up"][0].shape[1]
    outs = [
        ((rows, width), BF16), ((rows, inner), BF16), ((rows, width), F32), ((rows, width), BF16),
        ((rows, width), BF16), ((8, width), F32), ((1, inner), F32),
    ]
    names = ("out", "up", "down")
    plain = [d_feat, *(saved[k] for k in ("unit2", "scale2", "slope", "unit1", "scale1"))]
    return call(
        functools.partial(feed_back_kernel, layer), plain + [w["vec"]],
        [a for name in names for a in w[name]], outs, [room(w[name][0]) for name in names] + [DMA((3,))],
    )


def project_back_kernel(
    layer, first_ref, dq_ref, dk_ref, dv_ref, qkv_a, qkv_b, own_ref, parts_ref, sums_ref, qkv_v, sems
):
    rows, width = dq_ref.shape
    qkv = fetch(layer, qkv_a, qkv_b, qkv_v, sems.at[0])
    sums_ref[...] = jnp.zeros_like(sums_ref)
    sums_ref[0:1, :] = jnp.sum(dq_ref[...].astype(F32), axis=0, keepdims=True)
    sums_ref[1:2, :] = jnp.sum(dv_ref[...].astype(F32), axis=0, keepdims=True)
    qkv.wait()
    for begin in range(0, dk_ref.shape[0], rows):
        at = slice(begin, begin + rows)
        value = mt(dk_ref[at, :], qkv_v[:, width : 2 * width]) + mt(dv_ref[at, :], qkv_v[:, 2 * width :])
        if begin == 0:
            own_ref[...] = first_ref[...] + value + mt(dq_ref[...], qkv_v[:, 0:width])
        else:
            parts_ref[begin - rows : begin, :] = value.astype(BF16)


def project_back(layer, w, d_first, dq, dk, dv):
    rows, width = dq.shape
    outs = [((rows, width), F32), ((dk.shape[0] - rows, width), BF16), ((8, width), F32)]
    return call(
        functools.partial(project_back_kernel, layer), [d_first, dq, dk, dv], [*w["qkv"]], outs,
        [room(w["qkv"][0]), DMA((1,))],
    )


def chars_back_kernel(
    layer, grad_ref, chr_ref, proj_ref, live_ref, before_ref, entering_ref, gru_a, gru_b,
    dproj_ref, dc_ref, sums_ref,
    gru_v, state_ref, decay_ref, carry_ref, total_ref, inbox_ref, fetch_sem, total_sems,
):
    count = lax.axis_size(CTX)
    width = proj_ref.shape[1] // 4
    slots = proj_ref.shape[0]
    steps = slots // CHUNKS
    gru = fetch(layer, gru_a, gru_b, gru_v, fetch_sem.at[0])
    greet(range(1, count))
    unroll = 8

    def step(i, carry):
        state_f, decay_f, state_b, decay_b = carry
        for u in range(unroll):
            at = step_rows(steps - 1 - i * unroll - u)
            keep = gates(proj_ref, live_ref, at, 0, width)[0]
            whole = grad_ref[at, 0:width] + state_f
            state_ref[at, 0:width] = whole
            decay_ref[at, 0:width] = decay_f
            state_f = keep * whole
            decay_f = keep * decay_f
            at = step_rows(i * unroll + u)
            keep = gates(proj_ref, live_ref, at, 2 * width, width)[0]
            whole = grad_ref[at, width : 2 * width] + state_b
            state_ref[at, width : 2 * width] = whole
            decay_ref[at, width : 2 * width] = decay_b
            state_b = keep * whole
            decay_b = keep * decay_b
        return state_f, decay_f, state_b, decay_b

    zero = jnp.zeros((CHUNKS, width), F32)
    one = jnp.ones((CHUNKS, width), F32)
    state_f, decay_f, state_b, decay_b = lax.fori_loop(
        0, steps // unroll, step, (zero, one, zero, one)
    )
    join_chunks(carry_ref, total_ref, 0, state_f, decay_f, range(CHUNKS - 1, -1, -1))
    join_chunks(carry_ref, total_ref, 2, state_b, decay_b, range(CHUNKS))
    entering = entering_chunks(carry_ref, total_ref, inbox_ref, total_sems, True)
    live = live_ref[...] > 0.0
    for side, carried in enumerate(entering):
        at = slice(side * width, (side + 1) * width)
        whole = by_step(state_ref[:, at]) + by_step(decay_ref[:, at]) * carried[None]
        whole = whole.reshape(slots, width)
        edge = entering_ref[:, at]
        if side == 0:
            before = jnp.concatenate([edge, before_ref[0 : slots - CHUNKS, at]], axis=0)
        else:
            before = jnp.concatenate([before_ref[CHUNKS:slots, at], edge], axis=0)
        opened = jax.nn.sigmoid(proj_ref[:, 2 * side * width : (2 * side + 1) * width])
        target = proj_ref[:, (2 * side + 1) * width : (2 * side + 2) * width]
        flow = jnp.where(live, whole * opened, 0.0)
        for part, value in enumerate((flow * (1.0 - opened) * (target - before), flow)):
            column = slice((2 * side + part) * width, (2 * side + part + 1) * width)
            low = value.astype(BF16)
            dproj_ref[:, column] = low
            sums_ref[:, column] = jnp.sum(low.astype(F32), axis=0, keepdims=True)
    gru.wait()
    dc_ref[...] = (chr_ref[...] + mt(dproj_ref[...], gru_v[...])).astype(BF16)


def chars_back(layer, w, d_states, d_chr, saved, live):
    slots, width = d_states.shape
    count = lax.axis_size(CTX)
    half = width // 2
    outs = [((slots, 4 * half), BF16), ((slots, width), BF16), ((1, 4 * half), F32)]
    scratch = [
        room(w["gru"][0]), pltpu.VMEM((slots, width), F32), pltpu.VMEM((slots, width), F32),
        pltpu.VMEM((4, CHUNKS, half), F32), pltpu.VMEM((8, half), F32),
        pltpu.VMEM((count - 1, 8, half), F32), DMA((1,)), [DMA((count - 1,))] * 2,
    ]
    plain = [d_states, d_chr, saved["proj"], live, saved["states"], saved["entering"]]
    return call(
        functools.partial(chars_back_kernel, layer), plain, [*w["gru"]], outs, scratch, 8 + layer,
    )


def layer_forward(layer, w, x, c, ids, live, group, column, seen):
    x_all, chars, chars_low, proj, states, entering, pooled = chars_forward(layer, w, x, c, ids, live, group)
    (
        query, keys, values, lse, attended, unit1, scale1, normed_low, active, slope, unit2, scale2, features,
    ) = tokens_forward(layer, w, x_all, seen, x.shape[0])
    tok_out, chr_out, joined, mixed_slope, unit3, scale3, unit4, scale4 = uniting_forward(
        layer, w, features, pooled, chars, states, column
    )
    saved = dict(
        x=x, x_all=x_all, chars_low=chars_low, proj=proj, states=states, entering=entering, query=query,
        keys=keys, values=values, lse=lse, attended=attended, unit1=unit1, scale1=scale1,
        normed_low=normed_low, active=active, slope=slope, unit2=unit2, scale2=scale2, joined=joined,
        mixed_slope=mixed_slope, unit3=unit3, scale3=scale3, unit4=unit4, scale4=scale4,
    )
    return tok_out, chr_out, saved


def bits_of(axis):
    return [(axis, bit) for bit in range(lax.axis_size(axis).bit_length() - 1)]


def exchange_order(x_first):
    dp = bits_of(DP)
    return (dp if x_first else dp[::-1]) + bits_of(CTX)


def shard_at(place, order, n_ctx):
    index = {DP: lax.axis_index(DP), CTX: lax.axis_index(CTX)}
    shard = index[DP] * n_ctx + index[CTX]
    for nth, (axis, bit) in enumerate(order):
        if (place >> (len(order) - 1 - nth)) & 1:
            mine = (index[axis] // (1 << bit)) % 2
            shard = shard + (1 - 2 * mine) * ((1 << bit) * (n_ctx if axis == DP else 1))
    return shard


class Packing:
    def __init__(self, section, unit, groups):
        self.section, self.unit, self.groups = section, unit, groups
        self.arrays, self.moves, self.jobs, self.rows = [], [], [], [0] * len(groups)

    def operand(self, value, pieces=None):
        width = value.shape[1]
        self.arrays.append(value)
        self.moves.append([(0, 0, width)] if pieces is None else [(b, h, h) for b, h in pieces])
        return len(self.arrays) - 1

    def local(self, *values):
        self.arrays.extend(values)
        self.moves.extend([None] * len(values))
        return len(self.arrays) - len(values)

    def product(self, group, left, chunks, size):
        self.jobs.append(dict(group=group, left=left, chunks=chunks, rows=size, row=self.rows[group]))
        self.rows[group] += size * len(chunks)

    def plain(self, group, value, size):
        self.jobs.append(
            dict(group=group, left=None, plain=self.local(value), rows=size, row=self.rows[group])
        )
        self.rows[group] += size

    def run(self, collective_id):
        orders = [exchange_order(x_first) for x_first in self.groups]
        n_ctx = lax.axis_size(CTX)
        count = lax.axis_size(DP) * n_ctx
        unit = self.unit
        if any(job["rows"] % 16 for job in self.jobs):
            return self.run_plainly(orders, n_ctx, count)
        outs = [((count // 2, rows, unit), BF16) for rows in self.rows for _ in (0, 1)]
        most = max(job["rows"] * len(job.get("chunks", (0,))) for job in self.jobs) * count
        coming = [
            pltpu.VMEM((a.shape[0], sum(piece[2] for piece in move)), a.dtype)
            for a, move in zip(self.arrays, self.moves)
            if move
        ]
        copies = sum(len(move) for move in self.moves if move)
        scratch = [pltpu.VMEM((most, unit), BF16), coming, [DMA((copies,))] * 2]
        kernel = functools.partial(pack_kernel, self.jobs, self.moves, count, orders, n_ctx)
        results = call(kernel, self.arrays, [], outs, scratch, collective_id)
        return [(results[2 * i], results[2 * i + 1]) for i in range(len(orders))]

    def run_plainly(self, orders, n_ctx, count):
        blocks = [[] for _ in orders]
        for job in self.jobs:
            if job["left"] is None:
                blocks[job["group"]].append(self.arrays[job["plain"]].reshape(count, job["rows"], self.unit))
                continue
            for right, begin, half, _ in job["chunks"]:
                parts = []
                for core in (0, 1):
                    one = self.arrays[job["left"]]
                    if self.moves[right] is None:
                        two = self.arrays[right + core]
                    else:
                        two = swap(self.arrays[right]) if core else self.arrays[right]
                    two = lax.dynamic_slice_in_dim(two, begin + self.section * half, self.unit, 1)
                    parts.append(tm(swap(one) if core else one, two))
                value = (parts[0] + parts[1]).astype(BF16)
                blocks[job["group"]].append(value.reshape(count, job["rows"], self.unit))
        results = []
        for order, parts in zip(orders, blocks):
            shards = jnp.stack([shard_at(place, order, n_ctx) for place in range(count)])
            whole = jnp.take(jnp.concatenate(parts, axis=1), shards, axis=0)
            results.append((whole[count // 2 :], whole[: count // 2]))
        return results


def pack_kernel(jobs, moves, count, orders, n_ctx, *refs):
    arrays, rest = refs[: len(moves)], refs[len(moves) :]
    outs, (held, coming, semaphores) = rest[: 2 * len(orders)], rest[2 * len(orders) :]
    send_sems, recv_sems = semaphores
    section = lax.axis_index(SEC)
    unit = held.shape[1]
    barrier = pltpu.get_barrier_semaphore()
    pl.semaphore_signal(barrier, inc=1, device_id={SEC: 1 - section}, device_id_type=MESH)
    pl.semaphore_wait(barrier, 1)
    places, copies, pending, nth, slot = {}, [], {}, 0, 0
    for index, move in enumerate(moves):
        if not move:
            continue
        target, at = coming[slot], 0
        places[index] = target
        pending[index] = []
        slot += 1
        for begin, half, width in move:
            source = arrays[index]
            if half:
                source = source.at[:, pl.ds(pl.multiple_of(begin + (1 - section) * half, 128), width)]
            copy = pltpu.make_async_remote_copy(
                src_ref=source,
                dst_ref=target.at[:, at : at + width] if half else target,
                send_sem=send_sems.at[nth],
                recv_sem=recv_sems.at[nth],
                device_id={SEC: 1 - section},
                device_id_type=MESH,
            )
            copy.start()
            copies.append(copy)
            pending[index].append(copy)
            at += width
            nth += 1
    for job in jobs:
        at, size = job["row"], job["rows"]
        total = count * size
        if job["left"] is None:
            held[0:total, :] = arrays[job["plain"]][...]
            chunks = [None]
        else:
            left, chunks = job["left"], job["chunks"]
            mine, theirs = [], []
            for index in [left] + [chunk[0] for chunk in chunks]:
                for copy in pending.pop(index, ()):
                    copy.wait_recv()
            for right, begin, half, there in chunks:
                if moves[right]:
                    column = pl.multiple_of(begin + section * half, 128)
                    mine.append(arrays[right][:, pl.ds(column, unit)])
                    theirs.append(places[right][:, there : there + unit])
                else:
                    mine.append(arrays[right][:, begin : begin + unit])
                    theirs.append(arrays[right + 1][:, begin : begin + unit])
            mine = jnp.concatenate(mine, axis=1)
            theirs = jnp.concatenate(theirs, axis=1)
            for begin in range(0, total, 768):
                span = slice(begin, begin + 768)
                value = tm(arrays[left][:, span], mine) + tm(places[left][:, span], theirs)
                for nth in range(len(chunks)):
                    held[nth * total + begin : nth * total + begin + 768, :] = value[
                        :, nth * unit : (nth + 1) * unit
                    ].astype(BF16)
        sent_ref, kept_ref = outs[2 * job["group"] : 2 * job["group"] + 2]
        for place in range(count):
            shard = shard_at(place, orders[job["group"]], n_ctx) * size
            target = kept_ref if place < count // 2 else sent_ref
            for nth in range(len(chunks)):
                begin = pl.multiple_of(shard + nth * total, 16)
                row = at + nth * size
                target[place % (count // 2), row : row + size, :] = held[pl.ds(begin, size), :]
    for copy in copies:
        copy.wait_send()


class Halving:
    def __init__(self, packed, x_first):
        self.sent, self.kept = packed
        self.order = exchange_order(x_first)
        self.total = None

    def step(self, after):
        key, self.order = self.order[0], self.order[1:]
        got = flip(self.sent, *key)
        got, kept, after = lax.optimization_barrier((got, self.kept, after))
        if not self.order:
            self.total = kept[0].astype(F32) + got[0].astype(F32)
            self.total, after = lax.optimization_barrier((self.total, after))
            return after
        cut = kept.shape[0] // 2
        sent = (kept[cut:].astype(F32) + got[cut:].astype(F32)).astype(BF16)
        kept = (kept[:cut].astype(F32) + got[:cut].astype(F32)).astype(BF16)
        self.sent, self.kept, after = lax.optimization_barrier((sent, kept, after))
        return after


class Queue:
    def __init__(self):
        self.chains = []

    def add(self, chains):
        self.chains.extend(chains)

    def advance(self, value, layer, part):
        for chain in PLAN.get((layer, part), ()):
            if self.chains[chain].order:
                value = self.chains[chain].step(value)
        return value

    def finish(self):
        after = jnp.zeros((), F32)
        while any(chain.order for chain in self.chains):
            for chain in TAIL:
                if self.chains[chain].order:
                    after = self.chains[chain].step(after)


PLAN = {
    (1, 1): (0, 1),
    (0, 3): (0, 1),
    (0, 4): (0, 1),
    (0, 0): (2, 3),
    (0, 1): (0, 1),
}
TAIL = (0, 1, 4, 5, 2, 3, 6, 7)


def returned(d_x, parts):
    rows, n_ctx = d_x.shape[0], lax.axis_size(CTX)
    for j in range(1, n_ctx):
        d_x = d_x + turned(parts[(j - 1) * rows : j * rows], n_ctx - j).astype(F32)
    return d_x


def layer_backward(layer, w, saved, g_tok, g_chr, ids_both, live, group_row, column, seen, section, queue):
    rows, width = g_tok.shape
    count = lax.axis_size(DP) * lax.axis_size(CTX)
    unit = width // 2
    block = width // count
    d_feat, d_chr, d_states, around, sums_a = uniting_back(layer, w, g_tok, g_chr, saved, column, group_row)
    d_feat = queue.advance(d_feat, layer, 3)
    d_ffn, d_hidden, d_first, d_branch, d_attended, sums_b, inner_sums = feed_back(layer, w, d_feat, saved)
    d_attended = queue.advance(d_attended, layer, 4)
    early = Packing(section, unit, (True, False))
    taps = around.shape[1] // width
    right = early.operand(around, [(t * width, unit) for t in range(taps)])
    chunks = [(right, t * width, unit, t * unit) for t in range(taps)]
    early.product(0, early.operand(saved["joined"]), chunks, 2 * block)
    ups = d_hidden.shape[1] // 2
    right = early.operand(d_hidden, [(0, ups)])
    chunks = [(right, begin, ups, begin) for begin in range(0, ups, unit)]
    early.product(1, early.operand(saved["normed_low"]), chunks, block)
    right = early.operand(d_branch, [(0, unit)])
    early.product(1, early.operand(saved["attended"]), [(right, 0, unit, 0)], block)
    packs = early.run(0)
    packs, d_attended = lax.optimization_barrier((packs, d_attended))
    chains = [Halving(pack, x_first) for pack, x_first in zip(packs, early.groups)]
    queue.add(chains)
    dq, dk, dv = attend_back(
        saved["query"], saved["keys"], saved["values"], seen, saved["lse"], d_attended
    )
    dq = queue.advance(dq, layer, 0)
    d_x, parts, sums_c = project_back(layer, w, d_first, dq, dk, dv)
    if layer:
        d_x = returned(d_x, parts)
    d_proj, d_c, proj_sums = chars_back(layer, w, d_states, d_chr, saved, live)
    d_proj = queue.advance(d_proj, layer, 1)
    small = (
        jnp.stack([sums_c[0], sums_c[1], sums_b[5], sums_b[2], sums_a[0]]),
        inner_sums,
        jnp.stack([sums_b[3], sums_b[0], sums_a[1], sums_a[3]]),
        jnp.stack([sums_b[4], sums_b[1], sums_a[2], sums_a[4]]),
        proj_sums,
    )
    packed = jnp.concatenate(
        [jnp.swapaxes(p.reshape(p.shape[0], count, -1), 0, 1).reshape(count, -1) for p in small], axis=1
    )
    packed = jnp.pad(packed, ((0, 0), (0, 16 * unit - packed.shape[1])))
    late = Packing(section, unit, (True, False))
    right = late.operand(d_ffn, [(0, unit)])
    late.product(0, late.operand(saved["active"]), [(right, 0, unit, 0)], 4 * block)
    left = late.operand(d_c)
    split = w["table"][0].shape[0] // 2
    named = []
    for names in ids_both:
        names = names - section * split
        named.append((names == jnp.arange(2 * unit)[None, :]).astype(BF16))
    right = late.local(*named)
    late.product(0, left, [(right, 0, 0, 0), (right, unit, 0, 0)], block)
    right = late.operand(dq, [(0, unit)])
    late.product(1, late.operand(saved["x"]), [(right, 0, unit, 0)], block)
    rights = [late.operand(grad, [(0, unit)]) for grad in (dk, dv)]
    late.product(1, late.operand(saved["x_all"]), [(right, 0, unit, 0) for right in rights], block)
    right = late.operand(d_proj, [(0, width)])
    chunks = [(right, begin, width, begin) for begin in range(0, width, unit)]
    late.product(1, late.operand(saved["chars_low"]), chunks, block)
    late.plain(1, packed.astype(BF16).reshape(-1, unit), 16)
    packs = late.run(1)
    packs, d_c, parts = lax.optimization_barrier((packs, d_c, parts))
    if not layer:
        d_x = returned(d_x, parts)
    more = [Halving(pack, x_first) for pack, x_first in zip(packs, late.groups)]
    queue.add(more)
    d_c = queue.advance(d_c, layer, 2)
    sizes = [(p.shape[0], p.size // count // p.shape[0]) for p in small]
    return d_x.astype(BF16), d_c, chains + more, sizes


def on_device(
    ends, char_ends, char_ids, groups, lengths, w_qkv, biases, w_out, w_up, b_up, w_down,
    ln_gain, ln_shift, char_table, w_gru, b_gru, w_conv,
):
    section = lax.axis_index(SEC)
    n_dp, n_ctx = lax.axis_size(DP), lax.axis_size(CTX)
    is_first = section == 0
    def turned_rows(value):
        shape = value.shape
        return jnp.swapaxes(value.reshape((shape[0], CHUNKS, -1) + shape[2:]), 1, 2).reshape(shape)

    padded = jnp.pad(char_table[0], ((0, -char_table.shape[1] % 256), (0, 0)))
    rows_16 = jnp.concatenate([biases[0], ln_gain[0], ln_shift[0], jnp.zeros_like(biases[0, :3])])
    inner_own = jnp.concatenate([b_up, b_gru], axis=1)
    indices = turned_rows(jnp.concatenate([char_ids, groups]))
    (
        x, cot_tok, c, cot_chr, vec0, vec1, inner0, inner1, ids, ids_other, live, group_row, column, seen,
        gru_other, table_other,
    ) = deal(lengths, ends[0], turned_rows(char_ends[0]), indices, rows_16, inner_own, w_gru[0], padded)
    ids_both = (ids, ids_other)
    weights = {"gru": (w_gru[0], gru_other), "table": (padded, table_other)}
    for name, own in (
        ("qkv", w_qkv[0]), ("out", w_out[0]), ("up", w_up[0]), ("down", w_down[0]),
        ("conv", w_conv[0].reshape(-1, w_conv.shape[3])),
    ):
        tied, x = lax.optimization_barrier((own, x))
        weights[name] = (own, swap(tied))
    layers = [
        dict(weights, vec=vec, b_up=inner[:, : b_up.shape[1]], b_gru=inner[:, b_up.shape[1] :])
        for vec, inner in ((vec0, inner0), (vec1, inner1))
    ]
    rows, width = x.shape

    kept = []
    for layer in (0, 1):
        x, c, saved = layer_forward(
            layer, layers[layer], x, c, ids, live, group_row, column, seen
        )
        kept.append(saved)
    g_x, g_c = cot_tok, cot_chr
    queue = Queue()
    chains = [None, None]
    for layer in (1, 0):
        g_x, g_c, chains[layer], sizes = layer_backward(
            layer, layers[layer], kept[layer], g_x, g_c, ids_both, live, group_row, column, seen, section, queue
        )
    queue.finish()
    packs = [[chain.total for chain in four] for four in chains]

    def gathered(grad, value):
        got = swap(jnp.where(is_first, value, grad))
        return jnp.where(is_first, jnp.stack([grad, got]), jnp.stack([got, value]))[None]

    ends_out = gathered(g_x, x)
    char_ends_out = gathered(restore(g_c), restore(c))

    both = []
    for one, two in zip(*packs):
        mine = jnp.where(is_first, one, two)
        got = swap(jnp.where(is_first, two, one))
        both.append((jnp.where(is_first, mine, got), jnp.where(is_first, got, mine)))
    block = width // (n_dp * n_ctx)

    def columns(which, at, size, parts, crossed=False):
        cut = [[half[at + i * size : at + (i + 1) * size] for i in range(parts)] for half in both[which]]
        if crossed:
            return jnp.concatenate([half[i] for i in range(parts) for half in cut], axis=1)
        return jnp.concatenate(cut[0] + cut[1], axis=1)

    d_conv = jnp.stack([columns(0, tap * 2 * block, 2 * block, 1) for tap in range(w_conv.shape[1])])
    ups = w_up.shape[2] // width
    d_up = columns(1, 0, block, ups)
    d_out = columns(1, ups * block, block, 1)
    d_down = columns(2, 0, ups * block, 1)
    at = ups * block
    split = padded.shape[0] // 2
    d_table = jnp.concatenate(
        [
            jnp.concatenate([half[at : at + block], half[at + block : at + 2 * block]], axis=1)[:, :take]
            for half, take in zip(both[2], (split, char_table.shape[1] - split))
        ],
        axis=1,
    ).T
    d_qkv = columns(3, 0, block, 3, True)
    d_gru = columns(3, 3 * block, block, 2)
    vectors = (both[3][0][5 * block :] + both[3][1][5 * block :]).reshape(-1)
    sums, at = [], 0
    for parts, size in sizes:
        sums.append(vectors[at : at + parts * size].reshape(parts, size))
        at += parts * size
    return (
        ends_out,
        char_ends_out,
        d_qkv[None],
        sums[0][None],
        d_out[None],
        d_up[None],
        sums[1],
        d_down[None],
        sums[2][None],
        sums[3][None],
        d_table[None],
        d_gru[None],
        sums[4],
        d_conv[None],
    )


def solution(mesh):
    both = (DP, CTX)
    held, rows, columns = P(SEC, DP, CTX), P(SEC, both), P(SEC, None, both)
    layer = P(SEC)
    in_specs = (held, held, P(DP, CTX), P(DP, CTX), P(DP)) + (layer,) * 12
    out_specs = (
        held, held, rows, columns, rows, rows, rows, rows, columns, columns, columns, rows, rows, columns,
    )
    return jax.shard_map(
        on_device, mesh=mesh, in_specs=in_specs, out_specs=out_specs, check_vma=False
    )
```

time: 761 us -> 627 us (0.82)
  Pallas kernels: 148 us -> 357 us
  matrix products: 141 us -> 0 us
  waiting for transfers between devices: 236 us -> 142 us
  other arithmetic: 82.7 us -> 40.7 us
  local copies, waits for them, and re-layouts: 60.6 us -> 25.4 us
  starting transfers between devices: 76.7 us -> 50.8 us
    pallas_call x10 -> x19, Pallas kernels: 119 us -> 328 us  [the longest x18 315 us: call(): pl.pallas_call(kernel, in_specs=[VMEM_SPEC] * len(plain) + [ANY_SPEC] * l...]
    dot_general x46 -> x0, matrix products: 141 us -> none  [contract(): lax.dot_general(left, right, (dims, ((), ())), preferred_element_type=F32)]
    ppermute x30 -> x43, waiting for transfers between devices: 154 us -> 86.2 us  [flip(): lax.ppermute(value, axis, [(i, i ^ 1 << bit) for i in range(lax.axis_size...]
    ppermute x24 -> x6, starting transfers between devices: 36.8 us -> 6.69 us  [turned(): lax.ppermute(value, CTX, [(i, (i + by) % count) for i in range(count)])]
    ppermute x24 -> x6, waiting for transfers between devices: 81.3 us -> 56.2 us  [turned(): lax.ppermute(value, CTX, [(i, (i + by) % count) for i in range(count)])]
    reduce_sum x30 -> x0, other arithmetic: 24 us -> none  [the longest x11 11 us: column_sums(): return jnp.sum(values.astype(F32), axis=0)]
    ppermute x30 -> x43, starting transfers between devices: 21.6 us -> 44.1 us  [flip(): lax.ppermute(value, axis, [(i, i ^ 1 << bit) for i in range(lax.axis_size...]
    ppermute x8 -> x0, starting transfers between devices: 18.2 us -> none  [handed(): lax.ppermute(value, CTX, [(i, i + by) for i in range(count) if 0 <= i + b...]
  transfers between devices with their start and end apart: 62 -> 49, of which waited for: 14 -> 18; matrix products, arithmetic and copies ran while one was open for 29% -> 8% of each run, Pallas kernels for 18% -> 36%
where the time goes in v2:
time: 627 us; the launch traced here: 619 us
  Pallas kernels  357 us (57%)
  waiting for transfers between devices  142 us (23%)
  starting transfers between devices  50.8 us (8%)
  other arithmetic  40.7 us (6%)
  local copies, waits for them, and re-layouts  25.4 us (4%)
    pallas_call x18, Pallas kernels, call(): pl.pallas_call(kernel, in_specs=[VMEM_SPEC] * len(plain) + [ANY_SPEC] * l...  315 us
    ppermute x43, waiting for transfers between devices, flip(): lax.ppermute(value, axis, [(i, i ^ 1 << bit) for i in range(lax.axis_size...  86.2 us
    ppermute x6, waiting for transfers between devices, turned(): lax.ppermute(value, CTX, [(i, (i + by) % count) for i in range(count)])  56.2 us
    ppermute x43, starting transfers between devices, flip(): lax.ppermute(value, axis, [(i, i ^ 1 << bit) for i in range(lax.axis_size...  44.1 us
    pallas_call x2, Pallas kernels, attend_back(): pl.pallas_call(functools.partial(attend_back_kernel, size), grid=(steps,)...  29.2 us
    convert_element_type x24, other arithmetic, step(): kept = (kept[:cut].astype(F32) + got[:cut].astype(F32)).astype(BF16)  23.8 us
    pallas_call x1, Pallas kernels, deal(): pl.pallas_call(deal_kernel, in_specs=[pl.BlockSpec(memory_space=pltpu.SME...  12.9 us
  transfers between devices with their start and end apart: 49, of which 18 were waited for; matrix products, arithmetic and copies ran while one was open for 8% of the time, Pallas kernels for 36%

profile of v2, /device:TPU:1, one launch (start us, length us, event | category | flops | bytes accessed | tf_op | source)
XLA Modules:
  0.0 618.9 jit_solution(11972043817192484112)
XLA Ops:
  3.1 3.5 copy.60
  9.3 12.9 %shard_map.272 = (bf16[256,768]{1,0:T(8,128)(2,1)}, bf16[256,768]{1,0:T(8,128)(2,1)}, bf16[512,768]{1,0:T(8,128)(2,1)}, bf16[512,768]{1,0:T(8,128)(2,1)}, f32[16...) custom-call(s32[2]{0:T(128)} %lengths_ref.1, ...), custom_call_target="tpu_custom_call" | custom-call | flops 1 | bytes 1 | tf_op jit(solution)/shard_map/pallas_call | solution.py:425
  23.4 1.3 slice.541.bias_ref
  24.6 38.9 %shard_map.273 = (bf16[1024,768]{1,0:T(8,128)(2,1)}, f32[512,768]{1,0:T(8,128)}, bf16[512,768]{1,0:T(8,128)(2,1)}, f32[512,1536]{1,0:T(8,128)}, f32[512,768]{1,0...) custom-call(bf16[256,768]{1,0:T(8,128)(2,1)} %get-tuple-element.346.x_ref.refs_6_, ...), custom_call_target="tpu_custom_call" | custom-call | flops 1 | bytes 1 | tf_op jit(solution)/shard_map/pallas_call | solution.py:351
  65.4 23.5 %shard_map.274 = (bf16[256,768]{1,0:T(8,128)(2,1)}, bf16[1024,768]{1,0:T(8,128)(2,1)}, bf16[1024,768]{1,0:T(8,128)(2,1)}, f32[6,8,256]{2,1,0:T(8,128)}, bf16[256...) custom-call(bf16[1024,768]{1,0:T(8,128)(2,1)} %get-tuple-element.354, ...), custom_call_target="tpu_custom_call" | custom-call | flops 1 | bytes 1 | tf_op jit(solution)/shard_map/pallas_call | solution.py:351
  88.9 11.6 %shard_map.275 = (bf16[256,768]{1,0:T(8,128)(2,1)}, bf16[512,768]{1,0:T(8,128)(2,1)}, bf16[256,1536]{1,0:T(8,128)(2,1)}, f32[256,768]{1,0:T(8,128)}, f32[256,768...) custom-call(f32[256,768]{1,0:T(8,128)} %get-tuple-element.361.features_ref, ...), custom_call_target="tpu_custom_call" | custom-call | flops 1 | bytes 1 | tf_op jit(solution)/shard_map/pallas_call | solution.py:351
  100.5 30.9 %shard_map.276 = (bf16[1024,768]{1,0:T(8,128)(2,1)}, f32[512,768]{1,0:T(8,128)}, bf16[512,768]{1,0:T(8,128)(2,1)}, f32[512,1536]{1,0:T(8,128)}, f32[512,768]{1,0...) custom-call(bf16[256,768]{1,0:T(8,128)(2,1)} %get-tuple-element.367.x_ref.refs_6_, ...), custom_call_target="tpu_custom_call" | custom-call | flops 1 | bytes 1 | tf_op jit(solution)/shard_map/pallas_call | solution.py:351
  131.4 23.2 %shard_map.277 = (bf16[256,768]{1,0:T(8,128)(2,1)}, bf16[1024,768]{1,0:T(8,128)(2,1)}, bf16[1024,768]{1,0:T(8,128)(2,1)}, f32[6,8,256]{2,1,0:T(8,128)}, bf16[256...) custom-call(bf16[1024,768]{1,0:T(8,128)(2,1)} %get-tuple-element.370, ...), custom_call_target="tpu_custom_call" | custom-call | flops 1 | bytes 1 | tf_op jit(solution)/shard_map/pallas_call | solution.py:351
  154.6 11.6 %shard_map.278 = (bf16[256,768]{1,0:T(8,128)(2,1)}, bf16[512,768]{1,0:T(8,128)(2,1)}, bf16[256,1536]{1,0:T(8,128)(2,1)}, f32[256,768]{1,0:T(8,128)}, f32[256,768...) custom-call(f32[256,768]{1,0:T(8,128)} %get-tuple-element.372.features_ref, ...), custom_call_target="tpu_custom_call" | custom-call | flops 1 | bytes 1 | tf_op jit(solution)/shard_map/pallas_call | solution.py:351
  166.2 12.1 %shard_map.279 = (f32[256,768]{1,0:T(8,128)}, f32[512,768]{1,0:T(8,128)}, f32[512,768]{1,0:T(8,128)}, bf16[256,2304]{1,0:T(8,128)(2,1)}, f32[8,768]{1,0:T(8,128)}) custom-call(bf16[256,768]{1,0:T(8,128)(2,1)} %get-tuple-element.339.gt_ref, bf16[512,768]{1,0:T(8,128)(2,1)} %get-tuple-element.340.gc_ref, f32[256,768]{1,0:T(8,128)} %get-tuple-element.376.unit3_ref, ...), custom_call_target="tpu_custom_call" | custom-call | flops 1 | bytes 1 | tf_op jit(solution)/shard_map/pallas_call | solution.py:351
  178.3 11.1 %shard_map.280 = (bf16[256,768]{1,0:T(8,128)(2,1)}, bf16[256,3072]{1,0:T(8,128)(2,1)}, f32[256,768]{1,0:T(8,128)}, bf16[256,768]{1,0:T(8,128)(2,1)}, bf16[256,76...) custom-call(f32[256,768]{1,0:T(8,128)} %get-tuple-element.383.feat_ref, ...), custom_call_target="tpu_custom_call" | custom-call | flops 1 | bytes 1 | tf_op jit(solution)/shard_map/pallas_call | solution.py:351
  189.5 18.6 %shard_map.281 = (bf16[8,288,384]{2,1,0:T(8,128)(2,1)}, bf16[8,288,384]{2,1,0:T(8,128)(2,1)}, bf16[8,240,384]{2,1,0:T(8,128)(2,1)}, bf16[8,240,384]{2,1,0:T(8,128)(2,1)}) custom-call(bf16[256,2304]{1,0:T(8,128)(2,1)} %get-tuple-element.381.refs_0_, bf16[256,1536]{1,0:T(8,128)(2,1)} %get-tuple-element.382.refs_1_, ...), custom_call_target="tpu_custom_call" | custom-call | flops 1 | bytes 1 | tf_op jit(solution)/shard_map/pallas_call | solution.py:351
  213.1 13.1 %shard_map.282 = (bf16[512,1536]{1,0:T(8,128)(2,1)}, bf16[512,768]{1,0:T(8,128)(2,1)}, f32[1,1536]{1,0:T(1,128)}) custom-call(f32[512,768]{1,0:T(8,128)} %get-tuple-element.402.grad_ref, f32[512,768]{1,0:T(8,128)} %get-tuple-element.403.chr_ref, f32[512,1536]{1,0:T(8,128)} %get-tuple-element.404.proj_ref, f32[512,1]{1,0:T(8,128)} %get-tuple-element.349.live_ref, ...), custom_call_target="tpu_custom_call" | custom-call | flops 1 | bytes 1 | tf_op jit(solution)/shard_map/pallas_call | solution.py:351
  226.3 14.6 %shard_map.283 = (bf16[256,768]{1,0:T(8,128)(2,1)S(1)}, bf16[1024,768]{1,0:T(8,128)(2,1)S(1)}, bf16[1024,768]{1,0:T(8,128)(2,1)S(1)}) custom-call(bf16[256,768]{1,0:T(8,128)(2,1)S(1)} %copy-done.13, bf16[1024,768]{1,0:T(8,128)(2,1)S(1)} %copy-done.9, bf16[1024,768]{1,0:T(8,128)(2,1)S(1)} %copy-done.10, f32[1024,1]{1,0:T(8,128)S(1)} %copy-done, ...), custom_call_target="tpu_custom_call" | custom-call | flops 1 | bytes 1 | tf_op jit(solution)/shard_map/pallas_call | solution.py:96
  243.9 8.3 %shard_map.284 = (f32[256,768]{1,0:T(8,128)}, bf16[768,768]{1,0:T(8,128)(2,1)}, f32[8,768]{1,0:T(8,128)}) custom-call(f32[256,768]{1,0:T(8,128)} %get-tuple-element.418.first_ref, bf16[256,768]{1,0:T(8,128)(2,1)} %copy-done.5, bf16[1024,768]{1,0:T(8,128)(2,1)} %copy-done.1, bf16[1024,768]{1,0:T(8,128)(2,1)} %copy-done.2, bf16[768,2304]{1,0:T(8,128)(2,1)} %bitcast.100, ...), custom_call_target="tpu_custom_call" | custom-call | flops 1 | bytes 1 | tf_op jit(solution)/shard_map/pallas_call | solution.py:351
  254.9 1.3 fusion.5
  256.2 2.7 collective-permute-start.9
  259.5 2.9 add_convert_fusion.6
  262.6 1.7 add_convert_fusion.14
  265.2 9.3 %collective-permute-done.11 = bf16[256,768]{1,0:T(8,128)(2,1)S(1)} collective-permute-done((bf16[256,768]{1,0:T(8,128)(2,1)S(1)}, bf16[256,768]{1,0:T(8,128)(2,1)S(1)}, u32[]{:S(2)}, u32[]{:S(2)}) %collective-permute-start.11) | collective-permute-done | bytes 393248 | tf_op jit(solution)/shard_map/ppermute | solution.py:45
  274.5 16.6 %collective-permute-done.10 = bf16[256,768]{1,0:T(8,128)(2,1)S(1)} collective-permute-done((bf16[256,768]{1,0:T(8,128)(2,1)S(1)}, bf16[256,768]{1,0:T(8,128)(2,1)S(1)}, u32[]{:S(2)}, u32[]{:S(2)}) %collective-permute-start.10) | collective-permute-done | bytes 393248 | tf_op jit(solution)/shard_map/ppermute | solution.py:45
  292.0 26.3 %shard_map.285 = (bf16[8,288,384]{2,1,0:T(8,128)(2,1)}, bf16[8,288,384]{2,1,0:T(8,128)(2,1)}, bf16[8,256,384]{2,1,0:T(8,128)(2,1)}, bf16[8,256,384]{2,1,0:T(8,128)(2,1)}) custom-call(bf16[256,768]{1,0:T(8,128)(2,1)} %get-tuple-element.429.refs_0_, bf16[256,3072]{1,0:T(8,128)(2,1)} %get-tuple-element.430.refs_1_, ...), custom_call_target="tpu_custom_call" | custom-call | flops 1 | bytes 1 | tf_op jit(solution)/shard_map/pallas_call | solution.py:351
  318.3 12.2 %shard_map.286 = (f32[256,768]{1,0:T(8,128)}, f32[512,768]{1,0:T(8,128)}, f32[512,768]{1,0:T(8,128)}, bf16[256,2304]{1,0:T(8,128)(2,1)}, f32[8,768]{1,0:T(8,128)}) custom-call(bf16[256,768]{1,0:T(8,128)(2,1)} %add_convert_fusion.29.gt_ref, bf16[512,768]{1,0:T(8,128)(2,1)} %get-tuple-element.444.refs_2_.gc_ref, f32[256,768]{1,0:T(8,128)} %get-tuple-element.445.unit3_ref, ...), custom_call_target="tpu_custom_call" | custom-call | flops 1 | bytes 1 | tf_op jit(solution)/shard_map/pallas_call | solution.py:351
  330.5 12.6 %shard_map.291 = (bf16[512,1536]{1,0:T(8,128)(2,1)}, bf16[512,768]{1,0:T(8,128)(2,1)}, f32[1,1536]{1,0:T(1,128)}) custom-call(f32[512,768]{1,0:T(8,128)} %get-tuple-element.511.grad_ref, f32[512,768]{1,0:T(8,128)} %get-tuple-element.512.chr_ref, f32[512,1536]{1,0:T(8,128)} %get-tuple-element.513.proj_ref, f32[512,1]{1,0:T(8,128)} %get-tuple-element.349.live_ref, ...), custom_call_target="tpu_custom_call" | custom-call | flops 1 | bytes 1 | tf_op jit(solution)/shard_map/pallas_call | solution.py:351
  344.5 2.1 add_convert_fusion.22
  346.6 2.2 add_convert_fusion.32
  348.8 11.1 %shard_map.287 = (bf16[256,768]{1,0:T(8,128)(2,1)}, bf16[256,3072]{1,0:T(8,128)(2,1)}, f32[256,768]{1,0:T(8,128)}, bf16[256,768]{1,0:T(8,128)(2,1)}, bf16[256,76...) custom-call(f32[256,768]{1,0:T(8,128)} %get-tuple-element.458.feat_ref, ...), custom_call_target="tpu_custom_call" | custom-call | flops 1 | bytes 1 | tf_op jit(solution)/shard_map/pallas_call | solution.py:351
  363.0 16.6 %shard_map.288 = (bf16[8,288,384]{2,1,0:T(8,128)(2,1)}, bf16[8,288,384]{2,1,0:T(8,128)(2,1)}, bf16[8,240,384]{2,1,0:T(8,128)(2,1)}, bf16[8,240,384]{2,1,0:T(8,128)(2,1)}) custom-call(bf16[256,2304]{1,0:T(8,128)(2,1)} %get-tuple-element.473.refs_0_, bf16[256,1536]{1,0:T(8,128)(2,1)} %get-tuple-element.474.refs_1_, ...), custom_call_target="tpu_custom_call" | custom-call | flops 1 | bytes 1 | tf_op jit(solution)/shard_map/pallas_call | solution.py:351
  380.1 1.3 add_convert_fusion.40
  381.5 2.0 collective-permute-start.17
  383.5 1.3 add_convert_fusion.48
  386.5 1.4 copy-done.8
  388.1 14.6 %shard_map.289 = (bf16[256,768]{1,0:T(8,128)(2,1)S(1)}, bf16[1024,768]{1,0:T(8,128)(2,1)S(1)}, bf16[1024,768]{1,0:T(8,128)(2,1)S(1)}) custom-call(bf16[256,768]{1,0:T(8,128)(2,1)S(1)} %copy-done.11, bf16[1024,768]{1,0:T(8,128)(2,1)S(1)} %copy-done.7, bf16[1024,768]{1,0:T(8,128)(2,1)S(1)} %copy-done.8, f32[1024,1]{1,0:T(8,128)S(1)} %copy-done, ...), custom_call_target="tpu_custom_call" | custom-call | flops 1 | bytes 1 | tf_op jit(solution)/shard_map/pallas_call | solution.py:96
  404.1 2.9 add_convert_fusion.4
  407.1 2.9 add_convert_fusion.10
  410.0 8.2 %shard_map.290 = (f32[256,768]{1,0:T(8,128)}, bf16[768,768]{1,0:T(8,128)(2,1)}, f32[8,768]{1,0:T(8,128)}) custom-call(f32[256,768]{1,0:T(8,128)} %get-tuple-element.464.first_ref, bf16[256,768]{1,0:T(8,128)(2,1)} %copy-done.6, bf16[1024,768]{1,0:T(8,128)(2,1)} %copy-done.3, bf16[1024,768]{1,0:T(8,128)(2,1)} %copy-done.4, bf16[768,2304]{1,0:T(8,128)(2,1)} %bitcast.101, ...), custom_call_target="tpu_custom_call" | custom-call | flops 1 | bytes 1 | tf_op jit(solution)/shard_map/pallas_call | solution.py:351
  420.1 25.4 %shard_map.292 = (bf16[8,288,384]{2,1,0:T(8,128)(2,1)}, bf16[8,288,384]{2,1,0:T(8,128)(2,1)}, bf16[8,256,384]{2,1,0:T(8,128)(2,1)}, bf16[8,256,384]{2,1,0:T(8,128)(2,1)}) custom-call(bf16[256,768]{1,0:T(8,128)(2,1)} %get-tuple-element.509.refs_0_, bf16[256,3072]{1,0:T(8,128)(2,1)} %get-tuple-element.510.refs_1_, ...), custom_call_target="tpu_custom_call" | custom-call | flops 1 | bytes 1 | tf_op jit(solution)/shard_map/pallas_call | solution.py:351
  446.6 3.0 collective-permute-start.18
  450.3 7.6 %collective-permute-done.18 = bf16[256,768]{1,0:T(8,128)(2,1)} collective-permute-done((bf16[256,768]{1,0:T(8,128)(2,1)}, bf16[256,768]{1,0:T(8,128)(2,1)}, u32[]{:S(2)}, u32[]{:S(2)}) %collective-permute-start.18) | collective-permute-done | bytes 393248 | tf_op jit(solution)/shard_map/ppermute | solution.py:45
  457.9 2.3 collective-permute-start.22
  460.2 7.0 %collective-permute-done.20 = bf16[256,768]{1,0:T(8,128)(2,1)} collective-permute-done((bf16[256,768]{1,0:T(8,128)(2,1)}, bf16[256,768]{1,0:T(8,128)(2,1)}, u32[]{:S(2)}, u32[]{:S(2)}) %collective-permute-start.20) | collective-permute-done | bytes 393248 | tf_op jit(solution)/shard_map/ppermute | solution.py:45
  467.8 15.2 %collective-permute-done.19 = bf16[256,768]{1,0:T(8,128)(2,1)} collective-permute-done((bf16[256,768]{1,0:T(8,128)(2,1)}, bf16[256,768]{1,0:T(8,128)(2,1)}, u32[]{:S(2)}, u32[]{:S(2)}) %collective-permute-start.19) | collective-permute-done | bytes 393248 | tf_op jit(solution)/shard_map/ppermute | solution.py:45
  483.2 1.7 broadcast_select_fusion.1
  485.6 2.1 add_convert_fusion.2
  487.7 1.3 collective-permute-start.23
  489.0 1.7 add_convert_fusion.12
  490.7 12.1 %collective-permute-done.26 = bf16[4,288,384]{2,1,0:T(8,128)(2,1)S(1)} collective-permute-done((bf16[4,288,384]{2,1,0:T(8,128)(2,1)S(1)}, bf16[4,288,384]{2,1,0:T(8,128)(2,1)S(1)}, u32[]{:S(2)}, u32[]{:S(2)}) %collective-permute-start.26) | collective-permute-done | bytes 884768 | tf_op jit(solution)/shard_map/ppermute | solution.py:36
  502.8 4.1 collective-permute-start.21
  509.3 1.4 maximum_select_fusion
  512.2 6.0 collective-permute-done.31
  518.5 5.0 collective-permute-done.24
  523.9 12.6 %collective-permute-done.23 = bf16[8,256,384]{2,1,0:T(8,128)(2,1)S(1)} collective-permute-done((bf16[8,256,384]{2,1,0:T(8,128)(2,1)S(1)}, bf16[8,256,384]{2,1,0:T(8,128)(2,1)S(1)}, u32[]{:S(2)}, u32[]{:S(2)}) %collective-permute-start.23) | collective-permute-done | bytes 1572896 | tf_op jit(solution)/shard_map/ppermute | solution.py:36
  538.0 6.5 %collective-permute-done.45 = bf16[1,288,384]{2,1,0:T(8,128)(2,1)S(1)} collective-permute-done((bf16[1,288,384]{2,1,0:T(8,128)(2,1)S(1)}, bf16[1,288,384]{2,1,0:T(8,128)(2,1)S(1)}, u32[]{:S(2)}, u32[]{:S(2)}) %collective-permute-start.45) | collective-permute-done | bytes 221216 | tf_op jit(solution)/shard_map/ppermute | solution.py:36
  544.7 1.6 collective-permute-start.39
  546.3 9.1 %collective-permute-done.34 = bf16[4,288,384]{2,1,0:T(8,128)(2,1)S(1)} collective-permute-done((bf16[4,288,384]{2,1,0:T(8,128)(2,1)S(1)}, bf16[4,288,384]{2,1,0:T(8,128)(2,1)S(1)}, u32[]{:S(2)}, u32[]{:S(2)}) %collective-permute-start.34) | collective-permute-done | bytes 884768 | tf_op jit(solution)/shard_map/ppermute | solution.py:36
  555.9 2.0 collective-permute-start.41
  558.2 7.1 %collective-permute-done.41 = bf16[1,240,384]{2,1,0:T(8,128)(2,1)S(1)} collective-permute-done((bf16[1,240,384]{2,1,0:T(8,128)(2,1)S(1)}, bf16[1,240,384]{2,1,0:T(8,128)(2,1)S(1)}, u32[]{:S(2)}, u32[]{:S(2)}) %collective-permute-start.41) | collective-permute-done | bytes 184352 | tf_op jit(solution)/shard_map/ppermute | solution.py:36
  565.4 9.1 %collective-permute-start.42 = (f32[240,384]{1,0:T(8,128)S(1)}, f32[240,384]{1,0:T(8,128)S(1)}, u32[]{:S(2)}, u32[]{:S(2)}) collective-permute-start(f32[240,384]{1,0:T(8,128)S(1)} %broadcast_select_fusion.16), channel_id=1, source_target_pairs={{0,16},{16,0},{1,17},{17,1},{2,18},{18,2},{3,19},{19,3},{4,20},{20... | collective-permute-start | bytes 1105928 | tf_op jit(solution)/shard_map/ppermute | solution.py:36
  574.6 3.2 collective-permute-start.47
  578.0 8.6 %collective-permute-done.47 = bf16[1,288,384]{2,1,0:T(8,128)(2,1)S(1)} collective-permute-done((bf16[1,288,384]{2,1,0:T(8,128)(2,1)S(1)}, bf16[1,288,384]{2,1,0:T(8,128)(2,1)S(1)}, u32[]{:S(2)}, u32[]{:S(2)}) %collective-permute-start.47) | collective-permute-done | bytes 221216 | tf_op jit(solution)/shard_map/ppermute | solution.py:36
  586.8 2.4 collective-permute-start.48
  590.3 4.9 collective-permute-done.43
  595.4 10.3 %collective-permute-done.36 = bf16[1,256,384]{2,1,0:T(8,128)(2,1)S(1)} collective-permute-done((bf16[1,256,384]{2,1,0:T(8,128)(2,1)S(1)}, bf16[1,256,384]{2,1,0:T(8,128)(2,1)S(1)}, u32[]{:S(2)}, u32[]{:S(2)}) %collective-permute-start.36) | collective-permute-done | bytes 196640 | tf_op jit(solution)/shard_map/ppermute | solution.py:36
  607.1 3.4 collective-permute-done.44
  (314 shorter events, 52.5 us)
Async XLA Ops:
  22.1 66.8 %collective-permute-start.4 = (bf16[4608,768]{1,0:T(8,128)(2,1)}, bf16[4608,768]{1,0:T(8,128)(2,1)}, u32[]{:S(2)}, u32[]{:S(2)}) collective-permute-start(bf16[4608,768]{1,0:T(8,128)(2,1)} %bitcast.88), channel_id=1, source_target_pairs={{0,16},{16,0},{1,17},{17,1},{2,18},{18,2},{3,19},{19,3},{4,20},{20... | collective-permute-start | bytes 21233672 | tf_op jit(solution)/shard_map/ppermute | solution.py:36
  22.3 43.0 %collective-permute-start.3 = (bf16[3072,768]{1,0:T(8,128)(2,1)}, bf16[3072,768]{1,0:T(8,128)(2,1)}, u32[]{:S(2)}, u32[]{:S(2)}) collective-permute-start(bf16[3072,768]{1,0:T(8,128)(2,1)} %bitcast.13.down_a), channel_id=1, source_target_pairs={{0,16},{16,0},{1,17},{17,1},{2,18},{18,2},{3,19},{19,3},{4,20},{20... | collective-permute-start | bytes 14155784 | tf_op jit(solution)/shard_map/ppermute | solution.py:36
  22.7 42.7 %collective-permute-start.2 = (bf16[768,3072]{1,0:T(8,128)(2,1)}, bf16[768,3072]{1,0:T(8,128)(2,1)}, u32[]{:S(2)}, u32[]{:S(2)}) collective-permute-start(bf16[768,3072]{1,0:T(8,128)(2,1)} %bitcast.14.up_a), channel_id=1, source_target_pairs={{0,16},{16,0},{1,17},{17,1},{2,18},{18,2},{3,19},{19,3},{4,20},{20... | collective-permute-start | bytes 14155784 | tf_op jit(solution)/shard_map/ppermute | solution.py:36
  22.8 42.5 %collective-permute-start = (bf16[768,2304]{1,0:T(8,128)(2,1)S(1)}, bf16[768,2304]{1,0:T(8,128)(2,1)}, u32[]{:S(2)}, u32[]{:S(2)}) collective-permute-start(bf16[768,2304]{1,0:T(8,128)(2,1)S(1)} %bitcast.102), channel_id=1, source_target_pairs={{0,16},{16,0},{1,17},{17,1},{2,18},{18,2},{3,19},{19,3},{4,20},{20... | collective-permute-start | bytes 10616840 | tf_op jit(solution)/shard_map/ppermute | solution.py:36
  23.2 42.1 %collective-permute-start.1 = (bf16[768,768]{1,0:T(8,128)(2,1)}, bf16[768,768]{1,0:T(8,128)(2,1)}, u32[]{:S(2)}, u32[]{:S(2)}) collective-permute-start(bf16[768,768]{1,0:T(8,128)(2,1)} %bitcast.15.out_a), channel_id=1, source_target_pairs={{0,16},{16,0},{1,17},{17,1},{2,18},{18,2},{3,19},{19,3},{4,20},{20... | collective-permute-start | bytes 3538952 | tf_op jit(solution)/shard_map/ppermute | solution.py:36
  24.6 38.9 %copy-start.43 = (f32[1,4608]{1,0:T(1,128)S(1)}, f32[1,4608]{1,0:T(1,128)}, u32[]{:S(2)}) copy-start(f32[1,4608]{1,0:T(1,128)} %get-tuple-element.351) | copy-start | bytes 55300
  24.6 39.5 %copy-start.42 = (f32[1,4608]{1,0:T(1,128)S(1)}, f32[1,4608]{1,0:T(1,128)}, u32[]{:S(2)}) copy-start(f32[1,4608]{1,0:T(1,128)} %get-tuple-element.369) | copy-start | bytes 55300
  189.4 20.0 %copy-start.21 = (s32[512,1]{1,0:T(8,128)S(1)}, s32[512,1]{1,0:T(8,128)}, u32[]{:S(2)}) copy-start(s32[512,1]{1,0:T(8,128)} %get-tuple-element.348.ids_ref) | copy-start | bytes 6148
  189.5 19.9 %copy-start.38 = (s32[512,1]{1,0:T(8,128)S(1)}, s32[512,1]{1,0:T(8,128)}, u32[]{:S(2)}) copy-start(s32[512,1]{1,0:T(8,128)} %get-tuple-element.432) | copy-start | bytes 6148
  208.1 51.4 %collective-permute-start.6 = (bf16[8,288,384]{2,1,0:T(8,128)(2,1)}, bf16[8,288,384]{2,1,0:T(8,128)(2,1)}, u32[]{:S(2)}, u32[]{:S(2)}) collective-permute-start(bf16[8,288,384]{2,1,0:T(8,128)(2,1)} %get-tuple-element.400), channel_id=1, source_target_pairs={{0,4},{4,0},{8,12},{12,8},{1,5},{5,1},{9,13},{13,9},{2,6},{6,2},{1... | collective-permute-start | bytes 5308424 | tf_op jit(solution)/shard_map/ppermute | solution.py:36
  211.8 50.6 %collective-permute-start.5 = (bf16[8,240,384]{2,1,0:T(8,128)(2,1)}, bf16[8,240,384]{2,1,0:T(8,128)(2,1)}, u32[]{:S(2)}, u32[]{:S(2)}) collective-permute-start(bf16[8,240,384]{2,1,0:T(8,128)(2,1)} %get-tuple-element.398), channel_id=1, source_target_pairs={{0,8},{4,12},{8,0},{12,4},{1,9},{5,13},{9,1},{13,5},{2,10},{6,14},... | collective-permute-start | bytes 4423688 | tf_op jit(solution)/shard_map/ppermute | solution.py:36
  256.2 9.0 %collective-permute-start.9 = (bf16[256,768]{1,0:T(8,128)(2,1)S(1)}, bf16[256,768]{1,0:T(8,128)(2,1)S(1)}, u32[]{:S(2)}, u32[]{:S(2)}) collective-permute-start(bf16[256,768]{1,0:T(8,128)(2,1)S(1)} %get-tuple-element.707), channel_id=1, source_target_pairs={{0,3},{1,0},{2,1},{3,2},{4,7},{5,4},{6,5},{7,6},{8,11},{9,8},{10,9... | collective-permute-start | bytes 1179656 | tf_op jit(solution)/shard_map/ppermute | solution.py:45
  258.9 15.6 %collective-permute-start.11 = (bf16[256,768]{1,0:T(8,128)(2,1)S(1)}, bf16[256,768]{1,0:T(8,128)(2,1)S(1)}, u32[]{:S(2)}, u32[]{:S(2)}) collective-permute-start(bf16[256,768]{1,0:T(8,128)(2,1)S(1)} %get-tuple-element.708), channel_id=1, source_target_pairs={{0,1},{1,2},{2,3},{3,0},{4,5},{5,6},{6,7},{7,4},{8,9},{9,10},{10,1... | collective-permute-start | bytes 1179656 | tf_op jit(solution)/shard_map/ppermute | solution.py:45
  259.1 32.0 %collective-permute-start.10 = (bf16[256,768]{1,0:T(8,128)(2,1)S(1)}, bf16[256,768]{1,0:T(8,128)(2,1)S(1)}, u32[]{:S(2)}, u32[]{:S(2)}) collective-permute-start(bf16[256,768]{1,0:T(8,128)(2,1)S(1)} %get-tuple-element.709), channel_id=1, source_target_pairs={{0,2},{1,3},{2,0},{3,1},{4,6},{5,7},{6,4},{7,5},{8,10},{9,11},{10,... | collective-permute-start | bytes 1179656 | tf_op jit(solution)/shard_map/ppermute | solution.py:45
  262.4 28.6 %copy-start.36 = (f32[256,768]{1,0:T(8,128)S(1)}, f32[256,768]{1,0:T(8,128)}, u32[]{:S(2)}) copy-start(f32[256,768]{1,0:T(8,128)} %get-tuple-element.427) | copy-start | bytes 2359300
  262.4 82.1 %collective-permute-start.8 = (bf16[4,288,384]{2,1,0:T(8,128)(2,1)}, bf16[4,288,384]{2,1,0:T(8,128)(2,1)}, u32[]{:S(2)}, u32[]{:S(2)}) collective-permute-start(bf16[4,288,384]{2,1,0:T(8,128)(2,1)} %get-tuple-element.416), channel_id=1, source_target_pairs={{0,8},{4,12},{8,0},{12,4},{1,9},{5,13},{9,1},{13,5},{2,10},{6,14},... | collective-permute-start | bytes 2654216 | tf_op jit(solution)/shard_map/ppermute | solution.py:36
  264.4 82.2 %collective-permute-start.7 = (bf16[4,240,384]{2,1,0:T(8,128)(2,1)S(1)}, bf16[4,240,384]{2,1,0:T(8,128)(2,1)}, u32[]{:S(2)}, u32[]{:S(2)}) collective-permute-start(bf16[4,240,384]{2,1,0:T(8,128)(2,1)S(1)} %get-tuple-element.414), channel_id=1, source_target_pairs={{0,4},{4,0},{8,12},{12,8},{1,5},{5,1},{9,13},{13,9},{2,6},{6,2},{1... | collective-permute-start | bytes 2211848 | tf_op jit(solution)/shard_map/ppermute | solution.py:36
  343.9 63.2 %collective-permute-start.12 = (bf16[8,256,384]{2,1,0:T(8,128)(2,1)}, bf16[8,256,384]{2,1,0:T(8,128)(2,1)}, u32[]{:S(2)}, u32[]{:S(2)}) collective-permute-start(bf16[8,256,384]{2,1,0:T(8,128)(2,1)} %get-tuple-element.465), channel_id=1, source_target_pairs={{0,8},{4,12},{8,0},{12,4},{1,9},{5,13},{9,1},{13,5},{2,10},{6,14},... | collective-permute-start | bytes 4718600 | tf_op jit(solution)/shard_map/ppermute | solution.py:36
  344.2 59.9 %collective-permute-start.13 = (bf16[8,288,384]{2,1,0:T(8,128)(2,1)}, bf16[8,288,384]{2,1,0:T(8,128)(2,1)}, u32[]{:S(2)}, u32[]{:S(2)}) collective-permute-start(bf16[8,288,384]{2,1,0:T(8,128)(2,1)} %get-tuple-element.467), channel_id=1, source_target_pairs={{0,4},{4,0},{8,12},{12,8},{1,5},{5,1},{9,13},{13,9},{2,6},{6,2},{1... | collective-permute-start | bytes 5308424 | tf_op jit(solution)/shard_map/ppermute | solution.py:36
  360.7 19.5 %collective-permute-start.15 = (bf16[2,288,384]{2,1,0:T(8,128)(2,1)}, bf16[2,288,384]{2,1,0:T(8,128)(2,1)}, u32[]{:S(2)}, u32[]{:S(2)}) collective-permute-start(bf16[2,288,384]{2,1,0:T(8,128)(2,1)} %get-tuple-element.485), channel_id=1, source_target_pairs={{0,1},{1,0},{2,3},{3,2},{4,5},{5,4},{6,7},{7,6},{8,9},{9,8},{10,11... | collective-permute-start | bytes 1327112 | tf_op jit(solution)/shard_map/ppermute | solution.py:36
  362.3 19.2 %collective-permute-start.14 = (bf16[2,240,384]{2,1,0:T(8,128)(2,1)}, bf16[2,240,384]{2,1,0:T(8,128)(2,1)}, u32[]{:S(2)}, u32[]{:S(2)}) collective-permute-start(bf16[2,240,384]{2,1,0:T(8,128)(2,1)} %get-tuple-element.483), channel_id=1, source_target_pairs={{0,1},{1,0},{2,3},{3,2},{4,5},{5,4},{6,7},{7,6},{8,9},{9,8},{10,11... | collective-permute-start | bytes 1105928 | tf_op jit(solution)/shard_map/ppermute | solution.py:36
  381.5 21.3 %collective-permute-start.17 = (bf16[1,288,384]{2,1,0:T(8,128)(2,1)S(1)}, bf16[1,288,384]{2,1,0:T(8,128)(2,1)S(1)}, u32[]{:S(2)}, u32[]{:S(2)}) collective-permute-start(bf16[1,288,384]{2,1,0:T(8,128)(2,1)S(1)} %get-tuple-element.518), channel_id=1, source_target_pairs={{0,2},{1,3},{2,0},{3,1},{4,6},{5,7},{6,4},{7,5},{8,10},{9,11},{10,... | collective-permute-start | bytes 663560 | tf_op jit(solution)/shard_map/ppermute | solution.py:36
  384.8 19.3 %collective-permute-start.16 = (bf16[1,240,384]{2,1,0:T(8,128)(2,1)S(1)}, bf16[1,240,384]{2,1,0:T(8,128)(2,1)S(1)}, u32[]{:S(2)}, u32[]{:S(2)}) collective-permute-start(bf16[1,240,384]{2,1,0:T(8,128)(2,1)S(1)} %get-tuple-element.516), channel_id=1, source_target_pairs={{0,2},{1,3},{2,0},{3,1},{4,6},{5,7},{6,4},{7,5},{8,10},{9,11},{10,... | collective-permute-start | bytes 552968 | tf_op jit(solution)/shard_map/ppermute | solution.py:36
  385.3 102.4 %collective-permute-start.27 = (bf16[8,240,384]{2,1,0:T(8,128)(2,1)}, bf16[8,240,384]{2,1,0:T(8,128)(2,1)}, u32[]{:S(2)}, u32[]{:S(2)}) collective-permute-start(bf16[8,240,384]{2,1,0:T(8,128)(2,1)} %get-tuple-element.552), channel_id=1, source_target_pairs={{0,8},{4,12},{8,0},{12,4},{1,9},{5,13},{9,1},{13,5},{2,10},{6,14},... | collective-permute-start | bytes 4423688 | tf_op jit(solution)/shard_map/ppermute | solution.py:36
  388.1 16.1 %copy-start.24 = (bf16[8,288,384]{2,1,0:T(8,128)(2,1)S(1)}, bf16[8,288,384]{2,1,0:T(8,128)(2,1)}, u32[]{:S(2)}) copy-start(bf16[8,288,384]{2,1,0:T(8,128)(2,1)} %get-tuple-element.498) | copy-start | bytes 5308420
  402.7 82.2 %collective-permute-start.28 = (bf16[8,288,384]{2,1,0:T(8,128)(2,1)}, bf16[8,288,384]{2,1,0:T(8,128)(2,1)}, u32[]{:S(2)}, u32[]{:S(2)}) collective-permute-start(bf16[8,288,384]{2,1,0:T(8,128)(2,1)} %get-tuple-element.554), channel_id=1, source_target_pairs={{0,4},{4,0},{8,12},{12,8},{1,5},{5,1},{9,13},{13,9},{2,6},{6,2},{1... | collective-permute-start | bytes 5308424 | tf_op jit(solution)/shard_map/ppermute | solution.py:36
  420.1 25.4 %copy-start.33 = (bf16[768,768]{1,0:T(8,128)(2,1)S(1)}, bf16[768,768]{1,0:T(8,128)(2,1)}, u32[]{:S(2)}) copy-start(bf16[768,768]{1,0:T(8,128)(2,1)} %get-tuple-element.540) | copy-start | bytes 3538948
  446.6 11.3 %collective-permute-start.18 = (bf16[256,768]{1,0:T(8,128)(2,1)}, bf16[256,768]{1,0:T(8,128)(2,1)}, u32[]{:S(2)}, u32[]{:S(2)}) collective-permute-start(bf16[256,768]{1,0:T(8,128)(2,1)} %get-tuple-element.704), channel_id=1, source_target_pairs={{0,3},{1,0},{2,1},{3,2},{4,7},{5,4},{6,5},{7,6},{8,11},{9,8},{10,9... | collective-permute-start | bytes 1179656 | tf_op jit(solution)/shard_map/ppermute | solution.py:45
  449.5 17.6 %collective-permute-start.20 = (bf16[256,768]{1,0:T(8,128)(2,1)}, bf16[256,768]{1,0:T(8,128)(2,1)}, u32[]{:S(2)}, u32[]{:S(2)}) collective-permute-start(bf16[256,768]{1,0:T(8,128)(2,1)} %get-tuple-element.705), channel_id=1, source_target_pairs={{0,1},{1,2},{2,3},{3,0},{4,5},{5,6},{6,7},{7,4},{8,9},{9,10},{10,1... | collective-permute-start | bytes 1179656 | tf_op jit(solution)/shard_map/ppermute | solution.py:45
  449.5 33.4 %collective-permute-start.19 = (bf16[256,768]{1,0:T(8,128)(2,1)}, bf16[256,768]{1,0:T(8,128)(2,1)}, u32[]{:S(2)}, u32[]{:S(2)}) collective-permute-start(bf16[256,768]{1,0:T(8,128)(2,1)} %get-tuple-element.706), channel_id=1, source_target_pairs={{0,2},{1,3},{2,0},{3,1},{4,6},{5,7},{6,4},{7,5},{8,10},{9,11},{10,... | collective-permute-start | bytes 1179656 | tf_op jit(solution)/shard_map/ppermute | solution.py:45
  450.0 17.2 %copy-start.35 = (bf16[4,256,384]{2,1,0:T(8,128)(2,1)S(1)}, bf16[4,256,384]{2,1,0:T(8,128)(2,1)}, u32[]{:S(2)}) copy-start(bf16[4,256,384]{2,1,0:T(8,128)(2,1)} %get-tuple-element.548) | copy-start | bytes 2359300
  450.0 33.0 %copy-start.34 = (bf16[4,288,384]{2,1,0:T(8,128)(2,1)S(1)}, bf16[4,288,384]{2,1,0:T(8,128)(2,1)}, u32[]{:S(2)}) copy-start(bf16[4,288,384]{2,1,0:T(8,128)(2,1)} %get-tuple-element.550) | copy-start | bytes 2654212
  450.0 33.2 %copy-start.29 = (bf16[256,768]{1,0:T(8,128)(2,1)S(1)}, bf16[256,768]{1,0:T(8,128)(2,1)}, u32[]{:S(2)}) copy-start(bf16[256,768]{1,0:T(8,128)(2,1)} %get-tuple-element.541) | copy-start | bytes 1179652
  450.0 33.2 %copy-start.37 = (f32[256,768]{1,0:T(8,128)S(1)}, f32[256,768]{1,0:T(8,128)}, u32[]{:S(2)}) copy-start(f32[256,768]{1,0:T(8,128)} %get-tuple-element.508) | copy-start | bytes 2359300
  450.1 34.8 %copy-start.52 = (bf16[8,288,384]{2,1,0:T(8,128)(2,1)S(1)}, bf16[8,288,384]{2,1,0:T(8,128)(2,1)}, u32[]{:S(2)}) copy-start(bf16[8,288,384]{2,1,0:T(8,128)(2,1)} %get-tuple-element.546) | copy-start | bytes 5308420
  457.9 51.4 %collective-permute-start.22 = (bf16[512,768]{1,0:T(8,128)(2,1)S(1)}, bf16[512,768]{1,0:T(8,128)(2,1)S(1)}, u32[]{:S(2)}, u32[]{:S(2)}) collective-permute-start(bf16[512,768]{1,0:T(8,128)(2,1)S(1)} %bitcast.115), channel_id=1, source_target_pairs={{0,16},{16,0},{1,17},{17,1},{2,18},{18,2},{3,19},{19,3},{4,20},{20... | collective-permute-start | bytes 2359304 | tf_op jit(solution)/shard_map/ppermute | solution.py:36
  467.2 39.9 %collective-permute-start.25 = (bf16[4,256,384]{2,1,0:T(8,128)(2,1)S(1)}, bf16[4,256,384]{2,1,0:T(8,128)(2,1)S(1)}, u32[]{:S(2)}, u32[]{:S(2)}) collective-permute-start(bf16[4,256,384]{2,1,0:T(8,128)(2,1)S(1)} %copy-done.35), channel_id=1, source_target_pairs={{0,4},{4,0},{8,12},{12,8},{1,5},{5,1},{9,13},{13,9},{2,6},{6,2},{1... | collective-permute-start | bytes 2359304 | tf_op jit(solution)/shard_map/ppermute | solution.py:36
  483.0 19.8 %collective-permute-start.26 = (bf16[4,288,384]{2,1,0:T(8,128)(2,1)S(1)}, bf16[4,288,384]{2,1,0:T(8,128)(2,1)S(1)}, u32[]{:S(2)}, u32[]{:S(2)}) collective-permute-start(bf16[4,288,384]{2,1,0:T(8,128)(2,1)S(1)} %copy-done.34), channel_id=1, source_target_pairs={{0,8},{4,12},{8,0},{12,4},{1,9},{5,13},{9,1},{13,5},{2,10},{6,14},... | collective-permute-start | bytes 2654216 | tf_op jit(solution)/shard_map/ppermute | solution.py:36
  484.9 38.5 %collective-permute-start.24 = (bf16[8,288,384]{2,1,0:T(8,128)(2,1)S(1)}, bf16[8,288,384]{2,1,0:T(8,128)(2,1)S(1)}, u32[]{:S(2)}, u32[]{:S(2)}) collective-permute-start(bf16[8,288,384]{2,1,0:T(8,128)(2,1)S(1)} %copy-done.52), channel_id=1, source_target_pairs={{0,4},{4,0},{8,12},{12,8},{1,5},{5,1},{9,13},{13,9},{2,6},{6,2},{1... | collective-permute-start | bytes 5308424 | tf_op jit(solution)/shard_map/ppermute | solution.py:36
  487.7 48.8 %collective-permute-start.23 = (bf16[8,256,384]{2,1,0:T(8,128)(2,1)S(1)}, bf16[8,256,384]{2,1,0:T(8,128)(2,1)S(1)}, u32[]{:S(2)}, u32[]{:S(2)}) collective-permute-start(bf16[8,256,384]{2,1,0:T(8,128)(2,1)S(1)} %copy-done.53), channel_id=1, source_target_pairs={{0,8},{4,12},{8,0},{12,4},{1,9},{5,13},{9,1},{13,5},{2,10},{6,14},... | collective-permute-start | bytes 4718600 | tf_op jit(solution)/shard_map/ppermute | solution.py:36
  490.7 16.4 %copy-start.20 = (bf16[4,256,384]{2,1,0:T(8,128)(2,1)S(1)}, bf16[4,256,384]{2,1,0:T(8,128)(2,1)}, u32[]{:S(2)}) copy-start(bf16[4,256,384]{2,1,0:T(8,128)(2,1)} %get-tuple-element.568) | copy-start | bytes 2359300
  502.8 5.5 collective-permute-start.21
  507.4 10.8 %collective-permute-start.31 = (bf16[2,256,384]{2,1,0:T(8,128)(2,1)S(1)}, bf16[2,256,384]{2,1,0:T(8,128)(2,1)S(1)}, u32[]{:S(2)}, u32[]{:S(2)}) collective-permute-start(bf16[2,256,384]{2,1,0:T(8,128)(2,1)S(1)} %get-tuple-element.583), channel_id=1, source_target_pairs={{0,1},{1,0},{2,3},{3,2},{4,5},{5,4},{6,7},{7,6},{8,9},{9,8},{10,11... | collective-permute-start | bytes 1179656 | tf_op jit(solution)/shard_map/ppermute | solution.py:36
  510.7 26.2 %collective-permute-start.32 = (bf16[2,288,384]{2,1,0:T(8,128)(2,1)S(1)}, bf16[2,288,384]{2,1,0:T(8,128)(2,1)S(1)}, u32[]{:S(2)}, u32[]{:S(2)}) collective-permute-start(bf16[2,288,384]{2,1,0:T(8,128)(2,1)S(1)} %get-tuple-element.585), channel_id=1, source_target_pairs={{0,1},{1,0},{2,3},{3,2},{4,5},{5,4},{6,7},{7,6},{8,9},{9,8},{10,11... | collective-permute-start | bytes 1327112 | tf_op jit(solution)/shard_map/ppermute | solution.py:36
  511.6 32.9 %collective-permute-start.33 = (bf16[4,240,384]{2,1,0:T(8,128)(2,1)S(1)}, bf16[4,240,384]{2,1,0:T(8,128)(2,1)S(1)}, u32[]{:S(2)}, u32[]{:S(2)}) collective-permute-start(bf16[4,240,384]{2,1,0:T(8,128)(2,1)S(1)} %get-tuple-element.587), channel_id=1, source_target_pairs={{0,4},{4,0},{8,12},{12,8},{1,5},{5,1},{9,13},{13,9},{2,6},{6,2},{1... | collective-permute-start | bytes 2211848 | tf_op jit(solution)/shard_map/ppermute | solution.py:36
  518.2 37.3 %collective-permute-start.34 = (bf16[4,288,384]{2,1,0:T(8,128)(2,1)S(1)}, bf16[4,288,384]{2,1,0:T(8,128)(2,1)S(1)}, u32[]{:S(2)}, u32[]{:S(2)}) collective-permute-start(bf16[4,288,384]{2,1,0:T(8,128)(2,1)S(1)} %get-tuple-element.589), channel_id=1, source_target_pairs={{0,8},{4,12},{8,0},{12,4},{1,9},{5,13},{9,1},{13,5},{2,10},{6,14},... | collective-permute-start | bytes 2654216 | tf_op jit(solution)/shard_map/ppermute | solution.py:36
  518.5 18.0 %copy-start.28 = (bf16[8,256,384]{2,1,0:T(8,128)(2,1)S(1)}, bf16[8,256,384]{2,1,0:T(8,128)(2,1)}, u32[]{:S(2)}) copy-start(bf16[8,256,384]{2,1,0:T(8,128)(2,1)} %get-tuple-element.576) | copy-start | bytes 4718596
  523.4 14.3 %collective-permute-start.37 = (bf16[1,256,384]{2,1,0:T(8,128)(2,1)S(1)}, bf16[1,256,384]{2,1,0:T(8,128)(2,1)S(1)}, u32[]{:S(2)}, u32[]{:S(2)}) collective-permute-start(bf16[1,256,384]{2,1,0:T(8,128)(2,1)S(1)} %get-tuple-element.623), channel_id=1, source_target_pairs={{0,2},{1,3},{2,0},{3,1},{4,6},{5,7},{6,4},{7,5},{8,10},{9,11},{10,... | collective-permute-start | bytes 589832 | tf_op jit(solution)/shard_map/ppermute | solution.py:36
  537.0 7.5 %collective-permute-start.45 = (bf16[1,288,384]{2,1,0:T(8,128)(2,1)S(1)}, bf16[1,288,384]{2,1,0:T(8,128)(2,1)S(1)}, u32[]{:S(2)}, u32[]{:S(2)}) collective-permute-start(bf16[1,288,384]{2,1,0:T(8,128)(2,1)S(1)} %get-tuple-element.652), channel_id=1, source_target_pairs={{0,2},{1,3},{2,0},{3,1},{4,6},{5,7},{6,4},{7,5},{8,10},{9,11},{10,... | collective-permute-start | bytes 663560 | tf_op jit(solution)/shard_map/ppermute | solution.py:36
  537.1 20.8 %collective-permute-start.29 = (bf16[4,256,384]{2,1,0:T(8,128)(2,1)S(1)}, bf16[4,256,384]{2,1,0:T(8,128)(2,1)S(1)}, u32[]{:S(2)}, u32[]{:S(2)}) collective-permute-start(bf16[4,256,384]{2,1,0:T(8,128)(2,1)S(1)} %get-tuple-element.579), channel_id=1, source_target_pairs={{0,4},{4,0},{8,12},{12,8},{1,5},{5,1},{9,13},{13,9},{2,6},{6,2},{1... | collective-permute-start | bytes 2359304 | tf_op jit(solution)/shard_map/ppermute | solution.py:36
  537.8 36.7 %collective-permute-start.30 = (bf16[4,288,384]{2,1,0:T(8,128)(2,1)S(1)}, bf16[4,288,384]{2,1,0:T(8,128)(2,1)S(1)}, u32[]{:S(2)}, u32[]{:S(2)}) collective-permute-start(bf16[4,288,384]{2,1,0:T(8,128)(2,1)S(1)} %get-tuple-element.581), channel_id=1, source_target_pairs={{0,8},{4,12},{8,0},{12,4},{1,9},{5,13},{9,1},{13,5},{2,10},{6,14},... | collective-permute-start | bytes 2654216 | tf_op jit(solution)/shard_map/ppermute | solution.py:36
  544.7 11.1 %collective-permute-start.39 = (bf16[2,240,384]{2,1,0:T(8,128)(2,1)S(1)}, bf16[2,240,384]{2,1,0:T(8,128)(2,1)S(1)}, u32[]{:S(2)}, u32[]{:S(2)}) collective-permute-start(bf16[2,240,384]{2,1,0:T(8,128)(2,1)S(1)} %get-tuple-element.627), channel_id=1, source_target_pairs={{0,1},{1,0},{2,3},{3,2},{4,5},{5,4},{6,7},{7,6},{8,9},{9,8},{10,11... | collective-permute-start | bytes 1105928 | tf_op jit(solution)/shard_map/ppermute | solution.py:36
  555.7 18.8 %collective-permute-start.40 = (bf16[2,288,384]{2,1,0:T(8,128)(2,1)S(1)}, bf16[2,288,384]{2,1,0:T(8,128)(2,1)S(1)}, u32[]{:S(2)}, u32[]{:S(2)}) collective-permute-start(bf16[2,288,384]{2,1,0:T(8,128)(2,1)S(1)} %get-tuple-element.629), channel_id=1, source_target_pairs={{0,1},{1,0},{2,3},{3,2},{4,5},{5,4},{6,7},{7,6},{8,9},{9,8},{10,11... | collective-permute-start | bytes 1327112 | tf_op jit(solution)/shard_map/ppermute | solution.py:36
  555.9 9.4 %collective-permute-start.41 = (bf16[1,240,384]{2,1,0:T(8,128)(2,1)S(1)}, bf16[1,240,384]{2,1,0:T(8,128)(2,1)S(1)}, u32[]{:S(2)}, u32[]{:S(2)}) collective-permute-start(bf16[1,240,384]{2,1,0:T(8,128)(2,1)S(1)} %get-tuple-element.639), channel_id=1, source_target_pairs={{0,2},{1,3},{2,0},{3,1},{4,6},{5,7},{6,4},{7,5},{8,10},{9,11},{10,... | collective-permute-start | bytes 552968 | tf_op jit(solution)/shard_map/ppermute | solution.py:36
  558.1 31.1 %collective-permute-start.35 = (bf16[2,256,384]{2,1,0:T(8,128)(2,1)S(1)}, bf16[2,256,384]{2,1,0:T(8,128)(2,1)S(1)}, u32[]{:S(2)}, u32[]{:S(2)}) collective-permute-start(bf16[2,256,384]{2,1,0:T(8,128)(2,1)S(1)} %get-tuple-element.615), channel_id=1, source_target_pairs={{0,1},{1,0},{2,3},{3,2},{4,5},{5,4},{6,7},{7,6},{8,9},{9,8},{10,11... | collective-permute-start | bytes 1179656 | tf_op jit(solution)/shard_map/ppermute | solution.py:36
  565.4 24.0 %collective-permute-start.42 = (f32[240,384]{1,0:T(8,128)S(1)}, f32[240,384]{1,0:T(8,128)S(1)}, u32[]{:S(2)}, u32[]{:S(2)}) collective-permute-start(f32[240,384]{1,0:T(8,128)S(1)} %broadcast_select_fusion.16), channel_id=1, source_target_pairs={{0,16},{16,0},{1,17},{17,1},{2,18},{18,2},{3,19},{19,3},{4,20},{20... | collective-permute-start | bytes 1105928 | tf_op jit(solution)/shard_map/ppermute | solution.py:36
  574.6 12.1 %collective-permute-start.47 = (bf16[1,288,384]{2,1,0:T(8,128)(2,1)S(1)}, bf16[1,288,384]{2,1,0:T(8,128)(2,1)S(1)}, u32[]{:S(2)}, u32[]{:S(2)}) collective-permute-start(bf16[1,288,384]{2,1,0:T(8,128)(2,1)S(1)} %get-tuple-element.659), channel_id=1, source_target_pairs={{0,2},{1,3},{2,0},{3,1},{4,6},{5,7},{6,4},{7,5},{8,10},{9,11},{10,... | collective-permute-start | bytes 663560 | tf_op jit(solution)/shard_map/ppermute | solution.py:36
  578.0 17.3 %collective-permute-start.43 = (bf16[2,288,384]{2,1,0:T(8,128)(2,1)S(1)}, bf16[2,288,384]{2,1,0:T(8,128)(2,1)S(1)}, u32[]{:S(2)}, u32[]{:S(2)}) collective-permute-start(bf16[2,288,384]{2,1,0:T(8,128)(2,1)S(1)} %get-tuple-element.644), channel_id=1, source_target_pairs={{0,1},{1,0},{2,3},{3,2},{4,5},{5,4},{6,7},{7,6},{8,9},{9,8},{10,11... | collective-permute-start | bytes 1327112 | tf_op jit(solution)/shard_map/ppermute | solution.py:36
  586.8 24.7 %collective-permute-start.48 = (f32[288,384]{1,0:T(8,128)S(1)}, f32[288,384]{1,0:T(8,128)S(1)}, u32[]{:S(2)}, u32[]{:S(2)}) collective-permute-start(f32[288,384]{1,0:T(8,128)S(1)} %broadcast_select_fusion.4), channel_id=1, source_target_pairs={{0,16},{16,0},{1,17},{17,1},{2,18},{18,2},{3,19},{19,3},{4,20},{20... | collective-permute-start | bytes 1327112 | tf_op jit(solution)/shard_map/ppermute | solution.py:36
  589.3 16.5 %collective-permute-start.36 = (bf16[1,256,384]{2,1,0:T(8,128)(2,1)S(1)}, bf16[1,256,384]{2,1,0:T(8,128)(2,1)S(1)}, u32[]{:S(2)}, u32[]{:S(2)}) collective-permute-start(bf16[1,256,384]{2,1,0:T(8,128)(2,1)S(1)} %get-tuple-element.619), channel_id=1, source_target_pairs={{0,2},{1,3},{2,0},{3,1},{4,6},{5,7},{6,4},{7,5},{8,10},{9,11},{10,... | collective-permute-start | bytes 589832 | tf_op jit(solution)/shard_map/ppermute | solution.py:36
  589.6 16.3 %copy-start.49 = (f32[48,3072]{1,0:T(8,128)}, f32[48,3072]{1,0:T(8,128)S(1)}, u32[]{:S(2)}) copy-start(f32[48,3072]{1,0:T(8,128)S(1)} %get-tuple-element.744) | copy-start | bytes 1769476
  595.4 15.1 %collective-permute-start.44 = (bf16[1,288,384]{2,1,0:T(8,128)(2,1)S(1)}, bf16[1,288,384]{2,1,0:T(8,128)(2,1)S(1)}, u32[]{:S(2)}, u32[]{:S(2)}) collective-permute-start(bf16[1,288,384]{2,1,0:T(8,128)(2,1)S(1)} %get-tuple-element.648), channel_id=1, source_target_pairs={{0,2},{1,3},{2,0},{3,1},{4,6},{5,7},{6,4},{7,5},{8,10},{9,11},{10,... | collective-permute-start | bytes 663560 | tf_op jit(solution)/shard_map/ppermute | solution.py:36
  605.9 6.8 %collective-permute-start.38 = (f32[256,384]{1,0:T(8,128)S(1)}, f32[256,384]{1,0:T(8,128)S(1)}, u32[]{:S(2)}, u32[]{:S(2)}) collective-permute-start(f32[256,384]{1,0:T(8,128)S(1)} %broadcast_select_fusion.12), channel_id=1, source_target_pairs={{0,16},{16,0},{1,17},{17,1},{2,18},{18,2},{3,19},{19,3},{4,20},{20... | collective-permute-start | bytes 1179656 | tf_op jit(solution)/shard_map/ppermute | solution.py:36
  610.6 6.3 %collective-permute-start.46 = (f32[288,384]{1,0:T(8,128)S(1)}, f32[288,384]{1,0:T(8,128)S(1)}, u32[]{:S(2)}, u32[]{:S(2)}) collective-permute-start(f32[288,384]{1,0:T(8,128)S(1)} %broadcast_select_fusion.8), channel_id=1, source_target_pairs={{0,16},{16,0},{1,17},{17,1},{2,18},{18,2},{3,19},{19,3},{4,20},{20... | collective-permute-start | bytes 1327112 | tf_op jit(solution)/shard_map/ppermute | solution.py:36
  (39 other events, 250.3 us)

commit v3 on v2

--- a/solution.py
+++ b/solution.py
@@ -858,6 +858,10 @@
     dc_ref[...] = (chr_ref[...] + mt(dproj_ref[...], gru_v[...])).astype(BF16)
 
 
+def middle_hop():
+    return lax.axis_size(CTX) // 2
+
+
 def chars_back(layer, w, d_states, d_chr, saved, live):
     slots, width = d_states.shape
     count = lax.axis_size(CTX)
@@ -936,13 +940,14 @@
         )
         self.rows[group] += size
 
-    def run(self, collective_id):
+    def run(self, collective_id, parts=None):
         orders = [exchange_order(x_first) for x_first in self.groups]
         n_ctx = lax.axis_size(CTX)
         count = lax.axis_size(DP) * n_ctx
         unit = self.unit
         if any(job["rows"] % 16 for job in self.jobs):
-            return self.run_plainly(orders, n_ctx, count)
+            results = self.run_plainly(orders, n_ctx, count)
+            return results if parts is None else (results, came_back(parts))
         outs = [((count // 2, rows, unit), BF16) for rows in self.rows for _ in (0, 1)]
         most = max(job["rows"] * len(job.get("chunks", (0,))) for job in self.jobs) * count
         coming = [
@@ -952,9 +957,15 @@
         ]
         copies = sum(len(move) for move in self.moves if move)
         scratch = [pltpu.VMEM((most, unit), BF16), coming, [DMA((copies,))] * 2]
-        kernel = functools.partial(pack_kernel, self.jobs, self.moves, count, orders, n_ctx)
-        results = call(kernel, self.arrays, [], outs, scratch, collective_id)
-        return [(results[2 * i], results[2 * i + 1]) for i in range(len(orders))]
+        kernel = functools.partial(pack_kernel, self.jobs, self.moves, count, orders, n_ctx, parts is not None)
+        plain = list(self.arrays)
+        if parts is not None:
+            plain.append(parts)
+            outs.append((parts.shape, parts.dtype))
+            scratch.append([DMA((n_ctx - 1,))] * 2)
+        results = call(kernel, plain, [], outs, scratch, collective_id)
+        packs = [(results[2 * i], results[2 * i + 1]) for i in range(len(orders))]
+        return packs if parts is None else (packs, results[-1])
 
     def run_plainly(self, orders, n_ctx, count):
         blocks = [[] for _ in orders]
@@ -982,15 +993,33 @@
         return results
 
 
-def pack_kernel(jobs, moves, count, orders, n_ctx, *refs):
+def pack_kernel(jobs, moves, count, orders, n_ctx, beside, *refs):
     arrays, rest = refs[: len(moves)], refs[len(moves) :]
-    outs, (held, coming, semaphores) = rest[: 2 * len(orders)], rest[2 * len(orders) :]
+    if beside:
+        parts_ref, rest, part_sems = rest[0], rest[1:-1], rest[-1]
+    outs, rest = rest[: 2 * len(orders)], rest[2 * len(orders) :]
+    if beside:
+        back_ref, rest = rest[0], rest[1:]
+    held, coming, semaphores = rest
     send_sems, recv_sems = semaphores
     section = lax.axis_index(SEC)
     unit = held.shape[1]
     barrier = pltpu.get_barrier_semaphore()
     pl.semaphore_signal(barrier, inc=1, device_id={SEC: 1 - section}, device_id_type=MESH)
-    pl.semaphore_wait(barrier, 1)
+    if beside:
+        for hop in range(1, n_ctx):
+            to = lax.rem(lax.axis_index(CTX) + hop, n_ctx)
+            pl.semaphore_signal(barrier, inc=1, device_id={CTX: to}, device_id_type=MESH)
+    pl.semaphore_wait(barrier, n_ctx if beside else 1)
+    sides = []
+    if beside:
+        rows = parts_ref.shape[0] // (n_ctx - 1)
+        for j in range(1, n_ctx):
+            if j == middle_hop():
+                continue
+            at = slice((j - 1) * rows, j * rows)
+            sems = [sem.at[j - 1] for sem in part_sems]
+            sides.append(send(parts_ref.at[at, :], back_ref.at[at, :], n_ctx - j, *sems))
     places, copies, pending, nth, slot = {}, [], {}, 0, 0
     for index, move in enumerate(moves):
         if not move:
@@ -1055,6 +1084,8 @@
                 target[place % (count // 2), row : row + size, :] = held[pl.ds(begin, size), :]
     for copy in copies:
         copy.wait_send()
+    for copy in sides:
+        copy.wait()
 
 
 class Halving:
@@ -1091,29 +1122,32 @@
                 value = self.chains[chain].step(value)
         return value
 
-    def finish(self):
-        after = jnp.zeros((), F32)
+    def round(self, after):
+        for chain in TAIL:
+            if self.chains[chain].order:
+                after = self.chains[chain].step(after)
+        return after
+
+    def finish(self, after):
         while any(chain.order for chain in self.chains):
-            for chain in TAIL:
-                if self.chains[chain].order:
-                    after = self.chains[chain].step(after)
+            after = self.round(after)
+        return after
 
 
 PLAN = {
     (1, 1): (0, 1),
     (0, 3): (0, 1),
-    (0, 4): (0, 1),
-    (0, 0): (2, 3),
-    (0, 1): (0, 1),
+    (0, 4): (0, 1, 2, 3),
+    (0, 0): (0, 1, 2, 3),
+    (0, 1): (4,),
 }
-TAIL = (0, 1, 4, 5, 2, 3, 6, 7)
-
-
-def returned(d_x, parts):
-    rows, n_ctx = d_x.shape[0], lax.axis_size(CTX)
-    for j in range(1, n_ctx):
-        d_x = d_x + turned(parts[(j - 1) * rows : j * rows], n_ctx - j).astype(F32)
-    return d_x
+TAIL = (0, 1, 2, 3, 4, 5, 6, 7)
+
+
+def came_back(parts):
+    n_ctx = lax.axis_size(CTX)
+    rows = parts.shape[0] // (n_ctx - 1)
+    return jnp.concatenate([turned(parts[(j - 1) * rows : j * rows], n_ctx - j) for j in range(1, n_ctx)])
 
 
 def layer_backward(layer, w, saved, g_tok, g_chr, ids_both, live, group_row, column, seen, section, queue):
@@ -1144,10 +1178,13 @@
         saved["query"], saved["keys"], saved["values"], seen, saved["lse"], d_attended
     )
     dq = queue.advance(dq, layer, 0)
+    if layer:
+        d_states, dq = lax.optimization_barrier((d_states, dq))
+    d_proj, d_c, proj_sums = chars_back(layer, w, d_states, d_chr, saved, live)
+    dq, d_proj = lax.optimization_barrier((dq, d_proj))
     d_x, parts, sums_c = project_back(layer, w, d_first, dq, dk, dv)
-    if layer:
-        d_x = returned(d_x, parts)
-    d_proj, d_c, proj_sums = chars_back(layer, w, d_states, d_chr, saved, live)
+    middle = middle_hop() - 1
+    part_back = turned(parts[middle * rows : (middle + 1) * rows], lax.axis_size(CTX) - middle_hop())
     d_proj = queue.advance(d_proj, layer, 1)
     small = (
         jnp.stack([sums_c[0], sums_c[1], sums_b[5], sums_b[2], sums_a[0]]),
@@ -1179,15 +1216,18 @@
     chunks = [(right, begin, width, begin) for begin in range(0, width, unit)]
     late.product(1, late.operand(saved["chars_low"]), chunks, block)
     late.plain(1, packed.astype(BF16).reshape(-1, unit), 16)
-    packs = late.run(1)
-    packs, d_c, parts = lax.optimization_barrier((packs, d_c, parts))
-    if not layer:
-        d_x = returned(d_x, parts)
+    packs, back = late.run(1, parts)
+    packs, d_c, back = lax.optimization_barrier((packs, d_c, back))
+    g_x = d_x + part_back.astype(F32)
+    for j in range(len(back) // rows):
+        if j != middle:
+            g_x = g_x + back[j * rows : (j + 1) * rows].astype(F32)
+    g_x = g_x.astype(BF16)
     more = [Halving(pack, x_first) for pack, x_first in zip(packs, late.groups)]
     queue.add(more)
     d_c = queue.advance(d_c, layer, 2)
     sizes = [(p.shape[0], p.size // count // p.shape[0]) for p in small]
-    return d_x.astype(BF16), d_c, chains + more, sizes
+    return g_x, d_c, chains + more, sizes
 
 
 def on_device(
@@ -1236,7 +1276,7 @@
         g_x, g_c, chains[layer], sizes = layer_backward(
             layer, layers[layer], kept[layer], g_x, g_c, ids_both, live, group_row, column, seen, section, queue
         )
-    queue.finish()
+    queue.finish(jnp.zeros((), F32))
     packs = [[chain.total for chain in four] for four in chains]
 
     def gathered(grad, value):

time: 627 us -> 601 us (0.959)
  waiting for transfers between devices: 142 us -> 113 us
  Pallas kernels: 357 us -> 373 us
  starting transfers between devices: 50.8 us -> 37.2 us
    ppermute x6 -> x2, waiting for transfers between devices: 56.2 us -> 0.01 us  [turned(): lax.ppermute(value, CTX, [(i, (i + by) % count) for i in range(count)])]
    ppermute x43, waiting for transfers between devices: 86.2 us -> 113 us  [flip(): lax.ppermute(value, axis, [(i, i ^ 1 << bit) for i in range(lax.axis_size...]
    pallas_call x18, Pallas kernels: 315 us -> 331 us  [call(): pl.pallas_call(kernel, in_specs=[VMEM_SPEC] * len(plain) + [ANY_SPEC] * l...]
    ppermute x43, starting transfers between devices: 44.1 us -> 34.7 us  [flip(): lax.ppermute(value, axis, [(i, i ^ 1 << bit) for i in range(lax.axis_size...]
  transfers between devices with their start and end apart: 49 -> 45, of which waited for: 18 -> 16; matrix products, arithmetic and copies ran while one was open for 8% -> 10% of each run, Pallas kernels for 36% -> 39%
where the time goes in v3:
time: 601 us; the launch traced here: 597 us
  Pallas kernels  373 us (62%)
  waiting for transfers between devices  113 us (19%)
  other arithmetic  45.7 us (8%)
  starting transfers between devices  37.2 us (6%)
  local copies, waits for them, and re-layouts  25.4 us (4%)
    pallas_call x18, Pallas kernels, call(): pl.pallas_call(kernel, in_specs=[VMEM_SPEC] * len(plain) + [ANY_SPEC] * l...  331 us
    ppermute x43, waiting for transfers between devices, flip(): lax.ppermute(value, axis, [(i, i ^ 1 << bit) for i in range(lax.axis_size...  113 us
    ppermute x43, starting transfers between devices, flip(): lax.ppermute(value, axis, [(i, i ^ 1 << bit) for i in range(lax.axis_size...  34.7 us
    pallas_call x2, Pallas kernels, attend_back(): pl.pallas_call(functools.partial(attend_back_kernel, size), grid=(steps,)...  29.2 us
    convert_element_type x24, other arithmetic, step(): kept = (kept[:cut].astype(F32) + got[:cut].astype(F32)).astype(BF16)  26.6 us
    pallas_call x1, Pallas kernels, deal(): pl.pallas_call(deal_kernel, in_specs=[pl.BlockSpec(memory_space=pltpu.SME...  12.8 us
  transfers between devices with their start and end apart: 45, of which 16 were waited for; matrix products, arithmetic and copies ran while one was open for 10% of the time, Pallas kernels for 39%

profile of v3, /device:TPU:1, one launch (start us, length us, event | category | flops | bytes accessed | tf_op | source)
XLA Modules:
  0.0 597.0 jit_solution(2196624016216428410)
XLA Ops:
  2.4 3.5 copy.60
  8.6 12.8 %shard_map.272 = (bf16[256,768]{1,0:T(8,128)(2,1)}, bf16[256,768]{1,0:T(8,128)(2,1)}, bf16[512,768]{1,0:T(8,128)(2,1)}, bf16[512,768]{1,0:T(8,128)(2,1)}, f32[16...) custom-call(s32[2]{0:T(128)} %lengths_ref.1, ...), custom_call_target="tpu_custom_call" | custom-call | flops 1 | bytes 1 | tf_op jit(solution)/shard_map/pallas_call | solution.py:425
  22.7 1.3 slice.541.bias_ref
  23.9 38.9 %shard_map.273 = (bf16[1024,768]{1,0:T(8,128)(2,1)}, f32[512,768]{1,0:T(8,128)}, bf16[512,768]{1,0:T(8,128)(2,1)}, f32[512,1536]{1,0:T(8,128)}, f32[512,768]{1,0...) custom-call(bf16[256,768]{1,0:T(8,128)(2,1)} %get-tuple-element.356.x_ref.refs_6_, ...), custom_call_target="tpu_custom_call" | custom-call | flops 1 | bytes 1 | tf_op jit(solution)/shard_map/pallas_call | solution.py:351
  64.7 23.3 %shard_map.274 = (bf16[256,768]{1,0:T(8,128)(2,1)}, bf16[1024,768]{1,0:T(8,128)(2,1)}, bf16[1024,768]{1,0:T(8,128)(2,1)}, f32[6,8,256]{2,1,0:T(8,128)}, bf16[256...) custom-call(bf16[1024,768]{1,0:T(8,128)(2,1)} %get-tuple-element.364, ...), custom_call_target="tpu_custom_call" | custom-call | flops 1 | bytes 1 | tf_op jit(solution)/shard_map/pallas_call | solution.py:351
  88.0 11.6 %shard_map.275 = (bf16[256,768]{1,0:T(8,128)(2,1)}, bf16[512,768]{1,0:T(8,128)(2,1)}, bf16[256,1536]{1,0:T(8,128)(2,1)}, f32[256,768]{1,0:T(8,128)}, f32[256,768...) custom-call(f32[256,768]{1,0:T(8,128)} %get-tuple-element.371.features_ref, ...), custom_call_target="tpu_custom_call" | custom-call | flops 1 | bytes 1 | tf_op jit(solution)/shard_map/pallas_call | solution.py:351
  99.6 30.9 %shard_map.276 = (bf16[1024,768]{1,0:T(8,128)(2,1)}, f32[512,768]{1,0:T(8,128)}, bf16[512,768]{1,0:T(8,128)(2,1)}, f32[512,1536]{1,0:T(8,128)}, f32[512,768]{1,0...) custom-call(bf16[256,768]{1,0:T(8,128)(2,1)} %get-tuple-element.377.x_ref.refs_6_, ...), custom_call_target="tpu_custom_call" | custom-call | flops 1 | bytes 1 | tf_op jit(solution)/shard_map/pallas_call | solution.py:351
  130.5 31.9 %shard_map.277 = (bf16[256,768]{1,0:T(8,128)(2,1)}, bf16[1024,768]{1,0:T(8,128)(2,1)}, bf16[1024,768]{1,0:T(8,128)(2,1)}, f32[6,8,256]{2,1,0:T(8,128)}, bf16[256...) custom-call(bf16[1024,768]{1,0:T(8,128)(2,1)} %get-tuple-element.380, ...), custom_call_target="tpu_custom_call" | custom-call | flops 1 | bytes 1 | tf_op jit(solution)/shard_map/pallas_call | solution.py:351
  162.4 11.7 %shard_map.278 = (bf16[256,768]{1,0:T(8,128)(2,1)}, bf16[512,768]{1,0:T(8,128)(2,1)}, bf16[256,1536]{1,0:T(8,128)(2,1)}, f32[256,768]{1,0:T(8,128)}, f32[256,768...) custom-call(f32[256,768]{1,0:T(8,128)} %get-tuple-element.382.features_ref, ...), custom_call_target="tpu_custom_call" | custom-call | flops 1 | bytes 1 | tf_op jit(solution)/shard_map/pallas_call | solution.py:351
  174.1 12.1 %shard_map.279 = (f32[256,768]{1,0:T(8,128)}, f32[512,768]{1,0:T(8,128)}, f32[512,768]{1,0:T(8,128)}, bf16[256,2304]{1,0:T(8,128)(2,1)}, f32[8,768]{1,0:T(8,128)}) custom-call(bf16[256,768]{1,0:T(8,128)(2,1)} %get-tuple-element.349.gt_ref, bf16[512,768]{1,0:T(8,128)(2,1)} %get-tuple-element.350.gc_ref, f32[256,768]{1,0:T(8,128)} %get-tuple-element.386.unit3_ref, ...), custom_call_target="tpu_custom_call" | custom-call | flops 1 | bytes 1 | tf_op jit(solution)/shard_map/pallas_call | solution.py:351
  186.2 11.1 %shard_map.280 = (bf16[256,768]{1,0:T(8,128)(2,1)}, bf16[256,3072]{1,0:T(8,128)(2,1)}, f32[256,768]{1,0:T(8,128)}, bf16[256,768]{1,0:T(8,128)(2,1)}, bf16[256,76...) custom-call(f32[256,768]{1,0:T(8,128)} %get-tuple-element.393.feat_ref, ...), custom_call_target="tpu_custom_call" | custom-call | flops 1 | bytes 1 | tf_op jit(solution)/shard_map/pallas_call | solution.py:351
  197.4 18.7 %shard_map.281 = (bf16[8,288,384]{2,1,0:T(8,128)(2,1)}, bf16[8,288,384]{2,1,0:T(8,128)(2,1)}, bf16[8,240,384]{2,1,0:T(8,128)(2,1)}, bf16[8,240,384]{2,1,0:T(8,128)(2,1)}) custom-call(bf16[256,2304]{1,0:T(8,128)(2,1)} %get-tuple-element.391.refs_0_, bf16[256,1536]{1,0:T(8,128)(2,1)} %get-tuple-element.392.refs_1_, ...), custom_call_target="tpu_custom_call" | custom-call | flops 1 | bytes 1 | tf_op jit(solution)/shard_map/pallas_call | solution.py:351
  217.5 1.3 collective-permute-start.5
  221.0 1.4 copy-done.10
  222.4 14.6 %shard_map.282 = (bf16[256,768]{1,0:T(8,128)(2,1)S(1)}, bf16[1024,768]{1,0:T(8,128)(2,1)S(1)}, bf16[1024,768]{1,0:T(8,128)(2,1)S(1)}) custom-call(bf16[256,768]{1,0:T(8,128)(2,1)S(1)} %copy-done.13, bf16[1024,768]{1,0:T(8,128)(2,1)S(1)} %copy-done.9, bf16[1024,768]{1,0:T(8,128)(2,1)S(1)} %copy-done.10, f32[1024,1]{1,0:T(8,128)S(1)} %copy-done, ...), custom_call_target="tpu_custom_call" | custom-call | flops 1 | bytes 1 | tf_op jit(solution)/shard_map/pallas_call | solution.py:96
  240.0 12.8 %shard_map.283 = (bf16[512,1536]{1,0:T(8,128)(2,1)}, bf16[512,768]{1,0:T(8,128)(2,1)}, f32[1,1536]{1,0:T(1,128)}) custom-call(f32[512,768]{1,0:T(8,128)} %get-tuple-element.420.grad_ref, f32[512,768]{1,0:T(8,128)} %get-tuple-element.421.chr_ref, f32[512,1536]{1,0:T(8,128)} %get-tuple-element.422.proj_ref, f32[512,1]{1,0:T(8,128)} %get-tuple-element.359.live_ref, ...), custom_call_target="tpu_custom_call" | custom-call | flops 1 | bytes 1 | tf_op jit(solution)/shard_map/pallas_call | solution.py:351
  252.9 8.3 %shard_map.284 = (f32[256,768]{1,0:T(8,128)}, bf16[768,768]{1,0:T(8,128)(2,1)}, f32[8,768]{1,0:T(8,128)}) custom-call(f32[256,768]{1,0:T(8,128)} %get-tuple-element.437.first_ref, bf16[256,768]{1,0:T(8,128)(2,1)} %copy-done.6, bf16[1024,768]{1,0:T(8,128)(2,1)} %copy-done.3, bf16[1024,768]{1,0:T(8,128)(2,1)} %copy-done.4, bf16[768,2304]{1,0:T(8,128)(2,1)} %bitcast.113, ...), custom_call_target="tpu_custom_call" | custom-call | flops 1 | bytes 1 | tf_op jit(solution)/shard_map/pallas_call | solution.py:351
  264.8 1.7 collective-permute-start.9
  267.6 2.9 add_convert_fusion.6
  270.7 2.6 add_convert_fusion.14
  273.3 32.3 %shard_map.285 = (bf16[8,288,384]{2,1,0:T(8,128)(2,1)}, bf16[8,288,384]{2,1,0:T(8,128)(2,1)}, bf16[8,256,384]{2,1,0:T(8,128)(2,1)}, bf16[8,256,384]{2,1,0:T(8,128)(2,1)}, bf16[768,768]{1,0:T(8,128)(2,1)}) custom-call(bf16[256,768]{1,0:T(8,128)(2,1)} %get-tuple-element.443.refs_0_, bf16[256,3072]{1,0:T(8,128)(2,1)} %get-tuple-element.444.refs_1_, ...), custom_call_target="tpu_custom_call" | custom-call | flops 1 | bytes 1 | tf_op jit(solution)/shard_map/pallas_call | solution.py:351
  307.2 2.1 add_convert_fusion.29.gt_ref
  309.2 12.1 %shard_map.286 = (f32[256,768]{1,0:T(8,128)}, f32[512,768]{1,0:T(8,128)}, f32[512,768]{1,0:T(8,128)}, bf16[256,2304]{1,0:T(8,128)(2,1)}, f32[8,768]{1,0:T(8,128)}) custom-call(bf16[256,768]{1,0:T(8,128)(2,1)} %add_convert_fusion.29.gt_ref, bf16[512,768]{1,0:T(8,128)(2,1)} %get-tuple-element.460.refs_2_.gc_ref, f32[256,768]{1,0:T(8,128)} %get-tuple-element.461.unit3_ref, ...), custom_call_target="tpu_custom_call" | custom-call | flops 1 | bytes 1 | tf_op jit(solution)/shard_map/pallas_call | solution.py:351
  321.3 13.6 %shard_map.290 = (bf16[512,1536]{1,0:T(8,128)(2,1)}, bf16[512,768]{1,0:T(8,128)(2,1)}, f32[1,1536]{1,0:T(1,128)}) custom-call(f32[512,768]{1,0:T(8,128)} %get-tuple-element.546.grad_ref, f32[512,768]{1,0:T(8,128)} %get-tuple-element.547.chr_ref, f32[512,1536]{1,0:T(8,128)} %get-tuple-element.548.proj_ref, f32[512,1]{1,0:T(8,128)} %get-tuple-element.359.live_ref, ...), custom_call_target="tpu_custom_call" | custom-call | flops 1 | bytes 1 | tf_op jit(solution)/shard_map/pallas_call | solution.py:351
  337.0 1.3 add_convert_fusion.32
  338.9 11.1 %shard_map.287 = (bf16[256,768]{1,0:T(8,128)(2,1)}, bf16[256,3072]{1,0:T(8,128)(2,1)}, f32[256,768]{1,0:T(8,128)}, bf16[256,768]{1,0:T(8,128)(2,1)}, bf16[256,76...) custom-call(f32[256,768]{1,0:T(8,128)} %get-tuple-element.474.feat_ref, ...), custom_call_target="tpu_custom_call" | custom-call | flops 1 | bytes 1 | tf_op jit(solution)/shard_map/pallas_call | solution.py:351
  353.3 1.5 collective-permute-start.17
  354.8 6.7 %collective-permute-done.11 = bf16[8,288,384]{2,1,0:T(8,128)(2,1)} collective-permute-done((bf16[8,288,384]{2,1,0:T(8,128)(2,1)}, bf16[8,288,384]{2,1,0:T(8,128)(2,1)}, u32[]{:S(2)}, u32[]{:S(2)}) %collective-permute-start.11) | collective-permute-done | bytes 1769504 | tf_op jit(solution)/shard_map/ppermute | solution.py:36
  361.5 2.8 add_convert_fusion.4
  364.3 2.9 add_convert_fusion.10
  367.6 14.8 %shard_map.288 = (bf16[8,288,384]{2,1,0:T(8,128)(2,1)}, bf16[8,288,384]{2,1,0:T(8,128)(2,1)}, bf16[8,240,384]{2,1,0:T(8,128)(2,1)}, bf16[8,240,384]{2,1,0:T(8,128)(2,1)}) custom-call(bf16[256,2304]{1,0:T(8,128)(2,1)} %get-tuple-element.517.refs_0_, bf16[256,1536]{1,0:T(8,128)(2,1)} %get-tuple-element.518.refs_1_, ...), custom_call_target="tpu_custom_call" | custom-call | flops 1 | bytes 1 | tf_op jit(solution)/shard_map/pallas_call | solution.py:351
  382.4 1.9 collective-permute-start.16
  384.3 14.6 %shard_map.289 = (bf16[256,768]{1,0:T(8,128)(2,1)S(1)}, bf16[1024,768]{1,0:T(8,128)(2,1)S(1)}, bf16[1024,768]{1,0:T(8,128)(2,1)S(1)}) custom-call(bf16[256,768]{1,0:T(8,128)(2,1)S(1)} %copy-done.11, bf16[1024,768]{1,0:T(8,128)(2,1)S(1)} %copy-done.7, bf16[1024,768]{1,0:T(8,128)(2,1)S(1)} %copy-done.8, f32[1024,1]{1,0:T(8,128)S(1)} %copy-done, ...), custom_call_target="tpu_custom_call" | custom-call | flops 1 | bytes 1 | tf_op jit(solution)/shard_map/pallas_call | solution.py:96
  400.2 1.3 collective-permute-start.24
  401.6 1.3 collective-permute-start.19
  402.9 2.1 add_convert_fusion.20
  406.2 1.3 add_convert_fusion.27
  408.4 8.3 %shard_map.291 = (f32[256,768]{1,0:T(8,128)}, bf16[768,768]{1,0:T(8,128)(2,1)}, f32[8,768]{1,0:T(8,128)}) custom-call(f32[256,768]{1,0:T(8,128)} %get-tuple-element.480.first_ref, bf16[256,768]{1,0:T(8,128)(2,1)} %copy-done.5, bf16[1024,768]{1,0:T(8,128)(2,1)} %copy-done.1, bf16[1024,768]{1,0:T(8,128)(2,1)} %copy-done.2, bf16[768,2304]{1,0:T(8,128)(2,1)} %bitcast.114, ...), custom_call_target="tpu_custom_call" | custom-call | flops 1 | bytes 1 | tf_op jit(solution)/shard_map/pallas_call | solution.py:351
  420.7 5.1 collective-permute-done.26
  426.5 1.9 collective-permute-start.33
  428.3 5.3 collective-permute-done.24
  433.7 2.7 add_convert_fusion.12
  437.6 14.2 %collective-permute-done.32 = bf16[1,256,384]{2,1,0:T(8,128)(2,1)S(1)} collective-permute-done((bf16[1,256,384]{2,1,0:T(8,128)(2,1)S(1)}, bf16[1,256,384]{2,1,0:T(8,128)(2,1)S(1)}, u32[]{:S(2)}, u32[]{:S(2)}) %collective-permute-start.32) | collective-permute-done | bytes 196640 | tf_op jit(solution)/shard_map/ppermute | solution.py:36
  451.8 4.7 collective-permute-done.33
  456.6 2.8 add_convert_fusion.2
  459.6 28.1 %shard_map.292 = (bf16[8,288,384]{2,1,0:T(8,128)(2,1)}, bf16[8,288,384]{2,1,0:T(8,128)(2,1)}, bf16[8,256,384]{2,1,0:T(8,128)(2,1)}, bf16[8,256,384]{2,1,0:T(8,128)(2,1)}, bf16[768,768]{1,0:T(8,128)(2,1)}) custom-call(bf16[256,768]{1,0:T(8,128)(2,1)} %get-tuple-element.556.refs_0_, bf16[256,3072]{1,0:T(8,128)(2,1)} %get-tuple-element.557.refs_1_, ...), custom_call_target="tpu_custom_call" | custom-call | flops 1 | bytes 1 | tf_op jit(solution)/shard_map/pallas_call | solution.py:351
  487.7 1.3 collective-permute-start.22
  489.3 1.5 broadcast_select_fusion.1
  490.8 2.6 collective-permute-start.20
  493.4 1.3 add_convert_fusion.30
  497.3 7.5 %collective-permute-done.37 = bf16[2,240,384]{2,1,0:T(8,128)(2,1)S(1)} collective-permute-done((bf16[2,240,384]{2,1,0:T(8,128)(2,1)S(1)}, bf16[2,240,384]{2,1,0:T(8,128)(2,1)S(1)}, u32[]{:S(2)}, u32[]{:S(2)}) %collective-permute-start.37) | collective-permute-done | bytes 368672 | tf_op jit(solution)/shard_map/ppermute | solution.py:36
  505.9 10.1 %collective-permute-done.38 = bf16[1,240,384]{2,1,0:T(8,128)(2,1)S(1)} collective-permute-done((bf16[1,240,384]{2,1,0:T(8,128)(2,1)S(1)}, bf16[1,240,384]{2,1,0:T(8,128)(2,1)S(1)}, u32[]{:S(2)}, u32[]{:S(2)}) %collective-permute-start.38) | collective-permute-done | bytes 184352 | tf_op jit(solution)/shard_map/ppermute | solution.py:36
  517.1 1.4 maximum_select_fusion
  518.5 1.9 collective-permute-done.31
  522.3 10.6 %collective-permute-done.43 = bf16[1,288,384]{2,1,0:T(8,128)(2,1)S(1)} collective-permute-done((bf16[1,288,384]{2,1,0:T(8,128)(2,1)S(1)}, bf16[1,288,384]{2,1,0:T(8,128)(2,1)S(1)}, u32[]{:S(2)}, u32[]{:S(2)}) %collective-permute-start.43) | collective-permute-done | bytes 221216 | tf_op jit(solution)/shard_map/ppermute | solution.py:36
  536.2 17.0 %collective-permute-done.28 = bf16[4,256,384]{2,1,0:T(8,128)(2,1)S(1)} collective-permute-done((bf16[4,256,384]{2,1,0:T(8,128)(2,1)S(1)}, bf16[4,256,384]{2,1,0:T(8,128)(2,1)S(1)}, u32[]{:S(2)}, u32[]{:S(2)}) %collective-permute-start.28) | collective-permute-done | bytes 786464 | tf_op jit(solution)/shard_map/ppermute | solution.py:36
  553.6 3.2 collective-permute-done.29
  557.0 6.3 %collective-permute-done.34 = bf16[2,256,384]{2,1,0:T(8,128)(2,1)S(1)} collective-permute-done((bf16[2,256,384]{2,1,0:T(8,128)(2,1)S(1)}, bf16[2,256,384]{2,1,0:T(8,128)(2,1)S(1)}, u32[]{:S(2)}, u32[]{:S(2)}) %collective-permute-start.34) | collective-permute-done | bytes 393248 | tf_op jit(solution)/shard_map/ppermute | solution.py:36
  565.5 9.6 %collective-permute-done.35 = bf16[1,256,384]{2,1,0:T(8,128)(2,1)S(1)} collective-permute-done((bf16[1,256,384]{2,1,0:T(8,128)(2,1)S(1)}, bf16[1,256,384]{2,1,0:T(8,128)(2,1)S(1)}, u32[]{:S(2)}, u32[]{:S(2)}) %collective-permute-start.35) | collective-permute-done | bytes 196640 | tf_op jit(solution)/shard_map/ppermute | solution.py:36
  575.2 1.8 collective-permute-done.40
  577.1 1.3 collective-permute-start.41
  578.5 1.7 collective-permute-start.36
  580.3 9.1 %collective-permute-done.41 = bf16[1,288,384]{2,1,0:T(8,128)(2,1)S(1)} collective-permute-done((bf16[1,288,384]{2,1,0:T(8,128)(2,1)S(1)}, bf16[1,288,384]{2,1,0:T(8,128)(2,1)S(1)}, u32[]{:S(2)}, u32[]{:S(2)}) %collective-permute-start.41) | collective-permute-done | bytes 221216 | tf_op jit(solution)/shard_map/ppermute | solution.py:36
  589.4 1.4 collective-permute-start.42
  (309 shorter events, 55.3 us)
Async XLA Ops:
  1.4 20.6 %slice-start = ((s8[4718592]{0:T(1024)(128)(4,1)}), s8[524288]{0:T(1024)(128)(4,1)S(1)}, s32[]{:S(2)}) async-start(s8[4718592]{0:T(1024)(128)(4,1)} %bitcast.97), calls=%async_computation | async-start | bytes 1048576
  5.9 16.1 %slice-start.1 = ((s8[4718592]{0:T(1024)(128)(4,1)}), s8[4194304]{0:T(1024)(128)(4,1)S(1)}, s32[]{:S(2)}) async-start(s8[4718592]{0:T(1024)(128)(4,1)} %bitcast.97), calls=%async_computation.1 | async-start | bytes 8388608
  21.4 66.6 %collective-permute-start.4 = (bf16[4608,768]{1,0:T(8,128)(2,1)}, bf16[4608,768]{1,0:T(8,128)(2,1)}, u32[]{:S(2)}, u32[]{:S(2)}) collective-permute-start(bf16[4608,768]{1,0:T(8,128)(2,1)} %bitcast.88), channel_id=1, source_target_pairs={{0,16},{16,0},{1,17},{17,1},{2,18},{18,2},{3,19},{19,3},{4,20},{20... | collective-permute-start | bytes 21233672 | tf_op jit(solution)/shard_map/ppermute | solution.py:36
  21.6 43.1 %collective-permute-start.3 = (bf16[3072,768]{1,0:T(8,128)(2,1)}, bf16[3072,768]{1,0:T(8,128)(2,1)}, u32[]{:S(2)}, u32[]{:S(2)}) collective-permute-start(bf16[3072,768]{1,0:T(8,128)(2,1)} %bitcast.100), channel_id=1, source_target_pairs={{0,16},{16,0},{1,17},{17,1},{2,18},{18,2},{3,19},{19,3},{4,20},{20... | collective-permute-start | bytes 14155784 | tf_op jit(solution)/shard_map/ppermute | solution.py:36
  22.0 42.7 %collective-permute-start.2 = (bf16[768,3072]{1,0:T(8,128)(2,1)S(1)}, bf16[768,3072]{1,0:T(8,128)(2,1)}, u32[]{:S(2)}, u32[]{:S(2)}) collective-permute-start(bf16[768,3072]{1,0:T(8,128)(2,1)S(1)} %bitcast.99), channel_id=1, source_target_pairs={{0,16},{16,0},{1,17},{17,1},{2,18},{18,2},{3,19},{19,3},{4,20},{20... | collective-permute-start | bytes 14155784 | tf_op jit(solution)/shard_map/ppermute | solution.py:36
  22.1 42.5 %collective-permute-start = (bf16[768,2304]{1,0:T(8,128)(2,1)}, bf16[768,2304]{1,0:T(8,128)(2,1)}, u32[]{:S(2)}, u32[]{:S(2)}) collective-permute-start(bf16[768,2304]{1,0:T(8,128)(2,1)} %bitcast.110), channel_id=1, source_target_pairs={{0,16},{16,0},{1,17},{17,1},{2,18},{18,2},{3,19},{19,3},{4,20},{20... | collective-permute-start | bytes 10616840 | tf_op jit(solution)/shard_map/ppermute | solution.py:36
  22.5 42.2 %collective-permute-start.1 = (bf16[768,768]{1,0:T(8,128)(2,1)S(1)}, bf16[768,768]{1,0:T(8,128)(2,1)}, u32[]{:S(2)}, u32[]{:S(2)}) collective-permute-start(bf16[768,768]{1,0:T(8,128)(2,1)S(1)} %bitcast.119), channel_id=1, source_target_pairs={{0,16},{16,0},{1,17},{17,1},{2,18},{18,2},{3,19},{19,3},{4,20},{20... | collective-permute-start | bytes 3538952 | tf_op jit(solution)/shard_map/ppermute | solution.py:36
  23.9 38.9 %copy-start.43 = (f32[1,4608]{1,0:T(1,128)S(1)}, f32[1,4608]{1,0:T(1,128)}, u32[]{:S(2)}) copy-start(f32[1,4608]{1,0:T(1,128)} %get-tuple-element.361) | copy-start | bytes 55300
  23.9 39.5 %copy-start.42 = (f32[1,4608]{1,0:T(1,128)S(1)}, f32[1,4608]{1,0:T(1,128)}, u32[]{:S(2)}) copy-start(f32[1,4608]{1,0:T(1,128)} %get-tuple-element.379) | copy-start | bytes 55300
  197.3 20.0 %copy-start.23 = (s32[512,1]{1,0:T(8,128)S(1)}, s32[512,1]{1,0:T(8,128)}, u32[]{:S(2)}) copy-start(s32[512,1]{1,0:T(8,128)} %get-tuple-element.358.ids_ref) | copy-start | bytes 6148
  197.3 20.0 %copy-start.38 = (s32[512,1]{1,0:T(8,128)S(1)}, s32[512,1]{1,0:T(8,128)}, u32[]{:S(2)}) copy-start(s32[512,1]{1,0:T(8,128)} %get-tuple-element.446) | copy-start | bytes 6148
  197.3 23.7 %copy-start.13 = (bf16[256,768]{1,0:T(8,128)(2,1)S(1)}, bf16[256,768]{1,0:T(8,128)(2,1)}, u32[]{:S(2)}) copy-start(bf16[256,768]{1,0:T(8,128)(2,1)} %get-tuple-element.413.q_ref) | copy-start | bytes 1179652
  197.3 23.7 %copy-start.14 = (bf16[256,768]{1,0:T(8,128)(2,1)S(1)}, bf16[256,768]{1,0:T(8,128)(2,1)}, u32[]{:S(2)}) copy-start(bf16[256,768]{1,0:T(8,128)(2,1)} %get-tuple-element.417.do_ref) | copy-start | bytes 1179652
  197.3 23.7 %copy-start.16 = (f32[6,8,256]{2,1,0:T(8,128)S(1)}, f32[6,8,256]{2,1,0:T(8,128)}, u32[]{:S(2)}) copy-start(f32[6,8,256]{2,1,0:T(8,128)} %get-tuple-element.416.lse_ref) | copy-start | bytes 147460
  216.0 51.5 %collective-permute-start.6 = (bf16[8,288,384]{2,1,0:T(8,128)(2,1)}, bf16[8,288,384]{2,1,0:T(8,128)(2,1)}, u32[]{:S(2)}, u32[]{:S(2)}) collective-permute-start(bf16[8,288,384]{2,1,0:T(8,128)(2,1)} %get-tuple-element.410), channel_id=1, source_target_pairs={{0,4},{4,0},{8,12},{12,8},{1,5},{5,1},{9,13},{13,9},{2,6},{6,2},{1... | collective-permute-start | bytes 5308424 | tf_op jit(solution)/shard_map/ppermute | solution.py:36
  217.5 52.9 %collective-permute-start.5 = (bf16[8,240,384]{2,1,0:T(8,128)(2,1)}, bf16[8,240,384]{2,1,0:T(8,128)(2,1)}, u32[]{:S(2)}, u32[]{:S(2)}) collective-permute-start(bf16[8,240,384]{2,1,0:T(8,128)(2,1)} %get-tuple-element.408), channel_id=1, source_target_pairs={{0,8},{4,12},{8,0},{12,4},{1,9},{5,13},{9,1},{13,5},{2,10},{6,14},... | collective-permute-start | bytes 4423688 | tf_op jit(solution)/shard_map/ppermute | solution.py:36
  264.8 42.3 %collective-permute-start.9 = (bf16[256,768]{1,0:T(8,128)(2,1)S(1)}, bf16[256,768]{1,0:T(8,128)(2,1)S(1)}, u32[]{:S(2)}, u32[]{:S(2)}) collective-permute-start(bf16[256,768]{1,0:T(8,128)(2,1)S(1)} %slice.553), channel_id=1, source_target_pairs={{0,2},{1,3},{2,0},{3,1},{4,6},{5,7},{6,4},{7,5},{8,10},{9,11},{10,... | collective-permute-start | bytes 1179656 | tf_op jit(solution)/shard_map/ppermute | solution.py:45
  270.4 65.3 %collective-permute-start.8 = (bf16[4,288,384]{2,1,0:T(8,128)(2,1)}, bf16[4,288,384]{2,1,0:T(8,128)(2,1)S(1)}, u32[]{:S(2)}, u32[]{:S(2)}) collective-permute-start(bf16[4,288,384]{2,1,0:T(8,128)(2,1)} %get-tuple-element.435), channel_id=1, source_target_pairs={{0,8},{4,12},{8,0},{12,4},{1,9},{5,13},{9,1},{13,5},{2,10},{6,14},... | collective-permute-start | bytes 2654216 | tf_op jit(solution)/shard_map/ppermute | solution.py:36
  273.3 33.9 %copy-start.35 = (f32[256,768]{1,0:T(8,128)S(1)}, f32[256,768]{1,0:T(8,128)}, u32[]{:S(2)}) copy-start(f32[256,768]{1,0:T(8,128)} %get-tuple-element.441) | copy-start | bytes 2359300
  305.6 30.4 %collective-permute-start.7 = (bf16[4,240,384]{2,1,0:T(8,128)(2,1)}, bf16[4,240,384]{2,1,0:T(8,128)(2,1)}, u32[]{:S(2)}, u32[]{:S(2)}) collective-permute-start(bf16[4,240,384]{2,1,0:T(8,128)(2,1)} %get-tuple-element.433), channel_id=1, source_target_pairs={{0,4},{4,0},{8,12},{12,8},{1,5},{5,1},{9,13},{13,9},{2,6},{6,2},{1... | collective-permute-start | bytes 2211848 | tf_op jit(solution)/shard_map/ppermute | solution.py:36
  305.9 55.6 %collective-permute-start.11 = (bf16[8,288,384]{2,1,0:T(8,128)(2,1)}, bf16[8,288,384]{2,1,0:T(8,128)(2,1)}, u32[]{:S(2)}, u32[]{:S(2)}) collective-permute-start(bf16[8,288,384]{2,1,0:T(8,128)(2,1)} %get-tuple-element.483), channel_id=1, source_target_pairs={{0,4},{4,0},{8,12},{12,8},{1,5},{5,1},{9,13},{13,9},{2,6},{6,2},{1... | collective-permute-start | bytes 5308424 | tf_op jit(solution)/shard_map/ppermute | solution.py:36
  307.1 57.2 %collective-permute-start.10 = (bf16[8,256,384]{2,1,0:T(8,128)(2,1)}, bf16[8,256,384]{2,1,0:T(8,128)(2,1)}, u32[]{:S(2)}, u32[]{:S(2)}) collective-permute-start(bf16[8,256,384]{2,1,0:T(8,128)(2,1)} %get-tuple-element.481), channel_id=1, source_target_pairs={{0,8},{4,12},{8,0},{12,4},{1,9},{5,13},{9,1},{13,5},{2,10},{6,14},... | collective-permute-start | bytes 4718600 | tf_op jit(solution)/shard_map/ppermute | solution.py:36
  336.0 15.6 %collective-permute-start.13 = (bf16[2,288,384]{2,1,0:T(8,128)(2,1)S(1)}, bf16[2,288,384]{2,1,0:T(8,128)(2,1)S(1)}, u32[]{:S(2)}, u32[]{:S(2)}) collective-permute-start(bf16[2,288,384]{2,1,0:T(8,128)(2,1)S(1)} %get-tuple-element.487), channel_id=1, source_target_pairs={{0,1},{1,0},{2,3},{3,2},{4,5},{5,4},{6,7},{7,6},{8,9},{9,8},{10,11... | collective-permute-start | bytes 1327112 | tf_op jit(solution)/shard_map/ppermute | solution.py:36
  338.3 14.2 %collective-permute-start.12 = (bf16[2,240,384]{2,1,0:T(8,128)(2,1)S(1)}, bf16[2,240,384]{2,1,0:T(8,128)(2,1)S(1)}, u32[]{:S(2)}, u32[]{:S(2)}) collective-permute-start(bf16[2,240,384]{2,1,0:T(8,128)(2,1)S(1)} %get-tuple-element.485), channel_id=1, source_target_pairs={{0,1},{1,0},{2,3},{3,2},{4,5},{5,4},{6,7},{7,6},{8,9},{9,8},{10,11... | collective-permute-start | bytes 1105928 | tf_op jit(solution)/shard_map/ppermute | solution.py:36
  353.3 45.6 %collective-permute-start.17 = (bf16[1,288,384]{2,1,0:T(8,128)(2,1)}, bf16[1,288,384]{2,1,0:T(8,128)(2,1)}, u32[]{:S(2)}, u32[]{:S(2)}) collective-permute-start(bf16[1,288,384]{2,1,0:T(8,128)(2,1)} %get-tuple-element.511), channel_id=1, source_target_pairs={{0,2},{1,3},{2,0},{3,1},{4,6},{5,7},{6,4},{7,5},{8,10},{9,11},{10,... | collective-permute-start | bytes 663560 | tf_op jit(solution)/shard_map/ppermute | solution.py:36
  364.3 38.6 %collective-permute-start.15 = (bf16[4,288,384]{2,1,0:T(8,128)(2,1)}, bf16[4,288,384]{2,1,0:T(8,128)(2,1)}, u32[]{:S(2)}, u32[]{:S(2)}) collective-permute-start(bf16[4,288,384]{2,1,0:T(8,128)(2,1)} %get-tuple-element.507), channel_id=1, source_target_pairs={{0,8},{4,12},{8,0},{12,4},{1,9},{5,13},{9,1},{13,5},{2,10},{6,14},... | collective-permute-start | bytes 2654216 | tf_op jit(solution)/shard_map/ppermute | solution.py:36
  367.2 39.0 %collective-permute-start.14 = (bf16[4,256,384]{2,1,0:T(8,128)(2,1)}, bf16[4,256,384]{2,1,0:T(8,128)(2,1)}, u32[]{:S(2)}, u32[]{:S(2)}) collective-permute-start(bf16[4,256,384]{2,1,0:T(8,128)(2,1)} %get-tuple-element.505), channel_id=1, source_target_pairs={{0,4},{4,0},{8,12},{12,8},{1,5},{5,1},{9,13},{13,9},{2,6},{6,2},{1... | collective-permute-start | bytes 2359304 | tf_op jit(solution)/shard_map/ppermute | solution.py:36
  367.5 16.8 %copy-start.7 = (bf16[1024,768]{1,0:T(8,128)(2,1)S(1)}, bf16[1024,768]{1,0:T(8,128)(2,1)}, u32[]{:S(2)}) copy-start(bf16[1024,768]{1,0:T(8,128)(2,1)} %get-tuple-element.514.k_ref) | copy-start | bytes 4718596
  367.5 16.8 %copy-start.8 = (bf16[1024,768]{1,0:T(8,128)(2,1)S(1)}, bf16[1024,768]{1,0:T(8,128)(2,1)}, u32[]{:S(2)}) copy-start(bf16[1024,768]{1,0:T(8,128)(2,1)} %get-tuple-element.515.v_ref) | copy-start | bytes 4718596
  367.5 16.8 %copy-start.11 = (bf16[256,768]{1,0:T(8,128)(2,1)S(1)}, bf16[256,768]{1,0:T(8,128)(2,1)}, u32[]{:S(2)}) copy-start(bf16[256,768]{1,0:T(8,128)(2,1)} %get-tuple-element.513.q_ref) | copy-start | bytes 1179652
  367.5 16.8 %copy-start.12 = (bf16[256,768]{1,0:T(8,128)(2,1)S(1)}, bf16[256,768]{1,0:T(8,128)(2,1)}, u32[]{:S(2)}) copy-start(bf16[256,768]{1,0:T(8,128)(2,1)} %get-tuple-element.528.do_ref) | copy-start | bytes 1179652
  367.6 16.7 %copy-start.15 = (f32[6,8,256]{2,1,0:T(8,128)S(1)}, f32[6,8,256]{2,1,0:T(8,128)}, u32[]{:S(2)}) copy-start(f32[6,8,256]{2,1,0:T(8,128)} %get-tuple-element.516.lse_ref) | copy-start | bytes 147460
  382.4 17.8 %collective-permute-start.16 = (bf16[1,240,384]{2,1,0:T(8,128)(2,1)}, bf16[1,240,384]{2,1,0:T(8,128)(2,1)S(1)}, u32[]{:S(2)}, u32[]{:S(2)}) collective-permute-start(bf16[1,240,384]{2,1,0:T(8,128)(2,1)} %get-tuple-element.509), channel_id=1, source_target_pairs={{0,2},{1,3},{2,0},{3,1},{4,6},{5,7},{6,4},{7,5},{8,10},{9,11},{10,... | collective-permute-start | bytes 552968 | tf_op jit(solution)/shard_map/ppermute | solution.py:36
  384.3 17.2 %copy-start.37 = (bf16[1,240,384]{2,1,0:T(8,128)(2,1)S(1)}, bf16[1,240,384]{2,1,0:T(8,128)(2,1)}, u32[]{:S(2)}) copy-start(bf16[1,240,384]{2,1,0:T(8,128)(2,1)} %get-tuple-element.534) | copy-start | bytes 552964
  400.2 33.4 %collective-permute-start.24 = (bf16[8,240,384]{2,1,0:T(8,128)(2,1)}, bf16[8,240,384]{2,1,0:T(8,128)(2,1)}, u32[]{:S(2)}, u32[]{:S(2)}) collective-permute-start(bf16[8,240,384]{2,1,0:T(8,128)(2,1)} %get-tuple-element.585), channel_id=1, source_target_pairs={{0,8},{4,12},{8,0},{12,4},{1,9},{5,13},{9,1},{13,5},{2,10},{6,14},... | collective-permute-start | bytes 4423688 | tf_op jit(solution)/shard_map/ppermute | solution.py:36
  401.6 54.9 %collective-permute-start.19 = (bf16[8,288,384]{2,1,0:T(8,128)(2,1)}, bf16[8,288,384]{2,1,0:T(8,128)(2,1)}, u32[]{:S(2)}, u32[]{:S(2)}) collective-permute-start(bf16[8,288,384]{2,1,0:T(8,128)(2,1)} %get-tuple-element.559), channel_id=1, source_target_pairs={{0,4},{4,0},{8,12},{12,8},{1,5},{5,1},{9,13},{13,9},{2,6},{6,2},{1... | collective-permute-start | bytes 5308424 | tf_op jit(solution)/shard_map/ppermute | solution.py:36
  405.0 15.6 %collective-permute-start.27 = (bf16[2,288,384]{2,1,0:T(8,128)(2,1)}, bf16[2,288,384]{2,1,0:T(8,128)(2,1)S(1)}, u32[]{:S(2)}, u32[]{:S(2)}) collective-permute-start(bf16[2,288,384]{2,1,0:T(8,128)(2,1)} %get-tuple-element.591), channel_id=1, source_target_pairs={{0,1},{1,0},{2,3},{3,2},{4,5},{5,4},{6,7},{7,6},{8,9},{9,8},{10,11... | collective-permute-start | bytes 1327112 | tf_op jit(solution)/shard_map/ppermute | solution.py:36
  407.6 18.2 %collective-permute-start.26 = (bf16[2,256,384]{2,1,0:T(8,128)(2,1)S(1)}, bf16[2,256,384]{2,1,0:T(8,128)(2,1)S(1)}, u32[]{:S(2)}, u32[]{:S(2)}) collective-permute-start(bf16[2,256,384]{2,1,0:T(8,128)(2,1)S(1)} %get-tuple-element.589), channel_id=1, source_target_pairs={{0,1},{1,0},{2,3},{3,2},{4,5},{5,4},{6,7},{7,6},{8,9},{9,8},{10,11... | collective-permute-start | bytes 1179656 | tf_op jit(solution)/shard_map/ppermute | solution.py:36
  419.8 69.5 %collective-permute-start.18 = (bf16[256,768]{1,0:T(8,128)(2,1)S(1)}, bf16[256,768]{1,0:T(8,128)(2,1)}, u32[]{:S(2)}, u32[]{:S(2)}) collective-permute-start(bf16[256,768]{1,0:T(8,128)(2,1)S(1)} %slice.600), channel_id=1, source_target_pairs={{0,2},{1,3},{2,0},{3,1},{4,6},{5,7},{6,4},{7,5},{8,10},{9,11},{10,... | collective-permute-start | bytes 1179656 | tf_op jit(solution)/shard_map/ppermute | solution.py:45
  425.9 25.8 %collective-permute-start.32 = (bf16[1,256,384]{2,1,0:T(8,128)(2,1)S(1)}, bf16[1,256,384]{2,1,0:T(8,128)(2,1)S(1)}, u32[]{:S(2)}, u32[]{:S(2)}) collective-permute-start(bf16[1,256,384]{2,1,0:T(8,128)(2,1)S(1)} %get-tuple-element.624), channel_id=1, source_target_pairs={{0,2},{1,3},{2,0},{3,1},{4,6},{5,7},{6,4},{7,5},{8,10},{9,11},{10,... | collective-permute-start | bytes 589832 | tf_op jit(solution)/shard_map/ppermute | solution.py:36
  426.5 30.0 %collective-permute-start.33 = (bf16[1,288,384]{2,1,0:T(8,128)(2,1)S(1)}, bf16[1,288,384]{2,1,0:T(8,128)(2,1)S(1)}, u32[]{:S(2)}, u32[]{:S(2)}) collective-permute-start(bf16[1,288,384]{2,1,0:T(8,128)(2,1)S(1)} %get-tuple-element.626), channel_id=1, source_target_pairs={{0,2},{1,3},{2,0},{3,1},{4,6},{5,7},{6,4},{7,5},{8,10},{9,11},{10,... | collective-permute-start | bytes 663560 | tf_op jit(solution)/shard_map/ppermute | solution.py:36
  433.7 22.9 %copy-start.26 = (bf16[8,288,384]{2,1,0:T(8,128)(2,1)S(1)}, bf16[8,288,384]{2,1,0:T(8,128)(2,1)}, u32[]{:S(2)}) copy-start(bf16[8,288,384]{2,1,0:T(8,128)(2,1)} %get-tuple-element.562) | copy-start | bytes 5308420
  436.4 57.0 %collective-permute-start.30 = (bf16[4,240,384]{2,1,0:T(8,128)(2,1)}, bf16[4,240,384]{2,1,0:T(8,128)(2,1)}, u32[]{:S(2)}, u32[]{:S(2)}) collective-permute-start(bf16[4,240,384]{2,1,0:T(8,128)(2,1)} %get-tuple-element.620), channel_id=1, source_target_pairs={{0,4},{4,0},{8,12},{12,8},{1,5},{5,1},{9,13},{13,9},{2,6},{6,2},{1... | collective-permute-start | bytes 2211848 | tf_op jit(solution)/shard_map/ppermute | solution.py:36
  459.3 45.7 %collective-permute-start.25 = (bf16[4,288,384]{2,1,0:T(8,128)(2,1)}, bf16[4,288,384]{2,1,0:T(8,128)(2,1)S(1)}, u32[]{:S(2)}, u32[]{:S(2)}) collective-permute-start(bf16[4,288,384]{2,1,0:T(8,128)(2,1)} %get-tuple-element.587), channel_id=1, source_target_pairs={{0,8},{4,12},{8,0},{12,4},{1,9},{5,13},{9,1},{13,5},{2,10},{6,14},... | collective-permute-start | bytes 2654216 | tf_op jit(solution)/shard_map/ppermute | solution.py:36
  459.5 29.7 %copy-start.31 = (bf16[256,768]{1,0:T(8,128)(2,1)S(1)}, bf16[256,768]{1,0:T(8,128)(2,1)}, u32[]{:S(2)}) copy-start(bf16[256,768]{1,0:T(8,128)(2,1)} %get-tuple-element.578) | copy-start | bytes 1179652
  459.5 29.7 %copy-start.36 = (f32[256,768]{1,0:T(8,128)S(1)}, f32[256,768]{1,0:T(8,128)}, u32[]{:S(2)}) copy-start(f32[256,768]{1,0:T(8,128)} %get-tuple-element.554) | copy-start | bytes 2359300
  487.7 46.0 %collective-permute-start.22 = (bf16[8,256,384]{2,1,0:T(8,128)(2,1)}, bf16[8,256,384]{2,1,0:T(8,128)(2,1)S(1)}, u32[]{:S(2)}, u32[]{:S(2)}) collective-permute-start(bf16[8,256,384]{2,1,0:T(8,128)(2,1)} %get-tuple-element.581), channel_id=1, source_target_pairs={{0,8},{4,12},{8,0},{12,4},{1,9},{5,13},{9,1},{13,5},{2,10},{6,14},... | collective-permute-start | bytes 4718600 | tf_op jit(solution)/shard_map/ppermute | solution.py:36
  489.0 46.3 %collective-permute-start.23 = (bf16[8,288,384]{2,1,0:T(8,128)(2,1)}, bf16[8,288,384]{2,1,0:T(8,128)(2,1)S(1)}, u32[]{:S(2)}, u32[]{:S(2)}) collective-permute-start(bf16[8,288,384]{2,1,0:T(8,128)(2,1)} %get-tuple-element.583), channel_id=1, source_target_pairs={{0,4},{4,0},{8,12},{12,8},{1,5},{5,1},{9,13},{13,9},{2,6},{6,2},{1... | collective-permute-start | bytes 5308424 | tf_op jit(solution)/shard_map/ppermute | solution.py:36
  490.8 5.0 collective-permute-start.20
  494.7 10.1 %collective-permute-start.37 = (bf16[2,240,384]{2,1,0:T(8,128)(2,1)S(1)}, bf16[2,240,384]{2,1,0:T(8,128)(2,1)S(1)}, u32[]{:S(2)}, u32[]{:S(2)}) collective-permute-start(bf16[2,240,384]{2,1,0:T(8,128)(2,1)S(1)} %get-tuple-element.661), channel_id=1, source_target_pairs={{0,1},{1,0},{2,3},{3,2},{4,5},{5,4},{6,7},{7,6},{8,9},{9,8},{10,11... | collective-permute-start | bytes 1105928 | tf_op jit(solution)/shard_map/ppermute | solution.py:36
  495.8 21.4 %collective-permute-start.21 = (bf16[512,768]{1,0:T(8,128)(2,1)S(1)}, bf16[512,768]{1,0:T(8,128)(2,1)S(1)}, u32[]{:S(2)}, u32[]{:S(2)}) collective-permute-start(bf16[512,768]{1,0:T(8,128)(2,1)S(1)} %bitcast.132), channel_id=1, source_target_pairs={{0,16},{16,0},{1,17},{17,1},{2,18},{18,2},{3,19},{19,3},{4,20},{20... | collective-permute-start | bytes 2359304 | tf_op jit(solution)/shard_map/ppermute | solution.py:36
  504.9 11.1 %collective-permute-start.38 = (bf16[1,240,384]{2,1,0:T(8,128)(2,1)S(1)}, bf16[1,240,384]{2,1,0:T(8,128)(2,1)S(1)}, u32[]{:S(2)}, u32[]{:S(2)}) collective-permute-start(bf16[1,240,384]{2,1,0:T(8,128)(2,1)S(1)} %get-tuple-element.665), channel_id=1, source_target_pairs={{0,2},{1,3},{2,0},{3,1},{4,6},{5,7},{6,4},{7,5},{8,10},{9,11},{10,... | collective-permute-start | bytes 552968 | tf_op jit(solution)/shard_map/ppermute | solution.py:36
  505.2 15.2 %collective-permute-start.31 = (bf16[2,288,384]{2,1,0:T(8,128)(2,1)S(1)}, bf16[2,288,384]{2,1,0:T(8,128)(2,1)S(1)}, u32[]{:S(2)}, u32[]{:S(2)}) collective-permute-start(bf16[2,288,384]{2,1,0:T(8,128)(2,1)S(1)} %get-tuple-element.622), channel_id=1, source_target_pairs={{0,1},{1,0},{2,3},{3,2},{4,5},{5,4},{6,7},{7,6},{8,9},{9,8},{10,11... | collective-permute-start | bytes 1327112 | tf_op jit(solution)/shard_map/ppermute | solution.py:36
  516.1 5.3 collective-permute-start.39
  520.5 12.4 %collective-permute-start.43 = (bf16[1,288,384]{2,1,0:T(8,128)(2,1)S(1)}, bf16[1,288,384]{2,1,0:T(8,128)(2,1)S(1)}, u32[]{:S(2)}, u32[]{:S(2)}) collective-permute-start(bf16[1,288,384]{2,1,0:T(8,128)(2,1)S(1)} %get-tuple-element.679), channel_id=1, source_target_pairs={{0,2},{1,3},{2,0},{3,1},{4,6},{5,7},{6,4},{7,5},{8,10},{9,11},{10,... | collective-permute-start | bytes 663560 | tf_op jit(solution)/shard_map/ppermute | solution.py:36
  533.1 3.0 collective-permute-start.44
  534.0 19.2 %collective-permute-start.28 = (bf16[4,256,384]{2,1,0:T(8,128)(2,1)S(1)}, bf16[4,256,384]{2,1,0:T(8,128)(2,1)S(1)}, u32[]{:S(2)}, u32[]{:S(2)}) collective-permute-start(bf16[4,256,384]{2,1,0:T(8,128)(2,1)S(1)} %get-tuple-element.616), channel_id=1, source_target_pairs={{0,4},{4,0},{8,12},{12,8},{1,5},{5,1},{9,13},{13,9},{2,6},{6,2},{1... | collective-permute-start | bytes 2359304 | tf_op jit(solution)/shard_map/ppermute | solution.py:36
  535.8 21.0 %collective-permute-start.29 = (bf16[4,288,384]{2,1,0:T(8,128)(2,1)S(1)}, bf16[4,288,384]{2,1,0:T(8,128)(2,1)S(1)}, u32[]{:S(2)}, u32[]{:S(2)}) collective-permute-start(bf16[4,288,384]{2,1,0:T(8,128)(2,1)S(1)} %get-tuple-element.618), channel_id=1, source_target_pairs={{0,8},{4,12},{8,0},{12,4},{1,9},{5,13},{9,1},{13,5},{2,10},{6,14},... | collective-permute-start | bytes 2654216 | tf_op jit(solution)/shard_map/ppermute | solution.py:36
  553.4 9.9 %collective-permute-start.34 = (bf16[2,256,384]{2,1,0:T(8,128)(2,1)S(1)}, bf16[2,256,384]{2,1,0:T(8,128)(2,1)S(1)}, u32[]{:S(2)}, u32[]{:S(2)}) collective-permute-start(bf16[2,256,384]{2,1,0:T(8,128)(2,1)S(1)} %get-tuple-element.652), channel_id=1, source_target_pairs={{0,1},{1,0},{2,3},{3,2},{4,5},{5,4},{6,7},{7,6},{8,9},{9,8},{10,11... | collective-permute-start | bytes 1179656 | tf_op jit(solution)/shard_map/ppermute | solution.py:36
  557.0 20.0 %collective-permute-start.40 = (bf16[2,288,384]{2,1,0:T(8,128)(2,1)S(1)}, bf16[2,288,384]{2,1,0:T(8,128)(2,1)S(1)}, u32[]{:S(2)}, u32[]{:S(2)}) collective-permute-start(bf16[2,288,384]{2,1,0:T(8,128)(2,1)S(1)} %get-tuple-element.670), channel_id=1, source_target_pairs={{0,1},{1,0},{2,3},{3,2},{4,5},{5,4},{6,7},{7,6},{8,9},{9,8},{10,11... | collective-permute-start | bytes 1327112 | tf_op jit(solution)/shard_map/ppermute | solution.py:36
  563.4 11.7 %collective-permute-start.35 = (bf16[1,256,384]{2,1,0:T(8,128)(2,1)S(1)}, bf16[1,256,384]{2,1,0:T(8,128)(2,1)S(1)}, u32[]{:S(2)}, u32[]{:S(2)}) collective-permute-start(bf16[1,256,384]{2,1,0:T(8,128)(2,1)S(1)} %get-tuple-element.656), channel_id=1, source_target_pairs={{0,2},{1,3},{2,0},{3,1},{4,6},{5,7},{6,4},{7,5},{8,10},{9,11},{10,... | collective-permute-start | bytes 589832 | tf_op jit(solution)/shard_map/ppermute | solution.py:36
  577.1 12.2 %collective-permute-start.41 = (bf16[1,288,384]{2,1,0:T(8,128)(2,1)S(1)}, bf16[1,288,384]{2,1,0:T(8,128)(2,1)S(1)}, u32[]{:S(2)}, u32[]{:S(2)}) collective-permute-start(bf16[1,288,384]{2,1,0:T(8,128)(2,1)S(1)} %get-tuple-element.674), channel_id=1, source_target_pairs={{0,2},{1,3},{2,0},{3,1},{4,6},{5,7},{6,4},{7,5},{8,10},{9,11},{10,... | collective-permute-start | bytes 663560 | tf_op jit(solution)/shard_map/ppermute | solution.py:36
  578.5 12.3 %collective-permute-start.36 = (f32[256,384]{1,0:T(8,128)S(1)}, f32[256,384]{1,0:T(8,128)S(1)}, u32[]{:S(2)}, u32[]{:S(2)}) collective-permute-start(f32[256,384]{1,0:T(8,128)S(1)} %broadcast_select_fusion.12), channel_id=1, source_target_pairs={{0,16},{16,0},{1,17},{17,1},{2,18},{18,2},{3,19},{19,3},{4,20},{20... | collective-permute-start | bytes 1179656 | tf_op jit(solution)/shard_map/ppermute | solution.py:36
  589.4 5.6 collective-permute-start.42
  (36 other events, 229.3 us)

commit v4 on v3

--- a/solution.py
+++ b/solution.py
@@ -1139,7 +1139,6 @@
     (0, 3): (0, 1),
     (0, 4): (0, 1, 2, 3),
     (0, 0): (0, 1, 2, 3),
-    (0, 1): (4,),
 }
 TAIL = (0, 1, 2, 3, 4, 5, 6, 7)
 

time: 601 us -> 597 us (level)
  local copies, waits for them, and re-layouts: 25.4 us -> 34.2 us
  waiting for transfers between devices: 113 us -> 105 us
    ppermute x43, waiting for transfers between devices: 113 us -> 90.2 us  [flip(): lax.ppermute(value, axis, [(i, i ^ 1 << bit) for i in range(lax.axis_size...]
    ppermute x2, waiting for transfers between devices: 0.01 us -> 15.2 us  [turned(): lax.ppermute(value, CTX, [(i, (i + by) % count) for i in range(count)])]
  transfers between devices with their start and end apart: 45 -> 45, of which waited for: 16 -> 14; matrix products, arithmetic and copies ran while one was open for 10% -> 10% of each run, Pallas kernels for 39% -> 39%
where the time goes in v4:
time: 597 us; the launch traced here: 593 us
  Pallas kernels  373 us (62%)
  waiting for transfers between devices  105 us (18%)
  other arithmetic  43.8 us (7%)
  starting transfers between devices  34.4 us (6%)
  local copies, waits for them, and re-layouts  34.2 us (6%)
    pallas_call x18, Pallas kernels, call(): pl.pallas_call(kernel, in_specs=[VMEM_SPEC] * len(plain) + [ANY_SPEC] * l...  331 us
    ppermute x43, waiting for transfers between devices, flip(): lax.ppermute(value, axis, [(i, i ^ 1 << bit) for i in range(lax.axis_size...  90.2 us
    ppermute x43, starting transfers between devices, flip(): lax.ppermute(value, axis, [(i, i ^ 1 << bit) for i in range(lax.axis_size...  30.1 us
    pallas_call x2, Pallas kernels, attend_back(): pl.pallas_call(functools.partial(attend_back_kernel, size), grid=(steps,)...  29.1 us
    convert_element_type x24, other arithmetic, step(): kept = (kept[:cut].astype(F32) + got[:cut].astype(F32)).astype(BF16)  24.5 us
    ppermute x2, waiting for transfers between devices, turned(): lax.ppermute(value, CTX, [(i, (i + by) % count) for i in range(count)])  15.2 us
    pallas_call x1, Pallas kernels, deal(): pl.pallas_call(deal_kernel, in_specs=[pl.BlockSpec(memory_space=pltpu.SME...  12.8 us
  transfers between devices with their start and end apart: 45, of which 14 were waited for; matrix products, arithmetic and copies ran while one was open for 10% of the time, Pallas kernels for 39%

profile of v4, /device:TPU:1, one launch (start us, length us, event | category | flops | bytes accessed | tf_op | source)
XLA Modules:
  0.0 592.9 jit_solution(1911994846376974016)
XLA Ops:
  2.4 3.5 copy.60
  8.6 12.8 %shard_map.272 = (bf16[256,768]{1,0:T(8,128)(2,1)}, bf16[256,768]{1,0:T(8,128)(2,1)}, bf16[512,768]{1,0:T(8,128)(2,1)}, bf16[512,768]{1,0:T(8,128)(2,1)}, f32[16...) custom-call(s32[2]{0:T(128)} %lengths_ref.1, ...), custom_call_target="tpu_custom_call" | custom-call | flops 1 | bytes 1 | tf_op jit(solution)/shard_map/pallas_call | solution.py:425
  22.6 1.3 slice.541.bias_ref
  23.9 38.9 %shard_map.273 = (bf16[1024,768]{1,0:T(8,128)(2,1)}, f32[512,768]{1,0:T(8,128)}, bf16[512,768]{1,0:T(8,128)(2,1)}, f32[512,1536]{1,0:T(8,128)}, f32[512,768]{1,0...) custom-call(bf16[256,768]{1,0:T(8,128)(2,1)} %get-tuple-element.356.x_ref.refs_6_, ...), custom_call_target="tpu_custom_call" | custom-call | flops 1 | bytes 1 | tf_op jit(solution)/shard_map/pallas_call | solution.py:351
  64.7 23.3 %shard_map.274 = (bf16[256,768]{1,0:T(8,128)(2,1)}, bf16[1024,768]{1,0:T(8,128)(2,1)}, bf16[1024,768]{1,0:T(8,128)(2,1)}, f32[6,8,256]{2,1,0:T(8,128)}, bf16[256...) custom-call(bf16[1024,768]{1,0:T(8,128)(2,1)} %get-tuple-element.364, ...), custom_call_target="tpu_custom_call" | custom-call | flops 1 | bytes 1 | tf_op jit(solution)/shard_map/pallas_call | solution.py:351
  87.9 11.6 %shard_map.275 = (bf16[256,768]{1,0:T(8,128)(2,1)}, bf16[512,768]{1,0:T(8,128)(2,1)}, bf16[256,1536]{1,0:T(8,128)(2,1)}, f32[256,768]{1,0:T(8,128)}, f32[256,768...) custom-call(f32[256,768]{1,0:T(8,128)} %get-tuple-element.371.features_ref, ...), custom_call_target="tpu_custom_call" | custom-call | flops 1 | bytes 1 | tf_op jit(solution)/shard_map/pallas_call | solution.py:351
  99.6 31.0 %shard_map.276 = (bf16[1024,768]{1,0:T(8,128)(2,1)}, f32[512,768]{1,0:T(8,128)}, bf16[512,768]{1,0:T(8,128)(2,1)}, f32[512,1536]{1,0:T(8,128)}, f32[512,768]{1,0...) custom-call(bf16[256,768]{1,0:T(8,128)(2,1)} %get-tuple-element.377.x_ref.refs_6_, ...), custom_call_target="tpu_custom_call" | custom-call | flops 1 | bytes 1 | tf_op jit(solution)/shard_map/pallas_call | solution.py:351
  130.6 31.8 %shard_map.277 = (bf16[256,768]{1,0:T(8,128)(2,1)}, bf16[1024,768]{1,0:T(8,128)(2,1)}, bf16[1024,768]{1,0:T(8,128)(2,1)}, f32[6,8,256]{2,1,0:T(8,128)}, bf16[256...) custom-call(bf16[1024,768]{1,0:T(8,128)(2,1)} %get-tuple-element.380, ...), custom_call_target="tpu_custom_call" | custom-call | flops 1 | bytes 1 | tf_op jit(solution)/shard_map/pallas_call | solution.py:351
  162.3 11.6 %shard_map.278 = (bf16[256,768]{1,0:T(8,128)(2,1)}, bf16[512,768]{1,0:T(8,128)(2,1)}, bf16[256,1536]{1,0:T(8,128)(2,1)}, f32[256,768]{1,0:T(8,128)}, f32[256,768...) custom-call(f32[256,768]{1,0:T(8,128)} %get-tuple-element.382.features_ref, ...), custom_call_target="tpu_custom_call" | custom-call | flops 1 | bytes 1 | tf_op jit(solution)/shard_map/pallas_call | solution.py:351
  174.0 12.1 %shard_map.279 = (f32[256,768]{1,0:T(8,128)}, f32[512,768]{1,0:T(8,128)}, f32[512,768]{1,0:T(8,128)}, bf16[256,2304]{1,0:T(8,128)(2,1)}, f32[8,768]{1,0:T(8,128)}) custom-call(bf16[256,768]{1,0:T(8,128)(2,1)} %get-tuple-element.349.gt_ref, bf16[512,768]{1,0:T(8,128)(2,1)} %get-tuple-element.350.gc_ref, f32[256,768]{1,0:T(8,128)} %get-tuple-element.386.unit3_ref, ...), custom_call_target="tpu_custom_call" | custom-call | flops 1 | bytes 1 | tf_op jit(solution)/shard_map/pallas_call | solution.py:351
  186.1 11.1 %shard_map.280 = (bf16[256,768]{1,0:T(8,128)(2,1)}, bf16[256,3072]{1,0:T(8,128)(2,1)}, f32[256,768]{1,0:T(8,128)}, bf16[256,768]{1,0:T(8,128)(2,1)}, bf16[256,76...) custom-call(f32[256,768]{1,0:T(8,128)} %get-tuple-element.393.feat_ref, ...), custom_call_target="tpu_custom_call" | custom-call | flops 1 | bytes 1 | tf_op jit(solution)/shard_map/pallas_call | solution.py:351
  197.2 18.5 %shard_map.281 = (bf16[8,288,384]{2,1,0:T(8,128)(2,1)}, bf16[8,288,384]{2,1,0:T(8,128)(2,1)}, bf16[8,240,384]{2,1,0:T(8,128)(2,1)}, bf16[8,240,384]{2,1,0:T(8,128)(2,1)}) custom-call(bf16[256,2304]{1,0:T(8,128)(2,1)} %get-tuple-element.391.refs_0_, bf16[256,1536]{1,0:T(8,128)(2,1)} %get-tuple-element.392.refs_1_, ...), custom_call_target="tpu_custom_call" | custom-call | flops 1 | bytes 1 | tf_op jit(solution)/shard_map/pallas_call | solution.py:351
  215.8 1.3 collective-permute-start.6
  217.2 1.3 collective-permute-start.5
  220.8 1.4 copy-done.10
  222.2 14.6 %shard_map.282 = (bf16[256,768]{1,0:T(8,128)(2,1)S(1)}, bf16[1024,768]{1,0:T(8,128)(2,1)S(1)}, bf16[1024,768]{1,0:T(8,128)(2,1)S(1)}) custom-call(bf16[256,768]{1,0:T(8,128)(2,1)S(1)} %copy-done.13, bf16[1024,768]{1,0:T(8,128)(2,1)S(1)} %copy-done.9, bf16[1024,768]{1,0:T(8,128)(2,1)S(1)} %copy-done.10, f32[1024,1]{1,0:T(8,128)S(1)} %copy-done, ...), custom_call_target="tpu_custom_call" | custom-call | flops 1 | bytes 1 | tf_op jit(solution)/shard_map/pallas_call | solution.py:96
  239.8 12.7 %shard_map.283 = (bf16[512,1536]{1,0:T(8,128)(2,1)}, bf16[512,768]{1,0:T(8,128)(2,1)}, f32[1,1536]{1,0:T(1,128)}) custom-call(f32[512,768]{1,0:T(8,128)} %get-tuple-element.420.grad_ref, f32[512,768]{1,0:T(8,128)} %get-tuple-element.421.chr_ref, f32[512,1536]{1,0:T(8,128)} %get-tuple-element.422.proj_ref, f32[512,1]{1,0:T(8,128)} %get-tuple-element.359.live_ref, ...), custom_call_target="tpu_custom_call" | custom-call | flops 1 | bytes 1 | tf_op jit(solution)/shard_map/pallas_call | solution.py:351
  252.6 8.3 %shard_map.284 = (f32[256,768]{1,0:T(8,128)}, bf16[768,768]{1,0:T(8,128)(2,1)}, f32[8,768]{1,0:T(8,128)}) custom-call(f32[256,768]{1,0:T(8,128)} %get-tuple-element.437.first_ref, bf16[256,768]{1,0:T(8,128)(2,1)} %copy-done.5, bf16[1024,768]{1,0:T(8,128)(2,1)} %copy-done.1, bf16[1024,768]{1,0:T(8,128)(2,1)} %copy-done.2, bf16[768,2304]{1,0:T(8,128)(2,1)} %bitcast.113, ...), custom_call_target="tpu_custom_call" | custom-call | flops 1 | bytes 1 | tf_op jit(solution)/shard_map/pallas_call | solution.py:351
  264.6 1.6 collective-permute-start.9
  267.3 2.9 add_convert_fusion.6
  270.4 2.6 add_convert_fusion.14
  273.0 32.3 %shard_map.285 = (bf16[8,288,384]{2,1,0:T(8,128)(2,1)}, bf16[8,288,384]{2,1,0:T(8,128)(2,1)}, bf16[8,256,384]{2,1,0:T(8,128)(2,1)}, bf16[8,256,384]{2,1,0:T(8,128)(2,1)}, bf16[768,768]{1,0:T(8,128)(2,1)}) custom-call(bf16[256,768]{1,0:T(8,128)(2,1)} %get-tuple-element.443.refs_0_, bf16[256,3072]{1,0:T(8,128)(2,1)} %get-tuple-element.444.refs_1_, ...), custom_call_target="tpu_custom_call" | custom-call | flops 1 | bytes 1 | tf_op jit(solution)/shard_map/pallas_call | solution.py:351
  306.9 2.1 add_convert_fusion.29.gt_ref
  308.9 12.1 %shard_map.286 = (f32[256,768]{1,0:T(8,128)}, f32[512,768]{1,0:T(8,128)}, f32[512,768]{1,0:T(8,128)}, bf16[256,2304]{1,0:T(8,128)(2,1)}, f32[8,768]{1,0:T(8,128)}) custom-call(bf16[256,768]{1,0:T(8,128)(2,1)} %add_convert_fusion.29.gt_ref, bf16[512,768]{1,0:T(8,128)(2,1)} %get-tuple-element.460.refs_2_.gc_ref, f32[256,768]{1,0:T(8,128)} %get-tuple-element.461.unit3_ref, ...), custom_call_target="tpu_custom_call" | custom-call | flops 1 | bytes 1 | tf_op jit(solution)/shard_map/pallas_call | solution.py:351
  321.0 13.7 %shard_map.290 = (bf16[512,1536]{1,0:T(8,128)(2,1)}, bf16[512,768]{1,0:T(8,128)(2,1)}, f32[1,1536]{1,0:T(1,128)}) custom-call(f32[512,768]{1,0:T(8,128)} %get-tuple-element.546.grad_ref, f32[512,768]{1,0:T(8,128)} %get-tuple-element.547.chr_ref, f32[512,1536]{1,0:T(8,128)} %get-tuple-element.548.proj_ref, f32[512,1]{1,0:T(8,128)} %get-tuple-element.359.live_ref, ...), custom_call_target="tpu_custom_call" | custom-call | flops 1 | bytes 1 | tf_op jit(solution)/shard_map/pallas_call | solution.py:351
  336.9 1.3 add_convert_fusion.32
  339.8 11.1 %shard_map.287 = (bf16[256,768]{1,0:T(8,128)(2,1)}, bf16[256,3072]{1,0:T(8,128)(2,1)}, f32[256,768]{1,0:T(8,128)}, bf16[256,768]{1,0:T(8,128)(2,1)}, bf16[256,76...) custom-call(f32[256,768]{1,0:T(8,128)} %get-tuple-element.474.feat_ref, ...), custom_call_target="tpu_custom_call" | custom-call | flops 1 | bytes 1 | tf_op jit(solution)/shard_map/pallas_call | solution.py:351
  352.4 1.3 convert_reduce_fusion
  354.9 1.4 collective-permute-start.17
  356.2 5.0 collective-permute-done.11
  361.2 3.1 add_convert_fusion.4
  364.3 2.9 add_convert_fusion.10
  368.1 14.8 %shard_map.288 = (bf16[8,288,384]{2,1,0:T(8,128)(2,1)}, bf16[8,288,384]{2,1,0:T(8,128)(2,1)}, bf16[8,240,384]{2,1,0:T(8,128)(2,1)}, bf16[8,240,384]{2,1,0:T(8,128)(2,1)}) custom-call(bf16[256,2304]{1,0:T(8,128)(2,1)} %get-tuple-element.517.refs_0_, bf16[256,1536]{1,0:T(8,128)(2,1)} %get-tuple-element.518.refs_1_, ...), custom_call_target="tpu_custom_call" | custom-call | flops 1 | bytes 1 | tf_op jit(solution)/shard_map/pallas_call | solution.py:351
  385.4 1.8 collective-permute-start.16
  387.2 1.4 copy-done.8
  388.6 14.6 %shard_map.289 = (bf16[256,768]{1,0:T(8,128)(2,1)S(1)}, bf16[1024,768]{1,0:T(8,128)(2,1)S(1)}, bf16[1024,768]{1,0:T(8,128)(2,1)S(1)}) custom-call(bf16[256,768]{1,0:T(8,128)(2,1)S(1)} %copy-done.11, bf16[1024,768]{1,0:T(8,128)(2,1)S(1)} %copy-done.7, bf16[1024,768]{1,0:T(8,128)(2,1)S(1)} %copy-done.8, f32[1024,1]{1,0:T(8,128)S(1)} %copy-done, ...), custom_call_target="tpu_custom_call" | custom-call | flops 1 | bytes 1 | tf_op jit(solution)/shard_map/pallas_call | solution.py:96
  403.2 1.4 add_bitcast_fusion.3
  404.6 1.3 collective-permute-start.24
  406.0 1.3 collective-permute-start.23
  407.3 2.1 add_convert_fusion.20
  410.6 2.1 add_convert_fusion.27
  413.0 8.3 %shard_map.291 = (f32[256,768]{1,0:T(8,128)}, bf16[768,768]{1,0:T(8,128)(2,1)}, f32[8,768]{1,0:T(8,128)}) custom-call(f32[256,768]{1,0:T(8,128)} %get-tuple-element.480.first_ref, bf16[256,768]{1,0:T(8,128)(2,1)} %copy-done.6, bf16[1024,768]{1,0:T(8,128)(2,1)} %copy-done.3, bf16[1024,768]{1,0:T(8,128)(2,1)} %copy-done.4, bf16[768,2304]{1,0:T(8,128)(2,1)} %bitcast.114, ...), custom_call_target="tpu_custom_call" | custom-call | flops 1 | bytes 1 | tf_op jit(solution)/shard_map/pallas_call | solution.py:351
  423.1 1.7 reshape.268.refs_12_
  424.8 1.8 slice.600
  426.5 27.8 %shard_map.292 = (bf16[8,288,384]{2,1,0:T(8,128)(2,1)}, bf16[8,288,384]{2,1,0:T(8,128)(2,1)}, bf16[8,256,384]{2,1,0:T(8,128)(2,1)}, bf16[8,256,384]{2,1,0:T(8,128)(2,1)}, bf16[768,768]{1,0:T(8,128)(2,1)}) custom-call(bf16[256,768]{1,0:T(8,128)(2,1)} %get-tuple-element.556.refs_0_, bf16[256,3072]{1,0:T(8,128)(2,1)} %get-tuple-element.557.refs_1_, ...), custom_call_target="tpu_custom_call" | custom-call | flops 1 | bytes 1 | tf_op jit(solution)/shard_map/pallas_call | solution.py:351
  455.7 2.6 collective-permute-start.18
  461.0 15.2 %collective-permute-done.18 = bf16[256,768]{1,0:T(8,128)(2,1)S(1)} collective-permute-done((bf16[256,768]{1,0:T(8,128)(2,1)S(1)}, bf16[256,768]{1,0:T(8,128)(2,1)S(1)}, u32[]{:S(2)}, u32[]{:S(2)}) %collective-permute-start.18) | collective-permute-done | bytes 393248 | tf_op jit(solution)/shard_map/ppermute | solution.py:45
  476.5 10.1 %collective-permute-done.31 = bf16[1,256,384]{2,1,0:T(8,128)(2,1)S(1)} collective-permute-done((bf16[1,256,384]{2,1,0:T(8,128)(2,1)S(1)}, bf16[1,256,384]{2,1,0:T(8,128)(2,1)S(1)}, u32[]{:S(2)}, u32[]{:S(2)}) %collective-permute-start.31) | collective-permute-done | bytes 196640 | tf_op jit(solution)/shard_map/ppermute | solution.py:36
  488.5 1.7 add_convert_fusion.12
  490.3 10.5 %collective-permute-done.32 = bf16[1,288,384]{2,1,0:T(8,128)(2,1)S(1)} collective-permute-done((bf16[1,288,384]{2,1,0:T(8,128)(2,1)S(1)}, bf16[1,288,384]{2,1,0:T(8,128)(2,1)S(1)}, u32[]{:S(2)}, u32[]{:S(2)}) %collective-permute-start.32) | collective-permute-done | bytes 221216 | tf_op jit(solution)/shard_map/ppermute | solution.py:36
  503.1 1.4 maximum_select_fusion
  504.6 13.7 %collective-permute-done.29 = bf16[4,240,384]{2,1,0:T(8,128)(2,1)S(1)} collective-permute-done((bf16[4,240,384]{2,1,0:T(8,128)(2,1)S(1)}, bf16[4,240,384]{2,1,0:T(8,128)(2,1)S(1)}, u32[]{:S(2)}, u32[]{:S(2)}) %collective-permute-start.29) | collective-permute-done | bytes 737312 | tf_op jit(solution)/shard_map/ppermute | solution.py:36
  519.2 2.2 collective-permute-done.30
  521.8 5.5 collective-permute-done.36
  529.0 9.8 %collective-permute-done.37 = bf16[1,240,384]{2,1,0:T(8,128)(2,1)S(1)} collective-permute-done((bf16[1,240,384]{2,1,0:T(8,128)(2,1)S(1)}, bf16[1,240,384]{2,1,0:T(8,128)(2,1)S(1)}, u32[]{:S(2)}, u32[]{:S(2)}) %collective-permute-start.37) | collective-permute-done | bytes 184352 | tf_op jit(solution)/shard_map/ppermute | solution.py:36
  538.9 2.1 collective-permute-start.38
  541.1 3.2 collective-permute-start.43
  544.5 9.4 %collective-permute-done.43 = bf16[1,288,384]{2,1,0:T(8,128)(2,1)S(1)} collective-permute-done((bf16[1,288,384]{2,1,0:T(8,128)(2,1)S(1)}, bf16[1,288,384]{2,1,0:T(8,128)(2,1)S(1)}, u32[]{:S(2)}, u32[]{:S(2)}) %collective-permute-start.43) | collective-permute-done | bytes 221216 | tf_op jit(solution)/shard_map/ppermute | solution.py:36
  554.0 1.6 collective-permute-start.44
  556.9 1.7 collective-permute-done.33
  560.9 10.3 %collective-permute-done.34 = bf16[1,256,384]{2,1,0:T(8,128)(2,1)S(1)} collective-permute-done((bf16[1,256,384]{2,1,0:T(8,128)(2,1)S(1)}, bf16[1,256,384]{2,1,0:T(8,128)(2,1)S(1)}, u32[]{:S(2)}, u32[]{:S(2)}) %collective-permute-start.34) | collective-permute-done | bytes 196640 | tf_op jit(solution)/shard_map/ppermute | solution.py:36
  571.3 1.6 collective-permute-done.39
  572.9 1.6 collective-permute-start.40
  575.8 10.1 %collective-permute-done.40 = bf16[1,288,384]{2,1,0:T(8,128)(2,1)S(1)} collective-permute-done((bf16[1,288,384]{2,1,0:T(8,128)(2,1)S(1)}, bf16[1,288,384]{2,1,0:T(8,128)(2,1)S(1)}, u32[]{:S(2)}, u32[]{:S(2)}) %collective-permute-start.40) | collective-permute-done | bytes 221216 | tf_op jit(solution)/shard_map/ppermute | solution.py:36
  (325 shorter events, 55.7 us)
Async XLA Ops:
  1.4 20.5 %slice-start = ((s8[4718592]{0:T(1024)(128)(4,1)}), s8[524288]{0:T(1024)(128)(4,1)S(1)}, s32[]{:S(2)}) async-start(s8[4718592]{0:T(1024)(128)(4,1)} %bitcast.97), calls=%async_computation | async-start | bytes 1048576
  5.9 16.1 %slice-start.1 = ((s8[4718592]{0:T(1024)(128)(4,1)}), s8[4194304]{0:T(1024)(128)(4,1)S(1)}, s32[]{:S(2)}) async-start(s8[4718592]{0:T(1024)(128)(4,1)} %bitcast.97), calls=%async_computation.1 | async-start | bytes 8388608
  21.4 66.5 %collective-permute-start.4 = (bf16[4608,768]{1,0:T(8,128)(2,1)}, bf16[4608,768]{1,0:T(8,128)(2,1)}, u32[]{:S(2)}, u32[]{:S(2)}) collective-permute-start(bf16[4608,768]{1,0:T(8,128)(2,1)} %bitcast.88), channel_id=1, source_target_pairs={{0,16},{16,0},{1,17},{17,1},{2,18},{18,2},{3,19},{19,3},{4,20},{20... | collective-permute-start | bytes 21233672 | tf_op jit(solution)/shard_map/ppermute | solution.py:36
  21.6 43.0 %collective-permute-start.3 = (bf16[3072,768]{1,0:T(8,128)(2,1)}, bf16[3072,768]{1,0:T(8,128)(2,1)}, u32[]{:S(2)}, u32[]{:S(2)}) collective-permute-start(bf16[3072,768]{1,0:T(8,128)(2,1)} %bitcast.100), channel_id=1, source_target_pairs={{0,16},{16,0},{1,17},{17,1},{2,18},{18,2},{3,19},{19,3},{4,20},{20... | collective-permute-start | bytes 14155784 | tf_op jit(solution)/shard_map/ppermute | solution.py:36
  22.0 42.7 %collective-permute-start.2 = (bf16[768,3072]{1,0:T(8,128)(2,1)S(1)}, bf16[768,3072]{1,0:T(8,128)(2,1)}, u32[]{:S(2)}, u32[]{:S(2)}) collective-permute-start(bf16[768,3072]{1,0:T(8,128)(2,1)S(1)} %bitcast.99), channel_id=1, source_target_pairs={{0,16},{16,0},{1,17},{17,1},{2,18},{18,2},{3,19},{19,3},{4,20},{20... | collective-permute-start | bytes 14155784 | tf_op jit(solution)/shard_map/ppermute | solution.py:36
  22.1 42.5 %collective-permute-start = (bf16[768,2304]{1,0:T(8,128)(2,1)}, bf16[768,2304]{1,0:T(8,128)(2,1)}, u32[]{:S(2)}, u32[]{:S(2)}) collective-permute-start(bf16[768,2304]{1,0:T(8,128)(2,1)} %bitcast.110), channel_id=1, source_target_pairs={{0,16},{16,0},{1,17},{17,1},{2,18},{18,2},{3,19},{19,3},{4,20},{20... | collective-permute-start | bytes 10616840 | tf_op jit(solution)/shard_map/ppermute | solution.py:36
  22.5 42.1 %collective-permute-start.1 = (bf16[768,768]{1,0:T(8,128)(2,1)S(1)}, bf16[768,768]{1,0:T(8,128)(2,1)}, u32[]{:S(2)}, u32[]{:S(2)}) collective-permute-start(bf16[768,768]{1,0:T(8,128)(2,1)S(1)} %bitcast.119), channel_id=1, source_target_pairs={{0,16},{16,0},{1,17},{17,1},{2,18},{18,2},{3,19},{19,3},{4,20},{20... | collective-permute-start | bytes 3538952 | tf_op jit(solution)/shard_map/ppermute | solution.py:36
  23.9 38.9 %copy-start.46 = (f32[1,4608]{1,0:T(1,128)S(1)}, f32[1,4608]{1,0:T(1,128)}, u32[]{:S(2)}) copy-start(f32[1,4608]{1,0:T(1,128)} %get-tuple-element.361) | copy-start | bytes 55300
  23.9 39.5 %copy-start.45 = (f32[1,4608]{1,0:T(1,128)S(1)}, f32[1,4608]{1,0:T(1,128)}, u32[]{:S(2)}) copy-start(f32[1,4608]{1,0:T(1,128)} %get-tuple-element.379) | copy-start | bytes 55300
  197.2 19.9 %copy-start.24 = (s32[512,1]{1,0:T(8,128)S(1)}, s32[512,1]{1,0:T(8,128)}, u32[]{:S(2)}) copy-start(s32[512,1]{1,0:T(8,128)} %get-tuple-element.358.ids_ref) | copy-start | bytes 6148
  197.2 19.9 %copy-start.40 = (s32[512,1]{1,0:T(8,128)S(1)}, s32[512,1]{1,0:T(8,128)}, u32[]{:S(2)}) copy-start(s32[512,1]{1,0:T(8,128)} %get-tuple-element.446) | copy-start | bytes 6148
  197.2 23.6 %copy-start.13 = (bf16[256,768]{1,0:T(8,128)(2,1)S(1)}, bf16[256,768]{1,0:T(8,128)(2,1)}, u32[]{:S(2)}) copy-start(bf16[256,768]{1,0:T(8,128)(2,1)} %get-tuple-element.413.q_ref) | copy-start | bytes 1179652
  197.2 23.6 %copy-start.14 = (bf16[256,768]{1,0:T(8,128)(2,1)S(1)}, bf16[256,768]{1,0:T(8,128)(2,1)}, u32[]{:S(2)}) copy-start(bf16[256,768]{1,0:T(8,128)(2,1)} %get-tuple-element.417.do_ref) | copy-start | bytes 1179652
  197.2 23.6 %copy-start.16 = (f32[6,8,256]{2,1,0:T(8,128)S(1)}, f32[6,8,256]{2,1,0:T(8,128)}, u32[]{:S(2)}) copy-start(f32[6,8,256]{2,1,0:T(8,128)} %get-tuple-element.416.lse_ref) | copy-start | bytes 147460
  215.8 51.5 %collective-permute-start.6 = (bf16[8,288,384]{2,1,0:T(8,128)(2,1)}, bf16[8,288,384]{2,1,0:T(8,128)(2,1)}, u32[]{:S(2)}, u32[]{:S(2)}) collective-permute-start(bf16[8,288,384]{2,1,0:T(8,128)(2,1)} %get-tuple-element.410), channel_id=1, source_target_pairs={{0,4},{4,0},{8,12},{12,8},{1,5},{5,1},{9,13},{13,9},{2,6},{6,2},{1... | collective-permute-start | bytes 5308424 | tf_op jit(solution)/shard_map/ppermute | solution.py:36
  217.2 53.0 %collective-permute-start.5 = (bf16[8,240,384]{2,1,0:T(8,128)(2,1)}, bf16[8,240,384]{2,1,0:T(8,128)(2,1)}, u32[]{:S(2)}, u32[]{:S(2)}) collective-permute-start(bf16[8,240,384]{2,1,0:T(8,128)(2,1)} %get-tuple-element.408), channel_id=1, source_target_pairs={{0,8},{4,12},{8,0},{12,4},{1,9},{5,13},{9,1},{13,5},{2,10},{6,14},... | collective-permute-start | bytes 4423688 | tf_op jit(solution)/shard_map/ppermute | solution.py:36
  264.6 42.3 %collective-permute-start.9 = (bf16[256,768]{1,0:T(8,128)(2,1)S(1)}, bf16[256,768]{1,0:T(8,128)(2,1)S(1)}, u32[]{:S(2)}, u32[]{:S(2)}) collective-permute-start(bf16[256,768]{1,0:T(8,128)(2,1)S(1)} %slice.553), channel_id=1, source_target_pairs={{0,2},{1,3},{2,0},{3,1},{4,6},{5,7},{6,4},{7,5},{8,10},{9,11},{10,... | collective-permute-start | bytes 1179656 | tf_op jit(solution)/shard_map/ppermute | solution.py:45
  270.2 66.5 %collective-permute-start.8 = (bf16[4,288,384]{2,1,0:T(8,128)(2,1)}, bf16[4,288,384]{2,1,0:T(8,128)(2,1)S(1)}, u32[]{:S(2)}, u32[]{:S(2)}) collective-permute-start(bf16[4,288,384]{2,1,0:T(8,128)(2,1)} %get-tuple-element.435), channel_id=1, source_target_pairs={{0,8},{4,12},{8,0},{12,4},{1,9},{5,13},{9,1},{13,5},{2,10},{6,14},... | collective-permute-start | bytes 2654216 | tf_op jit(solution)/shard_map/ppermute | solution.py:36
  273.0 33.8 %copy-start.36 = (f32[256,768]{1,0:T(8,128)S(1)}, f32[256,768]{1,0:T(8,128)}, u32[]{:S(2)}) copy-start(f32[256,768]{1,0:T(8,128)} %get-tuple-element.441) | copy-start | bytes 2359300
  305.3 31.6 %collective-permute-start.7 = (bf16[4,240,384]{2,1,0:T(8,128)(2,1)}, bf16[4,240,384]{2,1,0:T(8,128)(2,1)}, u32[]{:S(2)}, u32[]{:S(2)}) collective-permute-start(bf16[4,240,384]{2,1,0:T(8,128)(2,1)} %get-tuple-element.433), channel_id=1, source_target_pairs={{0,4},{4,0},{8,12},{12,8},{1,5},{5,1},{9,13},{13,9},{2,6},{6,2},{1... | collective-permute-start | bytes 2211848 | tf_op jit(solution)/shard_map/ppermute | solution.py:36
  305.6 55.6 %collective-permute-start.11 = (bf16[8,288,384]{2,1,0:T(8,128)(2,1)}, bf16[8,288,384]{2,1,0:T(8,128)(2,1)}, u32[]{:S(2)}, u32[]{:S(2)}) collective-permute-start(bf16[8,288,384]{2,1,0:T(8,128)(2,1)} %get-tuple-element.483), channel_id=1, source_target_pairs={{0,4},{4,0},{8,12},{12,8},{1,5},{5,1},{9,13},{13,9},{2,6},{6,2},{1... | collective-permute-start | bytes 5308424 | tf_op jit(solution)/shard_map/ppermute | solution.py:36
  306.8 57.4 %collective-permute-start.10 = (bf16[8,256,384]{2,1,0:T(8,128)(2,1)}, bf16[8,256,384]{2,1,0:T(8,128)(2,1)}, u32[]{:S(2)}, u32[]{:S(2)}) collective-permute-start(bf16[8,256,384]{2,1,0:T(8,128)(2,1)} %get-tuple-element.481), channel_id=1, source_target_pairs={{0,8},{4,12},{8,0},{12,4},{1,9},{5,13},{9,1},{13,5},{2,10},{6,14},... | collective-permute-start | bytes 4718600 | tf_op jit(solution)/shard_map/ppermute | solution.py:36
  338.2 15.5 %collective-permute-start.13 = (bf16[2,288,384]{2,1,0:T(8,128)(2,1)S(1)}, bf16[2,288,384]{2,1,0:T(8,128)(2,1)S(1)}, u32[]{:S(2)}, u32[]{:S(2)}) collective-permute-start(bf16[2,288,384]{2,1,0:T(8,128)(2,1)S(1)} %get-tuple-element.487), channel_id=1, source_target_pairs={{0,1},{1,0},{2,3},{3,2},{4,5},{5,4},{6,7},{7,6},{8,9},{9,8},{10,11... | collective-permute-start | bytes 1327112 | tf_op jit(solution)/shard_map/ppermute | solution.py:36
  339.2 15.5 %collective-permute-start.12 = (bf16[2,240,384]{2,1,0:T(8,128)(2,1)S(1)}, bf16[2,240,384]{2,1,0:T(8,128)(2,1)S(1)}, u32[]{:S(2)}, u32[]{:S(2)}) collective-permute-start(bf16[2,240,384]{2,1,0:T(8,128)(2,1)S(1)} %get-tuple-element.485), channel_id=1, source_target_pairs={{0,1},{1,0},{2,3},{3,2},{4,5},{5,4},{6,7},{7,6},{8,9},{9,8},{10,11... | collective-permute-start | bytes 1105928 | tf_op jit(solution)/shard_map/ppermute | solution.py:36
  354.9 48.4 %collective-permute-start.17 = (bf16[1,288,384]{2,1,0:T(8,128)(2,1)}, bf16[1,288,384]{2,1,0:T(8,128)(2,1)}, u32[]{:S(2)}, u32[]{:S(2)}) collective-permute-start(bf16[1,288,384]{2,1,0:T(8,128)(2,1)} %get-tuple-element.511), channel_id=1, source_target_pairs={{0,2},{1,3},{2,0},{3,1},{4,6},{5,7},{6,4},{7,5},{8,10},{9,11},{10,... | collective-permute-start | bytes 663560 | tf_op jit(solution)/shard_map/ppermute | solution.py:36
  364.3 43.0 %collective-permute-start.15 = (bf16[4,288,384]{2,1,0:T(8,128)(2,1)}, bf16[4,288,384]{2,1,0:T(8,128)(2,1)}, u32[]{:S(2)}, u32[]{:S(2)}) collective-permute-start(bf16[4,288,384]{2,1,0:T(8,128)(2,1)} %get-tuple-element.507), channel_id=1, source_target_pairs={{0,8},{4,12},{8,0},{12,4},{1,9},{5,13},{9,1},{13,5},{2,10},{6,14},... | collective-permute-start | bytes 2654216 | tf_op jit(solution)/shard_map/ppermute | solution.py:36
  367.2 43.4 %collective-permute-start.14 = (bf16[4,256,384]{2,1,0:T(8,128)(2,1)}, bf16[4,256,384]{2,1,0:T(8,128)(2,1)}, u32[]{:S(2)}, u32[]{:S(2)}) collective-permute-start(bf16[4,256,384]{2,1,0:T(8,128)(2,1)} %get-tuple-element.505), channel_id=1, source_target_pairs={{0,4},{4,0},{8,12},{12,8},{1,5},{5,1},{9,13},{13,9},{2,6},{6,2},{1... | collective-permute-start | bytes 2359304 | tf_op jit(solution)/shard_map/ppermute | solution.py:36
  368.1 19.1 %copy-start.7 = (bf16[1024,768]{1,0:T(8,128)(2,1)S(1)}, bf16[1024,768]{1,0:T(8,128)(2,1)}, u32[]{:S(2)}) copy-start(bf16[1024,768]{1,0:T(8,128)(2,1)} %get-tuple-element.514.k_ref) | copy-start | bytes 4718596
  368.1 19.1 %copy-start.11 = (bf16[256,768]{1,0:T(8,128)(2,1)S(1)}, bf16[256,768]{1,0:T(8,128)(2,1)}, u32[]{:S(2)}) copy-start(bf16[256,768]{1,0:T(8,128)(2,1)} %get-tuple-element.513.q_ref) | copy-start | bytes 1179652
  368.1 19.1 %copy-start.12 = (bf16[256,768]{1,0:T(8,128)(2,1)S(1)}, bf16[256,768]{1,0:T(8,128)(2,1)}, u32[]{:S(2)}) copy-start(bf16[256,768]{1,0:T(8,128)(2,1)} %get-tuple-element.528.do_ref) | copy-start | bytes 1179652
  368.1 19.1 %copy-start.15 = (f32[6,8,256]{2,1,0:T(8,128)S(1)}, f32[6,8,256]{2,1,0:T(8,128)}, u32[]{:S(2)}) copy-start(f32[6,8,256]{2,1,0:T(8,128)} %get-tuple-element.516.lse_ref) | copy-start | bytes 147460
  385.4 19.2 %collective-permute-start.16 = (bf16[1,240,384]{2,1,0:T(8,128)(2,1)S(1)}, bf16[1,240,384]{2,1,0:T(8,128)(2,1)S(1)}, u32[]{:S(2)}, u32[]{:S(2)}) collective-permute-start(bf16[1,240,384]{2,1,0:T(8,128)(2,1)S(1)} %get-tuple-element.509), channel_id=1, source_target_pairs={{0,2},{1,3},{2,0},{3,1},{4,6},{5,7},{6,4},{7,5},{8,10},{9,11},{10,... | collective-permute-start | bytes 552968 | tf_op jit(solution)/shard_map/ppermute | solution.py:36
  404.6 82.5 %collective-permute-start.24 = (bf16[8,288,384]{2,1,0:T(8,128)(2,1)}, bf16[8,288,384]{2,1,0:T(8,128)(2,1)S(1)}, u32[]{:S(2)}, u32[]{:S(2)}) collective-permute-start(bf16[8,288,384]{2,1,0:T(8,128)(2,1)} %get-tuple-element.581), channel_id=1, source_target_pairs={{0,4},{4,0},{8,12},{12,8},{1,5},{5,1},{9,13},{13,9},{2,6},{6,2},{1... | collective-permute-start | bytes 5308424 | tf_op jit(solution)/shard_map/ppermute | solution.py:36
  406.0 81.7 %collective-permute-start.23 = (bf16[8,240,384]{2,1,0:T(8,128)(2,1)}, bf16[8,240,384]{2,1,0:T(8,128)(2,1)}, u32[]{:S(2)}, u32[]{:S(2)}) collective-permute-start(bf16[8,240,384]{2,1,0:T(8,128)(2,1)} %get-tuple-element.579), channel_id=1, source_target_pairs={{0,8},{4,12},{8,0},{12,4},{1,9},{5,13},{9,1},{13,5},{2,10},{6,14},... | collective-permute-start | bytes 4423688 | tf_op jit(solution)/shard_map/ppermute | solution.py:36
  409.4 45.7 %collective-permute-start.26 = (bf16[2,288,384]{2,1,0:T(8,128)(2,1)}, bf16[2,288,384]{2,1,0:T(8,128)(2,1)}, u32[]{:S(2)}, u32[]{:S(2)}) collective-permute-start(bf16[2,288,384]{2,1,0:T(8,128)(2,1)} %get-tuple-element.585), channel_id=1, source_target_pairs={{0,1},{1,0},{2,3},{3,2},{4,5},{5,4},{6,7},{7,6},{8,9},{9,8},{10,11... | collective-permute-start | bytes 1327112 | tf_op jit(solution)/shard_map/ppermute | solution.py:36
  412.7 46.9 %collective-permute-start.25 = (bf16[2,256,384]{2,1,0:T(8,128)(2,1)}, bf16[2,256,384]{2,1,0:T(8,128)(2,1)}, u32[]{:S(2)}, u32[]{:S(2)}) collective-permute-start(bf16[2,256,384]{2,1,0:T(8,128)(2,1)} %get-tuple-element.583), channel_id=1, source_target_pairs={{0,1},{1,0},{2,3},{3,2},{4,5},{5,4},{6,7},{7,6},{8,9},{9,8},{10,11... | collective-permute-start | bytes 1179656 | tf_op jit(solution)/shard_map/ppermute | solution.py:36
  426.5 28.1 %copy-start.18 = (bf16[512,768]{1,0:T(8,128)(2,1)S(1)}, bf16[512,768]{1,0:T(8,128)(2,1)}, u32[]{:S(2)}) copy-start(bf16[512,768]{1,0:T(8,128)(2,1)} %get-tuple-element.573.refs_2_) | copy-start | bytes 2359300
  426.5 28.1 %copy-start.21 = (bf16[512,768]{1,0:T(8,128)(2,1)S(1)}, bf16[512,768]{1,0:T(8,128)(2,1)}, u32[]{:S(2)}) copy-start(bf16[512,768]{1,0:T(8,128)(2,1)} %get-tuple-element.574) | copy-start | bytes 2359300
  454.4 50.2 %collective-permute-start.21 = (bf16[8,256,384]{2,1,0:T(8,128)(2,1)}, bf16[8,256,384]{2,1,0:T(8,128)(2,1)S(1)}, u32[]{:S(2)}, u32[]{:S(2)}) collective-permute-start(bf16[8,256,384]{2,1,0:T(8,128)(2,1)} %get-tuple-element.575), channel_id=1, source_target_pairs={{0,8},{4,12},{8,0},{12,4},{1,9},{5,13},{9,1},{13,5},{2,10},{6,14},... | collective-permute-start | bytes 4718600 | tf_op jit(solution)/shard_map/ppermute | solution.py:36
  455.1 21.2 %copy-start.32 = (bf16[256,768]{1,0:T(8,128)(2,1)S(1)}, bf16[256,768]{1,0:T(8,128)(2,1)}, u32[]{:S(2)}) copy-start(bf16[256,768]{1,0:T(8,128)(2,1)} %get-tuple-element.572) | copy-start | bytes 1179652
  455.1 21.1 %copy-start.37 = (f32[256,768]{1,0:T(8,128)S(1)}, f32[256,768]{1,0:T(8,128)}, u32[]{:S(2)}) copy-start(f32[256,768]{1,0:T(8,128)} %get-tuple-element.554) | copy-start | bytes 2359300
  455.1 21.1 %copy-start.38 = (bf16[768,768]{1,0:T(8,128)(2,1)S(1)}, bf16[768,768]{1,0:T(8,128)(2,1)}, u32[]{:S(2)}) copy-start(bf16[768,768]{1,0:T(8,128)(2,1)} %get-tuple-element.571) | copy-start | bytes 3538948
  455.7 20.5 %collective-permute-start.18 = (bf16[256,768]{1,0:T(8,128)(2,1)S(1)}, bf16[256,768]{1,0:T(8,128)(2,1)S(1)}, u32[]{:S(2)}, u32[]{:S(2)}) collective-permute-start(bf16[256,768]{1,0:T(8,128)(2,1)S(1)} %copy-done.39), channel_id=1, source_target_pairs={{0,2},{1,3},{2,0},{3,1},{4,6},{5,7},{6,4},{7,5},{8,10},{9,11},{10,... | collective-permute-start | bytes 1179656 | tf_op jit(solution)/shard_map/ppermute | solution.py:45
  459.6 62.2 %collective-permute-start.22 = (bf16[8,288,384]{2,1,0:T(8,128)(2,1)S(1)}, bf16[8,288,384]{2,1,0:T(8,128)(2,1)S(1)}, u32[]{:S(2)}, u32[]{:S(2)}) collective-permute-start(bf16[8,288,384]{2,1,0:T(8,128)(2,1)S(1)} %copy-done.60), channel_id=1, source_target_pairs={{0,4},{4,0},{8,12},{12,8},{1,5},{5,1},{9,13},{13,9},{2,6},{6,2},{1... | collective-permute-start | bytes 5308424 | tf_op jit(solution)/shard_map/ppermute | solution.py:36
  476.2 10.4 %collective-permute-start.31 = (bf16[1,256,384]{2,1,0:T(8,128)(2,1)S(1)}, bf16[1,256,384]{2,1,0:T(8,128)(2,1)S(1)}, u32[]{:S(2)}, u32[]{:S(2)}) collective-permute-start(bf16[1,256,384]{2,1,0:T(8,128)(2,1)S(1)} %get-tuple-element.618), channel_id=1, source_target_pairs={{0,2},{1,3},{2,0},{3,1},{4,6},{5,7},{6,4},{7,5},{8,10},{9,11},{10,... | collective-permute-start | bytes 589832 | tf_op jit(solution)/shard_map/ppermute | solution.py:36
  486.7 16.5 %collective-permute-start.20 = (bf16[512,768]{1,0:T(8,128)(2,1)S(1)}, bf16[512,768]{1,0:T(8,128)(2,1)S(1)}, u32[]{:S(2)}, u32[]{:S(2)}) collective-permute-start(bf16[512,768]{1,0:T(8,128)(2,1)S(1)} %bitcast.132), channel_id=1, source_target_pairs={{0,16},{16,0},{1,17},{17,1},{2,18},{18,2},{3,19},{19,3},{4,20},{20... | collective-permute-start | bytes 2359304 | tf_op jit(solution)/shard_map/ppermute | solution.py:36
  487.2 13.8 %collective-permute-start.19 = (bf16[256,768]{1,0:T(8,128)(2,1)S(1)}, bf16[256,768]{1,0:T(8,128)(2,1)S(1)}, u32[]{:S(2)}, u32[]{:S(2)}) collective-permute-start(bf16[256,768]{1,0:T(8,128)(2,1)S(1)} %get-tuple-element.684), channel_id=1, source_target_pairs={{0,16},{16,0},{1,17},{17,1},{2,18},{18,2},{3,19},{19,3},{4,20},{20... | collective-permute-start | bytes 1179656 | tf_op jit(solution)/shard_map/ppermute | solution.py:36
  487.7 13.0 %collective-permute-start.32 = (bf16[1,288,384]{2,1,0:T(8,128)(2,1)S(1)}, bf16[1,288,384]{2,1,0:T(8,128)(2,1)S(1)}, u32[]{:S(2)}, u32[]{:S(2)}) collective-permute-start(bf16[1,288,384]{2,1,0:T(8,128)(2,1)S(1)} %get-tuple-element.620), channel_id=1, source_target_pairs={{0,2},{1,3},{2,0},{3,1},{4,6},{5,7},{6,4},{7,5},{8,10},{9,11},{10,... | collective-permute-start | bytes 663560 | tf_op jit(solution)/shard_map/ppermute | solution.py:36
  500.7 17.6 %collective-permute-start.29 = (bf16[4,240,384]{2,1,0:T(8,128)(2,1)S(1)}, bf16[4,240,384]{2,1,0:T(8,128)(2,1)S(1)}, u32[]{:S(2)}, u32[]{:S(2)}) collective-permute-start(bf16[4,240,384]{2,1,0:T(8,128)(2,1)S(1)} %get-tuple-element.614), channel_id=1, source_target_pairs={{0,4},{4,0},{8,12},{12,8},{1,5},{5,1},{9,13},{13,9},{2,6},{6,2},{1... | collective-permute-start | bytes 2211848 | tf_op jit(solution)/shard_map/ppermute | solution.py:36
  501.0 20.5 %collective-permute-start.30 = (bf16[4,288,384]{2,1,0:T(8,128)(2,1)S(1)}, bf16[4,288,384]{2,1,0:T(8,128)(2,1)S(1)}, u32[]{:S(2)}, u32[]{:S(2)}) collective-permute-start(bf16[4,288,384]{2,1,0:T(8,128)(2,1)S(1)} %get-tuple-element.616), channel_id=1, source_target_pairs={{0,8},{4,12},{8,0},{12,4},{1,9},{5,13},{9,1},{13,5},{2,10},{6,14},... | collective-permute-start | bytes 2654216 | tf_op jit(solution)/shard_map/ppermute | solution.py:36
  518.5 8.8 %collective-permute-start.36 = (bf16[2,240,384]{2,1,0:T(8,128)(2,1)S(1)}, bf16[2,240,384]{2,1,0:T(8,128)(2,1)S(1)}, u32[]{:S(2)}, u32[]{:S(2)}) collective-permute-start(bf16[2,240,384]{2,1,0:T(8,128)(2,1)S(1)} %get-tuple-element.655), channel_id=1, source_target_pairs={{0,1},{1,0},{2,3},{3,2},{4,5},{5,4},{6,7},{7,6},{8,9},{9,8},{10,11... | collective-permute-start | bytes 1105928 | tf_op jit(solution)/shard_map/ppermute | solution.py:36
  519.0 25.3 %collective-permute-start.27 = (bf16[4,256,384]{2,1,0:T(8,128)(2,1)S(1)}, bf16[4,256,384]{2,1,0:T(8,128)(2,1)S(1)}, u32[]{:S(2)}, u32[]{:S(2)}) collective-permute-start(bf16[4,256,384]{2,1,0:T(8,128)(2,1)S(1)} %get-tuple-element.610), channel_id=1, source_target_pairs={{0,4},{4,0},{8,12},{12,8},{1,5},{5,1},{9,13},{13,9},{2,6},{6,2},{1... | collective-permute-start | bytes 2359304 | tf_op jit(solution)/shard_map/ppermute | solution.py:36
  521.7 19.3 %collective-permute-start.42 = (bf16[2,288,384]{2,1,0:T(8,128)(2,1)S(1)}, bf16[2,288,384]{2,1,0:T(8,128)(2,1)S(1)}, u32[]{:S(2)}, u32[]{:S(2)}) collective-permute-start(bf16[2,288,384]{2,1,0:T(8,128)(2,1)S(1)} %get-tuple-element.673), channel_id=1, source_target_pairs={{0,1},{1,0},{2,3},{3,2},{4,5},{5,4},{6,7},{7,6},{8,9},{9,8},{10,11... | collective-permute-start | bytes 1327112 | tf_op jit(solution)/shard_map/ppermute | solution.py:36
  527.4 11.4 %collective-permute-start.37 = (bf16[1,240,384]{2,1,0:T(8,128)(2,1)S(1)}, bf16[1,240,384]{2,1,0:T(8,128)(2,1)S(1)}, u32[]{:S(2)}, u32[]{:S(2)}) collective-permute-start(bf16[1,240,384]{2,1,0:T(8,128)(2,1)S(1)} %get-tuple-element.659), channel_id=1, source_target_pairs={{0,2},{1,3},{2,0},{3,1},{4,6},{5,7},{6,4},{7,5},{8,10},{9,11},{10,... | collective-permute-start | bytes 552968 | tf_op jit(solution)/shard_map/ppermute | solution.py:36
  527.9 28.6 %collective-permute-start.28 = (bf16[4,288,384]{2,1,0:T(8,128)(2,1)S(1)}, bf16[4,288,384]{2,1,0:T(8,128)(2,1)S(1)}, u32[]{:S(2)}, u32[]{:S(2)}) collective-permute-start(bf16[4,288,384]{2,1,0:T(8,128)(2,1)S(1)} %get-tuple-element.612), channel_id=1, source_target_pairs={{0,8},{4,12},{8,0},{12,4},{1,9},{5,13},{9,1},{13,5},{2,10},{6,14},... | collective-permute-start | bytes 2654216 | tf_op jit(solution)/shard_map/ppermute | solution.py:36
  538.9 16.8 %collective-permute-start.38 = (f32[240,384]{1,0:T(8,128)S(1)}, f32[240,384]{1,0:T(8,128)S(1)}, u32[]{:S(2)}, u32[]{:S(2)}) collective-permute-start(f32[240,384]{1,0:T(8,128)S(1)} %broadcast_select_fusion.16), channel_id=1, source_target_pairs={{0,16},{16,0},{1,17},{17,1},{2,18},{18,2},{3,19},{19,3},{4,20},{20... | collective-permute-start | bytes 1105928 | tf_op jit(solution)/shard_map/ppermute | solution.py:36
  541.1 12.8 %collective-permute-start.43 = (bf16[1,288,384]{2,1,0:T(8,128)(2,1)S(1)}, bf16[1,288,384]{2,1,0:T(8,128)(2,1)S(1)}, u32[]{:S(2)}, u32[]{:S(2)}) collective-permute-start(bf16[1,288,384]{2,1,0:T(8,128)(2,1)S(1)} %get-tuple-element.679), channel_id=1, source_target_pairs={{0,2},{1,3},{2,0},{3,1},{4,6},{5,7},{6,4},{7,5},{8,10},{9,11},{10,... | collective-permute-start | bytes 663560 | tf_op jit(solution)/shard_map/ppermute | solution.py:36
  544.4 14.2 %collective-permute-start.33 = (bf16[2,256,384]{2,1,0:T(8,128)(2,1)S(1)}, bf16[2,256,384]{2,1,0:T(8,128)(2,1)S(1)}, u32[]{:S(2)}, u32[]{:S(2)}) collective-permute-start(bf16[2,256,384]{2,1,0:T(8,128)(2,1)S(1)} %get-tuple-element.646), channel_id=1, source_target_pairs={{0,1},{1,0},{2,3},{3,2},{4,5},{5,4},{6,7},{7,6},{8,9},{9,8},{10,11... | collective-permute-start | bytes 1179656 | tf_op jit(solution)/shard_map/ppermute | solution.py:36
  554.0 5.7 collective-permute-start.44
  556.8 16.1 %collective-permute-start.39 = (bf16[2,288,384]{2,1,0:T(8,128)(2,1)S(1)}, bf16[2,288,384]{2,1,0:T(8,128)(2,1)S(1)}, u32[]{:S(2)}, u32[]{:S(2)}) collective-permute-start(bf16[2,288,384]{2,1,0:T(8,128)(2,1)S(1)} %get-tuple-element.664), channel_id=1, source_target_pairs={{0,1},{1,0},{2,3},{3,2},{4,5},{5,4},{6,7},{7,6},{8,9},{9,8},{10,11... | collective-permute-start | bytes 1327112 | tf_op jit(solution)/shard_map/ppermute | solution.py:36
  558.7 12.5 %collective-permute-start.34 = (bf16[1,256,384]{2,1,0:T(8,128)(2,1)S(1)}, bf16[1,256,384]{2,1,0:T(8,128)(2,1)S(1)}, u32[]{:S(2)}, u32[]{:S(2)}) collective-permute-start(bf16[1,256,384]{2,1,0:T(8,128)(2,1)S(1)} %get-tuple-element.650), channel_id=1, source_target_pairs={{0,2},{1,3},{2,0},{3,1},{4,6},{5,7},{6,4},{7,5},{8,10},{9,11},{10,... | collective-permute-start | bytes 589832 | tf_op jit(solution)/shard_map/ppermute | solution.py:36
  572.9 12.9 %collective-permute-start.40 = (bf16[1,288,384]{2,1,0:T(8,128)(2,1)S(1)}, bf16[1,288,384]{2,1,0:T(8,128)(2,1)S(1)}, u32[]{:S(2)}, u32[]{:S(2)}) collective-permute-start(bf16[1,288,384]{2,1,0:T(8,128)(2,1)S(1)} %get-tuple-element.668), channel_id=1, source_target_pairs={{0,2},{1,3},{2,0},{3,1},{4,6},{5,7},{6,4},{7,5},{8,10},{9,11},{10,... | collective-permute-start | bytes 663560 | tf_op jit(solution)/shard_map/ppermute | solution.py:36
  574.6 12.1 %collective-permute-start.35 = (f32[256,384]{1,0:T(8,128)S(1)}, f32[256,384]{1,0:T(8,128)S(1)}, u32[]{:S(2)}, u32[]{:S(2)}) collective-permute-start(f32[256,384]{1,0:T(8,128)S(1)} %broadcast_select_fusion.12), channel_id=1, source_target_pairs={{0,16},{16,0},{1,17},{17,1},{2,18},{18,2},{3,19},{19,3},{4,20},{20... | collective-permute-start | bytes 1179656 | tf_op jit(solution)/shard_map/ppermute | solution.py:36
  586.0 4.9 collective-permute-start.41
  (44 other events, 262.0 us)
